TPU v7x, 256 devices: a whole 4x4x8 slice. The times are simulated.
256 devices in a mesh: row: 16 (over y, x_lo, core), col: 16 (over x_hi, z).
Axes of the slice: x: 4 (x_hi: 2, x_lo: 2; x = x_hi * 2 + x_lo), y: 4, z: 8, core: 2. Of those that a mesh axis runs over, the one named last changes fastest.
Arguments:
- features: bfloat16 [131072, 128], P(('row', 'col')), may hold values from -6 to 6
- weight: bfloat16 [128, 256], replicated, may hold values from -0.5 to 0.5
- grad_out: bfloat16 [131072, 256], P(('row', 'col')), may hold values from -6 to 6
- tile_rows: int32 [16, 16, 48], P('row', 'col'), may hold values from 0 to 63
- tile_cols: int32 [16, 16, 48], P('row', 'col'), may hold values from 0 to 63
- tile_vals: bfloat16 [16, 16, 48, 128, 128], P('row', 'col'), as said below
- tile_count: int32 [16, 16], P('row', 'col'), may hold values from 12 to 48, as said below
Outputs:
- activation: bfloat16 [131072, 256], P(('row', 'col'))
- grad_features: bfloat16 [131072, 128], P(('row', 'col'))
- grad_weight: float32 [128, 256], replicated
Inputs may be any that keep to these rules, and one draw needn't show every extreme that they name: `tile_count`: one device holds exactly 48 live slots. `tile_vals`: each entry of a tile is nonzero with probability 2 / 128.
All inputs are finite; a program needn't handle non-finite values.
Results may differ from a plain program's by a relative error of at most 0.006.
Values may be sent and summed in bfloat16 or wider, within the bound.
No kernel may reach another device: no remote copies, remote signals or barrier semaphores. Data moves between devices by JAX's collectives and lax.ppermute only.
A program may use at most 64 MiB of HBM per device.

v0:
```python
import jax
import jax.numpy as jnp
from jax import lax
from jax.sharding import PartitionSpec as P


def body(features, weight, grad_out, tile_rows, tile_cols, tile_vals, tile_count):
    slot_count = tile_rows.shape[2]
    block = tile_vals.shape[3]
    width = weight.shape[1]
    rows_index = tile_rows[0, 0]
    cols_index = tile_cols[0, 0]
    values = tile_vals[0, 0]
    live = (jnp.arange(slot_count, dtype=jnp.int32) < tile_count[0, 0]).astype(jnp.float32)
    row_nodes = lax.axis_size("col") * features.shape[0]
    col_nodes = lax.axis_size("row") * features.shape[0]
    row_tiles = row_nodes // block
    col_tiles = col_nodes // block
    own_hidden = jnp.dot(features, weight, preferred_element_type=jnp.float32).astype(jnp.bfloat16)
    panel = lax.all_gather(own_hidden, "row", axis=0, tiled=True)
    col_blocks = panel.reshape(col_tiles, block, width)[cols_index]
    forward_prod = (
        jnp.einsum("tab,tbh->tah", values, col_blocks, preferred_element_type=jnp.float32)
        * live[:, None, None]
    )
    row_partial = jax.ops.segment_sum(forward_prod, rows_index, num_segments=row_tiles).reshape(
        row_nodes, width
    )
    pre = lax.psum_scatter(row_partial, "col", scatter_dimension=0, tiled=True)
    sig = 1.0 / (1.0 + jnp.exp(-pre))
    activation = (pre * sig).astype(jnp.bfloat16)
    grad_pre = (grad_out.astype(jnp.float32) * sig * (1.0 + pre * (1.0 - sig))).astype(jnp.bfloat16)
    grad_rows = lax.all_gather(grad_pre, "col", axis=0, tiled=True)
    row_blocks = grad_rows.reshape(row_tiles, block, width)[rows_index]
    backward_prod = (
        jnp.einsum("tab,tah->tbh", values, row_blocks, preferred_element_type=jnp.float32)
        * live[:, None, None]
    )
    col_partial = jax.ops.segment_sum(backward_prod, cols_index, num_segments=col_tiles).reshape(
        col_nodes, width
    )
    grad_hidden = lax.psum_scatter(col_partial, "row", scatter_dimension=0, tiled=True).astype(
        jnp.bfloat16
    )
    grad_features = lax.dot_general(
        grad_hidden, weight, (((1,), (1,)), ((), ())), preferred_element_type=jnp.float32
    ).astype(jnp.bfloat16)
    weight_part = lax.dot_general(
        features, grad_hidden, (((0,), (0,)), ((), ())), preferred_element_type=jnp.float32
    )
    grad_weight = lax.psum(weight_part, ("row", "col"))
    return (activation, grad_features, grad_weight)


def solution(mesh):
    return jax.shard_map(
        body,
        mesh=mesh,
        in_specs=(
            P(("row", "col"), None),
            P(),
            P(("row", "col"), None),
            P("row", "col", None),
            P("row", "col", None),
            P("row", "col", None, None, None),
            P("row", "col"),
        ),
        out_specs=(P(("row", "col"), None), P(("row", "col"), None), P()),
        check_vma=False,
    )
```

profile of v0, /device:TPU:1, one launch (start us, length us, event | category | flops | bytes accessed | tf_op | source)
XLA Modules:
  0.0 801.8 jit_solution(16912437263096915489)
XLA Ops:
  7.2 0.0 copy-start
  7.2 0.0 all-gather.3.cloned.1.call-start
  7.2 1.9 convolution_convert_fusion
  9.2 0.0 all-gather.3.cloned.1.call-update
  9.2 0.0 reduce-scatter.3.cloned.1.call-start
  9.9 0.7 fusion.4
  10.6 44.0 %all-gather.3.cloned.1.call-done = bf16[8192,256]{1,0:T(8,128)(2,1)} async-done(((bf16[512,256]{1,0:T(8,128)(2,1)}), bf16[8192,256]{1,0:T(8,128)(2,1)}) %all-gather.3.cloned.1.call-update) | async-done | bytes 4194320 | tf_op jit(solution)/shard_map/all_gather | solution.py:20
  54.6 4.7 gather_fusion
  59.3 5.9 multiply_bitcast_fusion.1
  65.2 6.6 copy.14
  71.9 4.3 broadcast.46.clone
  76.1 14.8 %scatter_fusion = f32[64,128,256]{2,1,0:T(8,128)} fusion(f32[64,128,256]{2,1,0:T(8,128)} %broadcast.46.clone, s32[48]{0:T(128)S(1)} %bitcast.37, f32[48,128,256]{2,1,0:T(8,128)} %copy.14), kind=kCustom, calls=%fused_computation.2 | custom fusion | flops 1572864 | bytes 18874560 | tf_op jit(solution)/shard_map/scatter-add | solution.py:26
  90.9 0.0 reduce-scatter.3.cloned.1.call-update
  91.0 0.0 all-gather.5.cloned.1.call-start
  91.0 218.5 %reduce-scatter.3.cloned.1.call-done = f32[512,256]{1,0:T(8,128)} async-done(((f32[8192,256]{1,0:T(8,128)}), f32[512,256]{1,0:T(8,128)}) %reduce-scatter.3.cloned.1.call-update) | async-done | bytes 524304 | tf_op jit(solution)/shard_map/reduce_scatter | solution.py:29
  309.6 2.1 multiply_convert_fusion
  311.6 0.0 all-gather.5.cloned.1.call-update
  311.7 0.0 reduce-scatter.5.cloned.1.call-start
  311.7 99.7 %all-gather.5.cloned.1.call-done = bf16[8192,256]{1,0:T(8,128)(2,1)} async-done(((bf16[512,256]{1,0:T(8,128)(2,1)}), bf16[8192,256]{1,0:T(8,128)(2,1)}) %all-gather.5.cloned.1.call-update) | async-done | bytes 4194320 | tf_op jit(solution)/shard_map/all_gather | solution.py:33
  411.4 4.7 gather_fusion.1
  416.2 5.9 multiply_bitcast_fusion
  422.1 6.6 copy.16
  428.7 4.3 broadcast.46
  433.0 14.7 %scatter_fusion.1 = f32[64,128,256]{2,1,0:T(8,128)} fusion(f32[64,128,256]{2,1,0:T(8,128)} %broadcast.46, s32[48]{0:T(128)S(1)} %bitcast.38, f32[48,128,256]{2,1,0:T(8,128)} %copy.16), kind=kCustom, calls=%fused_computation.3 | custom fusion | flops 1572864 | bytes 18874560 | tf_op jit(solution)/shard_map/scatter-add | solution.py:39
  447.6 0.0 reduce-scatter.5.cloned.1.call-update
  447.7 0.0 all-reduce.2.cloned.1.call-start
  447.7 98.6 %reduce-scatter.5.cloned.1.call-done = f32[512,256]{1,0:T(8,128)} async-done(((f32[8192,256]{1,0:T(8,128)}), f32[512,256]{1,0:T(8,128)}) %reduce-scatter.5.cloned.1.call-update) | async-done | bytes 524304 | tf_op jit(solution)/shard_map/reduce_scatter | solution.py:42
  546.3 2.0 convolution_bitcast_fusion
  548.3 0.0 all-reduce.2.cloned.1.call-update
  548.3 1.9 convolution_convert_fusion.1
  550.3 243.3 %all-reduce.2.cloned.1.call-done = f32[128,256]{0,1:T(8,128)} async-done(((f32[128,256]{0,1:T(8,128)}), f32[128,256]{0,1:T(8,128)}) %all-reduce.2.cloned.1.call-update) | async-done | bytes 131088 | tf_op jit(solution)/shard_map/psum | solution.py:51
  793.6 1.7 copy.17
  (15 shorter events, 0.0 us)
Async XLA Ops:
  7.2 52.2 %copy-start = (bf16[1,1,48,128,128]{4,3,2,1,0:T(8,128)(2,1)S(1)}, bf16[1,1,48,128,128]{4,3,2,1,0:T(8,128)(2,1)}, u32[]{:S(2)}) copy-start(bf16[1,1,48,128,128]{4,3,2,1,0:T(8,128)(2,1)} %param.12) | copy-start | bytes 4718596
  7.2 47.4 %all-gather.3.cloned.1.call-start = ((), (), s32[]{:S(2)}) async-start(), calls=%async_computation.2 | async-start | bytes 4456448 | tf_op jit(solution)/shard_map/all_gather | solution.py:20
  9.2 300.4 %reduce-scatter.3.cloned.1.call-start = ((), (), s32[]{:S(2)}) async-start(), calls=%async_computation.3 | async-start | bytes 8912896 | tf_op jit(solution)/shard_map/reduce_scatter | solution.py:29
  71.9 4.3 copy-start.4
  90.9 218.6 %copy-start.2 = (bf16[512,256]{1,0:T(8,128)(2,1)S(1)}, bf16[512,256]{1,0:T(8,128)(2,1)}, u32[]{:S(2)}) copy-start(bf16[512,256]{1,0:T(8,128)(2,1)} %param.9) | copy-start | bytes 786436
  91.0 320.4 %all-gather.5.cloned.1.call-start = ((), (), s32[]{:S(2)}) async-start(), calls=%async_computation.4 | async-start | bytes 4456448 | tf_op jit(solution)/shard_map/all_gather | solution.py:33
  311.7 234.7 %reduce-scatter.5.cloned.1.call-start = ((), (), s32[]{:S(2)}) async-start(), calls=%async_computation.5 | async-start | bytes 8912896 | tf_op jit(solution)/shard_map/reduce_scatter | solution.py:42
  428.7 4.3 copy-start.5
  447.6 98.7 %copy-start.1 = (bf16[512,128]{1,0:T(8,128)(2,1)S(1)}, bf16[512,128]{1,0:T(8,128)(2,1)}, u32[]{:S(2)}) copy-start(bf16[512,128]{1,0:T(8,128)(2,1)} %param.7) | copy-start | bytes 393220
  447.6 100.7 %copy-start.3 = (bf16[128,256]{1,0:T(8,128)(2,1)S(1)}, bf16[128,256]{1,0:T(8,128)(2,1)}, u32[]{:S(2)}) copy-start(bf16[128,256]{1,0:T(8,128)(2,1)} %param.8) | copy-start | bytes 196612
  447.7 345.9 %all-reduce.2.cloned.1.call-start = ((), (), s32[]{:S(2)}) async-start(), calls=%async_computation.6 | async-start | bytes 262144 | tf_op jit(solution)/shard_map/psum | solution.py:51
Sparse Core Ops, SparseCore 0:
  10.4 44.0 all-gather.2
  91.1 218.4 reduce-scatter.2
  312.1 99.2 all-gather.4
  447.8 98.4 reduce-scatter.4
  552.3 241.3 all-reduce.1
where the time goes:
time: 803 us; the launch traced here: 802 us
  waiting for transfers between devices  704 us (88%)
  local copies, waits for them, and re-layouts  32.9 us (4%)
  other arithmetic  32.2 us (4%)
  matrix products  17.7 us (2%)
  between operations  14.5 us (2%)
    psum x1, waiting for transfers between devices, body(): grad_weight = lax.psum(weight_part, ('row', 'col'))  243 us
    reduce_scatter x1, waiting for transfers between devices, body(): pre = lax.psum_scatter(row_partial, 'col', scatter_dimension=0, tiled=True)  219 us
    all_gather x1, waiting for transfers between devices, body(): grad_rows = lax.all_gather(grad_pre, 'col', axis=0, tiled=True)  99.7 us
    reduce_scatter x1, waiting for transfers between devices, body(): lax.psum_scatter(col_partial, 'row', scatter_dimension=0, tiled=True)  98.6 us
    all_gather x1, waiting for transfers between devices, body(): panel = lax.all_gather(own_hidden, 'row', axis=0, tiled=True)  44 us
  transfers between devices with their start and end apart: 5, of which 5 were waited for; matrix products, arithmetic and copies ran while one was open for 0% of the time, Pallas kernels for 0%

commit v1 on v0

v1 whole, which is shorter than its diff:
```python
import functools

import jax
import jax.numpy as jnp
from jax import lax
from jax.experimental import pallas as pl
from jax.experimental.pallas import tpu as pltpu
from jax.sharding import PartitionSpec as P

BF16 = jnp.bfloat16
F32 = jnp.float32
NY, NXL, NC, NXH, NZ = 4, 2, 2, 2, 8
SHARD = 512
BLOCK = 128
VMEM_LIMIT = 40 * 1024 * 1024


def send_row(x, dy=0, dx=0, dc=0):
    perm = []
    for y in range(NY):
        for a in range(NXL):
            for c in range(NC):
                perm.append(((y * NXL + a) * NC + c, ((y + dy) % NY * NXL + (a ^ dx)) * NC + (c ^ dc)))
    return lax.ppermute(x, "row", perm)


def send_col(x, dh=0, dz=0):
    perm = []
    for h in range(NXH):
        for z in range(NZ):
            perm.append((h * NZ + z, (h ^ dh) * NZ + (z + dz) % NZ))
    return lax.ppermute(x, "col", perm)


def swap(x, axis, count, bit):
    return lax.ppermute(x, axis, [(i, i ^ bit) for i in range(count)])


def all_reduce(x):
    for bit in (1, 2, 4, 8):
        x = x + swap(x, "row", 16, bit)
    for bit in (8, 1, 2, 4):
        x = x + swap(x, "col", 16, bit)
    return x


def row_slots(blocks):
    me = lax.axis_index("col")
    owner = blocks // 4
    rel = ((owner // NZ) ^ (me // NZ)) * NZ + (owner % NZ - me % NZ) % NZ
    return rel * 4 + blocks % 4


def col_slots(blocks):
    me = lax.axis_index("row")
    owner = blocks // 4
    rel_c = (owner % 2) ^ (me % 2)
    rel_x = (owner // 2 % 2) ^ (me // 2 % 2)
    rel_y = (owner // 4 - me // 4) % NY
    return (rel_c * 8 + rel_x * 4 + rel_y) * 4 + blocks % 4


def tile_kernel(places, outs, left, *refs):
    n_in = len(places)
    src_ref, dst_ref, count_ref, vals_ref = refs[:4]
    panel_refs = refs[4:4 + n_in]
    out_refs = refs[4 + n_in:4 + n_in + len(outs)]
    panel, acc, sem = refs[4 + n_in + len(outs):]
    copies = []
    for ref, pieces in zip(panel_refs, places):
        start = 0
        for first, rows in pieces:
            copy = pltpu.make_async_copy(
                ref.at[pl.ds(start, rows)], panel.at[pl.ds(first, rows)], sem.at[len(copies)]
            )
            copy.start()
            copies.append(copy)
            start += rows
    acc[...] = jnp.zeros_like(acc)
    for copy in copies:
        copy.wait()
    count = count_ref[0]
    unroll = 4

    def step(i, carry):
        prods = []
        for u in range(unroll):
            t = i * unroll + u
            tile = vals_ref[t]
            block = panel[pl.ds(pl.multiple_of(src_ref[t] * BLOCK, BLOCK), BLOCK), :]
            a, b = (tile, block) if left else (block, tile)
            prod = jnp.dot(a, b, preferred_element_type=F32)
            prods.append(jnp.where(t < count, prod, 0.0))
        for u in range(unroll):
            at = pl.ds(pl.multiple_of(dst_ref[i * unroll + u] * BLOCK, BLOCK), BLOCK)
            acc[at, :] = acc[at, :] + prods[u]
        return carry

    lax.fori_loop(0, (count + unroll - 1) // unroll, step, 0)
    for ref, pieces in zip(out_refs, outs):
        start = 0
        for first, rows in pieces:
            ref[pl.ds(start, rows), :] = acc[pl.ds(first, rows), :].astype(ref.dtype)
            start += rows


def tile_sums(src, dst, count, vals, panels, places, outs, dtypes, left):
    sizes = [sum(rows for _, rows in pieces) for pieces in outs]
    vmem = pl.BlockSpec(memory_space=pltpu.VMEM)
    smem = pl.BlockSpec(memory_space=pltpu.SMEM)
    n_copies = sum(len(pieces) for pieces in places)
    return pl.pallas_call(
        functools.partial(tile_kernel, places, outs, left),
        out_shape=[jax.ShapeDtypeStruct((rows, BLOCK), dt) for rows, dt in zip(sizes, dtypes)],
        in_specs=[smem, smem, smem, vmem] + [pl.BlockSpec(memory_space=pl.ANY)] * len(panels),
        out_specs=[vmem] * len(outs),
        scratch_shapes=[
            pltpu.VMEM((16 * SHARD, BLOCK), BF16),
            pltpu.VMEM((16 * SHARD, BLOCK), F32),
            pltpu.SemaphoreType.DMA((n_copies,)),
        ],
        compiler_params=pltpu.CompilerParams(vmem_limit_bytes=VMEM_LIMIT),
    )(src, dst, count, vals, *panels)


def mid_kernel(own_ref, r1, r2, r3, r4, r5, weight_ref, gout_ref, act_ref, gt_ref, gw_ref):
    ax = own_ref[...]
    for r in (r1, r2, r3, r4, r5):
        ax = ax + r[...].astype(F32)
    high = ax.astype(BF16)
    low = (ax - high.astype(F32)).astype(BF16)
    weight = weight_ref[...]
    pre = jnp.dot(high, weight, preferred_element_type=F32) + jnp.dot(
        low, weight, preferred_element_type=F32
    )
    sig = 1.0 / (1.0 + jnp.exp(-pre))
    act_ref[...] = (pre * sig).astype(BF16)
    gp = (gout_ref[...].astype(F32) * sig * (1.0 + pre * (1.0 - sig))).astype(BF16)
    for q in range(SHARD // BLOCK):
        at = slice(q * BLOCK, (q + 1) * BLOCK)
        gt_ref[at, :] = lax.dot_general(
            weight, gp[at, :], (((1,), (1,)), ((), ())), preferred_element_type=F32
        ).astype(BF16)
    first = (((0,), (0,)), ((), ()))
    gw_ref[...] = lax.dot_general(high, gp, first, preferred_element_type=F32) + lax.dot_general(
        low, gp, first, preferred_element_type=F32
    )


def last_kernel(own_ref, w_ref, r1, r2, r3, out_ref):
    total = own_ref[...] + w_ref[:SHARD, :].astype(F32)
    for r in (r1, r2, r3):
        total = total + r[...].astype(F32)
    for q in range(SHARD // BLOCK):
        at = slice(q * BLOCK, (q + 1) * BLOCK)
        out_ref[at, :] = total[at, :].T.astype(BF16)


def add(*terms):
    return functools.reduce(lambda a, b: a + b, [t.astype(F32) for t in terms])


def body(features, weight, grad_out, tile_rows, tile_cols, tile_vals, tile_count):
    params = pltpu.CompilerParams(vmem_limit_bytes=VMEM_LIMIT)
    values = tile_vals[0, 0]
    count = tile_count[0]
    row_at = row_slots(tile_rows[0, 0])
    col_at = col_slots(tile_cols[0, 0])
    S = SHARD

    a = send_row(features, dx=1)
    u = send_row(features, dy=1)
    d = send_row(features, dy=-1)
    ud = jnp.concatenate([u, d])
    xa = jnp.concatenate([features, a])
    w = send_row(xa, dy=2)
    v = send_row(ud, dx=1)
    h1 = jnp.concatenate([xa, ud])
    h2 = jnp.concatenate([w, v])
    c1 = send_row(h1, dc=1)
    c2 = send_row(h2, dc=1)
    p1 = [(0, S), (4 * S, S), (3 * S, S), (1 * S, S)]
    p2 = [(2 * S, S), (6 * S, S), (7 * S, S), (5 * S, S)]
    other = lambda pieces: [(f + 8 * S, r) for f, r in pieces]
    places = [p1, p2, other(p1), other(p2)]

    O = lambda k: (k % 8 * S, S)
    X = lambda k: ((8 + k % 8) * S, S)
    outs = [[X(-3)], [X(3)], [X(4)], [O(1)], [O(-1)], [O(-3), X(-1)], [O(3), X(1)],
            [X(-2)], [X(2)], [O(4)], [X(0)], [O(2)], [O(-2)], [O(0)]]
    (x5, x3, x4, o1, o7, e, g, x6, x2, o4, x0, o2, o6, o0) = tile_sums(
        col_at, row_at, count, values, [h1, h2, c1, c2], places, outs,
        [BF16] * 7 + [F32] * 7, True,
    )
    r5 = send_col(x5, dz=-1)
    r3 = send_col(x3, dz=1)
    r4 = send_col(x4, dh=1)
    s1 = send_col(o1, dz=1)
    s7 = send_col(o7, dz=-1)
    re = send_col(e, dz=-1)
    rg = send_col(g, dz=1)
    q = jnp.concatenate([add(x2, r3).astype(BF16), add(x6, r5).astype(BF16)])
    rq = send_col(q, dh=1)
    o4 = add(o4, r4).astype(BF16)
    rh = send_col(o4[: S // 2], dz=2)
    ri = send_col(o4[S // 2:], dz=-2)
    x0 = add(x0, re[S:], rg[S:]).astype(BF16)
    rx = send_col(x0, dh=1)
    zero = jnp.zeros((S // 2, BLOCK), F32)
    o2 = add(o2, rg[:S], rq[:S], jnp.concatenate([rh.astype(F32), zero])).astype(BF16)
    o6 = add(o6, re[:S], rq[S:], jnp.concatenate([zero, ri.astype(F32)])).astype(BF16)
    s2 = send_col(o2, dz=2)
    s6 = send_col(o6, dz=-2)

    activation, gt, weight_part = pl.pallas_call(
        mid_kernel,
        out_shape=[
            jax.ShapeDtypeStruct((S, 256), BF16),
            jax.ShapeDtypeStruct((S, BLOCK), BF16),
            jax.ShapeDtypeStruct((BLOCK, 256), F32),
        ],
        compiler_params=params,
    )(o0, s1, s7, rx, s2, s6, weight, grad_out)
    grad_weight = all_reduce(weight_part)

    a = send_col(gt, dh=1)
    u = send_col(gt, dz=1)
    d = send_col(gt, dz=-1)
    u2 = send_col(gt, dz=2)
    d2 = send_col(gt, dz=-2)
    e = send_col(jnp.concatenate([u2, a]), dz=1)
    g = send_col(jnp.concatenate([d2, a]), dz=-1)
    f1 = send_col(u2[: S // 2], dz=2)
    f2 = send_col(d2[S // 2:], dz=-2)
    q = send_col(jnp.concatenate([u2, d2]), dh=1)
    f4 = jnp.concatenate([f1, f2])
    m = send_col(q[:S], dz=1)
    n = send_col(q[S:], dz=-1)
    l = send_col(f4, dh=1)
    panels = [gt, a, u, d, u2, d2, e, g, f4, q, m, n, l]
    places = [[O(0)], [X(0)], [O(-1)], [O(1)], [O(-2)], [O(2)], [O(-3), X(-1)], [O(3), X(1)],
              [O(4)], [X(-2), X(2)], [X(-3)], [X(3)], [X(4)]]

    k = lambda dy, dx: ((dx * 4 + dy % 4) * S, S)
    order = [k(0, 0), k(0, 1), k(1, 0), k(-1, 0), k(1, 1), k(-1, 1), k(2, 0), k(2, 1)]
    own, away = tile_sums(
        row_at, col_at, count, values, panels, places, [order, other(order)], [F32, BF16], False
    )
    own = own + send_row(away, dc=1).astype(F32)
    w = send_row(own[6 * S:].astype(BF16), dy=2)
    v = send_row(own[4 * S:6 * S].astype(BF16), dx=1)
    o = add(own[S:2 * S], w[S:]).astype(BF16)
    ud = add(own[2 * S:4 * S], v).astype(BF16)
    ro = send_row(o, dx=1)
    ru = send_row(ud[:S], dy=1)
    rd = send_row(ud[S:], dy=-1)
    grad_features = pl.pallas_call(
        last_kernel,
        out_shape=jax.ShapeDtypeStruct((S, BLOCK), BF16),
        compiler_params=params,
    )(own[:S], w, ro, ru, rd)
    return (activation, grad_features, grad_weight)


def solution(mesh):
    return jax.shard_map(
        body,
        mesh=mesh,
        in_specs=(
            P(("row", "col"), None),
            P(),
            P(("row", "col"), None),
            P("row", "col", None),
            P("row", "col", None),
            P("row", "col", None, None, None),
            P("row", "col"),
        ),
        out_specs=(P(("row", "col"), None), P(("row", "col"), None), P()),
        check_vma=False,
    )
```

time: 803 us -> 167 us (0.21)
  the two profiles are of different devices: /device:TPU:1 before, /device:TPU:4 now
where the time goes in v1:
time: 167 us; the launch traced here: 164 us
  waiting for transfers between devices  91.2 us (55%)
  starting transfers between devices  54.7 us (33%)
  Pallas kernels  12.6 us (8%)
  other arithmetic  2.54 us (2%)
  between operations  1.71 us (1%)
    ppermute x8, waiting for transfers between devices, swap(): return lax.ppermute(x, axis, [(i, i ^ bit) for i in range(count)])  37.7 us
    ppermute x26, starting transfers between devices, send_col(): return lax.ppermute(x, 'col', perm)  37.3 us
    ppermute x26, waiting for transfers between devices, send_col(): return lax.ppermute(x, 'col', perm)  34.1 us
    ppermute x13, waiting for transfers between devices, send_row(): return lax.ppermute(x, 'row', perm)  19.4 us
    ppermute x13, starting transfers between devices, send_row(): return lax.ppermute(x, 'row', perm)  12.3 us
    pallas_call x2, Pallas kernels, tile_sums(): pl.pallas_call(functools.partial(tile_kernel, places, outs, left), out_sh...  10.5 us
    ppermute x8, starting transfers between devices, swap(): return lax.ppermute(x, axis, [(i, i ^ bit) for i in range(count)])  5.1 us
  transfers between devices with their start and end apart: 47, of which 29 were waited for; matrix products, arithmetic and copies ran while one was open for 2% of the time, Pallas kernels for 0%

profile of v1, /device:TPU:4, one launch (start us, length us, event | category | flops | bytes accessed | tf_op | source)
XLA Modules:
  0.0 164.0 jit_solution(13438175250385393747)
XLA Ops:
  0.7 3.1 %collective-permute-start.2 = (bf16[512,128]{1,0:T(8,128)(2,1)}, bf16[512,128]{1,0:T(8,128)(2,1)S(1)}, u32[]{:S(2)}, u32[]{:S(2)}) collective-permute-start(bf16[512,128]{1,0:T(8,128)(2,1)} %param.7), channel_id=1, source_target_pairs={{0,192},{16,208},{32,224},{48,240},{64,0},{80,16},{96,32},{112,48}... | collective-permute-start | bytes 393224 | tf_op jit(solution)/shard_map/ppermute | solution.py:24
  6.8 3.3 %collective-permute-done.1 = bf16[512,128]{1,0:T(8,128)(2,1)S(1)} collective-permute-done((bf16[512,128]{1,0:T(8,128)(2,1)}, bf16[512,128]{1,0:T(8,128)(2,1)S(1)}, u32[]{:S(2)}, u32[]{:S(2)}) %collective-permute-start.1) | collective-permute-done | bytes 131104 | tf_op jit(solution)/shard_map/ppermute | solution.py:24
  12.7 7.7 %collective-permute-done.3 = bf16[1024,128]{1,0:T(8,128)(2,1)S(1)} collective-permute-done((bf16[1024,128]{1,0:T(8,128)(2,1)S(1)}, bf16[1024,128]{1,0:T(8,128)(2,1)S(1)}, u32[]{:S(2)}, u32[]{:S(2)}) %collective-permute-start.3) | collective-permute-done | bytes 262176 | tf_op jit(solution)/shard_map/ppermute | solution.py:24
  22.5 5.4 %shard_map.94 = (bf16[512,128]{1,0:T(8,128)(2,1)S(1)}, bf16[512,128]{1,0:T(8,128)(2,1)S(1)}, bf16[512,128]{1,0:T(8,128)(2,1)S(1)}, bf16[512,128]{1,0:T(8,128)(2,...) custom-call(s32[48]{0:T(128)S(1)} %get-tuple-element.59.refs_0_.refs, ...), custom_call_target="tpu_custom_call" | custom-call | tf_op jit(solution)/shard_map/pallas_call | solution.py:112
  28.0 3.1 %collective-permute-start.12 = (bf16[512,128]{1,0:T(8,128)(2,1)S(1)}, bf16[512,128]{1,0:T(8,128)(2,1)S(1)}, u32[]{:S(2)}, u32[]{:S(2)}) collective-permute-start(bf16[512,128]{1,0:T(8,128)(2,1)S(1)} %get-tuple-element.30), channel_id=1, source_target_pairs={{0,1},{1,2},{2,3},{3,4},{4,5},{5,6},{6,7},{7,0},{8,9},{9,10},{10,1... | collective-permute-start | bytes 393224 | tf_op jit(solution)/shard_map/ppermute | solution.py:32
  31.1 3.3 %collective-permute-start.13 = (bf16[512,128]{1,0:T(8,128)(2,1)S(1)}, bf16[512,128]{1,0:T(8,128)(2,1)S(1)}, u32[]{:S(2)}, u32[]{:S(2)}) collective-permute-start(bf16[512,128]{1,0:T(8,128)(2,1)S(1)} %get-tuple-element.32), channel_id=1, source_target_pairs={{0,7},{1,0},{2,1},{3,2},{4,3},{5,4},{6,5},{7,6},{8,15},{9,8},{10,9... | collective-permute-start | bytes 393224 | tf_op jit(solution)/shard_map/ppermute | solution.py:32
  37.9 2.3 %collective-permute-start.14 = (bf16[1024,128]{1,0:T(8,128)(2,1)S(1)}, bf16[1024,128]{1,0:T(8,128)(2,1)S(1)}, u32[]{:S(2)}, u32[]{:S(2)}) collective-permute-start(bf16[1024,128]{1,0:T(8,128)(2,1)S(1)} %pad_maximum_fusion.5), channel_id=1, source_target_pairs={{0,8},{1,9},{2,10},{3,11},{4,12},{5,13},{6,14},{7,15},{8,0},{9,1},... | collective-permute-start | bytes 786440 | tf_op jit(solution)/shard_map/ppermute | solution.py:32
  40.9 2.1 %collective-permute-start.18 = (bf16[256,128]{1,0:T(8,128)(2,1)S(1)}, bf16[256,128]{1,0:T(8,128)(2,1)S(1)}, u32[]{:S(2)}, u32[]{:S(2)}) collective-permute-start(bf16[256,128]{1,0:T(8,128)(2,1)S(1)} %get-tuple-element.57), channel_id=1, source_target_pairs={{0,6},{1,7},{2,0},{3,1},{4,2},{5,3},{6,4},{7,5},{8,14},{9,15},{10,... | collective-permute-start | bytes 196616 | tf_op jit(solution)/shard_map/ppermute | solution.py:32
  43.9 2.3 %collective-permute-done.18 = bf16[256,128]{1,0:T(8,128)(2,1)S(1)} collective-permute-done((bf16[256,128]{1,0:T(8,128)(2,1)S(1)}, bf16[256,128]{1,0:T(8,128)(2,1)S(1)}, u32[]{:S(2)}, u32[]{:S(2)}) %collective-permute-start.18) | collective-permute-done | bytes 65568 | tf_op jit(solution)/shard_map/ppermute | solution.py:32
  48.1 2.2 %collective-permute-done.16 = bf16[256,128]{1,0:T(8,128)(2,1)S(1)} collective-permute-done((bf16[256,128]{1,0:T(8,128)(2,1)S(1)}, bf16[256,128]{1,0:T(8,128)(2,1)S(1)}, u32[]{:S(2)}, u32[]{:S(2)}) %collective-permute-start.16) | collective-permute-done | bytes 65568 | tf_op jit(solution)/shard_map/ppermute | solution.py:32
  50.6 4.7 %collective-permute-start.19 = (bf16[512,128]{1,0:T(8,128)(2,1)S(1)}, bf16[512,128]{1,0:T(8,128)(2,1)S(1)}, u32[]{:S(2)}, u32[]{:S(2)}) collective-permute-start(bf16[512,128]{1,0:T(8,128)(2,1)S(1)} %get-tuple-element.51), channel_id=1, source_target_pairs={{0,6},{1,7},{2,0},{3,1},{4,2},{5,3},{6,4},{7,5},{8,14},{9,15},{10,... | collective-permute-start | bytes 393224 | tf_op jit(solution)/shard_map/ppermute | solution.py:32
  55.3 2.4 %collective-permute-start.11 = (bf16[512,128]{1,0:T(8,128)(2,1)S(1)}, bf16[512,128]{1,0:T(8,128)(2,1)S(1)}, u32[]{:S(2)}, u32[]{:S(2)}) collective-permute-start(bf16[512,128]{1,0:T(8,128)(2,1)S(1)} %get-tuple-element.52), channel_id=1, source_target_pairs={{0,8},{1,9},{2,10},{3,11},{4,12},{5,13},{6,14},{7,15},{8,0},{9,1},... | collective-permute-start | bytes 393224 | tf_op jit(solution)/shard_map/ppermute | solution.py:32
  57.7 2.0 %collective-permute-done.19.r5 = bf16[512,128]{1,0:T(8,128)(2,1)S(1)} collective-permute-done((bf16[512,128]{1,0:T(8,128)(2,1)S(1)}, bf16[512,128]{1,0:T(8,128)(2,1)S(1)}, u32[]{:S(2)}, u32[]{:S(2)}) %collective-permute-start.19) | collective-permute-done | bytes 131104 | tf_op jit(solution)/shard_map/ppermute | solution.py:32
  59.7 2.0 %collective-permute-done.11.r3 = bf16[512,128]{1,0:T(8,128)(2,1)S(1)} collective-permute-done((bf16[512,128]{1,0:T(8,128)(2,1)S(1)}, bf16[512,128]{1,0:T(8,128)(2,1)S(1)}, u32[]{:S(2)}, u32[]{:S(2)}) %collective-permute-start.11) | collective-permute-done | bytes 131104 | tf_op jit(solution)/shard_map/ppermute | solution.py:32
  61.7 6.7 %collective-permute-done.17.r4 = bf16[512,128]{1,0:T(8,128)(2,1)S(1)} collective-permute-done((bf16[512,128]{1,0:T(8,128)(2,1)S(1)}, bf16[512,128]{1,0:T(8,128)(2,1)S(1)}, u32[]{:S(2)}, u32[]{:S(2)}) %collective-permute-start.17) | collective-permute-done | bytes 131104 | tf_op jit(solution)/shard_map/ppermute | solution.py:32
  69.9 4.1 %collective-permute-start.24 = (bf16[512,128]{1,0:T(8,128)(2,1)S(1)}, bf16[512,128]{1,0:T(8,128)(2,1)S(1)}, u32[]{:S(2)}, u32[]{:S(2)}) collective-permute-start(bf16[512,128]{1,0:T(8,128)(2,1)S(1)} %get-tuple-element.37.refs_4_), channel_id=1, source_target_pairs={{0,6},{1,7},{2,0},{3,1},{4,2},{5,3},{6,4},{7,5},{8,14},{9,15},{10,... | collective-permute-start | bytes 393224 | tf_op jit(solution)/shard_map/ppermute | solution.py:32
  74.0 3.1 %collective-permute-done.23.refs_8_ = bf16[512,128]{1,0:T(8,128)(2,1)S(1)} collective-permute-done((bf16[512,128]{1,0:T(8,128)(2,1)S(1)}, bf16[512,128]{1,0:T(8,128)(2,1)S(1)}, u32[]{:S(2)}, u32[]{:S(2)}) %collective-permute-start.23) | collective-permute-done | bytes 131104 | tf_op jit(solution)/shard_map/ppermute | solution.py:32
  77.3 3.2 %collective-permute-done.20.refs_5_ = bf16[512,128]{1,0:T(8,128)(2,1)S(1)} collective-permute-done((bf16[512,128]{1,0:T(8,128)(2,1)S(1)}, bf16[512,128]{1,0:T(8,128)(2,1)S(1)}, u32[]{:S(2)}, u32[]{:S(2)}) %collective-permute-start.20) | collective-permute-done | bytes 131104 | tf_op jit(solution)/shard_map/ppermute | solution.py:32
  85.5 4.2 %collective-permute-done.28 = bf16[256,128]{1,0:T(8,128)(2,1)S(1)} collective-permute-done((bf16[256,128]{1,0:T(8,128)(2,1)S(1)}, bf16[256,128]{1,0:T(8,128)(2,1)S(1)}, u32[]{:S(2)}, u32[]{:S(2)}) %collective-permute-start.28) | collective-permute-done | bytes 65568 | tf_op jit(solution)/shard_map/ppermute | solution.py:32
  91.9 3.3 %collective-permute-start.31 = (bf16[512,128]{1,0:T(8,128)(2,1)S(1)}, bf16[512,128]{1,0:T(8,128)(2,1)S(1)}, u32[]{:S(2)}, u32[]{:S(2)}) collective-permute-start(bf16[512,128]{1,0:T(8,128)(2,1)S(1)} %get-tuple-element.49), channel_id=1, source_target_pairs={{0,7},{1,0},{2,1},{3,2},{4,3},{5,4},{6,5},{7,6},{8,15},{9,8},{10,9... | collective-permute-start | bytes 393224 | tf_op jit(solution)/shard_map/ppermute | solution.py:32
  97.7 3.7 %collective-permute-done.30.refs_14_ = bf16[512,128]{1,0:T(8,128)(2,1)S(1)} collective-permute-done((bf16[512,128]{1,0:T(8,128)(2,1)S(1)}, bf16[512,128]{1,0:T(8,128)(2,1)S(1)}, u32[]{:S(2)}, u32[]{:S(2)}) %collective-permute-start.30) | collective-permute-done | bytes 131104 | tf_op jit(solution)/shard_map/ppermute | solution.py:32
  101.4 5.0 %shard_map.96 = (f32[4096,128]{1,0:T(8,128)S(1)}, bf16[4096,128]{1,0:T(8,128)(2,1)S(1)}) custom-call(s32[48]{0:T(128)S(1)} %get-tuple-element.60.refs_1_.refs_0_, s32[48]{0:T(128)S(1)} %get-tuple-element.59.refs_0_.refs_1_, s32[1]{0:T(128)} %bitcast.29.refs_2_, bf16[48,128,128]{2,1,0:T(8,128)(2,1)S(1)} %bitcast.31, ...), custom_call_target="tpu_custom_call" | custom-call | tf_op jit(solution)/shard_map/pallas_call | solution.py:112
  107.0 2.3 %collective-permute-done.39 = f32[128,256]{1,0:T(8,128)S(1)} collective-permute-done((f32[128,256]{1,0:T(8,128)S(1)}, f32[128,256]{1,0:T(8,128)S(1)}, u32[]{:S(2)}, u32[]{:S(2)}) %collective-permute-start.39) | collective-permute-done | bytes 131104 | tf_op jit(solution)/shard_map/ppermute | solution.py:36
  110.2 4.8 %collective-permute-done.40 = f32[128,256]{1,0:T(8,128)S(1)} collective-permute-done((f32[128,256]{1,0:T(8,128)S(1)}, f32[128,256]{1,0:T(8,128)S(1)}, u32[]{:S(2)}, u32[]{:S(2)}) %collective-permute-start.40) | collective-permute-done | bytes 131104 | tf_op jit(solution)/shard_map/ppermute | solution.py:36
  115.1 5.0 %collective-permute-done.41 = f32[128,256]{1,0:T(8,128)S(1)} collective-permute-done((f32[128,256]{1,0:T(8,128)S(1)}, f32[128,256]{1,0:T(8,128)S(1)}, u32[]{:S(2)}, u32[]{:S(2)}) %collective-permute-start.41) | collective-permute-done | bytes 131104 | tf_op jit(solution)/shard_map/ppermute | solution.py:36
  120.8 5.8 %collective-permute-done.42 = f32[128,256]{1,0:T(8,128)S(1)} collective-permute-done((f32[128,256]{1,0:T(8,128)S(1)}, f32[128,256]{1,0:T(8,128)S(1)}, u32[]{:S(2)}, u32[]{:S(2)}) %collective-permute-start.42) | collective-permute-done | bytes 131104 | tf_op jit(solution)/shard_map/ppermute | solution.py:36
  128.4 5.2 %collective-permute-done.43 = f32[128,256]{1,0:T(8,128)S(1)} collective-permute-done((f32[128,256]{1,0:T(8,128)S(1)}, f32[128,256]{1,0:T(8,128)S(1)}, u32[]{:S(2)}, u32[]{:S(2)}) %collective-permute-start.43) | collective-permute-done | bytes 131104 | tf_op jit(solution)/shard_map/ppermute | solution.py:36
  134.5 5.6 %collective-permute-done.44 = f32[128,256]{1,0:T(8,128)S(1)} collective-permute-done((f32[128,256]{1,0:T(8,128)S(1)}, f32[128,256]{1,0:T(8,128)S(1)}, u32[]{:S(2)}, u32[]{:S(2)}) %collective-permute-start.44) | collective-permute-done | bytes 131104 | tf_op jit(solution)/shard_map/ppermute | solution.py:36
  140.2 9.0 %collective-permute-done.45 = f32[128,256]{1,0:T(8,128)S(1)} collective-permute-done((f32[128,256]{1,0:T(8,128)S(1)}, f32[128,256]{1,0:T(8,128)S(1)}, u32[]{:S(2)}, u32[]{:S(2)}) %collective-permute-start.45) | collective-permute-done | bytes 131104 | tf_op jit(solution)/shard_map/ppermute | solution.py:36
  150.2 3.1 %collective-permute-start.34 = (bf16[1024,128]{1,0:T(8,128)(2,1)S(1)}, bf16[1024,128]{1,0:T(8,128)(2,1)S(1)}, u32[]{:S(2)}, u32[]{:S(2)}) collective-permute-start(bf16[1024,128]{1,0:T(8,128)(2,1)S(1)} %get-tuple-element.46), channel_id=1, source_target_pairs={{0,128},{16,144},{32,160},{48,176},{64,192},{80,208},{96,224},{112... | collective-permute-start | bytes 786440 | tf_op jit(solution)/shard_map/ppermute | solution.py:24
  155.5 2.6 %collective-permute-done.34.w_ref = bf16[1024,128]{1,0:T(8,128)(2,1)S(1)} collective-permute-done((bf16[1024,128]{1,0:T(8,128)(2,1)S(1)}, bf16[1024,128]{1,0:T(8,128)(2,1)S(1)}, u32[]{:S(2)}, u32[]{:S(2)}) %collective-permute-start.34) | collective-permute-done | bytes 262176 | tf_op jit(solution)/shard_map/ppermute | solution.py:24
  160.1 3.0 %collective-permute-done.35.r1 = bf16[512,128]{1,0:T(8,128)(2,1)S(1)} collective-permute-done((bf16[512,128]{1,0:T(8,128)(2,1)S(1)}, bf16[512,128]{1,0:T(8,128)(2,1)S(1)}, u32[]{:S(2)}, u32[]{:S(2)}) %collective-permute-start.35) | collective-permute-done | bytes 131104 | tf_op jit(solution)/shard_map/ppermute | solution.py:24
  (110 shorter events, 36.5 us)
Async XLA Ops:
  3.8 7.7 %collective-permute-start = (bf16[512,128]{1,0:T(8,128)(2,1)}, bf16[512,128]{1,0:T(8,128)(2,1)S(1)}, u32[]{:S(2)}, u32[]{:S(2)}) collective-permute-start(bf16[512,128]{1,0:T(8,128)(2,1)} %param.7), channel_id=1, source_target_pairs={{0,32},{16,48},{32,0},{48,16},{64,96},{80,112},{96,64},{112,80},{1... | collective-permute-start | bytes 393224 | tf_op jit(solution)/shard_map/ppermute | solution.py:24
  10.2 10.2 %collective-permute-start.4 = (bf16[1024,128]{1,0:T(8,128)(2,1)S(1)}, bf16[1024,128]{1,0:T(8,128)(2,1)S(1)}, u32[]{:S(2)}, u32[]{:S(2)}) collective-permute-start(bf16[1024,128]{1,0:T(8,128)(2,1)S(1)} %pad_maximum_fusion.4), channel_id=1, source_target_pairs={{0,32},{16,48},{32,0},{48,16},{64,96},{80,112},{96,64},{112,80},{1... | collective-permute-start | bytes 786440 | tf_op jit(solution)/shard_map/ppermute | solution.py:24
  12.4 8.0 %collective-permute-start.3 = (bf16[1024,128]{1,0:T(8,128)(2,1)S(1)}, bf16[1024,128]{1,0:T(8,128)(2,1)S(1)}, u32[]{:S(2)}, u32[]{:S(2)}) collective-permute-start(bf16[1024,128]{1,0:T(8,128)(2,1)S(1)} %pad_maximum_fusion.3), channel_id=1, source_target_pairs={{0,128},{16,144},{32,160},{48,176},{64,192},{80,208},{96,224},{112... | collective-permute-start | bytes 786440 | tf_op jit(solution)/shard_map/ppermute | solution.py:24
  12.6 8.7 %collective-permute-start.5 = (bf16[2048,128]{1,0:T(8,128)(2,1)S(1)}, bf16[2048,128]{1,0:T(8,128)(2,1)S(1)}, u32[]{:S(2)}, u32[]{:S(2)}) collective-permute-start(bf16[2048,128]{1,0:T(8,128)(2,1)S(1)} %constant_dynamic-update-slice_fusion.refs_4_), channel_id=1, source_target_pairs={{0,16},{16,0},{32,48},{48,32},{64,80},{80,64},{96,112},{112,96},{1... | collective-permute-start | bytes 1572872 | tf_op jit(solution)/shard_map/ppermute | solution.py:24
  28.0 9.7 %collective-permute-start.12 = (bf16[512,128]{1,0:T(8,128)(2,1)S(1)}, bf16[512,128]{1,0:T(8,128)(2,1)S(1)}, u32[]{:S(2)}, u32[]{:S(2)}) collective-permute-start(bf16[512,128]{1,0:T(8,128)(2,1)S(1)} %get-tuple-element.30), channel_id=1, source_target_pairs={{0,1},{1,2},{2,3},{3,4},{4,5},{5,6},{6,7},{7,0},{8,9},{9,10},{10,1... | collective-permute-start | bytes 393224 | tf_op jit(solution)/shard_map/ppermute | solution.py:32
  31.1 6.7 %collective-permute-start.13 = (bf16[512,128]{1,0:T(8,128)(2,1)S(1)}, bf16[512,128]{1,0:T(8,128)(2,1)S(1)}, u32[]{:S(2)}, u32[]{:S(2)}) collective-permute-start(bf16[512,128]{1,0:T(8,128)(2,1)S(1)} %get-tuple-element.32), channel_id=1, source_target_pairs={{0,7},{1,0},{2,1},{3,2},{4,3},{5,4},{6,5},{7,6},{8,15},{9,8},{10,9... | collective-permute-start | bytes 393224 | tf_op jit(solution)/shard_map/ppermute | solution.py:32
  34.4 6.5 %collective-permute-start.15 = (bf16[512,128]{1,0:T(8,128)(2,1)S(1)}, bf16[512,128]{1,0:T(8,128)(2,1)S(1)}, u32[]{:S(2)}, u32[]{:S(2)}) collective-permute-start(bf16[512,128]{1,0:T(8,128)(2,1)S(1)} %get-tuple-element.34), channel_id=1, source_target_pairs={{0,8},{1,9},{2,10},{3,11},{4,12},{5,13},{6,14},{7,15},{8,0},{9,1},... | collective-permute-start | bytes 393224 | tf_op jit(solution)/shard_map/ppermute | solution.py:32
  34.4 15.9 %collective-permute-start.9 = (bf16[1024,128]{1,0:T(8,128)(2,1)S(1)}, bf16[1024,128]{1,0:T(8,128)(2,1)S(1)}, u32[]{:S(2)}, u32[]{:S(2)}) collective-permute-start(bf16[1024,128]{1,0:T(8,128)(2,1)S(1)} %get-tuple-element.26), channel_id=1, source_target_pairs={{0,7},{1,0},{2,1},{3,2},{4,3},{5,4},{6,5},{7,6},{8,15},{9,8},{10,9... | collective-permute-start | bytes 786440 | tf_op jit(solution)/shard_map/ppermute | solution.py:32
  36.4 14.0 %collective-permute-start.10 = (bf16[1024,128]{1,0:T(8,128)(2,1)S(1)}, bf16[1024,128]{1,0:T(8,128)(2,1)S(1)}, u32[]{:S(2)}, u32[]{:S(2)}) collective-permute-start(bf16[1024,128]{1,0:T(8,128)(2,1)S(1)} %get-tuple-element.27), channel_id=1, source_target_pairs={{0,1},{1,2},{2,3},{3,4},{4,5},{5,6},{6,7},{7,0},{8,9},{9,10},{10,1... | collective-permute-start | bytes 786440 | tf_op jit(solution)/shard_map/ppermute | solution.py:32
  37.9 12.5 %collective-permute-start.14 = (bf16[1024,128]{1,0:T(8,128)(2,1)S(1)}, bf16[1024,128]{1,0:T(8,128)(2,1)S(1)}, u32[]{:S(2)}, u32[]{:S(2)}) collective-permute-start(bf16[1024,128]{1,0:T(8,128)(2,1)S(1)} %pad_maximum_fusion.5), channel_id=1, source_target_pairs={{0,8},{1,9},{2,10},{3,11},{4,12},{5,13},{6,14},{7,15},{8,0},{9,1},... | collective-permute-start | bytes 786440 | tf_op jit(solution)/shard_map/ppermute | solution.py:32
  43.0 7.4 %collective-permute-start.16 = (bf16[256,128]{1,0:T(8,128)(2,1)S(1)}, bf16[256,128]{1,0:T(8,128)(2,1)S(1)}, u32[]{:S(2)}, u32[]{:S(2)}) collective-permute-start(bf16[256,128]{1,0:T(8,128)(2,1)S(1)} %get-tuple-element.58), channel_id=1, source_target_pairs={{0,2},{1,3},{2,4},{3,5},{4,6},{5,7},{6,0},{7,1},{8,10},{9,11},{10,... | collective-permute-start | bytes 196616 | tf_op jit(solution)/shard_map/ppermute | solution.py:32
  46.2 11.5 %collective-permute-start.7 = (bf16[512,128]{1,0:T(8,128)(2,1)S(1)}, bf16[512,128]{1,0:T(8,128)(2,1)S(1)}, u32[]{:S(2)}, u32[]{:S(2)}) collective-permute-start(bf16[512,128]{1,0:T(8,128)(2,1)S(1)} %get-tuple-element.23), channel_id=1, source_target_pairs={{0,1},{1,2},{2,3},{3,4},{4,5},{5,6},{6,7},{7,0},{8,9},{9,10},{10,1... | collective-permute-start | bytes 393224 | tf_op jit(solution)/shard_map/ppermute | solution.py:32
  50.4 7.3 %collective-permute-start.8 = (bf16[512,128]{1,0:T(8,128)(2,1)S(1)}, bf16[512,128]{1,0:T(8,128)(2,1)S(1)}, u32[]{:S(2)}, u32[]{:S(2)}) collective-permute-start(bf16[512,128]{1,0:T(8,128)(2,1)S(1)} %get-tuple-element.24), channel_id=1, source_target_pairs={{0,7},{1,0},{2,1},{3,2},{4,3},{5,4},{6,5},{7,6},{8,15},{9,8},{10,9... | collective-permute-start | bytes 393224 | tf_op jit(solution)/shard_map/ppermute | solution.py:32
  50.6 9.2 %collective-permute-start.19 = (bf16[512,128]{1,0:T(8,128)(2,1)S(1)}, bf16[512,128]{1,0:T(8,128)(2,1)S(1)}, u32[]{:S(2)}, u32[]{:S(2)}) collective-permute-start(bf16[512,128]{1,0:T(8,128)(2,1)S(1)} %get-tuple-element.51), channel_id=1, source_target_pairs={{0,6},{1,7},{2,0},{3,1},{4,2},{5,3},{6,4},{7,5},{8,14},{9,15},{10,... | collective-permute-start | bytes 393224 | tf_op jit(solution)/shard_map/ppermute | solution.py:32
  55.3 6.5 %collective-permute-start.11 = (bf16[512,128]{1,0:T(8,128)(2,1)S(1)}, bf16[512,128]{1,0:T(8,128)(2,1)S(1)}, u32[]{:S(2)}, u32[]{:S(2)}) collective-permute-start(bf16[512,128]{1,0:T(8,128)(2,1)S(1)} %get-tuple-element.52), channel_id=1, source_target_pairs={{0,8},{1,9},{2,10},{3,11},{4,12},{5,13},{6,14},{7,15},{8,0},{9,1},... | collective-permute-start | bytes 393224 | tf_op jit(solution)/shard_map/ppermute | solution.py:32
  57.7 10.8 %collective-permute-start.17 = (bf16[512,128]{1,0:T(8,128)(2,1)S(1)}, bf16[512,128]{1,0:T(8,128)(2,1)S(1)}, u32[]{:S(2)}, u32[]{:S(2)}) collective-permute-start(bf16[512,128]{1,0:T(8,128)(2,1)S(1)} %get-tuple-element.53), channel_id=1, source_target_pairs={{0,2},{1,3},{2,4},{3,5},{4,6},{5,7},{6,0},{7,1},{8,10},{9,11},{10,... | collective-permute-start | bytes 393224 | tf_op jit(solution)/shard_map/ppermute | solution.py:32
  69.9 7.3 %collective-permute-start.23 = (bf16[512,128]{1,0:T(8,128)(2,1)S(1)}, bf16[512,128]{1,0:T(8,128)(2,1)S(1)}, u32[]{:S(2)}, u32[]{:S(2)}) collective-permute-start(bf16[512,128]{1,0:T(8,128)(2,1)S(1)} %get-tuple-element.37.refs_4_), channel_id=1, source_target_pairs={{0,2},{1,3},{2,4},{3,5},{4,6},{5,7},{6,0},{7,1},{8,10},{9,11},{10,... | collective-permute-start | bytes 393224 | tf_op jit(solution)/shard_map/ppermute | solution.py:32
  69.9 7.4 %collective-permute-start.24 = (bf16[512,128]{1,0:T(8,128)(2,1)S(1)}, bf16[512,128]{1,0:T(8,128)(2,1)S(1)}, u32[]{:S(2)}, u32[]{:S(2)}) collective-permute-start(bf16[512,128]{1,0:T(8,128)(2,1)S(1)} %get-tuple-element.37.refs_4_), channel_id=1, source_target_pairs={{0,6},{1,7},{2,0},{3,1},{4,2},{5,3},{6,4},{7,5},{8,14},{9,15},{10,... | collective-permute-start | bytes 393224 | tf_op jit(solution)/shard_map/ppermute | solution.py:32
  77.1 7.1 %collective-permute-start.27 = (bf16[256,128]{1,0:T(8,128)(2,1)S(1)}, bf16[256,128]{1,0:T(8,128)(2,1)S(1)}, u32[]{:S(2)}, u32[]{:S(2)}) collective-permute-start(bf16[256,128]{1,0:T(8,128)(2,1)S(1)} %slice.90), channel_id=1, source_target_pairs={{0,2},{1,3},{2,4},{3,5},{4,6},{5,7},{6,0},{7,1},{8,10},{9,11},{10,... | collective-permute-start | bytes 196616 | tf_op jit(solution)/shard_map/ppermute | solution.py:32
  80.6 9.5 %collective-permute-start.29 = (bf16[1024,128]{1,0:T(8,128)(2,1)S(1)}, bf16[1024,128]{1,0:T(8,128)(2,1)S(1)}, u32[]{:S(2)}, u32[]{:S(2)}) collective-permute-start(bf16[1024,128]{1,0:T(8,128)(2,1)S(1)} %get-tuple-element.54), channel_id=1, source_target_pairs={{0,8},{1,9},{2,10},{3,11},{4,12},{5,13},{6,14},{7,15},{8,0},{9,1},... | collective-permute-start | bytes 786440 | tf_op jit(solution)/shard_map/ppermute | solution.py:32
  82.1 9.7 %collective-permute-start.22 = (bf16[512,128]{1,0:T(8,128)(2,1)S(1)}, bf16[512,128]{1,0:T(8,128)(2,1)S(1)}, u32[]{:S(2)}, u32[]{:S(2)}) collective-permute-start(bf16[512,128]{1,0:T(8,128)(2,1)S(1)} %get-tuple-element.37.refs_4_), channel_id=1, source_target_pairs={{0,7},{1,0},{2,1},{3,2},{4,3},{5,4},{6,5},{7,6},{8,15},{9,8},{10,9... | collective-permute-start | bytes 393224 | tf_op jit(solution)/shard_map/ppermute | solution.py:32
  82.1 13.1 %collective-permute-start.21 = (bf16[512,128]{1,0:T(8,128)(2,1)S(1)}, bf16[512,128]{1,0:T(8,128)(2,1)S(1)}, u32[]{:S(2)}, u32[]{:S(2)}) collective-permute-start(bf16[512,128]{1,0:T(8,128)(2,1)S(1)} %get-tuple-element.37.refs_4_), channel_id=1, source_target_pairs={{0,1},{1,2},{2,3},{3,4},{4,5},{5,6},{6,7},{7,0},{8,9},{9,10},{10,1... | collective-permute-start | bytes 393224 | tf_op jit(solution)/shard_map/ppermute | solution.py:32
  84.3 12.4 %collective-permute-start.26 = (bf16[1024,128]{1,0:T(8,128)(2,1)S(1)}, bf16[1024,128]{1,0:T(8,128)(2,1)S(1)}, u32[]{:S(2)}, u32[]{:S(2)}) collective-permute-start(bf16[1024,128]{1,0:T(8,128)(2,1)S(1)} %get-tuple-element.55), channel_id=1, source_target_pairs={{0,7},{1,0},{2,1},{3,2},{4,3},{5,4},{6,5},{7,6},{8,15},{9,8},{10,9... | collective-permute-start | bytes 786440 | tf_op jit(solution)/shard_map/ppermute | solution.py:32
  89.7 7.6 %collective-permute-start.25 = (bf16[1024,128]{1,0:T(8,128)(2,1)S(1)}, bf16[1024,128]{1,0:T(8,128)(2,1)S(1)}, u32[]{:S(2)}, u32[]{:S(2)}) collective-permute-start(bf16[1024,128]{1,0:T(8,128)(2,1)S(1)} %get-tuple-element.56), channel_id=1, source_target_pairs={{0,1},{1,2},{2,3},{3,4},{4,5},{5,6},{6,7},{7,0},{8,9},{9,10},{10,1... | collective-permute-start | bytes 786440 | tf_op jit(solution)/shard_map/ppermute | solution.py:32
  90.1 6.6 %collective-permute-start.32 = (bf16[512,128]{1,0:T(8,128)(2,1)S(1)}, bf16[512,128]{1,0:T(8,128)(2,1)S(1)}, u32[]{:S(2)}, u32[]{:S(2)}) collective-permute-start(bf16[512,128]{1,0:T(8,128)(2,1)S(1)} %constant_dynamic-update-slice_fusion.6.refs_12_), channel_id=1, source_target_pairs={{0,8},{1,9},{2,10},{3,11},{4,12},{5,13},{6,14},{7,15},{8,0},{9,1},... | collective-permute-start | bytes 393224 | tf_op jit(solution)/shard_map/ppermute | solution.py:32
  106.4 27.4 %collective-permute-start.33 = (bf16[4096,128]{1,0:T(8,128)(2,1)S(1)}, bf16[4096,128]{1,0:T(8,128)(2,1)S(1)}, u32[]{:S(2)}, u32[]{:S(2)}) collective-permute-start(bf16[4096,128]{1,0:T(8,128)(2,1)S(1)} %get-tuple-element.39), channel_id=1, source_target_pairs={{0,16},{16,0},{32,48},{48,32},{64,80},{80,64},{96,112},{112,96},{1... | collective-permute-start | bytes 3145736 | tf_op jit(solution)/shard_map/ppermute | solution.py:24
  120.1 6.6 %collective-permute-start.42 = (f32[128,256]{1,0:T(8,128)S(1)}, f32[128,256]{1,0:T(8,128)S(1)}, u32[]{:S(2)}, u32[]{:S(2)}) collective-permute-start(f32[128,256]{1,0:T(8,128)S(1)} %add.164), channel_id=1, source_target_pairs={{0,128},{16,144},{32,160},{48,176},{64,192},{80,208},{96,224},{112... | collective-permute-start | bytes 393224 | tf_op jit(solution)/shard_map/ppermute | solution.py:36
  126.6 7.0 %collective-permute-start.43 = (f32[128,256]{1,0:T(8,128)S(1)}, f32[128,256]{1,0:T(8,128)S(1)}, u32[]{:S(2)}, u32[]{:S(2)}) collective-permute-start(f32[128,256]{1,0:T(8,128)S(1)} %add.165), channel_id=1, source_target_pairs={{0,8},{1,9},{2,10},{3,11},{4,12},{5,13},{6,14},{7,15},{8,0},{9,1},... | collective-permute-start | bytes 393224 | tf_op jit(solution)/shard_map/ppermute | solution.py:36
  134.1 19.2 %collective-permute-start.36 = (bf16[1024,128]{1,0:T(8,128)(2,1)S(1)}, bf16[1024,128]{1,0:T(8,128)(2,1)S(1)}, u32[]{:S(2)}, u32[]{:S(2)}) collective-permute-start(bf16[1024,128]{1,0:T(8,128)(2,1)S(1)} %get-tuple-element.45), channel_id=1, source_target_pairs={{0,32},{16,48},{32,0},{48,16},{64,96},{80,112},{96,64},{112,80},{1... | collective-permute-start | bytes 786440 | tf_op jit(solution)/shard_map/ppermute | solution.py:24
  140.1 9.1 %collective-permute-start.45 = (f32[128,256]{1,0:T(8,128)S(1)}, f32[128,256]{1,0:T(8,128)S(1)}, u32[]{:S(2)}, u32[]{:S(2)}) collective-permute-start(f32[128,256]{1,0:T(8,128)S(1)} %add.167), channel_id=1, source_target_pairs={{0,2},{1,3},{2,0},{3,1},{4,6},{5,7},{6,4},{7,5},{8,10},{9,11},{10,... | collective-permute-start | bytes 393224 | tf_op jit(solution)/shard_map/ppermute | solution.py:36
  149.3 9.6 %collective-permute-start.46 = (f32[128,256]{1,0:T(8,128)S(1)}, f32[128,256]{1,0:T(8,128)S(1)}, u32[]{:S(2)}, u32[]{:S(2)}) collective-permute-start(f32[128,256]{1,0:T(8,128)S(1)} %add.168), channel_id=1, source_target_pairs={{0,4},{1,5},{2,6},{3,7},{4,0},{5,1},{6,2},{7,3},{8,12},{9,13},{10,... | collective-permute-start | bytes 393224 | tf_op jit(solution)/shard_map/ppermute | solution.py:36
  150.2 7.9 %collective-permute-start.34 = (bf16[1024,128]{1,0:T(8,128)(2,1)S(1)}, bf16[1024,128]{1,0:T(8,128)(2,1)S(1)}, u32[]{:S(2)}, u32[]{:S(2)}) collective-permute-start(bf16[1024,128]{1,0:T(8,128)(2,1)S(1)} %get-tuple-element.46), channel_id=1, source_target_pairs={{0,128},{16,144},{32,160},{48,176},{64,192},{80,208},{96,224},{112... | collective-permute-start | bytes 786440 | tf_op jit(solution)/shard_map/ppermute | solution.py:24
  (20 other events, 205.8 us)

commit v2 on v1

--- a/solution.py
+++ b/solution.py
@@ -12,6 +12,7 @@
 NY, NXL, NC, NXH, NZ = 4, 2, 2, 2, 8
 SHARD = 512
 BLOCK = 128
+ROWS = SHARD + BLOCK
 VMEM_LIMIT = 40 * 1024 * 1024
 
 
@@ -32,18 +33,6 @@
     return lax.ppermute(x, "col", perm)
 
 
-def swap(x, axis, count, bit):
-    return lax.ppermute(x, axis, [(i, i ^ bit) for i in range(count)])
-
-
-def all_reduce(x):
-    for bit in (1, 2, 4, 8):
-        x = x + swap(x, "row", 16, bit)
-    for bit in (8, 1, 2, 4):
-        x = x + swap(x, "col", 16, bit)
-    return x
-
-
 def row_slots(blocks):
     me = lax.axis_index("col")
     owner = blocks // 4
@@ -62,10 +51,9 @@
 
 def tile_kernel(places, outs, left, *refs):
     n_in = len(places)
-    src_ref, dst_ref, count_ref, vals_ref = refs[:4]
-    panel_refs = refs[4:4 + n_in]
-    out_refs = refs[4 + n_in:4 + n_in + len(outs)]
-    panel, acc, sem = refs[4 + n_in + len(outs):]
+    src_ref, dst_ref, count_ref, scan_ref, vals_ref = refs[:5]
+    panel_refs = refs[5:5 + n_in]
+    *out_refs, panel, acc, sem = refs[5 + n_in:]
     copies = []
     for ref, pieces in zip(panel_refs, places):
         start = 0
@@ -102,28 +90,37 @@
         for first, rows in pieces:
             ref[pl.ds(start, rows), :] = acc[pl.ds(first, rows), :].astype(ref.dtype)
             start += rows
-
-
-def tile_sums(src, dst, count, vals, panels, places, outs, dtypes, left):
+    if not left:
+        share = jnp.zeros((BLOCK, BLOCK), F32)
+        for i in range(16):
+            at = pl.multiple_of(16 * SHARD + scan_ref[i] * BLOCK, BLOCK)
+            share = share + panel[pl.ds(at, BLOCK), :].astype(F32)
+        out_refs[-1][...] = share.astype(BF16)
+
+
+def tile_sums(src, dst, count, scan, vals, panels, places, outs, dtypes, left):
     sizes = [sum(rows for _, rows in pieces) for pieces in outs]
     vmem = pl.BlockSpec(memory_space=pltpu.VMEM)
     smem = pl.BlockSpec(memory_space=pltpu.SMEM)
     n_copies = sum(len(pieces) for pieces in places)
+    out_shape = [jax.ShapeDtypeStruct((rows, BLOCK), dt) for rows, dt in zip(sizes, dtypes)]
+    if not left:
+        out_shape.append(jax.ShapeDtypeStruct((BLOCK, BLOCK), BF16))
     return pl.pallas_call(
         functools.partial(tile_kernel, places, outs, left),
-        out_shape=[jax.ShapeDtypeStruct((rows, BLOCK), dt) for rows, dt in zip(sizes, dtypes)],
-        in_specs=[smem, smem, smem, vmem] + [pl.BlockSpec(memory_space=pl.ANY)] * len(panels),
-        out_specs=[vmem] * len(outs),
+        out_shape=out_shape,
+        in_specs=[smem] * 4 + [vmem] + [pl.BlockSpec(memory_space=pl.ANY)] * len(panels),
+        out_specs=[vmem] * len(out_shape),
         scratch_shapes=[
-            pltpu.VMEM((16 * SHARD, BLOCK), BF16),
+            pltpu.VMEM((16 * (SHARD if left else ROWS), BLOCK), BF16),
             pltpu.VMEM((16 * SHARD, BLOCK), F32),
             pltpu.SemaphoreType.DMA((n_copies,)),
         ],
         compiler_params=pltpu.CompilerParams(vmem_limit_bytes=VMEM_LIMIT),
-    )(src, dst, count, vals, *panels)
-
-
-def mid_kernel(own_ref, r1, r2, r3, r4, r5, weight_ref, gout_ref, act_ref, gt_ref, gw_ref):
+    )(src, dst, count, scan, vals, *panels)
+
+
+def mid_kernel(core_ref, own_ref, r1, r2, r3, r4, r5, weight_ref, gout_ref, act_ref, gt_ref, keep_ref, give_ref, gw_ref):
     ax = own_ref[...]
     for r in (r1, r2, r3, r4, r5):
         ax = ax + r[...].astype(F32)
@@ -145,12 +142,18 @@
     gw_ref[...] = lax.dot_general(high, gp, first, preferred_element_type=F32) + lax.dot_general(
         low, gp, first, preferred_element_type=F32
     )
+    core = core_ref[0]
+    half = BLOCK // 2
+    for ref, which in ((keep_ref, core), (give_ref, 1 - core)):
+        at = pl.ds(pl.multiple_of(which * half, half), half)
+        ref[:half, :] = gw_ref[at, :BLOCK]
+        ref[half:, :] = gw_ref[at, BLOCK:]
 
 
 def last_kernel(own_ref, w_ref, r1, r2, r3, out_ref):
     total = own_ref[...] + w_ref[:SHARD, :].astype(F32)
     for r in (r1, r2, r3):
-        total = total + r[...].astype(F32)
+        total = total + r[:SHARD, :].astype(F32)
     for q in range(SHARD // BLOCK):
         at = slice(q * BLOCK, (q + 1) * BLOCK)
         out_ref[at, :] = total[at, :].T.astype(BF16)
@@ -158,6 +161,10 @@
 
 def add(*terms):
     return functools.reduce(lambda a, b: a + b, [t.astype(F32) for t in terms])
+
+
+def rounded(x):
+    return lax.reduce_precision(x, 8, 7)
 
 
 def body(features, weight, grad_out, tile_rows, tile_cols, tile_vals, tile_count):
@@ -166,6 +173,8 @@
     count = tile_count[0]
     row_at = row_slots(tile_rows[0, 0])
     col_at = col_slots(tile_cols[0, 0])
+    core = lax.axis_index("row") % NC
+    scan = row_slots(jnp.arange(16, dtype=jnp.int32) * 4) // 4
     S = SHARD
 
     a = send_row(features, dx=1)
@@ -189,7 +198,7 @@
     outs = [[X(-3)], [X(3)], [X(4)], [O(1)], [O(-1)], [O(-3), X(-1)], [O(3), X(1)],
             [X(-2)], [X(2)], [O(4)], [X(0)], [O(2)], [O(-2)], [O(0)]]
     (x5, x3, x4, o1, o7, e, g, x6, x2, o4, x0, o2, o6, o0) = tile_sums(
-        col_at, row_at, count, values, [h1, h2, c1, c2], places, outs,
+        col_at, row_at, count, scan, values, [h1, h2, c1, c2], places, outs,
         [BF16] * 7 + [F32] * 7, True,
     )
     r5 = send_col(x5, dz=-1)
@@ -212,16 +221,21 @@
     s2 = send_col(o2, dz=2)
     s6 = send_col(o6, dz=-2)
 
-    activation, gt, weight_part = pl.pallas_call(
+    half = jax.ShapeDtypeStruct((BLOCK, BLOCK), F32)
+    activation, gt, keep, give = pl.pallas_call(
         mid_kernel,
         out_shape=[
             jax.ShapeDtypeStruct((S, 256), BF16),
             jax.ShapeDtypeStruct((S, BLOCK), BF16),
-            jax.ShapeDtypeStruct((BLOCK, 256), F32),
+            half,
+            half,
         ],
+        in_specs=[pl.BlockSpec(memory_space=pltpu.SMEM)] + [pl.BlockSpec(memory_space=pltpu.VMEM)] * 8,
+        scratch_shapes=[pltpu.VMEM((BLOCK, 256), F32)],
         compiler_params=params,
-    )(o0, s1, s7, rx, s2, s6, weight, grad_out)
-    grad_weight = all_reduce(weight_part)
+    )(core[None], o0, s1, s7, rx, s2, s6, weight, grad_out)
+    share = keep + send_row(give, dc=1)
+    gt = jnp.concatenate([gt, share.astype(BF16)])
 
     a = send_col(gt, dh=1)
     u = send_col(gt, dz=1)
@@ -230,35 +244,45 @@
     d2 = send_col(gt, dz=-2)
     e = send_col(jnp.concatenate([u2, a]), dz=1)
     g = send_col(jnp.concatenate([d2, a]), dz=-1)
-    f1 = send_col(u2[: S // 2], dz=2)
-    f2 = send_col(d2[S // 2:], dz=-2)
+    f1 = send_col(u2[: ROWS // 2], dz=2)
+    f2 = send_col(d2[ROWS // 2:], dz=-2)
     q = send_col(jnp.concatenate([u2, d2]), dh=1)
     f4 = jnp.concatenate([f1, f2])
-    m = send_col(q[:S], dz=1)
-    n = send_col(q[S:], dz=-1)
+    m = send_col(q[:ROWS], dz=1)
+    n = send_col(q[ROWS:], dz=-1)
     l = send_col(f4, dh=1)
     panels = [gt, a, u, d, u2, d2, e, g, f4, q, m, n, l]
-    places = [[O(0)], [X(0)], [O(-1)], [O(1)], [O(-2)], [O(2)], [O(-3), X(-1)], [O(3), X(1)],
-              [O(4)], [X(-2), X(2)], [X(-3)], [X(3)], [X(4)]]
+    both = lambda *slots: [p for f, r in slots for p in ((f, r), (16 * S + f // 4, BLOCK))]
+    places = [both(O(0)), both(X(0)), both(O(-1)), both(O(1)), both(O(-2)), both(O(2)),
+              both(O(-3), X(-1)), both(O(3), X(1)), both(O(4)), both(X(-2), X(2)),
+              both(X(-3)), both(X(3)), both(X(4))]
 
     k = lambda dy, dx: ((dx * 4 + dy % 4) * S, S)
     order = [k(0, 0), k(0, 1), k(1, 0), k(-1, 0), k(1, 1), k(-1, 1), k(2, 0), k(2, 1)]
-    own, away = tile_sums(
-        row_at, col_at, count, values, panels, places, [order, other(order)], [F32, BF16], False
+    own, away, share = tile_sums(
+        row_at, col_at, count, scan, values, panels, places, [order, other(order)], [F32, BF16], False
     )
     own = own + send_row(away, dc=1).astype(F32)
-    w = send_row(own[6 * S:].astype(BF16), dy=2)
-    v = send_row(own[4 * S:6 * S].astype(BF16), dx=1)
-    o = add(own[S:2 * S], w[S:]).astype(BF16)
-    ud = add(own[2 * S:4 * S], v).astype(BF16)
-    ro = send_row(o, dx=1)
-    ru = send_row(ud[:S], dy=1)
-    rd = send_row(ud[S:], dy=-1)
+    w = send_row(jnp.concatenate([own[6 * S:].astype(BF16), share]), dy=2)
+    v = send_row(jnp.concatenate([own[4 * S:6 * S].astype(BF16), share]), dx=1)
+    o = add(own[S:2 * S], w[S:2 * S]).astype(BF16)
+    ud = add(own[2 * S:4 * S], v[:2 * S]).astype(BF16)
+    here = rounded(add(share, w[2 * S:]))
+    across = v[2 * S:]
+    ro = send_row(jnp.concatenate([o, here.astype(BF16)]), dx=1)
+    ru = send_row(jnp.concatenate([ud[:S], here.astype(BF16), across]), dy=1)
+    rd = send_row(jnp.concatenate([ud[S:], across]), dy=-1)
+    beside = rounded(add(ru[S + BLOCK:], rd[S:]))
+    mine = add(here, ru[S:S + BLOCK]) + add(ro[S:], beside)
+    theirs = send_row(mine, dc=1)
     grad_features = pl.pallas_call(
         last_kernel,
         out_shape=jax.ShapeDtypeStruct((S, BLOCK), BF16),
         compiler_params=params,
     )(own[:S], w, ro, ru, rd)
+    wide = lambda x: jnp.concatenate([x[:BLOCK // 2], x[BLOCK // 2:]], axis=1)
+    top, bottom = jnp.where(core == 0, mine, theirs), jnp.where(core == 0, theirs, mine)
+    grad_weight = jnp.concatenate([wide(top), wide(bottom)])
     return (activation, grad_features, grad_weight)
 
 

time: 167 us -> 138 us (0.83)
  the two profiles are of different devices: /device:TPU:4 before, /device:TPU:1 now
where the time goes in v2:
time: 138 us
  starting transfers between devices  63.3 us (46%)
  waiting for transfers between devices  53.8 us (39%)
  Pallas kernels  15 us (11%)
  other arithmetic  2.63 us (2%)
  between operations  1.67 us (1%)
    ppermute x26, starting transfers between devices, send_col(): return lax.ppermute(x, 'col', perm)  35.9 us
    ppermute x26, waiting for transfers between devices, send_col(): return lax.ppermute(x, 'col', perm)  28.6 us
    ppermute x15, starting transfers between devices, send_row(): return lax.ppermute(x, 'row', perm)  27.4 us
    ppermute x15, waiting for transfers between devices, send_row(): return lax.ppermute(x, 'row', perm)  25.2 us
    pallas_call x2, Pallas kernels, tile_sums(): pl.pallas_call(functools.partial(tile_kernel, places, outs, left), out_sh...  12.9 us
  transfers between devices with their start and end apart: 41, of which 25 were waited for; matrix products, arithmetic and copies ran while one was open for 2% of the time, Pallas kernels for 1%

profile of v2, /device:TPU:1, one launch (start us, length us, event | category | flops | bytes accessed | tf_op | source)
XLA Modules:
  0.0 137.7 jit_solution(9174593316610917948)
XLA Ops:
  0.7 3.6 %collective-permute-start.2 = (bf16[512,128]{1,0:T(8,128)(2,1)}, bf16[512,128]{1,0:T(8,128)(2,1)S(1)}, u32[]{:S(2)}, u32[]{:S(2)}) collective-permute-start(bf16[512,128]{1,0:T(8,128)(2,1)} %param.7), channel_id=1, source_target_pairs={{0,192},{16,208},{32,224},{48,240},{64,0},{80,16},{96,32},{112,48}... | collective-permute-start | bytes 393224 | tf_op jit(solution)/shard_map/ppermute | solution.py:25
  6.8 2.8 %collective-permute-done.1 = bf16[512,128]{1,0:T(8,128)(2,1)S(1)} collective-permute-done((bf16[512,128]{1,0:T(8,128)(2,1)}, bf16[512,128]{1,0:T(8,128)(2,1)S(1)}, u32[]{:S(2)}, u32[]{:S(2)}) %collective-permute-start.1) | collective-permute-done | bytes 131104 | tf_op jit(solution)/shard_map/ppermute | solution.py:25
  12.0 2.5 %collective-permute-start.5 = (bf16[2048,128]{1,0:T(8,128)(2,1)S(1)}, bf16[2048,128]{1,0:T(8,128)(2,1)S(1)}, u32[]{:S(2)}, u32[]{:S(2)}) collective-permute-start(bf16[2048,128]{1,0:T(8,128)(2,1)S(1)} %constant_dynamic-update-slice_fusion.refs_5_), channel_id=1, source_target_pairs={{0,16},{16,0},{32,48},{48,32},{64,80},{80,64},{96,112},{112,96},{1... | collective-permute-start | bytes 1572872 | tf_op jit(solution)/shard_map/ppermute | solution.py:25
  14.4 4.2 %collective-permute-done.3 = bf16[1024,128]{1,0:T(8,128)(2,1)S(1)} collective-permute-done((bf16[1024,128]{1,0:T(8,128)(2,1)S(1)}, bf16[1024,128]{1,0:T(8,128)(2,1)S(1)}, u32[]{:S(2)}, u32[]{:S(2)}) %collective-permute-start.3) | collective-permute-done | bytes 262176 | tf_op jit(solution)/shard_map/ppermute | solution.py:25
  18.7 3.6 %collective-permute-start.6 = (bf16[2048,128]{1,0:T(8,128)(2,1)S(1)}, bf16[2048,128]{1,0:T(8,128)(2,1)}, u32[]{:S(2)}, u32[]{:S(2)}) collective-permute-start(bf16[2048,128]{1,0:T(8,128)(2,1)S(1)} %constant_dynamic-update-slice_fusion.4.refs_6_), channel_id=1, source_target_pairs={{0,16},{16,0},{32,48},{48,32},{64,80},{80,64},{96,112},{112,96},{1... | collective-permute-start | bytes 1572872 | tf_op jit(solution)/shard_map/ppermute | solution.py:25
  24.0 6.2 %shard_map.94 = (bf16[512,128]{1,0:T(8,128)(2,1)S(1)}, bf16[512,128]{1,0:T(8,128)(2,1)S(1)}, bf16[512,128]{1,0:T(8,128)(2,1)S(1)}, bf16[512,128]{1,0:T(8,128)(2,...) custom-call(s32[48]{0:T(128)S(1)} %get-tuple-element.71.refs_0_.refs, ...), custom_call_target="tpu_custom_call" | custom-call | tf_op jit(solution)/shard_map/pallas_call | solution.py:109
  31.1 3.7 %collective-permute-start.13 = (bf16[512,128]{1,0:T(8,128)(2,1)S(1)}, bf16[512,128]{1,0:T(8,128)(2,1)S(1)}, u32[]{:S(2)}, u32[]{:S(2)}) collective-permute-start(bf16[512,128]{1,0:T(8,128)(2,1)S(1)} %get-tuple-element.34), channel_id=1, source_target_pairs={{0,7},{1,0},{2,1},{3,2},{4,3},{5,4},{6,5},{7,6},{8,15},{9,8},{10,9... | collective-permute-start | bytes 393224 | tf_op jit(solution)/shard_map/ppermute | solution.py:33
  34.8 3.0 %collective-permute-start.15 = (bf16[512,128]{1,0:T(8,128)(2,1)S(1)}, bf16[512,128]{1,0:T(8,128)(2,1)S(1)}, u32[]{:S(2)}, u32[]{:S(2)}) collective-permute-start(bf16[512,128]{1,0:T(8,128)(2,1)S(1)} %get-tuple-element.36), channel_id=1, source_target_pairs={{0,8},{1,9},{2,10},{3,11},{4,12},{5,13},{6,14},{7,15},{8,0},{9,1},... | collective-permute-start | bytes 393224 | tf_op jit(solution)/shard_map/ppermute | solution.py:33
  39.4 1.9 %collective-permute-start.14 = (bf16[1024,128]{1,0:T(8,128)(2,1)S(1)}, bf16[1024,128]{1,0:T(8,128)(2,1)S(1)}, u32[]{:S(2)}, u32[]{:S(2)}) collective-permute-start(bf16[1024,128]{1,0:T(8,128)(2,1)S(1)} %pad_maximum_fusion.7), channel_id=1, source_target_pairs={{0,8},{1,9},{2,10},{3,11},{4,12},{5,13},{6,14},{7,15},{8,0},{9,1},... | collective-permute-start | bytes 786440 | tf_op jit(solution)/shard_map/ppermute | solution.py:33
  41.4 3.4 %collective-permute-start.18 = (bf16[256,128]{1,0:T(8,128)(2,1)S(1)}, bf16[256,128]{1,0:T(8,128)(2,1)S(1)}, u32[]{:S(2)}, u32[]{:S(2)}) collective-permute-start(bf16[256,128]{1,0:T(8,128)(2,1)S(1)} %get-tuple-element.63), channel_id=1, source_target_pairs={{0,6},{1,7},{2,0},{3,1},{4,2},{5,3},{6,4},{7,5},{8,14},{9,15},{10,... | collective-permute-start | bytes 196616 | tf_op jit(solution)/shard_map/ppermute | solution.py:33
  44.8 1.9 %collective-permute-done.18 = bf16[256,128]{1,0:T(8,128)(2,1)S(1)} collective-permute-done((bf16[256,128]{1,0:T(8,128)(2,1)S(1)}, bf16[256,128]{1,0:T(8,128)(2,1)S(1)}, u32[]{:S(2)}, u32[]{:S(2)}) %collective-permute-start.18) | collective-permute-done | bytes 65568 | tf_op jit(solution)/shard_map/ppermute | solution.py:33
  46.7 1.8 %collective-permute-start.7 = (bf16[512,128]{1,0:T(8,128)(2,1)S(1)}, bf16[512,128]{1,0:T(8,128)(2,1)S(1)}, u32[]{:S(2)}, u32[]{:S(2)}) collective-permute-start(bf16[512,128]{1,0:T(8,128)(2,1)S(1)} %get-tuple-element.25), channel_id=1, source_target_pairs={{0,1},{1,2},{2,3},{3,4},{4,5},{5,6},{6,7},{7,0},{8,9},{9,10},{10,1... | collective-permute-start | bytes 393224 | tf_op jit(solution)/shard_map/ppermute | solution.py:33
  48.5 2.1 %collective-permute-done.16 = bf16[256,128]{1,0:T(8,128)(2,1)S(1)} collective-permute-done((bf16[256,128]{1,0:T(8,128)(2,1)S(1)}, bf16[256,128]{1,0:T(8,128)(2,1)S(1)}, u32[]{:S(2)}, u32[]{:S(2)}) %collective-permute-start.16) | collective-permute-done | bytes 65568 | tf_op jit(solution)/shard_map/ppermute | solution.py:33
  51.0 3.3 %collective-permute-start.19 = (bf16[512,128]{1,0:T(8,128)(2,1)S(1)}, bf16[512,128]{1,0:T(8,128)(2,1)S(1)}, u32[]{:S(2)}, u32[]{:S(2)}) collective-permute-start(bf16[512,128]{1,0:T(8,128)(2,1)S(1)} %get-tuple-element.55), channel_id=1, source_target_pairs={{0,6},{1,7},{2,0},{3,1},{4,2},{5,3},{6,4},{7,5},{8,14},{9,15},{10,... | collective-permute-start | bytes 393224 | tf_op jit(solution)/shard_map/ppermute | solution.py:33
  55.1 4.8 %collective-permute-done.19.r5 = bf16[512,128]{1,0:T(8,128)(2,1)S(1)} collective-permute-done((bf16[512,128]{1,0:T(8,128)(2,1)S(1)}, bf16[512,128]{1,0:T(8,128)(2,1)S(1)}, u32[]{:S(2)}, u32[]{:S(2)}) %collective-permute-start.19) | collective-permute-done | bytes 131104 | tf_op jit(solution)/shard_map/ppermute | solution.py:33
  62.4 7.5 %collective-permute-start.20 = (f32[128,128]{1,0:T(8,128)S(1)}, f32[128,128]{1,0:T(8,128)S(1)}, u32[]{:S(2)}, u32[]{:S(2)}) collective-permute-start(f32[128,128]{1,0:T(8,128)S(1)} %get-tuple-element.41), channel_id=1, source_target_pairs={{0,16},{16,0},{32,48},{48,32},{64,80},{80,64},{96,112},{112,96},{1... | collective-permute-start | bytes 196616 | tf_op jit(solution)/shard_map/ppermute | solution.py:25
  70.9 2.4 %collective-permute-start.24 = (bf16[640,128]{1,0:T(8,128)(2,1)S(1)}, bf16[640,128]{1,0:T(8,128)(2,1)S(1)}, u32[]{:S(2)}, u32[]{:S(2)}) collective-permute-start(bf16[640,128]{1,0:T(8,128)(2,1)S(1)} %pad_maximum_fusion.9.refs_5_), channel_id=1, source_target_pairs={{0,2},{1,3},{2,4},{3,5},{4,6},{5,7},{6,0},{7,1},{8,10},{9,11},{10,... | collective-permute-start | bytes 491528 | tf_op jit(solution)/shard_map/ppermute | solution.py:33
  74.5 4.3 %collective-permute-done.25.refs_10_ = bf16[640,128]{1,0:T(8,128)(2,1)S(1)} collective-permute-done((bf16[640,128]{1,0:T(8,128)(2,1)S(1)}, bf16[640,128]{1,0:T(8,128)(2,1)S(1)}, u32[]{:S(2)}, u32[]{:S(2)}) %collective-permute-start.25) | collective-permute-done | bytes 163872 | tf_op jit(solution)/shard_map/ppermute | solution.py:33
  78.8 2.7 %collective-permute-done.24.refs_9_ = bf16[640,128]{1,0:T(8,128)(2,1)S(1)} collective-permute-done((bf16[640,128]{1,0:T(8,128)(2,1)S(1)}, bf16[640,128]{1,0:T(8,128)(2,1)S(1)}, u32[]{:S(2)}, u32[]{:S(2)}) %collective-permute-start.24) | collective-permute-done | bytes 163872 | tf_op jit(solution)/shard_map/ppermute | solution.py:33
  85.8 2.0 %collective-permute-start.29 = (bf16[320,128]{1,0:T(8,128)(2,1)S(1)}, bf16[320,128]{1,0:T(8,128)(2,1)S(1)}, u32[]{:S(2)}, u32[]{:S(2)}) collective-permute-start(bf16[320,128]{1,0:T(8,128)(2,1)S(1)} %slice.135), channel_id=1, source_target_pairs={{0,6},{1,7},{2,0},{3,1},{4,2},{5,3},{6,4},{7,5},{8,14},{9,15},{10,... | collective-permute-start | bytes 245768 | tf_op jit(solution)/shard_map/ppermute | solution.py:33
  88.7 3.3 %collective-permute-done.29 = bf16[320,128]{1,0:T(8,128)(2,1)S(1)} collective-permute-done((bf16[320,128]{1,0:T(8,128)(2,1)S(1)}, bf16[320,128]{1,0:T(8,128)(2,1)S(1)}, u32[]{:S(2)}, u32[]{:S(2)}) %collective-permute-start.29) | collective-permute-done | bytes 81952 | tf_op jit(solution)/shard_map/ppermute | solution.py:33
  92.0 2.1 %collective-permute-start.33 = (bf16[640,128]{1,0:T(8,128)(2,1)S(1)}, bf16[640,128]{1,0:T(8,128)(2,1)S(1)}, u32[]{:S(2)}, u32[]{:S(2)}) collective-permute-start(bf16[640,128]{1,0:T(8,128)(2,1)S(1)} %constant_dynamic-update-slice_fusion.6.refs_13_), channel_id=1, source_target_pairs={{0,8},{1,9},{2,10},{3,11},{4,12},{5,13},{6,14},{7,15},{8,0},{9,1},... | collective-permute-start | bytes 491528 | tf_op jit(solution)/shard_map/ppermute | solution.py:33
  94.2 3.4 %collective-permute-start.32 = (bf16[640,128]{1,0:T(8,128)(2,1)S(1)}, bf16[640,128]{1,0:T(8,128)(2,1)S(1)}, u32[]{:S(2)}, u32[]{:S(2)}) collective-permute-start(bf16[640,128]{1,0:T(8,128)(2,1)S(1)} %get-tuple-element.51), channel_id=1, source_target_pairs={{0,7},{1,0},{2,1},{3,2},{4,3},{5,4},{6,5},{7,6},{8,15},{9,8},{10,9... | collective-permute-start | bytes 491528 | tf_op jit(solution)/shard_map/ppermute | solution.py:33
  99.1 3.4 %collective-permute-done.32.refs_16_ = bf16[640,128]{1,0:T(8,128)(2,1)S(1)} collective-permute-done((bf16[640,128]{1,0:T(8,128)(2,1)S(1)}, bf16[640,128]{1,0:T(8,128)(2,1)S(1)}, u32[]{:S(2)}, u32[]{:S(2)}) %collective-permute-start.32) | collective-permute-done | bytes 163872 | tf_op jit(solution)/shard_map/ppermute | solution.py:33
  102.6 2.5 %collective-permute-done.31.refs_15_ = bf16[640,128]{1,0:T(8,128)(2,1)S(1)} collective-permute-done((bf16[640,128]{1,0:T(8,128)(2,1)S(1)}, bf16[640,128]{1,0:T(8,128)(2,1)S(1)}, u32[]{:S(2)}, u32[]{:S(2)}) %collective-permute-start.31) | collective-permute-done | bytes 163872 | tf_op jit(solution)/shard_map/ppermute | solution.py:33
  105.1 6.7 %shard_map.96 = (f32[4096,128]{1,0:T(8,128)S(1)}, bf16[4096,128]{1,0:T(8,128)(2,1)S(1)}, bf16[128,128]{1,0:T(8,128)(2,1)S(1)}) custom-call(s32[48]{0:T(128)S(1)} %get-tuple-element.72.refs_1_.refs_0_, s32[48]{0:T(128)S(1)} %get-tuple-element.71.refs_0_.refs_1_, s32[1]{0:T(128)} %bitcast.30.refs_2_, s32[16]{0:T(128)S(1)} %and_select_fusion.refs_3_, ...), custom_call_target="tpu_custom_call" | custom-call | tf_op jit(solution)/shard_map/pallas_call | solution.py:109
  111.8 2.4 %collective-permute-start.34 = (bf16[4096,128]{1,0:T(8,128)(2,1)S(1)}, bf16[4096,128]{1,0:T(8,128)(2,1)S(1)}, u32[]{:S(2)}, u32[]{:S(2)}) collective-permute-start(bf16[4096,128]{1,0:T(8,128)(2,1)S(1)} %get-tuple-element.43), channel_id=1, source_target_pairs={{0,16},{16,0},{32,48},{48,32},{64,80},{80,64},{96,112},{112,96},{1... | collective-permute-start | bytes 3145736 | tf_op jit(solution)/shard_map/ppermute | solution.py:25
  114.2 2.3 %collective-permute-done.34 = bf16[4096,128]{1,0:T(8,128)(2,1)S(1)} collective-permute-done((bf16[4096,128]{1,0:T(8,128)(2,1)S(1)}, bf16[4096,128]{1,0:T(8,128)(2,1)S(1)}, u32[]{:S(2)}, u32[]{:S(2)}) %collective-permute-start.34) | collective-permute-done | bytes 1048608 | tf_op jit(solution)/shard_map/ppermute | solution.py:25
  118.3 6.8 %collective-permute-done.37 = bf16[1152,128]{1,0:T(8,128)(2,1)S(1)} collective-permute-done((bf16[1152,128]{1,0:T(8,128)(2,1)S(1)}, bf16[1152,128]{1,0:T(8,128)(2,1)S(1)}, u32[]{:S(2)}, u32[]{:S(2)}) %collective-permute-start.37) | collective-permute-done | bytes 294944 | tf_op jit(solution)/shard_map/ppermute | solution.py:25
  128.1 1.7 %collective-permute-done.39.r3 = bf16[640,128]{1,0:T(8,128)(2,1)S(1)} collective-permute-done((bf16[640,128]{1,0:T(8,128)(2,1)S(1)}, bf16[640,128]{1,0:T(8,128)(2,1)S(1)}, u32[]{:S(2)}, u32[]{:S(2)}) %collective-permute-start.39) | collective-permute-done | bytes 163872 | tf_op jit(solution)/shard_map/ppermute | solution.py:25
  129.8 1.9 %collective-permute-done.36.r1 = bf16[640,128]{1,0:T(8,128)(2,1)S(1)} collective-permute-done((bf16[640,128]{1,0:T(8,128)(2,1)S(1)}, bf16[640,128]{1,0:T(8,128)(2,1)S(1)}, u32[]{:S(2)}, u32[]{:S(2)}) %collective-permute-start.36) | collective-permute-done | bytes 163872 | tf_op jit(solution)/shard_map/ppermute | solution.py:25
  133.5 2.5 %collective-permute-start.40 = (f32[128,128]{1,0:T(8,128)S(1)}, f32[128,128]{1,0:T(8,128)S(1)}, u32[]{:S(2)}, u32[]{:S(2)}) collective-permute-start(f32[128,128]{1,0:T(8,128)S(1)} %add_add_fusion), channel_id=1, source_target_pairs={{0,16},{16,0},{32,48},{48,32},{64,80},{80,64},{96,112},{112,96},{1... | collective-permute-start | bytes 196616 | tf_op jit(solution)/shard_map/ppermute | solution.py:25
  (104 shorter events, 29.2 us)
Async XLA Ops:
  0.7 6.1 %collective-permute-start.2 = (bf16[512,128]{1,0:T(8,128)(2,1)}, bf16[512,128]{1,0:T(8,128)(2,1)S(1)}, u32[]{:S(2)}, u32[]{:S(2)}) collective-permute-start(bf16[512,128]{1,0:T(8,128)(2,1)} %param.7), channel_id=1, source_target_pairs={{0,192},{16,208},{32,224},{48,240},{64,0},{80,16},{96,32},{112,48}... | collective-permute-start | bytes 393224 | tf_op jit(solution)/shard_map/ppermute | solution.py:25
  4.3 6.6 %collective-permute-start = (bf16[512,128]{1,0:T(8,128)(2,1)}, bf16[512,128]{1,0:T(8,128)(2,1)S(1)}, u32[]{:S(2)}, u32[]{:S(2)}) collective-permute-start(bf16[512,128]{1,0:T(8,128)(2,1)} %param.7), channel_id=1, source_target_pairs={{0,32},{16,48},{32,0},{48,16},{64,96},{80,112},{96,64},{112,80},{1... | collective-permute-start | bytes 393224 | tf_op jit(solution)/shard_map/ppermute | solution.py:25
  9.6 9.1 %collective-permute-start.4 = (bf16[1024,128]{1,0:T(8,128)(2,1)S(1)}, bf16[1024,128]{1,0:T(8,128)(2,1)S(1)}, u32[]{:S(2)}, u32[]{:S(2)}) collective-permute-start(bf16[1024,128]{1,0:T(8,128)(2,1)S(1)} %pad_maximum_fusion.6), channel_id=1, source_target_pairs={{0,32},{16,48},{32,0},{48,16},{64,96},{80,112},{96,64},{112,80},{1... | collective-permute-start | bytes 786440 | tf_op jit(solution)/shard_map/ppermute | solution.py:25
  11.8 6.8 %collective-permute-start.3 = (bf16[1024,128]{1,0:T(8,128)(2,1)S(1)}, bf16[1024,128]{1,0:T(8,128)(2,1)S(1)}, u32[]{:S(2)}, u32[]{:S(2)}) collective-permute-start(bf16[1024,128]{1,0:T(8,128)(2,1)S(1)} %pad_maximum_fusion.5), channel_id=1, source_target_pairs={{0,128},{16,144},{32,160},{48,176},{64,192},{80,208},{96,224},{112... | collective-permute-start | bytes 786440 | tf_op jit(solution)/shard_map/ppermute | solution.py:25
  12.0 11.1 %collective-permute-start.5 = (bf16[2048,128]{1,0:T(8,128)(2,1)S(1)}, bf16[2048,128]{1,0:T(8,128)(2,1)S(1)}, u32[]{:S(2)}, u32[]{:S(2)}) collective-permute-start(bf16[2048,128]{1,0:T(8,128)(2,1)S(1)} %constant_dynamic-update-slice_fusion.refs_5_), channel_id=1, source_target_pairs={{0,16},{16,0},{32,48},{48,32},{64,80},{80,64},{96,112},{112,96},{1... | collective-permute-start | bytes 1572872 | tf_op jit(solution)/shard_map/ppermute | solution.py:25
  30.2 9.1 %collective-permute-start.12 = (bf16[512,128]{1,0:T(8,128)(2,1)S(1)}, bf16[512,128]{1,0:T(8,128)(2,1)S(1)}, u32[]{:S(2)}, u32[]{:S(2)}) collective-permute-start(bf16[512,128]{1,0:T(8,128)(2,1)S(1)} %get-tuple-element.32), channel_id=1, source_target_pairs={{0,1},{1,2},{2,3},{3,4},{4,5},{5,6},{6,7},{7,0},{8,9},{9,10},{10,1... | collective-permute-start | bytes 393224 | tf_op jit(solution)/shard_map/ppermute | solution.py:33
  31.1 8.2 %collective-permute-start.13 = (bf16[512,128]{1,0:T(8,128)(2,1)S(1)}, bf16[512,128]{1,0:T(8,128)(2,1)S(1)}, u32[]{:S(2)}, u32[]{:S(2)}) collective-permute-start(bf16[512,128]{1,0:T(8,128)(2,1)S(1)} %get-tuple-element.34), channel_id=1, source_target_pairs={{0,7},{1,0},{2,1},{3,2},{4,3},{5,4},{6,5},{7,6},{8,15},{9,8},{10,9... | collective-permute-start | bytes 393224 | tf_op jit(solution)/shard_map/ppermute | solution.py:33
  34.8 6.5 %collective-permute-start.15 = (bf16[512,128]{1,0:T(8,128)(2,1)S(1)}, bf16[512,128]{1,0:T(8,128)(2,1)S(1)}, u32[]{:S(2)}, u32[]{:S(2)}) collective-permute-start(bf16[512,128]{1,0:T(8,128)(2,1)S(1)} %get-tuple-element.36), channel_id=1, source_target_pairs={{0,8},{1,9},{2,10},{3,11},{4,12},{5,13},{6,14},{7,15},{8,0},{9,1},... | collective-permute-start | bytes 393224 | tf_op jit(solution)/shard_map/ppermute | solution.py:33
  37.8 13.0 %collective-permute-start.9 = (bf16[1024,128]{1,0:T(8,128)(2,1)S(1)}, bf16[1024,128]{1,0:T(8,128)(2,1)S(1)}, u32[]{:S(2)}, u32[]{:S(2)}) collective-permute-start(bf16[1024,128]{1,0:T(8,128)(2,1)S(1)} %get-tuple-element.28), channel_id=1, source_target_pairs={{0,7},{1,0},{2,1},{3,2},{4,3},{5,4},{6,5},{7,6},{8,15},{9,8},{10,9... | collective-permute-start | bytes 786440 | tf_op jit(solution)/shard_map/ppermute | solution.py:33
  39.3 11.6 %collective-permute-start.10 = (bf16[1024,128]{1,0:T(8,128)(2,1)S(1)}, bf16[1024,128]{1,0:T(8,128)(2,1)S(1)}, u32[]{:S(2)}, u32[]{:S(2)}) collective-permute-start(bf16[1024,128]{1,0:T(8,128)(2,1)S(1)} %get-tuple-element.29), channel_id=1, source_target_pairs={{0,1},{1,2},{2,3},{3,4},{4,5},{5,6},{6,7},{7,0},{8,9},{9,10},{10,1... | collective-permute-start | bytes 786440 | tf_op jit(solution)/shard_map/ppermute | solution.py:33
  39.4 11.4 %collective-permute-start.14 = (bf16[1024,128]{1,0:T(8,128)(2,1)S(1)}, bf16[1024,128]{1,0:T(8,128)(2,1)S(1)}, u32[]{:S(2)}, u32[]{:S(2)}) collective-permute-start(bf16[1024,128]{1,0:T(8,128)(2,1)S(1)} %pad_maximum_fusion.7), channel_id=1, source_target_pairs={{0,8},{1,9},{2,10},{3,11},{4,12},{5,13},{6,14},{7,15},{8,0},{9,1},... | collective-permute-start | bytes 786440 | tf_op jit(solution)/shard_map/ppermute | solution.py:33
  44.8 5.8 %collective-permute-start.16 = (bf16[256,128]{1,0:T(8,128)(2,1)S(1)}, bf16[256,128]{1,0:T(8,128)(2,1)S(1)}, u32[]{:S(2)}, u32[]{:S(2)}) collective-permute-start(bf16[256,128]{1,0:T(8,128)(2,1)S(1)} %get-tuple-element.64), channel_id=1, source_target_pairs={{0,2},{1,3},{2,4},{3,5},{4,6},{5,7},{6,0},{7,1},{8,10},{9,11},{10,... | collective-permute-start | bytes 196616 | tf_op jit(solution)/shard_map/ppermute | solution.py:33
  46.7 8.4 %collective-permute-start.7 = (bf16[512,128]{1,0:T(8,128)(2,1)S(1)}, bf16[512,128]{1,0:T(8,128)(2,1)S(1)}, u32[]{:S(2)}, u32[]{:S(2)}) collective-permute-start(bf16[512,128]{1,0:T(8,128)(2,1)S(1)} %get-tuple-element.25), channel_id=1, source_target_pairs={{0,1},{1,2},{2,3},{3,4},{4,5},{5,6},{6,7},{7,0},{8,9},{9,10},{10,1... | collective-permute-start | bytes 393224 | tf_op jit(solution)/shard_map/ppermute | solution.py:33
  51.0 8.9 %collective-permute-start.19 = (bf16[512,128]{1,0:T(8,128)(2,1)S(1)}, bf16[512,128]{1,0:T(8,128)(2,1)S(1)}, u32[]{:S(2)}, u32[]{:S(2)}) collective-permute-start(bf16[512,128]{1,0:T(8,128)(2,1)S(1)} %get-tuple-element.55), channel_id=1, source_target_pairs={{0,6},{1,7},{2,0},{3,1},{4,2},{5,3},{6,4},{7,5},{8,14},{9,15},{10,... | collective-permute-start | bytes 393224 | tf_op jit(solution)/shard_map/ppermute | solution.py:33
  55.1 5.9 %collective-permute-start.17 = (bf16[512,128]{1,0:T(8,128)(2,1)S(1)}, bf16[512,128]{1,0:T(8,128)(2,1)S(1)}, u32[]{:S(2)}, u32[]{:S(2)}) collective-permute-start(bf16[512,128]{1,0:T(8,128)(2,1)S(1)} %get-tuple-element.57), channel_id=1, source_target_pairs={{0,2},{1,3},{2,4},{3,5},{4,6},{5,7},{6,0},{7,1},{8,10},{9,11},{10,... | collective-permute-start | bytes 393224 | tf_op jit(solution)/shard_map/ppermute | solution.py:33
  62.4 8.4 %collective-permute-start.20 = (f32[128,128]{1,0:T(8,128)S(1)}, f32[128,128]{1,0:T(8,128)S(1)}, u32[]{:S(2)}, u32[]{:S(2)}) collective-permute-start(f32[128,128]{1,0:T(8,128)S(1)} %get-tuple-element.41), channel_id=1, source_target_pairs={{0,16},{16,0},{32,48},{48,32},{64,80},{80,64},{96,112},{112,96},{1... | collective-permute-start | bytes 196616 | tf_op jit(solution)/shard_map/ppermute | solution.py:25
  70.8 8.0 %collective-permute-start.25 = (bf16[640,128]{1,0:T(8,128)(2,1)S(1)}, bf16[640,128]{1,0:T(8,128)(2,1)S(1)}, u32[]{:S(2)}, u32[]{:S(2)}) collective-permute-start(bf16[640,128]{1,0:T(8,128)(2,1)S(1)} %pad_maximum_fusion.9.refs_5_), channel_id=1, source_target_pairs={{0,6},{1,7},{2,0},{3,1},{4,2},{5,3},{6,4},{7,5},{8,14},{9,15},{10,... | collective-permute-start | bytes 491528 | tf_op jit(solution)/shard_map/ppermute | solution.py:33
  70.9 10.6 %collective-permute-start.24 = (bf16[640,128]{1,0:T(8,128)(2,1)S(1)}, bf16[640,128]{1,0:T(8,128)(2,1)S(1)}, u32[]{:S(2)}, u32[]{:S(2)}) collective-permute-start(bf16[640,128]{1,0:T(8,128)(2,1)S(1)} %pad_maximum_fusion.9.refs_5_), channel_id=1, source_target_pairs={{0,2},{1,3},{2,4},{3,5},{4,6},{5,7},{6,0},{7,1},{8,10},{9,11},{10,... | collective-permute-start | bytes 491528 | tf_op jit(solution)/shard_map/ppermute | solution.py:33
  73.3 8.2 %collective-permute-start.21 = (bf16[640,128]{1,0:T(8,128)(2,1)S(1)}, bf16[640,128]{1,0:T(8,128)(2,1)S(1)}, u32[]{:S(2)}, u32[]{:S(2)}) collective-permute-start(bf16[640,128]{1,0:T(8,128)(2,1)S(1)} %pad_maximum_fusion.9.refs_5_), channel_id=1, source_target_pairs={{0,8},{1,9},{2,10},{3,11},{4,12},{5,13},{6,14},{7,15},{8,0},{9,1},... | collective-permute-start | bytes 491528 | tf_op jit(solution)/shard_map/ppermute | solution.py:33
  81.7 10.4 %collective-permute-start.30 = (bf16[1280,128]{1,0:T(8,128)(2,1)S(1)}, bf16[1280,128]{1,0:T(8,128)(2,1)S(1)}, u32[]{:S(2)}, u32[]{:S(2)}) collective-permute-start(bf16[1280,128]{1,0:T(8,128)(2,1)S(1)} %get-tuple-element.58), channel_id=1, source_target_pairs={{0,8},{1,9},{2,10},{3,11},{4,12},{5,13},{6,14},{7,15},{8,0},{9,1},... | collective-permute-start | bytes 983048 | tf_op jit(solution)/shard_map/ppermute | solution.py:33
  82.8 5.9 %collective-permute-start.28 = (bf16[320,128]{1,0:T(8,128)(2,1)S(1)}, bf16[320,128]{1,0:T(8,128)(2,1)S(1)}, u32[]{:S(2)}, u32[]{:S(2)}) collective-permute-start(bf16[320,128]{1,0:T(8,128)(2,1)S(1)} %slice.134), channel_id=1, source_target_pairs={{0,2},{1,3},{2,4},{3,5},{4,6},{5,7},{6,0},{7,1},{8,10},{9,11},{10,... | collective-permute-start | bytes 245768 | tf_op jit(solution)/shard_map/ppermute | solution.py:33
  84.3 9.9 %collective-permute-start.23 = (bf16[640,128]{1,0:T(8,128)(2,1)S(1)}, bf16[640,128]{1,0:T(8,128)(2,1)S(1)}, u32[]{:S(2)}, u32[]{:S(2)}) collective-permute-start(bf16[640,128]{1,0:T(8,128)(2,1)S(1)} %pad_maximum_fusion.9.refs_5_), channel_id=1, source_target_pairs={{0,7},{1,0},{2,1},{3,2},{4,3},{5,4},{6,5},{7,6},{8,15},{9,8},{10,9... | collective-permute-start | bytes 491528 | tf_op jit(solution)/shard_map/ppermute | solution.py:33
  84.3 13.3 %collective-permute-start.22 = (bf16[640,128]{1,0:T(8,128)(2,1)S(1)}, bf16[640,128]{1,0:T(8,128)(2,1)S(1)}, u32[]{:S(2)}, u32[]{:S(2)}) collective-permute-start(bf16[640,128]{1,0:T(8,128)(2,1)S(1)} %pad_maximum_fusion.9.refs_5_), channel_id=1, source_target_pairs={{0,1},{1,2},{2,3},{3,4},{4,5},{5,6},{6,7},{7,0},{8,9},{9,10},{10,1... | collective-permute-start | bytes 491528 | tf_op jit(solution)/shard_map/ppermute | solution.py:33
  85.8 6.2 %collective-permute-start.29 = (bf16[320,128]{1,0:T(8,128)(2,1)S(1)}, bf16[320,128]{1,0:T(8,128)(2,1)S(1)}, u32[]{:S(2)}, u32[]{:S(2)}) collective-permute-start(bf16[320,128]{1,0:T(8,128)(2,1)S(1)} %slice.135), channel_id=1, source_target_pairs={{0,6},{1,7},{2,0},{3,1},{4,2},{5,3},{6,4},{7,5},{8,14},{9,15},{10,... | collective-permute-start | bytes 245768 | tf_op jit(solution)/shard_map/ppermute | solution.py:33
  88.7 10.4 %collective-permute-start.27 = (bf16[1280,128]{1,0:T(8,128)(2,1)S(1)}, bf16[1280,128]{1,0:T(8,128)(2,1)S(1)}, u32[]{:S(2)}, u32[]{:S(2)}) collective-permute-start(bf16[1280,128]{1,0:T(8,128)(2,1)S(1)} %get-tuple-element.59), channel_id=1, source_target_pairs={{0,7},{1,0},{2,1},{3,2},{4,3},{5,4},{6,5},{7,6},{8,15},{9,8},{10,9... | collective-permute-start | bytes 983048 | tf_op jit(solution)/shard_map/ppermute | solution.py:33
  92.0 7.1 %collective-permute-start.26 = (bf16[1280,128]{1,0:T(8,128)(2,1)S(1)}, bf16[1280,128]{1,0:T(8,128)(2,1)S(1)}, u32[]{:S(2)}, u32[]{:S(2)}) collective-permute-start(bf16[1280,128]{1,0:T(8,128)(2,1)S(1)} %get-tuple-element.60), channel_id=1, source_target_pairs={{0,1},{1,2},{2,3},{3,4},{4,5},{5,6},{6,7},{7,0},{8,9},{9,10},{10,1... | collective-permute-start | bytes 983048 | tf_op jit(solution)/shard_map/ppermute | solution.py:33
  92.0 5.8 %collective-permute-start.33 = (bf16[640,128]{1,0:T(8,128)(2,1)S(1)}, bf16[640,128]{1,0:T(8,128)(2,1)S(1)}, u32[]{:S(2)}, u32[]{:S(2)}) collective-permute-start(bf16[640,128]{1,0:T(8,128)(2,1)S(1)} %constant_dynamic-update-slice_fusion.6.refs_13_), channel_id=1, source_target_pairs={{0,8},{1,9},{2,10},{3,11},{4,12},{5,13},{6,14},{7,15},{8,0},{9,1},... | collective-permute-start | bytes 491528 | tf_op jit(solution)/shard_map/ppermute | solution.py:33
  94.2 8.4 %collective-permute-start.32 = (bf16[640,128]{1,0:T(8,128)(2,1)S(1)}, bf16[640,128]{1,0:T(8,128)(2,1)S(1)}, u32[]{:S(2)}, u32[]{:S(2)}) collective-permute-start(bf16[640,128]{1,0:T(8,128)(2,1)S(1)} %get-tuple-element.51), channel_id=1, source_target_pairs={{0,7},{1,0},{2,1},{3,2},{4,3},{5,4},{6,5},{7,6},{8,15},{9,8},{10,9... | collective-permute-start | bytes 491528 | tf_op jit(solution)/shard_map/ppermute | solution.py:33
  97.6 7.4 %collective-permute-start.31 = (bf16[640,128]{1,0:T(8,128)(2,1)S(1)}, bf16[640,128]{1,0:T(8,128)(2,1)S(1)}, u32[]{:S(2)}, u32[]{:S(2)}) collective-permute-start(bf16[640,128]{1,0:T(8,128)(2,1)S(1)} %get-tuple-element.52), channel_id=1, source_target_pairs={{0,1},{1,2},{2,3},{3,4},{4,5},{5,6},{6,7},{7,0},{8,9},{9,10},{10,1... | collective-permute-start | bytes 491528 | tf_op jit(solution)/shard_map/ppermute | solution.py:33
  116.8 8.3 %collective-permute-start.37 = (bf16[1152,128]{1,0:T(8,128)(2,1)S(1)}, bf16[1152,128]{1,0:T(8,128)(2,1)S(1)}, u32[]{:S(2)}, u32[]{:S(2)}) collective-permute-start(bf16[1152,128]{1,0:T(8,128)(2,1)S(1)} %get-tuple-element.69), channel_id=1, source_target_pairs={{0,32},{16,48},{32,0},{48,16},{64,96},{80,112},{96,64},{112,80},{1... | collective-permute-start | bytes 884744 | tf_op jit(solution)/shard_map/ppermute | solution.py:25
  117.9 9.4 %collective-permute-start.35 = (bf16[1152,128]{1,0:T(8,128)(2,1)S(1)}, bf16[1152,128]{1,0:T(8,128)(2,1)S(1)}, u32[]{:S(2)}, u32[]{:S(2)}) collective-permute-start(bf16[1152,128]{1,0:T(8,128)(2,1)S(1)} %get-tuple-element.70), channel_id=1, source_target_pairs={{0,128},{16,144},{32,160},{48,176},{64,192},{80,208},{96,224},{112... | collective-permute-start | bytes 884744 | tf_op jit(solution)/shard_map/ppermute | solution.py:25
  127.3 6.2 %collective-permute-start.38 = (bf16[768,128]{1,0:T(8,128)(2,1)S(1)}, bf16[768,128]{1,0:T(8,128)(2,1)S(1)}, u32[]{:S(2)}, u32[]{:S(2)}) collective-permute-start(bf16[768,128]{1,0:T(8,128)(2,1)S(1)} %pad_maximum_fusion.8), channel_id=1, source_target_pairs={{0,64},{16,80},{32,96},{48,112},{64,128},{80,144},{96,160},{112,17... | collective-permute-start | bytes 589832 | tf_op jit(solution)/shard_map/ppermute | solution.py:25
  (14 other events, 154.5 us)

commit v3 on v2

--- a/solution.py
+++ b/solution.py
@@ -13,7 +13,7 @@
 SHARD = 512
 BLOCK = 128
 ROWS = SHARD + BLOCK
-VMEM_LIMIT = 40 * 1024 * 1024
+VMEM_LIMIT = 24 * 1024 * 1024
 
 
 def send_row(x, dy=0, dx=0, dc=0):
@@ -53,22 +53,15 @@
     n_in = len(places)
     src_ref, dst_ref, count_ref, scan_ref, vals_ref = refs[:5]
     panel_refs = refs[5:5 + n_in]
-    *out_refs, panel, acc, sem = refs[5 + n_in:]
-    copies = []
+    *out_refs, panel, acc = refs[5 + n_in:]
     for ref, pieces in zip(panel_refs, places):
         start = 0
         for first, rows in pieces:
-            copy = pltpu.make_async_copy(
-                ref.at[pl.ds(start, rows)], panel.at[pl.ds(first, rows)], sem.at[len(copies)]
-            )
-            copy.start()
-            copies.append(copy)
+            panel[pl.ds(first, rows), :] = ref[pl.ds(start, rows), :]
             start += rows
     acc[...] = jnp.zeros_like(acc)
-    for copy in copies:
-        copy.wait()
     count = count_ref[0]
-    unroll = 4
+    unroll = 12
 
     def step(i, carry):
         prods = []
@@ -102,19 +95,17 @@
     sizes = [sum(rows for _, rows in pieces) for pieces in outs]
     vmem = pl.BlockSpec(memory_space=pltpu.VMEM)
     smem = pl.BlockSpec(memory_space=pltpu.SMEM)
-    n_copies = sum(len(pieces) for pieces in places)
     out_shape = [jax.ShapeDtypeStruct((rows, BLOCK), dt) for rows, dt in zip(sizes, dtypes)]
     if not left:
         out_shape.append(jax.ShapeDtypeStruct((BLOCK, BLOCK), BF16))
     return pl.pallas_call(
         functools.partial(tile_kernel, places, outs, left),
         out_shape=out_shape,
-        in_specs=[smem] * 4 + [vmem] + [pl.BlockSpec(memory_space=pl.ANY)] * len(panels),
+        in_specs=[smem] * 4 + [vmem] * (1 + len(panels)),
         out_specs=[vmem] * len(out_shape),
         scratch_shapes=[
             pltpu.VMEM((16 * (SHARD if left else ROWS), BLOCK), BF16),
             pltpu.VMEM((16 * SHARD, BLOCK), F32),
-            pltpu.SemaphoreType.DMA((n_copies,)),
         ],
         compiler_params=pltpu.CompilerParams(vmem_limit_bytes=VMEM_LIMIT),
     )(src, dst, count, scan, vals, *panels)

time: 138 us -> 130 us (0.942)
  Pallas kernels: 15 us -> 7.32 us
  starting transfers between devices: 63.3 us -> 67.6 us
  waiting for transfers between devices: 53.8 us -> 49.8 us
    pallas_call x2, Pallas kernels: 12.9 us -> 5.15 us  [tile_sums(): pl.pallas_call(functools.partial(tile_kernel, places, outs, left), out_sh...]
    ppermute x26, starting transfers between devices: 35.9 us -> 43.4 us  [send_col(): return lax.ppermute(x, 'col', perm)]
    ppermute x26, waiting for transfers between devices: 28.6 us -> 24.5 us  [send_col(): return lax.ppermute(x, 'col', perm)]
    ppermute x15, starting transfers between devices: 27.4 us -> 24.2 us  [send_row(): return lax.ppermute(x, 'row', perm)]
  transfers between devices with their start and end apart: 41 -> 41, of which waited for: 25 -> 28; matrix products, arithmetic and copies ran while one was open for 2% -> 2% of each run, Pallas kernels for 1% -> 1%
where the time goes in v3:
time: 130 us
  starting transfers between devices  67.6 us (52%)
  waiting for transfers between devices  49.8 us (38%)
  Pallas kernels  7.32 us (6%)
  other arithmetic  2.63 us (2%)
  between operations  1.65 us (1%)
    ppermute x26, starting transfers between devices, send_col(): return lax.ppermute(x, 'col', perm)  43.4 us
    ppermute x15, waiting for transfers between devices, send_row(): return lax.ppermute(x, 'row', perm)  25.3 us
    ppermute x26, waiting for transfers between devices, send_col(): return lax.ppermute(x, 'col', perm)  24.5 us
    ppermute x15, starting transfers between devices, send_row(): return lax.ppermute(x, 'row', perm)  24.2 us
    pallas_call x2, Pallas kernels, tile_sums(): pl.pallas_call(functools.partial(tile_kernel, places, outs, left), out_sh...  5.15 us
  transfers between devices with their start and end apart: 41, of which 28 were waited for; matrix products, arithmetic and copies ran while one was open for 2% of the time, Pallas kernels for 1%

profile of v3, /device:TPU:1, one launch (start us, length us, event | category | flops | bytes accessed | tf_op | source)
XLA Modules:
  0.0 130.2 jit_solution(9547035720796392451)
XLA Ops:
  0.7 3.6 %collective-permute-start.2 = (bf16[512,128]{1,0:T(8,128)(2,1)}, bf16[512,128]{1,0:T(8,128)(2,1)S(1)}, u32[]{:S(2)}, u32[]{:S(2)}) collective-permute-start(bf16[512,128]{1,0:T(8,128)(2,1)} %param.7), channel_id=1, source_target_pairs={{0,192},{16,208},{32,224},{48,240},{64,0},{80,16},{96,32},{112,48}... | collective-permute-start | bytes 393224 | tf_op jit(solution)/shard_map/ppermute | solution.py:25
  6.8 2.8 %collective-permute-done.1 = bf16[512,128]{1,0:T(8,128)(2,1)S(1)} collective-permute-done((bf16[512,128]{1,0:T(8,128)(2,1)}, bf16[512,128]{1,0:T(8,128)(2,1)S(1)}, u32[]{:S(2)}, u32[]{:S(2)}) %collective-permute-start.1) | collective-permute-done | bytes 131104 | tf_op jit(solution)/shard_map/ppermute | solution.py:25
  12.0 2.5 %collective-permute-start.5 = (bf16[2048,128]{1,0:T(8,128)(2,1)S(1)}, bf16[2048,128]{1,0:T(8,128)(2,1)S(1)}, u32[]{:S(2)}, u32[]{:S(2)}) collective-permute-start(bf16[2048,128]{1,0:T(8,128)(2,1)S(1)} %constant_dynamic-update-slice_fusion.refs_5_), channel_id=1, source_target_pairs={{0,16},{16,0},{32,48},{48,32},{64,80},{80,64},{96,112},{112,96},{1... | collective-permute-start | bytes 1572872 | tf_op jit(solution)/shard_map/ppermute | solution.py:25
  14.4 4.2 %collective-permute-done.3 = bf16[1024,128]{1,0:T(8,128)(2,1)S(1)} collective-permute-done((bf16[1024,128]{1,0:T(8,128)(2,1)S(1)}, bf16[1024,128]{1,0:T(8,128)(2,1)S(1)}, u32[]{:S(2)}, u32[]{:S(2)}) %collective-permute-start.3) | collective-permute-done | bytes 262176 | tf_op jit(solution)/shard_map/ppermute | solution.py:25
  18.7 3.6 %collective-permute-start.6 = (bf16[2048,128]{1,0:T(8,128)(2,1)S(1)}, bf16[2048,128]{1,0:T(8,128)(2,1)}, u32[]{:S(2)}, u32[]{:S(2)}) collective-permute-start(bf16[2048,128]{1,0:T(8,128)(2,1)S(1)} %constant_dynamic-update-slice_fusion.4.refs_6_), channel_id=1, source_target_pairs={{0,16},{16,0},{32,48},{48,32},{64,80},{80,64},{96,112},{112,96},{1... | collective-permute-start | bytes 1572872 | tf_op jit(solution)/shard_map/ppermute | solution.py:25
  24.0 2.8 %shard_map.94 = (bf16[512,128]{1,0:T(8,128)(2,1)S(1)}, bf16[512,128]{1,0:T(8,128)(2,1)S(1)}, bf16[512,128]{1,0:T(8,128)(2,1)S(1)}, bf16[512,128]{1,0:T(8,128)(2,...) custom-call(s32[48]{0:T(128)S(1)} %get-tuple-element.71.refs_0_.refs, ...), custom_call_target="tpu_custom_call" | custom-call | tf_op jit(solution)/shard_map/pallas_call | solution.py:101
  28.5 4.0 %collective-permute-start.13 = (bf16[512,128]{1,0:T(8,128)(2,1)S(1)}, bf16[512,128]{1,0:T(8,128)(2,1)S(1)}, u32[]{:S(2)}, u32[]{:S(2)}) collective-permute-start(bf16[512,128]{1,0:T(8,128)(2,1)S(1)} %get-tuple-element.34), channel_id=1, source_target_pairs={{0,7},{1,0},{2,1},{3,2},{4,3},{5,4},{6,5},{7,6},{8,15},{9,8},{10,9... | collective-permute-start | bytes 393224 | tf_op jit(solution)/shard_map/ppermute | solution.py:33
  32.5 1.9 %collective-permute-start.15 = (bf16[512,128]{1,0:T(8,128)(2,1)S(1)}, bf16[512,128]{1,0:T(8,128)(2,1)S(1)}, u32[]{:S(2)}, u32[]{:S(2)}) collective-permute-start(bf16[512,128]{1,0:T(8,128)(2,1)S(1)} %get-tuple-element.36), channel_id=1, source_target_pairs={{0,8},{1,9},{2,10},{3,11},{4,12},{5,13},{6,14},{7,15},{8,0},{9,1},... | collective-permute-start | bytes 393224 | tf_op jit(solution)/shard_map/ppermute | solution.py:33
  36.6 1.8 %collective-permute-start.14 = (bf16[1024,128]{1,0:T(8,128)(2,1)S(1)}, bf16[1024,128]{1,0:T(8,128)(2,1)S(1)}, u32[]{:S(2)}, u32[]{:S(2)}) collective-permute-start(bf16[1024,128]{1,0:T(8,128)(2,1)S(1)} %pad_maximum_fusion.7), channel_id=1, source_target_pairs={{0,8},{1,9},{2,10},{3,11},{4,12},{5,13},{6,14},{7,15},{8,0},{9,1},... | collective-permute-start | bytes 786440 | tf_op jit(solution)/shard_map/ppermute | solution.py:33
  41.5 1.9 %collective-permute-done.18 = bf16[256,128]{1,0:T(8,128)(2,1)S(1)} collective-permute-done((bf16[256,128]{1,0:T(8,128)(2,1)S(1)}, bf16[256,128]{1,0:T(8,128)(2,1)S(1)}, u32[]{:S(2)}, u32[]{:S(2)}) %collective-permute-start.18) | collective-permute-done | bytes 65568 | tf_op jit(solution)/shard_map/ppermute | solution.py:33
  43.4 1.9 %collective-permute-start.7 = (bf16[512,128]{1,0:T(8,128)(2,1)S(1)}, bf16[512,128]{1,0:T(8,128)(2,1)S(1)}, u32[]{:S(2)}, u32[]{:S(2)}) collective-permute-start(bf16[512,128]{1,0:T(8,128)(2,1)S(1)} %get-tuple-element.25), channel_id=1, source_target_pairs={{0,1},{1,2},{2,3},{3,4},{4,5},{5,6},{6,7},{7,0},{8,9},{9,10},{10,1... | collective-permute-start | bytes 393224 | tf_op jit(solution)/shard_map/ppermute | solution.py:33
  46.2 2.1 %collective-permute-start.8 = (bf16[512,128]{1,0:T(8,128)(2,1)S(1)}, bf16[512,128]{1,0:T(8,128)(2,1)S(1)}, u32[]{:S(2)}, u32[]{:S(2)}) collective-permute-start(bf16[512,128]{1,0:T(8,128)(2,1)S(1)} %get-tuple-element.26), channel_id=1, source_target_pairs={{0,7},{1,0},{2,1},{3,2},{4,3},{5,4},{6,5},{7,6},{8,15},{9,8},{10,9... | collective-permute-start | bytes 393224 | tf_op jit(solution)/shard_map/ppermute | solution.py:33
  48.6 2.8 %collective-permute-start.19 = (bf16[512,128]{1,0:T(8,128)(2,1)S(1)}, bf16[512,128]{1,0:T(8,128)(2,1)S(1)}, u32[]{:S(2)}, u32[]{:S(2)}) collective-permute-start(bf16[512,128]{1,0:T(8,128)(2,1)S(1)} %get-tuple-element.55), channel_id=1, source_target_pairs={{0,6},{1,7},{2,0},{3,1},{4,2},{5,3},{6,4},{7,5},{8,14},{9,15},{10,... | collective-permute-start | bytes 393224 | tf_op jit(solution)/shard_map/ppermute | solution.py:33
  54.6 2.1 %collective-permute-done.11.r3 = bf16[512,128]{1,0:T(8,128)(2,1)S(1)} collective-permute-done((bf16[512,128]{1,0:T(8,128)(2,1)S(1)}, bf16[512,128]{1,0:T(8,128)(2,1)S(1)}, u32[]{:S(2)}, u32[]{:S(2)}) %collective-permute-start.11) | collective-permute-done | bytes 131104 | tf_op jit(solution)/shard_map/ppermute | solution.py:33
  56.6 2.0 %collective-permute-done.17.r4 = bf16[512,128]{1,0:T(8,128)(2,1)S(1)} collective-permute-done((bf16[512,128]{1,0:T(8,128)(2,1)S(1)}, bf16[512,128]{1,0:T(8,128)(2,1)S(1)}, u32[]{:S(2)}, u32[]{:S(2)}) %collective-permute-start.17) | collective-permute-done | bytes 131104 | tf_op jit(solution)/shard_map/ppermute | solution.py:33
  60.1 3.8 %collective-permute-start.20 = (f32[128,128]{1,0:T(8,128)S(1)}, f32[128,128]{1,0:T(8,128)S(1)}, u32[]{:S(2)}, u32[]{:S(2)}) collective-permute-start(f32[128,128]{1,0:T(8,128)S(1)} %get-tuple-element.41), channel_id=1, source_target_pairs={{0,16},{16,0},{32,48},{48,32},{64,80},{80,64},{96,112},{112,96},{1... | collective-permute-start | bytes 196616 | tf_op jit(solution)/shard_map/ppermute | solution.py:25
  67.3 3.1 %collective-permute-start.21 = (bf16[640,128]{1,0:T(8,128)(2,1)S(1)}, bf16[640,128]{1,0:T(8,128)(2,1)S(1)}, u32[]{:S(2)}, u32[]{:S(2)}) collective-permute-start(bf16[640,128]{1,0:T(8,128)(2,1)S(1)} %pad_maximum_fusion.9.refs_5_), channel_id=1, source_target_pairs={{0,8},{1,9},{2,10},{3,11},{4,12},{5,13},{6,14},{7,15},{8,0},{9,1},... | collective-permute-start | bytes 491528 | tf_op jit(solution)/shard_map/ppermute | solution.py:33
  70.4 2.7 %collective-permute-done.25.refs_10_ = bf16[640,128]{1,0:T(8,128)(2,1)S(1)} collective-permute-done((bf16[640,128]{1,0:T(8,128)(2,1)S(1)}, bf16[640,128]{1,0:T(8,128)(2,1)S(1)}, u32[]{:S(2)}, u32[]{:S(2)}) %collective-permute-start.25) | collective-permute-done | bytes 163872 | tf_op jit(solution)/shard_map/ppermute | solution.py:33
  73.1 1.8 %collective-permute-done.24.refs_9_ = bf16[640,128]{1,0:T(8,128)(2,1)S(1)} collective-permute-done((bf16[640,128]{1,0:T(8,128)(2,1)S(1)}, bf16[640,128]{1,0:T(8,128)(2,1)S(1)}, u32[]{:S(2)}, u32[]{:S(2)}) %collective-permute-start.24) | collective-permute-done | bytes 163872 | tf_op jit(solution)/shard_map/ppermute | solution.py:33
  75.0 4.0 %collective-permute-start.30 = (bf16[1280,128]{1,0:T(8,128)(2,1)S(1)}, bf16[1280,128]{1,0:T(8,128)(2,1)S(1)}, u32[]{:S(2)}, u32[]{:S(2)}) collective-permute-start(bf16[1280,128]{1,0:T(8,128)(2,1)S(1)} %get-tuple-element.58), channel_id=1, source_target_pairs={{0,8},{1,9},{2,10},{3,11},{4,12},{5,13},{6,14},{7,15},{8,0},{9,1},... | collective-permute-start | bytes 983048 | tf_op jit(solution)/shard_map/ppermute | solution.py:33
  79.0 1.9 %collective-permute-start.28 = (bf16[320,128]{1,0:T(8,128)(2,1)S(1)}, bf16[320,128]{1,0:T(8,128)(2,1)S(1)}, u32[]{:S(2)}, u32[]{:S(2)}) collective-permute-start(bf16[320,128]{1,0:T(8,128)(2,1)S(1)} %slice.134), channel_id=1, source_target_pairs={{0,2},{1,3},{2,4},{3,5},{4,6},{5,7},{6,0},{7,1},{8,10},{9,11},{10,... | collective-permute-start | bytes 245768 | tf_op jit(solution)/shard_map/ppermute | solution.py:33
  87.5 1.9 %collective-permute-start.26 = (bf16[1280,128]{1,0:T(8,128)(2,1)S(1)}, bf16[1280,128]{1,0:T(8,128)(2,1)S(1)}, u32[]{:S(2)}, u32[]{:S(2)}) collective-permute-start(bf16[1280,128]{1,0:T(8,128)(2,1)S(1)} %get-tuple-element.60), channel_id=1, source_target_pairs={{0,1},{1,2},{2,3},{3,4},{4,5},{5,6},{6,7},{7,0},{8,9},{9,10},{10,1... | collective-permute-start | bytes 983048 | tf_op jit(solution)/shard_map/ppermute | solution.py:33
  90.6 3.3 %collective-permute-start.32 = (bf16[640,128]{1,0:T(8,128)(2,1)S(1)}, bf16[640,128]{1,0:T(8,128)(2,1)S(1)}, u32[]{:S(2)}, u32[]{:S(2)}) collective-permute-start(bf16[640,128]{1,0:T(8,128)(2,1)S(1)} %get-tuple-element.51), channel_id=1, source_target_pairs={{0,7},{1,0},{2,1},{3,2},{4,3},{5,4},{6,5},{7,6},{8,15},{9,8},{10,9... | collective-permute-start | bytes 491528 | tf_op jit(solution)/shard_map/ppermute | solution.py:33
  95.5 2.4 %collective-permute-done.26.refs_11_ = bf16[1280,128]{1,0:T(8,128)(2,1)S(1)} collective-permute-done((bf16[1280,128]{1,0:T(8,128)(2,1)S(1)}, bf16[1280,128]{1,0:T(8,128)(2,1)S(1)}, u32[]{:S(2)}, u32[]{:S(2)}) %collective-permute-start.26) | collective-permute-done | bytes 327712 | tf_op jit(solution)/shard_map/ppermute | solution.py:33
  99.0 2.4 %collective-permute-done.31.refs_15_ = bf16[640,128]{1,0:T(8,128)(2,1)S(1)} collective-permute-done((bf16[640,128]{1,0:T(8,128)(2,1)S(1)}, bf16[640,128]{1,0:T(8,128)(2,1)S(1)}, u32[]{:S(2)}, u32[]{:S(2)}) %collective-permute-start.31) | collective-permute-done | bytes 163872 | tf_op jit(solution)/shard_map/ppermute | solution.py:33
  101.4 2.4 %shard_map.96 = (f32[4096,128]{1,0:T(8,128)S(1)}, bf16[4096,128]{1,0:T(8,128)(2,1)S(1)}, bf16[128,128]{1,0:T(8,128)(2,1)S(1)}) custom-call(s32[48]{0:T(128)S(1)} %get-tuple-element.72.refs_1_.refs_0_, s32[48]{0:T(128)S(1)} %get-tuple-element.71.refs_0_.refs_1_, s32[1]{0:T(128)} %bitcast.30.refs_2_, s32[16]{0:T(128)S(1)} %and_select_fusion.refs_3_, ...), custom_call_target="tpu_custom_call" | custom-call | tf_op jit(solution)/shard_map/pallas_call | solution.py:101
  103.8 3.1 %collective-permute-start.34 = (bf16[4096,128]{1,0:T(8,128)(2,1)S(1)}, bf16[4096,128]{1,0:T(8,128)(2,1)S(1)}, u32[]{:S(2)}, u32[]{:S(2)}) collective-permute-start(bf16[4096,128]{1,0:T(8,128)(2,1)S(1)} %get-tuple-element.43), channel_id=1, source_target_pairs={{0,16},{16,0},{32,48},{48,32},{64,80},{80,64},{96,112},{112,96},{1... | collective-permute-start | bytes 3145736 | tf_op jit(solution)/shard_map/ppermute | solution.py:25
  106.9 2.3 %collective-permute-done.34 = bf16[4096,128]{1,0:T(8,128)(2,1)S(1)} collective-permute-done((bf16[4096,128]{1,0:T(8,128)(2,1)S(1)}, bf16[4096,128]{1,0:T(8,128)(2,1)S(1)}, u32[]{:S(2)}, u32[]{:S(2)}) %collective-permute-start.34) | collective-permute-done | bytes 1048608 | tf_op jit(solution)/shard_map/ppermute | solution.py:25
  110.6 7.3 %collective-permute-done.37 = bf16[1152,128]{1,0:T(8,128)(2,1)S(1)} collective-permute-done((bf16[1152,128]{1,0:T(8,128)(2,1)S(1)}, bf16[1152,128]{1,0:T(8,128)(2,1)S(1)}, u32[]{:S(2)}, u32[]{:S(2)}) %collective-permute-start.37) | collective-permute-done | bytes 294944 | tf_op jit(solution)/shard_map/ppermute | solution.py:25
  120.8 1.7 %collective-permute-done.39.r3 = bf16[640,128]{1,0:T(8,128)(2,1)S(1)} collective-permute-done((bf16[640,128]{1,0:T(8,128)(2,1)S(1)}, bf16[640,128]{1,0:T(8,128)(2,1)S(1)}, u32[]{:S(2)}, u32[]{:S(2)}) %collective-permute-start.39) | collective-permute-done | bytes 163872 | tf_op jit(solution)/shard_map/ppermute | solution.py:25
  122.5 1.8 %collective-permute-done.36.r1 = bf16[640,128]{1,0:T(8,128)(2,1)S(1)} collective-permute-done((bf16[640,128]{1,0:T(8,128)(2,1)S(1)}, bf16[640,128]{1,0:T(8,128)(2,1)S(1)}, u32[]{:S(2)}, u32[]{:S(2)}) %collective-permute-start.36) | collective-permute-done | bytes 163872 | tf_op jit(solution)/shard_map/ppermute | solution.py:25
  126.1 2.5 %collective-permute-start.40 = (f32[128,128]{1,0:T(8,128)S(1)}, f32[128,128]{1,0:T(8,128)S(1)}, u32[]{:S(2)}, u32[]{:S(2)}) collective-permute-start(f32[128,128]{1,0:T(8,128)S(1)} %add_add_fusion), channel_id=1, source_target_pairs={{0,16},{16,0},{32,48},{48,32},{64,80},{80,64},{96,112},{112,96},{1... | collective-permute-start | bytes 196616 | tf_op jit(solution)/shard_map/ppermute | solution.py:25
  (104 shorter events, 40.3 us)
Async XLA Ops:
  0.7 6.1 %collective-permute-start.2 = (bf16[512,128]{1,0:T(8,128)(2,1)}, bf16[512,128]{1,0:T(8,128)(2,1)S(1)}, u32[]{:S(2)}, u32[]{:S(2)}) collective-permute-start(bf16[512,128]{1,0:T(8,128)(2,1)} %param.7), channel_id=1, source_target_pairs={{0,192},{16,208},{32,224},{48,240},{64,0},{80,16},{96,32},{112,48}... | collective-permute-start | bytes 393224 | tf_op jit(solution)/shard_map/ppermute | solution.py:25
  4.3 6.6 %collective-permute-start = (bf16[512,128]{1,0:T(8,128)(2,1)}, bf16[512,128]{1,0:T(8,128)(2,1)S(1)}, u32[]{:S(2)}, u32[]{:S(2)}) collective-permute-start(bf16[512,128]{1,0:T(8,128)(2,1)} %param.7), channel_id=1, source_target_pairs={{0,32},{16,48},{32,0},{48,16},{64,96},{80,112},{96,64},{112,80},{1... | collective-permute-start | bytes 393224 | tf_op jit(solution)/shard_map/ppermute | solution.py:25
  9.6 9.1 %collective-permute-start.4 = (bf16[1024,128]{1,0:T(8,128)(2,1)S(1)}, bf16[1024,128]{1,0:T(8,128)(2,1)S(1)}, u32[]{:S(2)}, u32[]{:S(2)}) collective-permute-start(bf16[1024,128]{1,0:T(8,128)(2,1)S(1)} %pad_maximum_fusion.6), channel_id=1, source_target_pairs={{0,32},{16,48},{32,0},{48,16},{64,96},{80,112},{96,64},{112,80},{1... | collective-permute-start | bytes 786440 | tf_op jit(solution)/shard_map/ppermute | solution.py:25
  11.8 6.8 %collective-permute-start.3 = (bf16[1024,128]{1,0:T(8,128)(2,1)S(1)}, bf16[1024,128]{1,0:T(8,128)(2,1)S(1)}, u32[]{:S(2)}, u32[]{:S(2)}) collective-permute-start(bf16[1024,128]{1,0:T(8,128)(2,1)S(1)} %pad_maximum_fusion.5), channel_id=1, source_target_pairs={{0,128},{16,144},{32,160},{48,176},{64,192},{80,208},{96,224},{112... | collective-permute-start | bytes 786440 | tf_op jit(solution)/shard_map/ppermute | solution.py:25
  12.0 11.1 %collective-permute-start.5 = (bf16[2048,128]{1,0:T(8,128)(2,1)S(1)}, bf16[2048,128]{1,0:T(8,128)(2,1)S(1)}, u32[]{:S(2)}, u32[]{:S(2)}) collective-permute-start(bf16[2048,128]{1,0:T(8,128)(2,1)S(1)} %constant_dynamic-update-slice_fusion.refs_5_), channel_id=1, source_target_pairs={{0,16},{16,0},{32,48},{48,32},{64,80},{80,64},{96,112},{112,96},{1... | collective-permute-start | bytes 1572872 | tf_op jit(solution)/shard_map/ppermute | solution.py:25
  26.8 9.7 %collective-permute-start.12 = (bf16[512,128]{1,0:T(8,128)(2,1)S(1)}, bf16[512,128]{1,0:T(8,128)(2,1)S(1)}, u32[]{:S(2)}, u32[]{:S(2)}) collective-permute-start(bf16[512,128]{1,0:T(8,128)(2,1)S(1)} %get-tuple-element.32), channel_id=1, source_target_pairs={{0,1},{1,2},{2,3},{3,4},{4,5},{5,6},{6,7},{7,0},{8,9},{9,10},{10,1... | collective-permute-start | bytes 393224 | tf_op jit(solution)/shard_map/ppermute | solution.py:33
  28.5 8.0 %collective-permute-start.13 = (bf16[512,128]{1,0:T(8,128)(2,1)S(1)}, bf16[512,128]{1,0:T(8,128)(2,1)S(1)}, u32[]{:S(2)}, u32[]{:S(2)}) collective-permute-start(bf16[512,128]{1,0:T(8,128)(2,1)S(1)} %get-tuple-element.34), channel_id=1, source_target_pairs={{0,7},{1,0},{2,1},{3,2},{4,3},{5,4},{6,5},{7,6},{8,15},{9,8},{10,9... | collective-permute-start | bytes 393224 | tf_op jit(solution)/shard_map/ppermute | solution.py:33
  32.5 6.5 %collective-permute-start.15 = (bf16[512,128]{1,0:T(8,128)(2,1)S(1)}, bf16[512,128]{1,0:T(8,128)(2,1)S(1)}, u32[]{:S(2)}, u32[]{:S(2)}) collective-permute-start(bf16[512,128]{1,0:T(8,128)(2,1)S(1)} %get-tuple-element.36), channel_id=1, source_target_pairs={{0,8},{1,9},{2,10},{3,11},{4,12},{5,13},{6,14},{7,15},{8,0},{9,1},... | collective-permute-start | bytes 393224 | tf_op jit(solution)/shard_map/ppermute | solution.py:33
  34.4 13.9 %collective-permute-start.9 = (bf16[1024,128]{1,0:T(8,128)(2,1)S(1)}, bf16[1024,128]{1,0:T(8,128)(2,1)S(1)}, u32[]{:S(2)}, u32[]{:S(2)}) collective-permute-start(bf16[1024,128]{1,0:T(8,128)(2,1)S(1)} %get-tuple-element.28), channel_id=1, source_target_pairs={{0,7},{1,0},{2,1},{3,2},{4,3},{5,4},{6,5},{7,6},{8,15},{9,8},{10,9... | collective-permute-start | bytes 786440 | tf_op jit(solution)/shard_map/ppermute | solution.py:33
  35.8 12.6 %collective-permute-start.10 = (bf16[1024,128]{1,0:T(8,128)(2,1)S(1)}, bf16[1024,128]{1,0:T(8,128)(2,1)S(1)}, u32[]{:S(2)}, u32[]{:S(2)}) collective-permute-start(bf16[1024,128]{1,0:T(8,128)(2,1)S(1)} %get-tuple-element.29), channel_id=1, source_target_pairs={{0,1},{1,2},{2,3},{3,4},{4,5},{5,6},{6,7},{7,0},{8,9},{9,10},{10,1... | collective-permute-start | bytes 786440 | tf_op jit(solution)/shard_map/ppermute | solution.py:33
  36.6 11.8 %collective-permute-start.14 = (bf16[1024,128]{1,0:T(8,128)(2,1)S(1)}, bf16[1024,128]{1,0:T(8,128)(2,1)S(1)}, u32[]{:S(2)}, u32[]{:S(2)}) collective-permute-start(bf16[1024,128]{1,0:T(8,128)(2,1)S(1)} %pad_maximum_fusion.7), channel_id=1, source_target_pairs={{0,8},{1,9},{2,10},{3,11},{4,12},{5,13},{6,14},{7,15},{8,0},{9,1},... | collective-permute-start | bytes 786440 | tf_op jit(solution)/shard_map/ppermute | solution.py:33
  40.7 5.5 %collective-permute-start.16 = (bf16[256,128]{1,0:T(8,128)(2,1)S(1)}, bf16[256,128]{1,0:T(8,128)(2,1)S(1)}, u32[]{:S(2)}, u32[]{:S(2)}) collective-permute-start(bf16[256,128]{1,0:T(8,128)(2,1)S(1)} %get-tuple-element.64), channel_id=1, source_target_pairs={{0,2},{1,3},{2,4},{3,5},{4,6},{5,7},{6,0},{7,1},{8,10},{9,11},{10,... | collective-permute-start | bytes 196616 | tf_op jit(solution)/shard_map/ppermute | solution.py:33
  43.4 9.6 %collective-permute-start.7 = (bf16[512,128]{1,0:T(8,128)(2,1)S(1)}, bf16[512,128]{1,0:T(8,128)(2,1)S(1)}, u32[]{:S(2)}, u32[]{:S(2)}) collective-permute-start(bf16[512,128]{1,0:T(8,128)(2,1)S(1)} %get-tuple-element.25), channel_id=1, source_target_pairs={{0,1},{1,2},{2,3},{3,4},{4,5},{5,6},{6,7},{7,0},{8,9},{9,10},{10,1... | collective-permute-start | bytes 393224 | tf_op jit(solution)/shard_map/ppermute | solution.py:33
  46.2 6.8 %collective-permute-start.8 = (bf16[512,128]{1,0:T(8,128)(2,1)S(1)}, bf16[512,128]{1,0:T(8,128)(2,1)S(1)}, u32[]{:S(2)}, u32[]{:S(2)}) collective-permute-start(bf16[512,128]{1,0:T(8,128)(2,1)S(1)} %get-tuple-element.26), channel_id=1, source_target_pairs={{0,7},{1,0},{2,1},{3,2},{4,3},{5,4},{6,5},{7,6},{8,15},{9,8},{10,9... | collective-permute-start | bytes 393224 | tf_op jit(solution)/shard_map/ppermute | solution.py:33
  48.6 6.0 %collective-permute-start.19 = (bf16[512,128]{1,0:T(8,128)(2,1)S(1)}, bf16[512,128]{1,0:T(8,128)(2,1)S(1)}, u32[]{:S(2)}, u32[]{:S(2)}) collective-permute-start(bf16[512,128]{1,0:T(8,128)(2,1)S(1)} %get-tuple-element.55), channel_id=1, source_target_pairs={{0,6},{1,7},{2,0},{3,1},{4,2},{5,3},{6,4},{7,5},{8,14},{9,15},{10,... | collective-permute-start | bytes 393224 | tf_op jit(solution)/shard_map/ppermute | solution.py:33
  51.8 6.9 %collective-permute-start.17 = (bf16[512,128]{1,0:T(8,128)(2,1)S(1)}, bf16[512,128]{1,0:T(8,128)(2,1)S(1)}, u32[]{:S(2)}, u32[]{:S(2)}) collective-permute-start(bf16[512,128]{1,0:T(8,128)(2,1)S(1)} %get-tuple-element.57), channel_id=1, source_target_pairs={{0,2},{1,3},{2,4},{3,5},{4,6},{5,7},{6,0},{7,1},{8,10},{9,11},{10,... | collective-permute-start | bytes 393224 | tf_op jit(solution)/shard_map/ppermute | solution.py:33
  64.8 8.3 %collective-permute-start.25 = (bf16[640,128]{1,0:T(8,128)(2,1)S(1)}, bf16[640,128]{1,0:T(8,128)(2,1)S(1)}, u32[]{:S(2)}, u32[]{:S(2)}) collective-permute-start(bf16[640,128]{1,0:T(8,128)(2,1)S(1)} %pad_maximum_fusion.9.refs_5_), channel_id=1, source_target_pairs={{0,6},{1,7},{2,0},{3,1},{4,2},{5,3},{6,4},{7,5},{8,14},{9,15},{10,... | collective-permute-start | bytes 491528 | tf_op jit(solution)/shard_map/ppermute | solution.py:33
  65.6 9.3 %collective-permute-start.24 = (bf16[640,128]{1,0:T(8,128)(2,1)S(1)}, bf16[640,128]{1,0:T(8,128)(2,1)S(1)}, u32[]{:S(2)}, u32[]{:S(2)}) collective-permute-start(bf16[640,128]{1,0:T(8,128)(2,1)S(1)} %pad_maximum_fusion.9.refs_5_), channel_id=1, source_target_pairs={{0,2},{1,3},{2,4},{3,5},{4,6},{5,7},{6,0},{7,1},{8,10},{9,11},{10,... | collective-permute-start | bytes 491528 | tf_op jit(solution)/shard_map/ppermute | solution.py:33
  67.3 7.6 %collective-permute-start.21 = (bf16[640,128]{1,0:T(8,128)(2,1)S(1)}, bf16[640,128]{1,0:T(8,128)(2,1)S(1)}, u32[]{:S(2)}, u32[]{:S(2)}) collective-permute-start(bf16[640,128]{1,0:T(8,128)(2,1)S(1)} %pad_maximum_fusion.9.refs_5_), channel_id=1, source_target_pairs={{0,8},{1,9},{2,10},{3,11},{4,12},{5,13},{6,14},{7,15},{8,0},{9,1},... | collective-permute-start | bytes 491528 | tf_op jit(solution)/shard_map/ppermute | solution.py:33
  75.0 14.4 %collective-permute-start.30 = (bf16[1280,128]{1,0:T(8,128)(2,1)S(1)}, bf16[1280,128]{1,0:T(8,128)(2,1)S(1)}, u32[]{:S(2)}, u32[]{:S(2)}) collective-permute-start(bf16[1280,128]{1,0:T(8,128)(2,1)S(1)} %get-tuple-element.58), channel_id=1, source_target_pairs={{0,8},{1,9},{2,10},{3,11},{4,12},{5,13},{6,14},{7,15},{8,0},{9,1},... | collective-permute-start | bytes 983048 | tf_op jit(solution)/shard_map/ppermute | solution.py:33
  79.0 6.6 %collective-permute-start.28 = (bf16[320,128]{1,0:T(8,128)(2,1)S(1)}, bf16[320,128]{1,0:T(8,128)(2,1)S(1)}, u32[]{:S(2)}, u32[]{:S(2)}) collective-permute-start(bf16[320,128]{1,0:T(8,128)(2,1)S(1)} %slice.134), channel_id=1, source_target_pairs={{0,2},{1,3},{2,4},{3,5},{4,6},{5,7},{6,0},{7,1},{8,10},{9,11},{10,... | collective-permute-start | bytes 245768 | tf_op jit(solution)/shard_map/ppermute | solution.py:33
  80.9 9.7 %collective-permute-start.23 = (bf16[640,128]{1,0:T(8,128)(2,1)S(1)}, bf16[640,128]{1,0:T(8,128)(2,1)S(1)}, u32[]{:S(2)}, u32[]{:S(2)}) collective-permute-start(bf16[640,128]{1,0:T(8,128)(2,1)S(1)} %pad_maximum_fusion.9.refs_5_), channel_id=1, source_target_pairs={{0,7},{1,0},{2,1},{3,2},{4,3},{5,4},{6,5},{7,6},{8,15},{9,8},{10,9... | collective-permute-start | bytes 491528 | tf_op jit(solution)/shard_map/ppermute | solution.py:33
  81.3 12.6 %collective-permute-start.22 = (bf16[640,128]{1,0:T(8,128)(2,1)S(1)}, bf16[640,128]{1,0:T(8,128)(2,1)S(1)}, u32[]{:S(2)}, u32[]{:S(2)}) collective-permute-start(bf16[640,128]{1,0:T(8,128)(2,1)S(1)} %pad_maximum_fusion.9.refs_5_), channel_id=1, source_target_pairs={{0,1},{1,2},{2,3},{3,4},{4,5},{5,6},{6,7},{7,0},{8,9},{9,10},{10,1... | collective-permute-start | bytes 491528 | tf_op jit(solution)/shard_map/ppermute | solution.py:33
  85.6 9.9 %collective-permute-start.27 = (bf16[1280,128]{1,0:T(8,128)(2,1)S(1)}, bf16[1280,128]{1,0:T(8,128)(2,1)S(1)}, u32[]{:S(2)}, u32[]{:S(2)}) collective-permute-start(bf16[1280,128]{1,0:T(8,128)(2,1)S(1)} %get-tuple-element.59), channel_id=1, source_target_pairs={{0,7},{1,0},{2,1},{3,2},{4,3},{5,4},{6,5},{7,6},{8,15},{9,8},{10,9... | collective-permute-start | bytes 983048 | tf_op jit(solution)/shard_map/ppermute | solution.py:33
  87.5 10.3 %collective-permute-start.26 = (bf16[1280,128]{1,0:T(8,128)(2,1)S(1)}, bf16[1280,128]{1,0:T(8,128)(2,1)S(1)}, u32[]{:S(2)}, u32[]{:S(2)}) collective-permute-start(bf16[1280,128]{1,0:T(8,128)(2,1)S(1)} %get-tuple-element.60), channel_id=1, source_target_pairs={{0,1},{1,2},{2,3},{3,4},{4,5},{5,6},{6,7},{7,0},{8,9},{9,10},{10,1... | collective-permute-start | bytes 983048 | tf_op jit(solution)/shard_map/ppermute | solution.py:33
  89.4 5.8 %collective-permute-start.33 = (bf16[640,128]{1,0:T(8,128)(2,1)S(1)}, bf16[640,128]{1,0:T(8,128)(2,1)S(1)}, u32[]{:S(2)}, u32[]{:S(2)}) collective-permute-start(bf16[640,128]{1,0:T(8,128)(2,1)S(1)} %constant_dynamic-update-slice_fusion.6.refs_13_), channel_id=1, source_target_pairs={{0,8},{1,9},{2,10},{3,11},{4,12},{5,13},{6,14},{7,15},{8,0},{9,1},... | collective-permute-start | bytes 491528 | tf_op jit(solution)/shard_map/ppermute | solution.py:33
  90.6 8.4 %collective-permute-start.32 = (bf16[640,128]{1,0:T(8,128)(2,1)S(1)}, bf16[640,128]{1,0:T(8,128)(2,1)S(1)}, u32[]{:S(2)}, u32[]{:S(2)}) collective-permute-start(bf16[640,128]{1,0:T(8,128)(2,1)S(1)} %get-tuple-element.51), channel_id=1, source_target_pairs={{0,7},{1,0},{2,1},{3,2},{4,3},{5,4},{6,5},{7,6},{8,15},{9,8},{10,9... | collective-permute-start | bytes 491528 | tf_op jit(solution)/shard_map/ppermute | solution.py:33
  93.9 7.5 %collective-permute-start.31 = (bf16[640,128]{1,0:T(8,128)(2,1)S(1)}, bf16[640,128]{1,0:T(8,128)(2,1)S(1)}, u32[]{:S(2)}, u32[]{:S(2)}) collective-permute-start(bf16[640,128]{1,0:T(8,128)(2,1)S(1)} %get-tuple-element.52), channel_id=1, source_target_pairs={{0,1},{1,2},{2,3},{3,4},{4,5},{5,6},{6,7},{7,0},{8,9},{9,10},{10,1... | collective-permute-start | bytes 491528 | tf_op jit(solution)/shard_map/ppermute | solution.py:33
  103.8 5.4 %collective-permute-start.34 = (bf16[4096,128]{1,0:T(8,128)(2,1)S(1)}, bf16[4096,128]{1,0:T(8,128)(2,1)S(1)}, u32[]{:S(2)}, u32[]{:S(2)}) collective-permute-start(bf16[4096,128]{1,0:T(8,128)(2,1)S(1)} %get-tuple-element.43), channel_id=1, source_target_pairs={{0,16},{16,0},{32,48},{48,32},{64,80},{80,64},{96,112},{112,96},{1... | collective-permute-start | bytes 3145736 | tf_op jit(solution)/shard_map/ppermute | solution.py:25
  109.5 8.3 %collective-permute-start.37 = (bf16[1152,128]{1,0:T(8,128)(2,1)S(1)}, bf16[1152,128]{1,0:T(8,128)(2,1)S(1)}, u32[]{:S(2)}, u32[]{:S(2)}) collective-permute-start(bf16[1152,128]{1,0:T(8,128)(2,1)S(1)} %get-tuple-element.69), channel_id=1, source_target_pairs={{0,32},{16,48},{32,0},{48,16},{64,96},{80,112},{96,64},{112,80},{1... | collective-permute-start | bytes 884744 | tf_op jit(solution)/shard_map/ppermute | solution.py:25
  110.4 9.4 %collective-permute-start.35 = (bf16[1152,128]{1,0:T(8,128)(2,1)S(1)}, bf16[1152,128]{1,0:T(8,128)(2,1)S(1)}, u32[]{:S(2)}, u32[]{:S(2)}) collective-permute-start(bf16[1152,128]{1,0:T(8,128)(2,1)S(1)} %get-tuple-element.70), channel_id=1, source_target_pairs={{0,128},{16,144},{32,160},{48,176},{64,192},{80,208},{96,224},{112... | collective-permute-start | bytes 884744 | tf_op jit(solution)/shard_map/ppermute | solution.py:25
  119.9 6.2 %collective-permute-start.38 = (bf16[768,128]{1,0:T(8,128)(2,1)S(1)}, bf16[768,128]{1,0:T(8,128)(2,1)S(1)}, u32[]{:S(2)}, u32[]{:S(2)}) collective-permute-start(bf16[768,128]{1,0:T(8,128)(2,1)S(1)} %pad_maximum_fusion.8), channel_id=1, source_target_pairs={{0,64},{16,80},{32,96},{48,112},{64,128},{80,144},{96,160},{112,17... | collective-permute-start | bytes 589832 | tf_op jit(solution)/shard_map/ppermute | solution.py:25
  (14 other events, 154.8 us)

commit v4 on v3

--- a/solution.py
+++ b/solution.py
@@ -31,6 +31,20 @@
         for z in range(NZ):
             perm.append((h * NZ + z, (h ^ dh) * NZ + (z + dz) % NZ))
     return lax.ppermute(x, "col", perm)
+
+
+def send_apart(x, dz):
+    perm = []
+    for r in range(NY * NXL * NC):
+        for h in range(NXH):
+            for z in range(NZ):
+                to = h * NZ + (z + (dz if r % NC == 0 else -dz)) % NZ
+                perm.append(((r * NXH + h) * NZ + z, r * NXH * NZ + to))
+    return lax.ppermute(x, ("row", "col"), perm)
+
+
+def copy_kernel(x_ref, out_ref):
+    out_ref[...] = x_ref[...]
 
 
 def row_slots(blocks):
@@ -114,7 +128,7 @@
 def mid_kernel(core_ref, own_ref, r1, r2, r3, r4, r5, weight_ref, gout_ref, act_ref, gt_ref, keep_ref, give_ref, gw_ref):
     ax = own_ref[...]
     for r in (r1, r2, r3, r4, r5):
-        ax = ax + r[...].astype(F32)
+        ax = ax + r[:SHARD, :].astype(F32)
     high = ax.astype(BF16)
     low = (ax - high.astype(F32)).astype(BF16)
     weight = weight_ref[...]
@@ -134,11 +148,8 @@
         low, gp, first, preferred_element_type=F32
     )
     core = core_ref[0]
-    half = BLOCK // 2
     for ref, which in ((keep_ref, core), (give_ref, 1 - core)):
-        at = pl.ds(pl.multiple_of(which * half, half), half)
-        ref[:half, :] = gw_ref[at, :BLOCK]
-        ref[half:, :] = gw_ref[at, BLOCK:]
+        ref[...] = gw_ref[:, pl.ds(pl.multiple_of(which * BLOCK, BLOCK), BLOCK)]
 
 
 def last_kernel(own_ref, w_ref, r1, r2, r3, out_ref):
@@ -172,7 +183,10 @@
     u = send_row(features, dy=1)
     d = send_row(features, dy=-1)
     ud = jnp.concatenate([u, d])
-    xa = jnp.concatenate([features, a])
+    near = pl.pallas_call(
+        copy_kernel, out_shape=jax.ShapeDtypeStruct((S, BLOCK), BF16), compiler_params=params
+    )(features)
+    xa = jnp.concatenate([near, a])
     w = send_row(xa, dy=2)
     v = send_row(ud, dx=1)
     h1 = jnp.concatenate([xa, ud])
@@ -186,29 +200,23 @@
 
     O = lambda k: (k % 8 * S, S)
     X = lambda k: ((8 + k % 8) * S, S)
-    outs = [[X(-3)], [X(3)], [X(4)], [O(1)], [O(-1)], [O(-3), X(-1)], [O(3), X(1)],
+    outs = [[X(-1), X(-3)], [X(1), X(3)], [X(4)], [O(-1), O(-3)], [O(1), O(3)],
             [X(-2)], [X(2)], [O(4)], [X(0)], [O(2)], [O(-2)], [O(0)]]
-    (x5, x3, x4, o1, o7, e, g, x6, x2, o4, x0, o2, o6, o0) = tile_sums(
+    m, n, l, e, g, x6, x2, o4, x0, o2, o6, o0 = tile_sums(
         col_at, row_at, count, scan, values, [h1, h2, c1, c2], places, outs,
-        [BF16] * 7 + [F32] * 7, True,
-    )
-    r5 = send_col(x5, dz=-1)
-    r3 = send_col(x3, dz=1)
-    r4 = send_col(x4, dh=1)
-    s1 = send_col(o1, dz=1)
-    s7 = send_col(o7, dz=-1)
-    re = send_col(e, dz=-1)
-    rg = send_col(g, dz=1)
-    q = jnp.concatenate([add(x2, r3).astype(BF16), add(x6, r5).astype(BF16)])
-    rq = send_col(q, dh=1)
-    o4 = add(o4, r4).astype(BF16)
-    rh = send_col(o4[: S // 2], dz=2)
-    ri = send_col(o4[S // 2:], dz=-2)
-    x0 = add(x0, re[S:], rg[S:]).astype(BF16)
-    rx = send_col(x0, dh=1)
-    zero = jnp.zeros((S // 2, BLOCK), F32)
-    o2 = add(o2, rg[:S], rq[:S], jnp.concatenate([rh.astype(F32), zero])).astype(BF16)
-    o6 = add(o6, re[:S], rq[S:], jnp.concatenate([zero, ri.astype(F32)])).astype(BF16)
+        [BF16] * 5 + [F32] * 7, True,
+    )
+    m = send_col(m, dz=-1)
+    n = send_col(n, dz=1)
+    l = send_col(l, dh=1)
+    e = send_col(e, dz=-1)
+    g = send_col(g, dz=1)
+    q = jnp.concatenate([add(x2, n[S:]).astype(BF16), add(x6, m[S:]).astype(BF16)])
+    q = send_col(q, dh=1)
+    h = send_apart(add(o4, l).astype(BF16), -2).astype(F32)
+    rx = send_col(add(x0, m[:S], n[:S]).astype(BF16), dh=1)
+    o2 = add(o2, g[S:], q[:S], jnp.where(core == 0, 0.0, h)).astype(BF16)
+    o6 = add(o6, e[S:], q[S:], jnp.where(core == 0, h, 0.0)).astype(BF16)
     s2 = send_col(o2, dz=2)
     s6 = send_col(o6, dz=-2)
 
@@ -224,38 +232,36 @@
         in_specs=[pl.BlockSpec(memory_space=pltpu.SMEM)] + [pl.BlockSpec(memory_space=pltpu.VMEM)] * 8,
         scratch_shapes=[pltpu.VMEM((BLOCK, 256), F32)],
         compiler_params=params,
-    )(core[None], o0, s1, s7, rx, s2, s6, weight, grad_out)
+    )(core[None], o0, e, g, rx, s2, s6, weight, grad_out)
     share = keep + send_row(give, dc=1)
     gt = jnp.concatenate([gt, share.astype(BF16)])
 
-    a = send_col(gt, dh=1)
-    u = send_col(gt, dz=1)
-    d = send_col(gt, dz=-1)
     u2 = send_col(gt, dz=2)
     d2 = send_col(gt, dz=-2)
-    e = send_col(jnp.concatenate([u2, a]), dz=1)
-    g = send_col(jnp.concatenate([d2, a]), dz=-1)
-    f1 = send_col(u2[: ROWS // 2], dz=2)
-    f2 = send_col(d2[ROWS // 2:], dz=-2)
+    a = send_col(gt, dh=1)
     q = send_col(jnp.concatenate([u2, d2]), dh=1)
-    f4 = jnp.concatenate([f1, f2])
-    m = send_col(q[:ROWS], dz=1)
-    n = send_col(q[ROWS:], dz=-1)
+    f4 = send_apart(jnp.where(core == 0, u2, d2), 2)
+    e = send_col(jnp.concatenate([gt, u2]), dz=1)
+    g = send_col(jnp.concatenate([gt, d2]), dz=-1)
+    m = send_col(jnp.concatenate([a, q[:ROWS]]), dz=1)
+    n = send_col(jnp.concatenate([a, q[ROWS:]]), dz=-1)
     l = send_col(f4, dh=1)
-    panels = [gt, a, u, d, u2, d2, e, g, f4, q, m, n, l]
+    panels = [gt, a, u2, d2, q, f4, e, g, m, n, l]
     both = lambda *slots: [p for f, r in slots for p in ((f, r), (16 * S + f // 4, BLOCK))]
-    places = [both(O(0)), both(X(0)), both(O(-1)), both(O(1)), both(O(-2)), both(O(2)),
-              both(O(-3), X(-1)), both(O(3), X(1)), both(O(4)), both(X(-2), X(2)),
-              both(X(-3)), both(X(3)), both(X(4))]
+    places = [both(O(0)), both(X(0)), both(O(-2)), both(O(2)), both(X(-2), X(2)), both(O(4)),
+              both(O(-1), O(-3)), both(O(1), O(3)), both(X(-1), X(-3)), both(X(1), X(3)), both(X(4))]
 
     k = lambda dy, dx: ((dx * 4 + dy % 4) * S, S)
-    order = [k(0, 0), k(0, 1), k(1, 0), k(-1, 0), k(1, 1), k(-1, 1), k(2, 0), k(2, 1)]
-    own, away, share = tile_sums(
-        row_at, col_at, count, scan, values, panels, places, [order, other(order)], [F32, BF16], False
-    )
-    own = own + send_row(away, dc=1).astype(F32)
-    w = send_row(jnp.concatenate([own[6 * S:].astype(BF16), share]), dy=2)
-    v = send_row(jnp.concatenate([own[4 * S:6 * S].astype(BF16), share]), dx=1)
+    last = [k(0, 0), k(0, 1), k(1, 0), k(-1, 0)]
+    early = [k(1, 1), k(-1, 1), k(2, 0), k(2, 1)]
+    own, away, own1, away1, share = tile_sums(
+        row_at, col_at, count, scan, values, panels, places,
+        [last, other(last), early, other(early)], [F32, BF16] * 2, False,
+    )
+    own1 = add(own1, send_row(away1, dc=1)).astype(BF16)
+    own = add(own, send_row(away, dc=1))
+    w = send_row(jnp.concatenate([own1[2 * S:], share]), dy=2)
+    v = send_row(jnp.concatenate([own1[:2 * S], share]), dx=1)
     o = add(own[S:2 * S], w[S:2 * S]).astype(BF16)
     ud = add(own[2 * S:4 * S], v[:2 * S]).astype(BF16)
     here = rounded(add(share, w[2 * S:]))
@@ -271,9 +277,8 @@
         out_shape=jax.ShapeDtypeStruct((S, BLOCK), BF16),
         compiler_params=params,
     )(own[:S], w, ro, ru, rd)
-    wide = lambda x: jnp.concatenate([x[:BLOCK // 2], x[BLOCK // 2:]], axis=1)
-    top, bottom = jnp.where(core == 0, mine, theirs), jnp.where(core == 0, theirs, mine)
-    grad_weight = jnp.concatenate([wide(top), wide(bottom)])
+    first, second = jnp.where(core == 0, mine, theirs), jnp.where(core == 0, theirs, mine)
+    grad_weight = jnp.concatenate([first, second], axis=1)
     return (activation, grad_features, grad_weight)
 
 

time: 130 us -> 134 us (1.031)
  waiting for transfers between devices: 49.8 us -> 55.1 us
  starting transfers between devices: 67.6 us -> 64.8 us
    ppermute x26 -> x18, starting transfers between devices: 43.4 us -> 32.3 us  [send_col(): return lax.ppermute(x, 'col', perm)]
    ppermute x0 -> x2, waiting for transfers between devices: none -> 7.18 us  [send_apart(): return lax.ppermute(x, ('row', 'col'), perm)]
    ppermute x15 -> x16, starting transfers between devices: 24.2 us -> 30.2 us  [send_row(): return lax.ppermute(x, 'row', perm)]
    ppermute x15 -> x16, waiting for transfers between devices: 25.3 us -> 20 us  [send_row(): return lax.ppermute(x, 'row', perm)]
    ppermute x26 -> x18, waiting for transfers between devices: 24.5 us -> 28 us  [send_col(): return lax.ppermute(x, 'col', perm)]
    ppermute x0 -> x2, starting transfers between devices: none -> 2.31 us  [send_apart(): return lax.ppermute(x, ('row', 'col'), perm)]
    convert_element_type x4, other arithmetic: 0.26 us -> 2.16 us  [the longest x1 1.24 us: body(): o6 = add(o6, e[S:], q[S:], jnp.where(core == 0, h, 0.0)).astype(BF16)]
  transfers between devices with their start and end apart: 41 -> 36, of which waited for: 28 -> 21; matrix products, arithmetic and copies ran while one was open for 2% -> 2% of each run, Pallas kernels for 1% -> 1%
where the time goes in v4:
time: 134 us
  starting transfers between devices  64.8 us (48%)
  waiting for transfers between devices  55.1 us (41%)
  Pallas kernels  7.93 us (6%)
  other arithmetic  3.53 us (3%)
  between operations  1.62 us (1%)
    ppermute x18, starting transfers between devices, send_col(): return lax.ppermute(x, 'col', perm)  32.3 us
    ppermute x16, starting transfers between devices, send_row(): return lax.ppermute(x, 'row', perm)  30.2 us
    ppermute x18, waiting for transfers between devices, send_col(): return lax.ppermute(x, 'col', perm)  28 us
    ppermute x16, waiting for transfers between devices, send_row(): return lax.ppermute(x, 'row', perm)  20 us
    ppermute x2, waiting for transfers between devices, send_apart(): return lax.ppermute(x, ('row', 'col'), perm)  7.18 us
    pallas_call x2, Pallas kernels, tile_sums(): pl.pallas_call(functools.partial(tile_kernel, places, outs, left), out_sh...  5.75 us
  transfers between devices with their start and end apart: 36, of which 21 were waited for; matrix products, arithmetic and copies ran while one was open for 2% of the time, Pallas kernels for 1%

profile of v4, /device:TPU:1, one launch (start us, length us, event | category | flops | bytes accessed | tf_op | source)
XLA Modules:
  0.0 134.2 jit_solution(9079653654606842)
XLA Ops:
  0.6 2.1 %collective-permute-start = (bf16[512,128]{1,0:T(8,128)(2,1)}, bf16[512,128]{1,0:T(8,128)(2,1)S(1)}, u32[]{:S(2)}, u32[]{:S(2)}) collective-permute-start(bf16[512,128]{1,0:T(8,128)(2,1)} %x_ref.1), channel_id=1, source_target_pairs={{0,32},{16,48},{32,0},{48,16},{64,96},{80,112},{96,64},{112,80},{1... | collective-permute-start | bytes 393224 | tf_op jit(solution)/shard_map/ppermute | solution.py:25
  2.8 2.7 %collective-permute-start.2 = (bf16[512,128]{1,0:T(8,128)(2,1)}, bf16[512,128]{1,0:T(8,128)(2,1)S(1)}, u32[]{:S(2)}, u32[]{:S(2)}) collective-permute-start(bf16[512,128]{1,0:T(8,128)(2,1)} %x_ref.1), channel_id=1, source_target_pairs={{0,192},{16,208},{32,224},{48,240},{64,0},{80,16},{96,32},{112,48}... | collective-permute-start | bytes 393224 | tf_op jit(solution)/shard_map/ppermute | solution.py:25
  6.6 2.6 %collective-permute-start.3 = (bf16[1024,128]{1,0:T(8,128)(2,1)S(1)}, bf16[1024,128]{1,0:T(8,128)(2,1)S(1)}, u32[]{:S(2)}, u32[]{:S(2)}) collective-permute-start(bf16[1024,128]{1,0:T(8,128)(2,1)S(1)} %pad_maximum_fusion.9), channel_id=1, source_target_pairs={{0,128},{16,144},{32,160},{48,176},{64,192},{80,208},{96,224},{112... | collective-permute-start | bytes 786440 | tf_op jit(solution)/shard_map/ppermute | solution.py:25
  9.1 1.8 %collective-permute-done.1 = bf16[512,128]{1,0:T(8,128)(2,1)S(1)} collective-permute-done((bf16[512,128]{1,0:T(8,128)(2,1)}, bf16[512,128]{1,0:T(8,128)(2,1)S(1)}, u32[]{:S(2)}, u32[]{:S(2)}) %collective-permute-start.1) | collective-permute-done | bytes 131104 | tf_op jit(solution)/shard_map/ppermute | solution.py:25
  11.1 8.4 %collective-permute-start.5 = (bf16[2048,128]{1,0:T(8,128)(2,1)S(1)}, bf16[2048,128]{1,0:T(8,128)(2,1)S(1)}, u32[]{:S(2)}, u32[]{:S(2)}) collective-permute-start(bf16[2048,128]{1,0:T(8,128)(2,1)S(1)} %pad_maximum_fusion.refs_5_), channel_id=1, source_target_pairs={{0,16},{16,0},{32,48},{48,32},{64,80},{80,64},{96,112},{112,96},{1... | collective-permute-start | bytes 1572872 | tf_op jit(solution)/shard_map/ppermute | solution.py:25
  19.6 5.5 %collective-permute-start.6 = (bf16[2048,128]{1,0:T(8,128)(2,1)S(1)}, bf16[2048,128]{1,0:T(8,128)(2,1)}, u32[]{:S(2)}, u32[]{:S(2)}) collective-permute-start(bf16[2048,128]{1,0:T(8,128)(2,1)S(1)} %constant_dynamic-update-slice_fusion.refs_6_), channel_id=1, source_target_pairs={{0,16},{16,0},{32,48},{48,32},{64,80},{80,64},{96,112},{112,96},{1... | collective-permute-start | bytes 1572872 | tf_op jit(solution)/shard_map/ppermute | solution.py:25
  26.8 3.4 %shard_map.95 = (bf16[1024,128]{1,0:T(8,128)(2,1)S(1)}, bf16[1024,128]{1,0:T(8,128)(2,1)S(1)}, bf16[512,128]{1,0:T(8,128)(2,1)S(1)}, bf16[1024,128]{1,0:T(8,128)...) custom-call(s32[48]{0:T(128)S(1)} %get-tuple-element.67.refs_0_.refs, ...), custom_call_target="tpu_custom_call" | custom-call | tf_op jit(solution)/shard_map/pallas_call | solution.py:115
  30.1 5.3 %collective-permute-start.9 = (bf16[1024,128]{1,0:T(8,128)(2,1)S(1)}, bf16[1024,128]{1,0:T(8,128)(2,1)S(1)}, u32[]{:S(2)}, u32[]{:S(2)}) collective-permute-start(bf16[1024,128]{1,0:T(8,128)(2,1)S(1)} %get-tuple-element.28), channel_id=1, source_target_pairs={{0,7},{1,0},{2,1},{3,2},{4,3},{5,4},{6,5},{7,6},{8,15},{9,8},{10,9... | collective-permute-start | bytes 786440 | tf_op jit(solution)/shard_map/ppermute | solution.py:33
  35.4 2.7 %collective-permute-start.13 = (bf16[512,128]{1,0:T(8,128)(2,1)S(1)}, bf16[512,128]{1,0:T(8,128)(2,1)S(1)}, u32[]{:S(2)}, u32[]{:S(2)}) collective-permute-start(bf16[512,128]{1,0:T(8,128)(2,1)S(1)} %get-tuple-element.34), channel_id=1, source_target_pairs={{0,8},{1,9},{2,10},{3,11},{4,12},{5,13},{6,14},{7,15},{8,0},{9,1},... | collective-permute-start | bytes 393224 | tf_op jit(solution)/shard_map/ppermute | solution.py:33
  38.1 2.7 %collective-permute-start.7 = (bf16[1024,128]{1,0:T(8,128)(2,1)}, bf16[1024,128]{1,0:T(8,128)(2,1)S(1)}, u32[]{:S(2)}, u32[]{:S(2)}) collective-permute-start(bf16[1024,128]{1,0:T(8,128)(2,1)} %get-tuple-element.25), channel_id=1, source_target_pairs={{0,7},{1,0},{2,1},{3,2},{4,3},{5,4},{6,5},{7,6},{8,15},{9,8},{10,9... | collective-permute-start | bytes 786440 | tf_op jit(solution)/shard_map/ppermute | solution.py:33
  40.8 2.7 %collective-permute-done.10 = bf16[1024,128]{1,0:T(8,128)(2,1)S(1)} collective-permute-done((bf16[1024,128]{1,0:T(8,128)(2,1)S(1)}, bf16[1024,128]{1,0:T(8,128)(2,1)S(1)}, u32[]{:S(2)}, u32[]{:S(2)}) %collective-permute-start.10) | collective-permute-done | bytes 262176 | tf_op jit(solution)/shard_map/ppermute | solution.py:33
  44.3 3.1 %collective-permute-start.12 = (bf16[1024,128]{1,0:T(8,128)(2,1)S(1)}, bf16[1024,128]{1,0:T(8,128)(2,1)S(1)}, u32[]{:S(2)}, u32[]{:S(2)}) collective-permute-start(bf16[1024,128]{1,0:T(8,128)(2,1)S(1)} %pad_maximum_fusion.11), channel_id=1, source_target_pairs={{0,8},{1,9},{2,10},{3,11},{4,12},{5,13},{6,14},{7,15},{8,0},{9,1},... | collective-permute-start | bytes 786440 | tf_op jit(solution)/shard_map/ppermute | solution.py:33
  47.7 7.2 %collective-permute-done.14 = bf16[512,128]{1,0:T(8,128)(2,1)} collective-permute-done((bf16[512,128]{1,0:T(8,128)(2,1)S(1)}, bf16[512,128]{1,0:T(8,128)(2,1)}, u32[]{:S(2)}, u32[]{:S(2)}) %collective-permute-start.14) | collective-permute-done | bytes 131104 | tf_op jit(solution)/shard_map/ppermute | solution.py:43
  56.4 2.4 %collective-permute-start.15 = (bf16[512,128]{1,0:T(8,128)(2,1)S(1)}, bf16[512,128]{1,0:T(8,128)(2,1)S(1)}, u32[]{:S(2)}, u32[]{:S(2)}) collective-permute-start(bf16[512,128]{1,0:T(8,128)(2,1)S(1)} %get-tuple-element.50), channel_id=1, source_target_pairs={{0,2},{1,3},{2,4},{3,5},{4,6},{5,7},{6,0},{7,1},{8,10},{9,11},{10,... | collective-permute-start | bytes 393224 | tf_op jit(solution)/shard_map/ppermute | solution.py:33
  58.8 4.9 %collective-permute-done.16.r5 = bf16[512,128]{1,0:T(8,128)(2,1)S(1)} collective-permute-done((bf16[512,128]{1,0:T(8,128)(2,1)S(1)}, bf16[512,128]{1,0:T(8,128)(2,1)S(1)}, u32[]{:S(2)}, u32[]{:S(2)}) %collective-permute-start.16) | collective-permute-done | bytes 131104 | tf_op jit(solution)/shard_map/ppermute | solution.py:33
  66.3 2.8 %collective-permute-start.17 = (f32[128,128]{1,0:T(8,128)S(1)}, f32[128,128]{1,0:T(8,128)S(1)}, u32[]{:S(2)}, u32[]{:S(2)}) collective-permute-start(f32[128,128]{1,0:T(8,128)S(1)} %get-tuple-element.39), channel_id=1, source_target_pairs={{0,16},{16,0},{32,48},{48,32},{64,80},{80,64},{96,112},{112,96},{1... | collective-permute-start | bytes 196616 | tf_op jit(solution)/shard_map/ppermute | solution.py:25
  72.5 6.8 %collective-permute-done.20.refs_8_ = bf16[640,128]{1,0:T(8,128)(2,1)S(1)} collective-permute-done((bf16[640,128]{1,0:T(8,128)(2,1)S(1)}, bf16[640,128]{1,0:T(8,128)(2,1)S(1)}, u32[]{:S(2)}, u32[]{:S(2)}) %collective-permute-start.20) | collective-permute-done | bytes 163872 | tf_op jit(solution)/shard_map/ppermute | solution.py:33
  79.4 2.1 %collective-permute-start.21 = (bf16[1280,128]{1,0:T(8,128)(2,1)S(1)}, bf16[1280,128]{1,0:T(8,128)(2,1)S(1)}, u32[]{:S(2)}, u32[]{:S(2)}) collective-permute-start(bf16[1280,128]{1,0:T(8,128)(2,1)S(1)} %get-tuple-element.62), channel_id=1, source_target_pairs={{0,8},{1,9},{2,10},{3,11},{4,12},{5,13},{6,14},{7,15},{8,0},{9,1},... | collective-permute-start | bytes 983048 | tf_op jit(solution)/shard_map/ppermute | solution.py:33
  82.5 2.2 %collective-permute-start.22 = (bf16[640,128]{1,0:T(8,128)(2,1)S(1)}, bf16[640,128]{1,0:T(8,128)(2,1)S(1)}, u32[]{:S(2)}, u32[]{:S(2)}) collective-permute-start(bf16[640,128]{1,0:T(8,128)(2,1)S(1)} %broadcast_select_fusion), channel_id=1, source_target_pairs={{0,2},{1,3},{2,4},{3,5},{4,6},{5,7},{6,0},{7,1},{8,10},{9,11},{10,... | collective-permute-start | bytes 491528 | tf_op jit(solution)/shard_map/ppermute | solution.py:43
  84.7 3.3 %collective-permute-start.24 = (bf16[1280,128]{1,0:T(8,128)(2,1)S(1)}, bf16[1280,128]{1,0:T(8,128)(2,1)S(1)}, u32[]{:S(2)}, u32[]{:S(2)}) collective-permute-start(bf16[1280,128]{1,0:T(8,128)(2,1)S(1)} %get-tuple-element.60), channel_id=1, source_target_pairs={{0,7},{1,0},{2,1},{3,2},{4,3},{5,4},{6,5},{7,6},{8,15},{9,8},{10,9... | collective-permute-start | bytes 983048 | tf_op jit(solution)/shard_map/ppermute | solution.py:33
  88.0 2.8 %collective-permute-done.18.refs_6_ = bf16[640,128]{1,0:T(8,128)(2,1)S(1)} collective-permute-done((bf16[640,128]{1,0:T(8,128)(2,1)S(1)}, bf16[640,128]{1,0:T(8,128)(2,1)S(1)}, u32[]{:S(2)}, u32[]{:S(2)}) %collective-permute-start.18) | collective-permute-done | bytes 163872 | tf_op jit(solution)/shard_map/ppermute | solution.py:33
  90.9 4.1 %collective-permute-start.26 = (bf16[1280,128]{1,0:T(8,128)(2,1)S(1)}, bf16[1280,128]{1,0:T(8,128)(2,1)S(1)}, u32[]{:S(2)}, u32[]{:S(2)}) collective-permute-start(bf16[1280,128]{1,0:T(8,128)(2,1)S(1)} %get-tuple-element.58), channel_id=1, source_target_pairs={{0,7},{1,0},{2,1},{3,2},{4,3},{5,4},{6,5},{7,6},{8,15},{9,8},{10,9... | collective-permute-start | bytes 983048 | tf_op jit(solution)/shard_map/ppermute | solution.py:33
  95.0 2.3 %collective-permute-start.25 = (bf16[1280,128]{1,0:T(8,128)(2,1)S(1)}, bf16[1280,128]{1,0:T(8,128)(2,1)S(1)}, u32[]{:S(2)}, u32[]{:S(2)}) collective-permute-start(bf16[1280,128]{1,0:T(8,128)(2,1)S(1)} %get-tuple-element.59), channel_id=1, source_target_pairs={{0,1},{1,2},{2,3},{3,4},{4,5},{5,6},{6,7},{7,0},{8,9},{9,10},{10,1... | collective-permute-start | bytes 983048 | tf_op jit(solution)/shard_map/ppermute | solution.py:33
  97.9 2.5 %collective-permute-done.23.refs_11_ = bf16[1280,128]{1,0:T(8,128)(2,1)S(1)} collective-permute-done((bf16[1280,128]{1,0:T(8,128)(2,1)S(1)}, bf16[1280,128]{1,0:T(8,128)(2,1)S(1)}, u32[]{:S(2)}, u32[]{:S(2)}) %collective-permute-start.23) | collective-permute-done | bytes 327712 | tf_op jit(solution)/shard_map/ppermute | solution.py:33
  100.3 2.7 %collective-permute-done.27.refs_15_ = bf16[640,128]{1,0:T(8,128)(2,1)S(1)} collective-permute-done((bf16[640,128]{1,0:T(8,128)(2,1)S(1)}, bf16[640,128]{1,0:T(8,128)(2,1)S(1)}, u32[]{:S(2)}, u32[]{:S(2)}) %collective-permute-start.27) | collective-permute-done | bytes 163872 | tf_op jit(solution)/shard_map/ppermute | solution.py:33
  103.7 3.6 %collective-permute-done.25.refs_13_ = bf16[1280,128]{1,0:T(8,128)(2,1)S(1)} collective-permute-done((bf16[1280,128]{1,0:T(8,128)(2,1)S(1)}, bf16[1280,128]{1,0:T(8,128)(2,1)S(1)}, u32[]{:S(2)}, u32[]{:S(2)}) %collective-permute-start.25) | collective-permute-done | bytes 327712 | tf_op jit(solution)/shard_map/ppermute | solution.py:33
  107.3 2.4 %shard_map.97 = (f32[2048,128]{1,0:T(8,128)S(1)}, bf16[2048,128]{1,0:T(8,128)(2,1)S(1)}, f32[2048,128]{1,0:T(8,128)S(1)}, bf16[2048,128]{1,0:T(8,128)(2,1)S(1)}, bf16[128,128]{1,0:T(8,128)(2,1)S(1)}) custom-call(s32[48]{0:T(128)S(1)} %get-tuple-element.68.refs_1_.refs_0_, s32[48]{0:T(128)S(1)} %get-tuple-element.67.refs_0_.refs_1_, s32[1]{0:T(128)} %bitcast.30.refs_2_, ...), custom_call_target="tpu_custom_call" | custom-call | tf_op jit(solution)/shard_map/pallas_call | solution.py:115
  109.7 2.3 %collective-permute-start.29 = (bf16[2048,128]{1,0:T(8,128)(2,1)S(1)}, bf16[2048,128]{1,0:T(8,128)(2,1)S(1)}, u32[]{:S(2)}, u32[]{:S(2)}) collective-permute-start(bf16[2048,128]{1,0:T(8,128)(2,1)S(1)} %get-tuple-element.43), channel_id=1, source_target_pairs={{0,16},{16,0},{32,48},{48,32},{64,80},{80,64},{96,112},{112,96},{1... | collective-permute-start | bytes 1572872 | tf_op jit(solution)/shard_map/ppermute | solution.py:25
  114.3 7.7 %collective-permute-done.32 = bf16[1152,128]{1,0:T(8,128)(2,1)S(1)} collective-permute-done((bf16[1152,128]{1,0:T(8,128)(2,1)S(1)}, bf16[1152,128]{1,0:T(8,128)(2,1)S(1)}, u32[]{:S(2)}, u32[]{:S(2)}) %collective-permute-start.32) | collective-permute-done | bytes 294944 | tf_op jit(solution)/shard_map/ppermute | solution.py:25
  125.0 1.7 %collective-permute-done.34.r3 = bf16[640,128]{1,0:T(8,128)(2,1)S(1)} collective-permute-done((bf16[640,128]{1,0:T(8,128)(2,1)S(1)}, bf16[640,128]{1,0:T(8,128)(2,1)S(1)}, u32[]{:S(2)}, u32[]{:S(2)}) %collective-permute-start.34) | collective-permute-done | bytes 163872 | tf_op jit(solution)/shard_map/ppermute | solution.py:25
  128.4 1.9 %collective-permute-done.33.r2 = bf16[768,128]{1,0:T(8,128)(2,1)S(1)} collective-permute-done((bf16[768,128]{1,0:T(8,128)(2,1)S(1)}, bf16[768,128]{1,0:T(8,128)(2,1)S(1)}, u32[]{:S(2)}, u32[]{:S(2)}) %collective-permute-start.33) | collective-permute-done | bytes 196640 | tf_op jit(solution)/shard_map/ppermute | solution.py:25
  130.4 2.2 %collective-permute-start.35 = (f32[128,128]{1,0:T(8,128)S(1)}, f32[128,128]{1,0:T(8,128)S(1)}, u32[]{:S(2)}, u32[]{:S(2)}) collective-permute-start(f32[128,128]{1,0:T(8,128)S(1)} %add_add_fusion), channel_id=1, source_target_pairs={{0,16},{16,0},{32,48},{48,32},{64,80},{80,64},{96,112},{112,96},{1... | collective-permute-start | bytes 196616 | tf_op jit(solution)/shard_map/ppermute | solution.py:25
  (93 shorter events, 21.8 us)
Async XLA Ops:
  0.6 5.9 %collective-permute-start = (bf16[512,128]{1,0:T(8,128)(2,1)}, bf16[512,128]{1,0:T(8,128)(2,1)S(1)}, u32[]{:S(2)}, u32[]{:S(2)}) collective-permute-start(bf16[512,128]{1,0:T(8,128)(2,1)} %x_ref.1), channel_id=1, source_target_pairs={{0,32},{16,48},{32,0},{48,16},{64,96},{80,112},{96,64},{112,80},{1... | collective-permute-start | bytes 393224 | tf_op jit(solution)/shard_map/ppermute | solution.py:25
  2.8 6.4 %collective-permute-start.2 = (bf16[512,128]{1,0:T(8,128)(2,1)}, bf16[512,128]{1,0:T(8,128)(2,1)S(1)}, u32[]{:S(2)}, u32[]{:S(2)}) collective-permute-start(bf16[512,128]{1,0:T(8,128)(2,1)} %x_ref.1), channel_id=1, source_target_pairs={{0,192},{16,208},{32,224},{48,240},{64,0},{80,16},{96,32},{112,48}... | collective-permute-start | bytes 393224 | tf_op jit(solution)/shard_map/ppermute | solution.py:25
  5.5 5.5 %collective-permute-start.1 = (bf16[512,128]{1,0:T(8,128)(2,1)}, bf16[512,128]{1,0:T(8,128)(2,1)S(1)}, u32[]{:S(2)}, u32[]{:S(2)}) collective-permute-start(bf16[512,128]{1,0:T(8,128)(2,1)} %x_ref.1), channel_id=1, source_target_pairs={{0,64},{16,80},{32,96},{48,112},{64,128},{80,144},{96,160},{112,17... | collective-permute-start | bytes 393224 | tf_op jit(solution)/shard_map/ppermute | solution.py:25
  6.6 13.0 %collective-permute-start.3 = (bf16[1024,128]{1,0:T(8,128)(2,1)S(1)}, bf16[1024,128]{1,0:T(8,128)(2,1)S(1)}, u32[]{:S(2)}, u32[]{:S(2)}) collective-permute-start(bf16[1024,128]{1,0:T(8,128)(2,1)S(1)} %pad_maximum_fusion.9), channel_id=1, source_target_pairs={{0,128},{16,144},{32,160},{48,176},{64,192},{80,208},{96,224},{112... | collective-permute-start | bytes 786440 | tf_op jit(solution)/shard_map/ppermute | solution.py:25
  11.0 8.6 %collective-permute-start.4 = (bf16[1024,128]{1,0:T(8,128)(2,1)S(1)}, bf16[1024,128]{1,0:T(8,128)(2,1)S(1)}, u32[]{:S(2)}, u32[]{:S(2)}) collective-permute-start(bf16[1024,128]{1,0:T(8,128)(2,1)S(1)} %pad_maximum_fusion.10), channel_id=1, source_target_pairs={{0,32},{16,48},{32,0},{48,16},{64,96},{80,112},{96,64},{112,80},{1... | collective-permute-start | bytes 786440 | tf_op jit(solution)/shard_map/ppermute | solution.py:25
  11.1 14.7 %collective-permute-start.5 = (bf16[2048,128]{1,0:T(8,128)(2,1)S(1)}, bf16[2048,128]{1,0:T(8,128)(2,1)S(1)}, u32[]{:S(2)}, u32[]{:S(2)}) collective-permute-start(bf16[2048,128]{1,0:T(8,128)(2,1)S(1)} %pad_maximum_fusion.refs_5_), channel_id=1, source_target_pairs={{0,16},{16,0},{32,48},{48,32},{64,80},{80,64},{96,112},{112,96},{1... | collective-permute-start | bytes 1572872 | tf_op jit(solution)/shard_map/ppermute | solution.py:25
  19.6 7.2 %collective-permute-start.6 = (bf16[2048,128]{1,0:T(8,128)(2,1)S(1)}, bf16[2048,128]{1,0:T(8,128)(2,1)}, u32[]{:S(2)}, u32[]{:S(2)}) collective-permute-start(bf16[2048,128]{1,0:T(8,128)(2,1)S(1)} %constant_dynamic-update-slice_fusion.refs_6_), channel_id=1, source_target_pairs={{0,16},{16,0},{32,48},{48,32},{64,80},{80,64},{96,112},{112,96},{1... | collective-permute-start | bytes 1572872 | tf_op jit(solution)/shard_map/ppermute | solution.py:25
  30.1 10.7 %collective-permute-start.9 = (bf16[1024,128]{1,0:T(8,128)(2,1)S(1)}, bf16[1024,128]{1,0:T(8,128)(2,1)S(1)}, u32[]{:S(2)}, u32[]{:S(2)}) collective-permute-start(bf16[1024,128]{1,0:T(8,128)(2,1)S(1)} %get-tuple-element.28), channel_id=1, source_target_pairs={{0,7},{1,0},{2,1},{3,2},{4,3},{5,4},{6,5},{7,6},{8,15},{9,8},{10,9... | collective-permute-start | bytes 786440 | tf_op jit(solution)/shard_map/ppermute | solution.py:33
  35.4 8.1 %collective-permute-start.10 = (bf16[1024,128]{1,0:T(8,128)(2,1)S(1)}, bf16[1024,128]{1,0:T(8,128)(2,1)S(1)}, u32[]{:S(2)}, u32[]{:S(2)}) collective-permute-start(bf16[1024,128]{1,0:T(8,128)(2,1)S(1)} %get-tuple-element.29), channel_id=1, source_target_pairs={{0,1},{1,2},{2,3},{3,4},{4,5},{5,6},{6,7},{7,0},{8,9},{9,10},{10,1... | collective-permute-start | bytes 786440 | tf_op jit(solution)/shard_map/ppermute | solution.py:33
  35.4 12.0 %collective-permute-start.13 = (bf16[512,128]{1,0:T(8,128)(2,1)S(1)}, bf16[512,128]{1,0:T(8,128)(2,1)S(1)}, u32[]{:S(2)}, u32[]{:S(2)}) collective-permute-start(bf16[512,128]{1,0:T(8,128)(2,1)S(1)} %get-tuple-element.34), channel_id=1, source_target_pairs={{0,8},{1,9},{2,10},{3,11},{4,12},{5,13},{6,14},{7,15},{8,0},{9,1},... | collective-permute-start | bytes 393224 | tf_op jit(solution)/shard_map/ppermute | solution.py:33
  38.1 16.7 %collective-permute-start.7 = (bf16[1024,128]{1,0:T(8,128)(2,1)}, bf16[1024,128]{1,0:T(8,128)(2,1)S(1)}, u32[]{:S(2)}, u32[]{:S(2)}) collective-permute-start(bf16[1024,128]{1,0:T(8,128)(2,1)} %get-tuple-element.25), channel_id=1, source_target_pairs={{0,7},{1,0},{2,1},{3,2},{4,3},{5,4},{6,5},{7,6},{8,15},{9,8},{10,9... | collective-permute-start | bytes 786440 | tf_op jit(solution)/shard_map/ppermute | solution.py:33
  40.8 14.1 %collective-permute-start.8 = (bf16[1024,128]{1,0:T(8,128)(2,1)}, bf16[1024,128]{1,0:T(8,128)(2,1)S(1)}, u32[]{:S(2)}, u32[]{:S(2)}) collective-permute-start(bf16[1024,128]{1,0:T(8,128)(2,1)} %get-tuple-element.26), channel_id=1, source_target_pairs={{0,1},{1,2},{2,3},{3,4},{4,5},{5,6},{6,7},{7,0},{8,9},{9,10},{10,1... | collective-permute-start | bytes 786440 | tf_op jit(solution)/shard_map/ppermute | solution.py:33
  44.3 10.6 %collective-permute-start.12 = (bf16[1024,128]{1,0:T(8,128)(2,1)S(1)}, bf16[1024,128]{1,0:T(8,128)(2,1)S(1)}, u32[]{:S(2)}, u32[]{:S(2)}) collective-permute-start(bf16[1024,128]{1,0:T(8,128)(2,1)S(1)} %pad_maximum_fusion.11), channel_id=1, source_target_pairs={{0,8},{1,9},{2,10},{3,11},{4,12},{5,13},{6,14},{7,15},{8,0},{9,1},... | collective-permute-start | bytes 786440 | tf_op jit(solution)/shard_map/ppermute | solution.py:33
  47.5 7.4 %collective-permute-start.14 = (bf16[512,128]{1,0:T(8,128)(2,1)S(1)}, bf16[512,128]{1,0:T(8,128)(2,1)}, u32[]{:S(2)}, u32[]{:S(2)}) collective-permute-start(bf16[512,128]{1,0:T(8,128)(2,1)S(1)} %add_convert_fusion.1), channel_id=1, source_target_pairs={{0,6},{1,7},{2,0},{3,1},{4,2},{5,3},{6,4},{7,5},{8,14},{9,15},{10,... | collective-permute-start | bytes 393224 | tf_op jit(solution)/shard_map/ppermute | solution.py:43
  47.6 11.2 %collective-permute-start.11 = (bf16[512,128]{1,0:T(8,128)(2,1)}, bf16[512,128]{1,0:T(8,128)(2,1)S(1)}, u32[]{:S(2)}, u32[]{:S(2)}) collective-permute-start(bf16[512,128]{1,0:T(8,128)(2,1)} %get-tuple-element.56), channel_id=1, source_target_pairs={{0,8},{1,9},{2,10},{3,11},{4,12},{5,13},{6,14},{7,15},{8,0},{9,1},... | collective-permute-start | bytes 393224 | tf_op jit(solution)/shard_map/ppermute | solution.py:33
  56.2 7.5 %collective-permute-start.16 = (bf16[512,128]{1,0:T(8,128)(2,1)S(1)}, bf16[512,128]{1,0:T(8,128)(2,1)S(1)}, u32[]{:S(2)}, u32[]{:S(2)}) collective-permute-start(bf16[512,128]{1,0:T(8,128)(2,1)S(1)} %get-tuple-element.49), channel_id=1, source_target_pairs={{0,6},{1,7},{2,0},{3,1},{4,2},{5,3},{6,4},{7,5},{8,14},{9,15},{10,... | collective-permute-start | bytes 393224 | tf_op jit(solution)/shard_map/ppermute | solution.py:33
  56.4 8.5 %collective-permute-start.15 = (bf16[512,128]{1,0:T(8,128)(2,1)S(1)}, bf16[512,128]{1,0:T(8,128)(2,1)S(1)}, u32[]{:S(2)}, u32[]{:S(2)}) collective-permute-start(bf16[512,128]{1,0:T(8,128)(2,1)S(1)} %get-tuple-element.50), channel_id=1, source_target_pairs={{0,2},{1,3},{2,4},{3,5},{4,6},{5,7},{6,0},{7,1},{8,10},{9,11},{10,... | collective-permute-start | bytes 393224 | tf_op jit(solution)/shard_map/ppermute | solution.py:33
  70.0 9.2 %collective-permute-start.20 = (bf16[640,128]{1,0:T(8,128)(2,1)S(1)}, bf16[640,128]{1,0:T(8,128)(2,1)S(1)}, u32[]{:S(2)}, u32[]{:S(2)}) collective-permute-start(bf16[640,128]{1,0:T(8,128)(2,1)S(1)} %pad_maximum_fusion.13.refs_5_), channel_id=1, source_target_pairs={{0,6},{1,7},{2,0},{3,1},{4,2},{5,3},{6,4},{7,5},{8,14},{9,15},{10,... | collective-permute-start | bytes 491528 | tf_op jit(solution)/shard_map/ppermute | solution.py:33
  70.7 8.5 %collective-permute-start.19 = (bf16[640,128]{1,0:T(8,128)(2,1)S(1)}, bf16[640,128]{1,0:T(8,128)(2,1)S(1)}, u32[]{:S(2)}, u32[]{:S(2)}) collective-permute-start(bf16[640,128]{1,0:T(8,128)(2,1)S(1)} %pad_maximum_fusion.13.refs_5_), channel_id=1, source_target_pairs={{0,2},{1,3},{2,4},{3,5},{4,6},{5,7},{6,0},{7,1},{8,10},{9,11},{10,... | collective-permute-start | bytes 491528 | tf_op jit(solution)/shard_map/ppermute | solution.py:33
  79.4 8.6 %collective-permute-start.21 = (bf16[1280,128]{1,0:T(8,128)(2,1)S(1)}, bf16[1280,128]{1,0:T(8,128)(2,1)S(1)}, u32[]{:S(2)}, u32[]{:S(2)}) collective-permute-start(bf16[1280,128]{1,0:T(8,128)(2,1)S(1)} %get-tuple-element.62), channel_id=1, source_target_pairs={{0,8},{1,9},{2,10},{3,11},{4,12},{5,13},{6,14},{7,15},{8,0},{9,1},... | collective-permute-start | bytes 983048 | tf_op jit(solution)/shard_map/ppermute | solution.py:33
  81.5 9.4 %collective-permute-start.18 = (bf16[640,128]{1,0:T(8,128)(2,1)S(1)}, bf16[640,128]{1,0:T(8,128)(2,1)S(1)}, u32[]{:S(2)}, u32[]{:S(2)}) collective-permute-start(bf16[640,128]{1,0:T(8,128)(2,1)S(1)} %pad_maximum_fusion.13.refs_5_), channel_id=1, source_target_pairs={{0,8},{1,9},{2,10},{3,11},{4,12},{5,13},{6,14},{7,15},{8,0},{9,1},... | collective-permute-start | bytes 491528 | tf_op jit(solution)/shard_map/ppermute | solution.py:33
  82.5 14.9 %collective-permute-start.22 = (bf16[640,128]{1,0:T(8,128)(2,1)S(1)}, bf16[640,128]{1,0:T(8,128)(2,1)S(1)}, u32[]{:S(2)}, u32[]{:S(2)}) collective-permute-start(bf16[640,128]{1,0:T(8,128)(2,1)S(1)} %broadcast_select_fusion), channel_id=1, source_target_pairs={{0,2},{1,3},{2,4},{3,5},{4,6},{5,7},{6,0},{7,1},{8,10},{9,11},{10,... | collective-permute-start | bytes 491528 | tf_op jit(solution)/shard_map/ppermute | solution.py:43
  84.7 13.2 %collective-permute-start.24 = (bf16[1280,128]{1,0:T(8,128)(2,1)S(1)}, bf16[1280,128]{1,0:T(8,128)(2,1)S(1)}, u32[]{:S(2)}, u32[]{:S(2)}) collective-permute-start(bf16[1280,128]{1,0:T(8,128)(2,1)S(1)} %get-tuple-element.60), channel_id=1, source_target_pairs={{0,7},{1,0},{2,1},{3,2},{4,3},{5,4},{6,5},{7,6},{8,15},{9,8},{10,9... | collective-permute-start | bytes 983048 | tf_op jit(solution)/shard_map/ppermute | solution.py:33
  88.0 12.3 %collective-permute-start.23 = (bf16[1280,128]{1,0:T(8,128)(2,1)S(1)}, bf16[1280,128]{1,0:T(8,128)(2,1)S(1)}, u32[]{:S(2)}, u32[]{:S(2)}) collective-permute-start(bf16[1280,128]{1,0:T(8,128)(2,1)S(1)} %get-tuple-element.61), channel_id=1, source_target_pairs={{0,1},{1,2},{2,3},{3,4},{4,5},{5,6},{6,7},{7,0},{8,9},{9,10},{10,1... | collective-permute-start | bytes 983048 | tf_op jit(solution)/shard_map/ppermute | solution.py:33
  90.9 12.8 %collective-permute-start.26 = (bf16[1280,128]{1,0:T(8,128)(2,1)S(1)}, bf16[1280,128]{1,0:T(8,128)(2,1)S(1)}, u32[]{:S(2)}, u32[]{:S(2)}) collective-permute-start(bf16[1280,128]{1,0:T(8,128)(2,1)S(1)} %get-tuple-element.58), channel_id=1, source_target_pairs={{0,7},{1,0},{2,1},{3,2},{4,3},{5,4},{6,5},{7,6},{8,15},{9,8},{10,9... | collective-permute-start | bytes 983048 | tf_op jit(solution)/shard_map/ppermute | solution.py:33
  95.0 12.3 %collective-permute-start.25 = (bf16[1280,128]{1,0:T(8,128)(2,1)S(1)}, bf16[1280,128]{1,0:T(8,128)(2,1)S(1)}, u32[]{:S(2)}, u32[]{:S(2)}) collective-permute-start(bf16[1280,128]{1,0:T(8,128)(2,1)S(1)} %get-tuple-element.59), channel_id=1, source_target_pairs={{0,1},{1,2},{2,3},{3,4},{4,5},{5,6},{6,7},{7,0},{8,9},{9,10},{10,1... | collective-permute-start | bytes 983048 | tf_op jit(solution)/shard_map/ppermute | solution.py:33
  97.3 5.7 %collective-permute-start.27 = (bf16[640,128]{1,0:T(8,128)(2,1)S(1)}, bf16[640,128]{1,0:T(8,128)(2,1)S(1)}, u32[]{:S(2)}, u32[]{:S(2)}) collective-permute-start(bf16[640,128]{1,0:T(8,128)(2,1)S(1)} %collective-permute-done.22.refs_10_), channel_id=1, source_target_pairs={{0,8},{1,9},{2,10},{3,11},{4,12},{5,13},{6,14},{7,15},{8,0},{9,1},... | collective-permute-start | bytes 491528 | tf_op jit(solution)/shard_map/ppermute | solution.py:33
  113.7 8.3 %collective-permute-start.32 = (bf16[1152,128]{1,0:T(8,128)(2,1)S(1)}, bf16[1152,128]{1,0:T(8,128)(2,1)S(1)}, u32[]{:S(2)}, u32[]{:S(2)}) collective-permute-start(bf16[1152,128]{1,0:T(8,128)(2,1)S(1)} %get-tuple-element.65), channel_id=1, source_target_pairs={{0,32},{16,48},{32,0},{48,16},{64,96},{80,112},{96,64},{112,80},{1... | collective-permute-start | bytes 884744 | tf_op jit(solution)/shard_map/ppermute | solution.py:25
  113.8 10.0 %collective-permute-start.30 = (bf16[1152,128]{1,0:T(8,128)(2,1)S(1)}, bf16[1152,128]{1,0:T(8,128)(2,1)S(1)}, u32[]{:S(2)}, u32[]{:S(2)}) collective-permute-start(bf16[1152,128]{1,0:T(8,128)(2,1)S(1)} %get-tuple-element.66), channel_id=1, source_target_pairs={{0,128},{16,144},{32,160},{48,176},{64,192},{80,208},{96,224},{112... | collective-permute-start | bytes 884744 | tf_op jit(solution)/shard_map/ppermute | solution.py:25
  122.1 4.6 %collective-permute-start.34 = (bf16[640,128]{1,0:T(8,128)(2,1)S(1)}, bf16[640,128]{1,0:T(8,128)(2,1)S(1)}, u32[]{:S(2)}, u32[]{:S(2)}) collective-permute-start(bf16[640,128]{1,0:T(8,128)(2,1)S(1)} %pad_maximum_fusion.15), channel_id=1, source_target_pairs={{0,192},{16,208},{32,224},{48,240},{64,0},{80,16},{96,32},{112,48}... | collective-permute-start | bytes 491528 | tf_op jit(solution)/shard_map/ppermute | solution.py:25
  123.9 6.5 %collective-permute-start.33 = (bf16[768,128]{1,0:T(8,128)(2,1)S(1)}, bf16[768,128]{1,0:T(8,128)(2,1)S(1)}, u32[]{:S(2)}, u32[]{:S(2)}) collective-permute-start(bf16[768,128]{1,0:T(8,128)(2,1)S(1)} %pad_maximum_fusion.12), channel_id=1, source_target_pairs={{0,64},{16,80},{32,96},{48,112},{64,128},{80,144},{96,160},{112,17... | collective-permute-start | bytes 589832 | tf_op jit(solution)/shard_map/ppermute | solution.py:25
  124.0 4.4 %collective-permute-start.31 = (bf16[640,128]{1,0:T(8,128)(2,1)S(1)}, bf16[640,128]{1,0:T(8,128)(2,1)S(1)}, u32[]{:S(2)}, u32[]{:S(2)}) collective-permute-start(bf16[640,128]{1,0:T(8,128)(2,1)S(1)} %pad_maximum_fusion.14), channel_id=1, source_target_pairs={{0,32},{16,48},{32,0},{48,16},{64,96},{80,112},{96,64},{112,80},{1... | collective-permute-start | bytes 491528 | tf_op jit(solution)/shard_map/ppermute | solution.py:25
  (12 other events, 148.7 us)

commit v5 on v4

--- a/solution.py
+++ b/solution.py
@@ -12,8 +12,7 @@
 NY, NXL, NC, NXH, NZ = 4, 2, 2, 2, 8
 SHARD = 512
 BLOCK = 128
-ROWS = SHARD + BLOCK
-VMEM_LIMIT = 24 * 1024 * 1024
+VMEM_LIMIT = 16 * 1024 * 1024
 
 
 def send_row(x, dy=0, dx=0, dc=0):
@@ -65,9 +64,9 @@
 
 def tile_kernel(places, outs, left, *refs):
     n_in = len(places)
-    src_ref, dst_ref, count_ref, scan_ref, vals_ref = refs[:5]
-    panel_refs = refs[5:5 + n_in]
-    *out_refs, panel, acc = refs[5 + n_in:]
+    src_ref, dst_ref, count_ref, vals_ref = refs[:4]
+    panel_refs = refs[4:4 + n_in]
+    *out_refs, panel, acc = refs[4 + n_in:]
     for ref, pieces in zip(panel_refs, places):
         start = 0
         for first, rows in pieces:
@@ -97,32 +96,24 @@
         for first, rows in pieces:
             ref[pl.ds(start, rows), :] = acc[pl.ds(first, rows), :].astype(ref.dtype)
             start += rows
-    if not left:
-        share = jnp.zeros((BLOCK, BLOCK), F32)
-        for i in range(16):
-            at = pl.multiple_of(16 * SHARD + scan_ref[i] * BLOCK, BLOCK)
-            share = share + panel[pl.ds(at, BLOCK), :].astype(F32)
-        out_refs[-1][...] = share.astype(BF16)
-
-
-def tile_sums(src, dst, count, scan, vals, panels, places, outs, dtypes, left):
+
+
+def tile_sums(src, dst, count, vals, panels, places, outs, dtypes, left):
     sizes = [sum(rows for _, rows in pieces) for pieces in outs]
     vmem = pl.BlockSpec(memory_space=pltpu.VMEM)
     smem = pl.BlockSpec(memory_space=pltpu.SMEM)
     out_shape = [jax.ShapeDtypeStruct((rows, BLOCK), dt) for rows, dt in zip(sizes, dtypes)]
-    if not left:
-        out_shape.append(jax.ShapeDtypeStruct((BLOCK, BLOCK), BF16))
     return pl.pallas_call(
         functools.partial(tile_kernel, places, outs, left),
         out_shape=out_shape,
-        in_specs=[smem] * 4 + [vmem] * (1 + len(panels)),
+        in_specs=[smem] * 3 + [vmem] * (1 + len(panels)),
         out_specs=[vmem] * len(out_shape),
         scratch_shapes=[
-            pltpu.VMEM((16 * (SHARD if left else ROWS), BLOCK), BF16),
+            pltpu.VMEM((16 * SHARD, BLOCK), BF16),
             pltpu.VMEM((16 * SHARD, BLOCK), F32),
         ],
         compiler_params=pltpu.CompilerParams(vmem_limit_bytes=VMEM_LIMIT),
-    )(src, dst, count, scan, vals, *panels)
+    )(src, dst, count, vals, *panels)
 
 
 def mid_kernel(core_ref, own_ref, r1, r2, r3, r4, r5, weight_ref, gout_ref, act_ref, gt_ref, keep_ref, give_ref, gw_ref):
@@ -165,8 +156,12 @@
     return functools.reduce(lambda a, b: a + b, [t.astype(F32) for t in terms])
 
 
-def rounded(x):
-    return lax.reduce_precision(x, 8, 7)
+def swap(x, axis, bit):
+    return lax.ppermute(x, axis, [(i, i ^ bit) for i in range(16)])
+
+
+def tied(*arrays):
+    return lax.optimization_barrier(arrays)
 
 
 def body(features, weight, grad_out, tile_rows, tile_cols, tile_vals, tile_count):
@@ -176,7 +171,6 @@
     row_at = row_slots(tile_rows[0, 0])
     col_at = col_slots(tile_cols[0, 0])
     core = lax.axis_index("row") % NC
-    scan = row_slots(jnp.arange(16, dtype=jnp.int32) * 4) // 4
     S = SHARD
 
     a = send_row(features, dx=1)
@@ -200,10 +194,10 @@
 
     O = lambda k: (k % 8 * S, S)
     X = lambda k: ((8 + k % 8) * S, S)
-    outs = [[X(-1), X(-3)], [X(1), X(3)], [X(4)], [O(-1), O(-3)], [O(1), O(3)],
+    outs = [[X(-3)], [X(3)], [X(4)], [O(-1), O(-3), X(-1)], [O(1), O(3), X(1)],
             [X(-2)], [X(2)], [O(4)], [X(0)], [O(2)], [O(-2)], [O(0)]]
     m, n, l, e, g, x6, x2, o4, x0, o2, o6, o0 = tile_sums(
-        col_at, row_at, count, scan, values, [h1, h2, c1, c2], places, outs,
+        col_at, row_at, count, values, [h1, h2, c1, c2], places, outs,
         [BF16] * 5 + [F32] * 7, True,
     )
     m = send_col(m, dz=-1)
@@ -211,12 +205,12 @@
     l = send_col(l, dh=1)
     e = send_col(e, dz=-1)
     g = send_col(g, dz=1)
-    q = jnp.concatenate([add(x2, n[S:]).astype(BF16), add(x6, m[S:]).astype(BF16)])
+    q = jnp.concatenate([add(x2, n).astype(BF16), add(x6, m).astype(BF16)])
     q = send_col(q, dh=1)
     h = send_apart(add(o4, l).astype(BF16), -2).astype(F32)
-    rx = send_col(add(x0, m[:S], n[:S]).astype(BF16), dh=1)
-    o2 = add(o2, g[S:], q[:S], jnp.where(core == 0, 0.0, h)).astype(BF16)
-    o6 = add(o6, e[S:], q[S:], jnp.where(core == 0, h, 0.0)).astype(BF16)
+    rx = send_col(add(x0, e[2 * S:], g[2 * S:]).astype(BF16), dh=1)
+    o2 = add(o2, g[S:2 * S], q[:S], jnp.where(core == 0, 0.0, h)).astype(BF16)
+    o6 = add(o6, e[S:2 * S], q[S:], jnp.where(core == 0, h, 0.0)).astype(BF16)
     s2 = send_col(o2, dz=2)
     s6 = send_col(o6, dz=-2)
 
@@ -234,50 +228,56 @@
         compiler_params=params,
     )(core[None], o0, e, g, rx, s2, s6, weight, grad_out)
     share = keep + send_row(give, dc=1)
-    gt = jnp.concatenate([gt, share.astype(BF16)])
 
     u2 = send_col(gt, dz=2)
     d2 = send_col(gt, dz=-2)
     a = send_col(gt, dh=1)
+    share = share + swap(share, "row", 2)
+    share, u2, d2 = tied(share, u2, d2)
+    share = share + swap(share, "row", 4)
     q = send_col(jnp.concatenate([u2, d2]), dh=1)
     f4 = send_apart(jnp.where(core == 0, u2, d2), 2)
-    e = send_col(jnp.concatenate([gt, u2]), dz=1)
-    g = send_col(jnp.concatenate([gt, d2]), dz=-1)
-    m = send_col(jnp.concatenate([a, q[:ROWS]]), dz=1)
-    n = send_col(jnp.concatenate([a, q[ROWS:]]), dz=-1)
+    e = send_col(jnp.concatenate([gt, u2, a]), dz=1)
+    g = send_col(jnp.concatenate([gt, d2, a]), dz=-1)
+    share, f4 = tied(share, f4)
+    share = share + swap(share, "row", 8)
+    m = send_col(q[:S], dz=1)
+    n = send_col(q[S:], dz=-1)
     l = send_col(f4, dh=1)
+    share, e, g = tied(share, e, g)
+    share = share + swap(share, "col", 8)
     panels = [gt, a, u2, d2, q, f4, e, g, m, n, l]
-    both = lambda *slots: [p for f, r in slots for p in ((f, r), (16 * S + f // 4, BLOCK))]
-    places = [both(O(0)), both(X(0)), both(O(-2)), both(O(2)), both(X(-2), X(2)), both(O(4)),
-              both(O(-1), O(-3)), both(O(1), O(3)), both(X(-1), X(-3)), both(X(1), X(3)), both(X(4))]
+    places = [[O(0)], [X(0)], [O(-2)], [O(2)], [X(-2), X(2)], [O(4)],
+              [O(-1), O(-3), X(-1)], [O(1), O(3), X(1)], [X(-3)], [X(3)], [X(4)]]
 
     k = lambda dy, dx: ((dx * 4 + dy % 4) * S, S)
     last = [k(0, 0), k(0, 1), k(1, 0), k(-1, 0)]
     early = [k(1, 1), k(-1, 1), k(2, 0), k(2, 1)]
-    own, away, own1, away1, share = tile_sums(
-        row_at, col_at, count, scan, values, panels, places,
+    own, away, own1, away1 = tile_sums(
+        row_at, col_at, count, values, panels, places,
         [last, other(last), early, other(early)], [F32, BF16] * 2, False,
     )
     own1 = add(own1, send_row(away1, dc=1)).astype(BF16)
+    share, own1 = tied(share, own1)
+    share = share + swap(share, "col", 4)
     own = add(own, send_row(away, dc=1))
-    w = send_row(jnp.concatenate([own1[2 * S:], share]), dy=2)
-    v = send_row(jnp.concatenate([own1[:2 * S], share]), dx=1)
-    o = add(own[S:2 * S], w[S:2 * S]).astype(BF16)
-    ud = add(own[2 * S:4 * S], v[:2 * S]).astype(BF16)
-    here = rounded(add(share, w[2 * S:]))
-    across = v[2 * S:]
-    ro = send_row(jnp.concatenate([o, here.astype(BF16)]), dx=1)
-    ru = send_row(jnp.concatenate([ud[:S], here.astype(BF16), across]), dy=1)
-    rd = send_row(jnp.concatenate([ud[S:], across]), dy=-1)
-    beside = rounded(add(ru[S + BLOCK:], rd[S:]))
-    mine = add(here, ru[S:S + BLOCK]) + add(ro[S:], beside)
-    theirs = send_row(mine, dc=1)
+    w = send_row(own1[2 * S:], dy=2)
+    v = send_row(own1[:2 * S], dx=1)
+    share, v = tied(share, v)
+    for bit in (2, 1):
+        share = share + swap(share, "col", bit)
+    theirs = send_row(share, dc=1)
+    o = add(own[S:2 * S], w[S:]).astype(BF16)
+    ud = add(own[2 * S:], v).astype(BF16)
+    ro = send_row(o, dx=1)
+    ru = send_row(ud[:S], dy=1)
+    rd = send_row(ud[S:], dy=-1)
     grad_features = pl.pallas_call(
         last_kernel,
         out_shape=jax.ShapeDtypeStruct((S, BLOCK), BF16),
         compiler_params=params,
     )(own[:S], w, ro, ru, rd)
-    first, second = jnp.where(core == 0, mine, theirs), jnp.where(core == 0, theirs, mine)
+    first, second = jnp.where(core == 0, share, theirs), jnp.where(core == 0, theirs, share)
     grad_weight = jnp.concatenate([first, second], axis=1)
     return (activation, grad_features, grad_weight)
 

time: 134 us -> 133 us (level)
  waiting for transfers between devices: 55.1 us -> 42.7 us
  starting transfers between devices: 64.8 us -> 74.4 us
  local copies, waits for them, and re-layouts: 1.14 us -> 2.58 us
    ppermute x16, waiting for transfers between devices: 20 us -> 4.38 us  [send_row(): return lax.ppermute(x, 'row', perm)]
    ppermute x0 -> x7, waiting for transfers between devices: none -> 10.2 us  [swap(): return lax.ppermute(x, axis, [(i, i ^ bit) for i in range(16)])]
    ppermute x0 -> x7, starting transfers between devices: none -> 6.88 us  [swap(): return lax.ppermute(x, axis, [(i, i ^ bit) for i in range(16)])]
    ppermute x18, waiting for transfers between devices: 28 us -> 21.3 us  [send_col(): return lax.ppermute(x, 'col', perm)]
    ppermute x16, starting transfers between devices: 30.2 us -> 35.7 us  [send_row(): return lax.ppermute(x, 'row', perm)]
    ppermute x18, starting transfers between devices: 32.3 us -> 27.4 us  [send_col(): return lax.ppermute(x, 'col', perm)]
    ppermute x2, starting transfers between devices: 2.31 us -> 4.43 us  [send_apart(): return lax.ppermute(x, ('row', 'col'), perm)]
    unnamed x17 -> x25, local copies, waits for them, and re-layouts: 1.02 us -> 2.47 us
  transfers between devices with their start and end apart: 36 -> 43, of which waited for: 21 -> 20; matrix products, arithmetic and copies ran while one was open for 2% -> 2% of each run, Pallas kernels for 1% -> 1%
where the time goes in v5:
time: 133 us
  starting transfers between devices  74.4 us (56%)
  waiting for transfers between devices  42.7 us (32%)
  Pallas kernels  7.49 us (6%)
  other arithmetic  3.93 us (3%)
  local copies, waits for them, and re-layouts  2.58 us (2%)
  between operations  1.63 us (1%)
    ppermute x16, starting transfers between devices, send_row(): return lax.ppermute(x, 'row', perm)  35.7 us
    ppermute x18, starting transfers between devices, send_col(): return lax.ppermute(x, 'col', perm)  27.4 us
    ppermute x18, waiting for transfers between devices, send_col(): return lax.ppermute(x, 'col', perm)  21.3 us
    ppermute x7, waiting for transfers between devices, swap(): return lax.ppermute(x, axis, [(i, i ^ bit) for i in range(16)])  10.2 us
    ppermute x7, starting transfers between devices, swap(): return lax.ppermute(x, axis, [(i, i ^ bit) for i in range(16)])  6.88 us
    ppermute x2, waiting for transfers between devices, send_apart(): return lax.ppermute(x, ('row', 'col'), perm)  6.85 us
    pallas_call x2, Pallas kernels, tile_sums(): pl.pallas_call(functools.partial(tile_kernel, places, outs, left), out_sh...  5.29 us
    ppermute x2, starting transfers between devices, send_apart(): return lax.ppermute(x, ('row', 'col'), perm)  4.43 us
  transfers between devices with their start and end apart: 43, of which 20 were waited for; matrix products, arithmetic and copies ran while one was open for 2% of the time, Pallas kernels for 1%

profile of v5, /device:TPU:1, one launch (start us, length us, event | category | flops | bytes accessed | tf_op | source)
XLA Modules:
  0.0 132.7 jit_solution(535790658970556736)
XLA Ops:
  0.6 2.1 %collective-permute-start = (bf16[512,128]{1,0:T(8,128)(2,1)}, bf16[512,128]{1,0:T(8,128)(2,1)S(1)}, u32[]{:S(2)}, u32[]{:S(2)}) collective-permute-start(bf16[512,128]{1,0:T(8,128)(2,1)} %x_ref.1), channel_id=1, source_target_pairs={{0,32},{16,48},{32,0},{48,16},{64,96},{80,112},{96,64},{112,80},{1... | collective-permute-start | bytes 393224 | tf_op jit(solution)/shard_map/ppermute | solution.py:24
  2.8 2.7 %collective-permute-start.2 = (bf16[512,128]{1,0:T(8,128)(2,1)}, bf16[512,128]{1,0:T(8,128)(2,1)S(1)}, u32[]{:S(2)}, u32[]{:S(2)}) collective-permute-start(bf16[512,128]{1,0:T(8,128)(2,1)} %x_ref.1), channel_id=1, source_target_pairs={{0,192},{16,208},{32,224},{48,240},{64,0},{80,16},{96,32},{112,48}... | collective-permute-start | bytes 393224 | tf_op jit(solution)/shard_map/ppermute | solution.py:24
  6.6 2.6 %collective-permute-start.3 = (bf16[1024,128]{1,0:T(8,128)(2,1)S(1)}, bf16[1024,128]{1,0:T(8,128)(2,1)S(1)}, u32[]{:S(2)}, u32[]{:S(2)}) collective-permute-start(bf16[1024,128]{1,0:T(8,128)(2,1)S(1)} %pad_maximum_fusion.5), channel_id=1, source_target_pairs={{0,128},{16,144},{32,160},{48,176},{64,192},{80,208},{96,224},{112... | collective-permute-start | bytes 786440 | tf_op jit(solution)/shard_map/ppermute | solution.py:24
  9.1 1.8 %collective-permute-done.1 = bf16[512,128]{1,0:T(8,128)(2,1)S(1)} collective-permute-done((bf16[512,128]{1,0:T(8,128)(2,1)}, bf16[512,128]{1,0:T(8,128)(2,1)S(1)}, u32[]{:S(2)}, u32[]{:S(2)}) %collective-permute-start.1) | collective-permute-done | bytes 131104 | tf_op jit(solution)/shard_map/ppermute | solution.py:24
  11.1 8.4 %collective-permute-start.5 = (bf16[2048,128]{1,0:T(8,128)(2,1)S(1)}, bf16[2048,128]{1,0:T(8,128)(2,1)S(1)}, u32[]{:S(2)}, u32[]{:S(2)}) collective-permute-start(bf16[2048,128]{1,0:T(8,128)(2,1)S(1)} %pad_maximum_fusion.refs_4_), channel_id=1, source_target_pairs={{0,16},{16,0},{32,48},{48,32},{64,80},{80,64},{96,112},{112,96},{1... | collective-permute-start | bytes 1572872 | tf_op jit(solution)/shard_map/ppermute | solution.py:24
  19.6 5.5 %collective-permute-start.6 = (bf16[2048,128]{1,0:T(8,128)(2,1)S(1)}, bf16[2048,128]{1,0:T(8,128)(2,1)}, u32[]{:S(2)}, u32[]{:S(2)}) collective-permute-start(bf16[2048,128]{1,0:T(8,128)(2,1)S(1)} %constant_dynamic-update-slice_fusion.refs_5_), channel_id=1, source_target_pairs={{0,16},{16,0},{32,48},{48,32},{64,80},{80,64},{96,112},{112,96},{1... | collective-permute-start | bytes 1572872 | tf_op jit(solution)/shard_map/ppermute | solution.py:24
  26.8 3.3 %shard_map.95 = (bf16[512,128]{1,0:T(8,128)(2,1)S(1)}, bf16[512,128]{1,0:T(8,128)(2,1)S(1)}, bf16[512,128]{1,0:T(8,128)(2,1)S(1)}, bf16[1536,128]{1,0:T(8,128)(2...) custom-call(s32[48]{0:T(128)S(1)} %get-tuple-element.82.refs_0_.refs, ...), custom_call_target="tpu_custom_call" | custom-call | tf_op jit(solution)/shard_map/pallas_call | solution.py:106
  32.9 4.3 %collective-permute-start.11 = (bf16[512,128]{1,0:T(8,128)(2,1)S(1)}, bf16[512,128]{1,0:T(8,128)(2,1)S(1)}, u32[]{:S(2)}, u32[]{:S(2)}) collective-permute-start(bf16[512,128]{1,0:T(8,128)(2,1)S(1)} %get-tuple-element.43), channel_id=1, source_target_pairs={{0,7},{1,0},{2,1},{3,2},{4,3},{5,4},{6,5},{7,6},{8,15},{9,8},{10,9... | collective-permute-start | bytes 393224 | tf_op jit(solution)/shard_map/ppermute | solution.py:32
  37.2 2.2 %collective-permute-start.13 = (bf16[512,128]{1,0:T(8,128)(2,1)S(1)}, bf16[512,128]{1,0:T(8,128)(2,1)S(1)}, u32[]{:S(2)}, u32[]{:S(2)}) collective-permute-start(bf16[512,128]{1,0:T(8,128)(2,1)S(1)} %get-tuple-element.45), channel_id=1, source_target_pairs={{0,8},{1,9},{2,10},{3,11},{4,12},{5,13},{6,14},{7,15},{8,0},{9,1},... | collective-permute-start | bytes 393224 | tf_op jit(solution)/shard_map/ppermute | solution.py:32
  41.6 1.7 %collective-permute-start.12 = (bf16[1024,128]{1,0:T(8,128)(2,1)}, bf16[1024,128]{1,0:T(8,128)(2,1)}, u32[]{:S(2)}, u32[]{:S(2)}) collective-permute-start(bf16[1024,128]{1,0:T(8,128)(2,1)} %pad_maximum_fusion.7), channel_id=1, source_target_pairs={{0,8},{1,9},{2,10},{3,11},{4,12},{5,13},{6,14},{7,15},{8,0},{9,1},... | collective-permute-start | bytes 786440 | tf_op jit(solution)/shard_map/ppermute | solution.py:32
  44.0 2.9 %collective-permute-start.14 = (bf16[512,128]{1,0:T(8,128)(2,1)}, bf16[512,128]{1,0:T(8,128)(2,1)}, u32[]{:S(2)}, u32[]{:S(2)}) collective-permute-start(bf16[512,128]{1,0:T(8,128)(2,1)} %add_convert_fusion.1), channel_id=1, source_target_pairs={{0,6},{1,7},{2,0},{3,1},{4,2},{5,3},{6,4},{7,5},{8,14},{9,15},{10,... | collective-permute-start | bytes 393224 | tf_op jit(solution)/shard_map/ppermute | solution.py:42
  46.9 6.8 %collective-permute-done.14 = bf16[512,128]{1,0:T(8,128)(2,1)} collective-permute-done((bf16[512,128]{1,0:T(8,128)(2,1)}, bf16[512,128]{1,0:T(8,128)(2,1)}, u32[]{:S(2)}, u32[]{:S(2)}) %collective-permute-start.14) | collective-permute-done | bytes 131104 | tf_op jit(solution)/shard_map/ppermute | solution.py:42
  55.0 3.4 %collective-permute-start.16 = (bf16[512,128]{1,0:T(8,128)(2,1)S(1)}, bf16[512,128]{1,0:T(8,128)(2,1)S(1)}, u32[]{:S(2)}, u32[]{:S(2)}) collective-permute-start(bf16[512,128]{1,0:T(8,128)(2,1)S(1)} %get-tuple-element.71), channel_id=1, source_target_pairs={{0,6},{1,7},{2,0},{3,1},{4,2},{5,3},{6,4},{7,5},{8,14},{9,15},{10,... | collective-permute-start | bytes 393224 | tf_op jit(solution)/shard_map/ppermute | solution.py:32
  58.8 4.1 %collective-permute-done.16.r5 = bf16[512,128]{1,0:T(8,128)(2,1)S(1)} collective-permute-done((bf16[512,128]{1,0:T(8,128)(2,1)S(1)}, bf16[512,128]{1,0:T(8,128)(2,1)S(1)}, u32[]{:S(2)}, u32[]{:S(2)}) %collective-permute-start.16) | collective-permute-done | bytes 131104 | tf_op jit(solution)/shard_map/ppermute | solution.py:32
  63.8 4.8 %collective-permute-done.15.r4 = bf16[512,128]{1,0:T(8,128)(2,1)S(1)} collective-permute-done((bf16[512,128]{1,0:T(8,128)(2,1)S(1)}, bf16[512,128]{1,0:T(8,128)(2,1)S(1)}, u32[]{:S(2)}, u32[]{:S(2)}) %collective-permute-start.15) | collective-permute-done | bytes 131104 | tf_op jit(solution)/shard_map/ppermute | solution.py:32
  71.1 2.4 %collective-permute-start.20 = (bf16[512,128]{1,0:T(8,128)(2,1)S(1)}, bf16[512,128]{1,0:T(8,128)(2,1)S(1)}, u32[]{:S(2)}, u32[]{:S(2)}) collective-permute-start(bf16[512,128]{1,0:T(8,128)(2,1)S(1)} %get-tuple-element.48.refs_4_), channel_id=1, source_target_pairs={{0,2},{1,3},{2,4},{3,5},{4,6},{5,7},{6,0},{7,1},{8,10},{9,11},{10,... | collective-permute-start | bytes 393224 | tf_op jit(solution)/shard_map/ppermute | solution.py:32
  73.6 2.7 %collective-permute-start.17 = (bf16[512,128]{1,0:T(8,128)(2,1)S(1)}, bf16[512,128]{1,0:T(8,128)(2,1)S(1)}, u32[]{:S(2)}, u32[]{:S(2)}) collective-permute-start(bf16[512,128]{1,0:T(8,128)(2,1)S(1)} %get-tuple-element.48.refs_4_), channel_id=1, source_target_pairs={{0,8},{1,9},{2,10},{3,11},{4,12},{5,13},{6,14},{7,15},{8,0},{9,1},... | collective-permute-start | bytes 393224 | tf_op jit(solution)/shard_map/ppermute | solution.py:32
  77.0 1.8 %collective-permute-done.21.refs_7_ = bf16[512,128]{1,0:T(8,128)(2,1)S(1)} collective-permute-done((bf16[512,128]{1,0:T(8,128)(2,1)S(1)}, bf16[512,128]{1,0:T(8,128)(2,1)S(1)}, u32[]{:S(2)}, u32[]{:S(2)}) %collective-permute-start.21) | collective-permute-done | bytes 131104 | tf_op jit(solution)/shard_map/ppermute | solution.py:32
  78.7 2.7 %collective-permute-done.20.refs_6_ = bf16[512,128]{1,0:T(8,128)(2,1)S(1)} collective-permute-done((bf16[512,128]{1,0:T(8,128)(2,1)S(1)}, bf16[512,128]{1,0:T(8,128)(2,1)S(1)}, u32[]{:S(2)}, u32[]{:S(2)}) %collective-permute-start.20) | collective-permute-done | bytes 131104 | tf_op jit(solution)/shard_map/ppermute | solution.py:32
  87.6 2.6 %collective-permute-start.30 = (bf16[512,128]{1,0:T(8,128)(2,1)S(1)}, bf16[512,128]{1,0:T(8,128)(2,1)S(1)}, u32[]{:S(2)}, u32[]{:S(2)}) collective-permute-start(bf16[512,128]{1,0:T(8,128)(2,1)S(1)} %collective-permute-done.24.refs_9_), channel_id=1, source_target_pairs={{0,8},{1,9},{2,10},{3,11},{4,12},{5,13},{6,14},{7,15},{8,0},{9,1},... | collective-permute-start | bytes 393224 | tf_op jit(solution)/shard_map/ppermute | solution.py:32
  90.3 1.7 %collective-permute-done.22.refs_8_ = bf16[1024,128]{1,0:T(8,128)(2,1)S(1)} collective-permute-done((bf16[1024,128]{1,0:T(8,128)(2,1)S(1)}, bf16[1024,128]{1,0:T(8,128)(2,1)S(1)}, u32[]{:S(2)}, u32[]{:S(2)}) %collective-permute-start.22) | collective-permute-done | bytes 262176 | tf_op jit(solution)/shard_map/ppermute | solution.py:32
  94.3 3.2 %collective-permute-done.29.refs_13_ = bf16[512,128]{1,0:T(8,128)(2,1)S(1)} collective-permute-done((bf16[512,128]{1,0:T(8,128)(2,1)S(1)}, bf16[512,128]{1,0:T(8,128)(2,1)S(1)}, u32[]{:S(2)}, u32[]{:S(2)}) %collective-permute-start.29) | collective-permute-done | bytes 131104 | tf_op jit(solution)/shard_map/ppermute | solution.py:32
  98.9 2.0 %shard_map.97 = (f32[2048,128]{1,0:T(8,128)S(1)}, bf16[2048,128]{1,0:T(8,128)(2,1)S(1)}, f32[2048,128]{1,0:T(8,128)S(1)}, bf16[2048,128]{1,0:T(8,128)(2,1)S(1)}) custom-call(s32[48]{0:T(128)S(1)} %get-tuple-element.83.refs_1_.refs_0_, s32[48]{0:T(128)S(1)} %get-tuple-element.82.refs_0_.refs_1_, s32[1]{0:T(128)} %bitcast.30.refs_2_, ...), custom_call_target="tpu_custom_call" | custom-call | tf_op jit(solution)/shard_map/pallas_call | solution.py:106
  100.9 2.5 %collective-permute-start.33 = (bf16[2048,128]{1,0:T(8,128)(2,1)S(1)}, bf16[2048,128]{1,0:T(8,128)(2,1)S(1)}, u32[]{:S(2)}, u32[]{:S(2)}) collective-permute-start(bf16[2048,128]{1,0:T(8,128)(2,1)S(1)} %get-tuple-element.62), channel_id=1, source_target_pairs={{0,16},{16,0},{32,48},{48,32},{64,80},{80,64},{96,112},{112,96},{1... | collective-permute-start | bytes 1572872 | tf_op jit(solution)/shard_map/ppermute | solution.py:24
  103.4 4.7 %collective-permute-start.32 = (f32[128,128]{1,0:T(8,128)S(1)}, f32[128,128]{1,0:T(8,128)S(1)}, u32[]{:S(2)}, u32[]{:S(2)}) collective-permute-start(f32[128,128]{1,0:T(8,128)S(1)} %add.162), channel_id=1, source_target_pairs={{0,8},{1,9},{2,10},{3,11},{4,12},{5,13},{6,14},{7,15},{8,0},{9,1},... | collective-permute-start | bytes 196616 | tf_op jit(solution)/shard_map/ppermute | solution.py:160
  108.7 1.6 %collective-permute-done.32 = f32[128,128]{1,0:T(8,128)S(1)} collective-permute-done((f32[128,128]{1,0:T(8,128)S(1)}, f32[128,128]{1,0:T(8,128)S(1)}, u32[]{:S(2)}, u32[]{:S(2)}) %collective-permute-start.32) | collective-permute-done | bytes 65568 | tf_op jit(solution)/shard_map/ppermute | solution.py:160
  111.4 2.2 %collective-permute-start.37 = (bf16[1024,128]{1,0:T(8,128)(2,1)S(1)}, bf16[1024,128]{1,0:T(8,128)(2,1)S(1)}, u32[]{:S(2)}, u32[]{:S(2)}) collective-permute-start(bf16[1024,128]{1,0:T(8,128)(2,1)S(1)} %get-tuple-element.69), channel_id=1, source_target_pairs={{0,32},{16,48},{32,0},{48,16},{64,96},{80,112},{96,64},{112,80},{1... | collective-permute-start | bytes 786440 | tf_op jit(solution)/shard_map/ppermute | solution.py:24
  114.0 3.5 %collective-permute-done.36 = f32[128,128]{1,0:T(8,128)S(1)} collective-permute-done((f32[128,128]{1,0:T(8,128)S(1)}, f32[128,128]{1,0:T(8,128)S(1)}, u32[]{:S(2)}, u32[]{:S(2)}) %collective-permute-start.36) | collective-permute-done | bytes 65568 | tf_op jit(solution)/shard_map/ppermute | solution.py:160
  117.6 1.5 %collective-permute-done.37 = bf16[1024,128]{1,0:T(8,128)(2,1)S(1)} collective-permute-done((bf16[1024,128]{1,0:T(8,128)(2,1)S(1)}, bf16[1024,128]{1,0:T(8,128)(2,1)S(1)}, u32[]{:S(2)}, u32[]{:S(2)}) %collective-permute-start.37) | collective-permute-done | bytes 262176 | tf_op jit(solution)/shard_map/ppermute | solution.py:24
  119.2 3.0 %collective-permute-start.39 = (bf16[512,128]{1,0:T(8,128)(2,1)S(1)}, bf16[512,128]{1,0:T(8,128)(2,1)S(1)}, u32[]{:S(2)}, u32[]{:S(2)}) collective-permute-start(bf16[512,128]{1,0:T(8,128)(2,1)S(1)} %get-tuple-element.74), channel_id=1, source_target_pairs={{0,192},{16,208},{32,224},{48,240},{64,0},{80,16},{96,32},{112,48}... | collective-permute-start | bytes 393224 | tf_op jit(solution)/shard_map/ppermute | solution.py:24
  123.9 3.1 %collective-permute-done.41 = f32[128,128]{1,0:T(8,128)S(1)} collective-permute-done((f32[128,128]{1,0:T(8,128)S(1)}, f32[128,128]{1,0:T(8,128)S(1)}, u32[]{:S(2)}, u32[]{:S(2)}) %collective-permute-start.41) | collective-permute-done | bytes 65568 | tf_op jit(solution)/shard_map/ppermute | solution.py:160
  127.0 4.1 %collective-permute-start.42 = (f32[128,128]{1,0:T(8,128)S(1)}, f32[128,128]{1,0:T(8,128)S(1)}, u32[]{:S(2)}, u32[]{:S(2)}) collective-permute-start(f32[128,128]{1,0:T(8,128)S(1)} %add.170), channel_id=1, source_target_pairs={{0,16},{16,0},{32,48},{48,32},{64,80},{80,64},{96,112},{112,96},{1... | collective-permute-start | bytes 196616 | tf_op jit(solution)/shard_map/ppermute | solution.py:24
  (114 shorter events, 29.2 us)
Async XLA Ops:
  0.6 5.9 %collective-permute-start = (bf16[512,128]{1,0:T(8,128)(2,1)}, bf16[512,128]{1,0:T(8,128)(2,1)S(1)}, u32[]{:S(2)}, u32[]{:S(2)}) collective-permute-start(bf16[512,128]{1,0:T(8,128)(2,1)} %x_ref.1), channel_id=1, source_target_pairs={{0,32},{16,48},{32,0},{48,16},{64,96},{80,112},{96,64},{112,80},{1... | collective-permute-start | bytes 393224 | tf_op jit(solution)/shard_map/ppermute | solution.py:24
  2.8 6.4 %collective-permute-start.2 = (bf16[512,128]{1,0:T(8,128)(2,1)}, bf16[512,128]{1,0:T(8,128)(2,1)S(1)}, u32[]{:S(2)}, u32[]{:S(2)}) collective-permute-start(bf16[512,128]{1,0:T(8,128)(2,1)} %x_ref.1), channel_id=1, source_target_pairs={{0,192},{16,208},{32,224},{48,240},{64,0},{80,16},{96,32},{112,48}... | collective-permute-start | bytes 393224 | tf_op jit(solution)/shard_map/ppermute | solution.py:24
  6.6 13.0 %collective-permute-start.3 = (bf16[1024,128]{1,0:T(8,128)(2,1)S(1)}, bf16[1024,128]{1,0:T(8,128)(2,1)S(1)}, u32[]{:S(2)}, u32[]{:S(2)}) collective-permute-start(bf16[1024,128]{1,0:T(8,128)(2,1)S(1)} %pad_maximum_fusion.5), channel_id=1, source_target_pairs={{0,128},{16,144},{32,160},{48,176},{64,192},{80,208},{96,224},{112... | collective-permute-start | bytes 786440 | tf_op jit(solution)/shard_map/ppermute | solution.py:24
  11.0 8.6 %collective-permute-start.4 = (bf16[1024,128]{1,0:T(8,128)(2,1)S(1)}, bf16[1024,128]{1,0:T(8,128)(2,1)S(1)}, u32[]{:S(2)}, u32[]{:S(2)}) collective-permute-start(bf16[1024,128]{1,0:T(8,128)(2,1)S(1)} %pad_maximum_fusion.6), channel_id=1, source_target_pairs={{0,32},{16,48},{32,0},{48,16},{64,96},{80,112},{96,64},{112,80},{1... | collective-permute-start | bytes 786440 | tf_op jit(solution)/shard_map/ppermute | solution.py:24
  11.1 14.7 %collective-permute-start.5 = (bf16[2048,128]{1,0:T(8,128)(2,1)S(1)}, bf16[2048,128]{1,0:T(8,128)(2,1)S(1)}, u32[]{:S(2)}, u32[]{:S(2)}) collective-permute-start(bf16[2048,128]{1,0:T(8,128)(2,1)S(1)} %pad_maximum_fusion.refs_4_), channel_id=1, source_target_pairs={{0,16},{16,0},{32,48},{48,32},{64,80},{80,64},{96,112},{112,96},{1... | collective-permute-start | bytes 1572872 | tf_op jit(solution)/shard_map/ppermute | solution.py:24
  19.6 7.2 %collective-permute-start.6 = (bf16[2048,128]{1,0:T(8,128)(2,1)S(1)}, bf16[2048,128]{1,0:T(8,128)(2,1)}, u32[]{:S(2)}, u32[]{:S(2)}) collective-permute-start(bf16[2048,128]{1,0:T(8,128)(2,1)S(1)} %constant_dynamic-update-slice_fusion.refs_5_), channel_id=1, source_target_pairs={{0,16},{16,0},{32,48},{48,32},{64,80},{80,64},{96,112},{112,96},{1... | collective-permute-start | bytes 1572872 | tf_op jit(solution)/shard_map/ppermute | solution.py:24
  31.5 9.3 %collective-permute-start.10 = (bf16[512,128]{1,0:T(8,128)(2,1)S(1)}, bf16[512,128]{1,0:T(8,128)(2,1)S(1)}, u32[]{:S(2)}, u32[]{:S(2)}) collective-permute-start(bf16[512,128]{1,0:T(8,128)(2,1)S(1)} %get-tuple-element.41), channel_id=1, source_target_pairs={{0,1},{1,2},{2,3},{3,4},{4,5},{5,6},{6,7},{7,0},{8,9},{9,10},{10,1... | collective-permute-start | bytes 393224 | tf_op jit(solution)/shard_map/ppermute | solution.py:32
  32.9 8.0 %collective-permute-start.11 = (bf16[512,128]{1,0:T(8,128)(2,1)S(1)}, bf16[512,128]{1,0:T(8,128)(2,1)S(1)}, u32[]{:S(2)}, u32[]{:S(2)}) collective-permute-start(bf16[512,128]{1,0:T(8,128)(2,1)S(1)} %get-tuple-element.43), channel_id=1, source_target_pairs={{0,7},{1,0},{2,1},{3,2},{4,3},{5,4},{6,5},{7,6},{8,15},{9,8},{10,9... | collective-permute-start | bytes 393224 | tf_op jit(solution)/shard_map/ppermute | solution.py:32
  37.2 6.2 %collective-permute-start.13 = (bf16[512,128]{1,0:T(8,128)(2,1)S(1)}, bf16[512,128]{1,0:T(8,128)(2,1)S(1)}, u32[]{:S(2)}, u32[]{:S(2)}) collective-permute-start(bf16[512,128]{1,0:T(8,128)(2,1)S(1)} %get-tuple-element.45), channel_id=1, source_target_pairs={{0,8},{1,9},{2,10},{3,11},{4,12},{5,13},{6,14},{7,15},{8,0},{9,1},... | collective-permute-start | bytes 393224 | tf_op jit(solution)/shard_map/ppermute | solution.py:32
  39.3 14.5 %collective-permute-start.7 = (bf16[1536,128]{1,0:T(8,128)(2,1)}, bf16[1536,128]{1,0:T(8,128)(2,1)S(1)}, u32[]{:S(2)}, u32[]{:S(2)}) collective-permute-start(bf16[1536,128]{1,0:T(8,128)(2,1)} %get-tuple-element.36), channel_id=1, source_target_pairs={{0,7},{1,0},{2,1},{3,2},{4,3},{5,4},{6,5},{7,6},{8,15},{9,8},{10,9... | collective-permute-start | bytes 1179656 | tf_op jit(solution)/shard_map/ppermute | solution.py:32
  40.7 13.1 %collective-permute-start.8 = (bf16[1536,128]{1,0:T(8,128)(2,1)}, bf16[1536,128]{1,0:T(8,128)(2,1)S(1)}, u32[]{:S(2)}, u32[]{:S(2)}) collective-permute-start(bf16[1536,128]{1,0:T(8,128)(2,1)} %get-tuple-element.37), channel_id=1, source_target_pairs={{0,1},{1,2},{2,3},{3,4},{4,5},{5,6},{6,7},{7,0},{8,9},{9,10},{10,1... | collective-permute-start | bytes 1179656 | tf_op jit(solution)/shard_map/ppermute | solution.py:32
  41.6 12.2 %collective-permute-start.12 = (bf16[1024,128]{1,0:T(8,128)(2,1)}, bf16[1024,128]{1,0:T(8,128)(2,1)}, u32[]{:S(2)}, u32[]{:S(2)}) collective-permute-start(bf16[1024,128]{1,0:T(8,128)(2,1)} %pad_maximum_fusion.7), channel_id=1, source_target_pairs={{0,8},{1,9},{2,10},{3,11},{4,12},{5,13},{6,14},{7,15},{8,0},{9,1},... | collective-permute-start | bytes 786440 | tf_op jit(solution)/shard_map/ppermute | solution.py:32
  44.0 9.8 %collective-permute-start.14 = (bf16[512,128]{1,0:T(8,128)(2,1)}, bf16[512,128]{1,0:T(8,128)(2,1)}, u32[]{:S(2)}, u32[]{:S(2)}) collective-permute-start(bf16[512,128]{1,0:T(8,128)(2,1)} %add_convert_fusion.1), channel_id=1, source_target_pairs={{0,6},{1,7},{2,0},{3,1},{4,2},{5,3},{6,4},{7,5},{8,14},{9,15},{10,... | collective-permute-start | bytes 393224 | tf_op jit(solution)/shard_map/ppermute | solution.py:42
  55.0 8.0 %collective-permute-start.16 = (bf16[512,128]{1,0:T(8,128)(2,1)S(1)}, bf16[512,128]{1,0:T(8,128)(2,1)S(1)}, u32[]{:S(2)}, u32[]{:S(2)}) collective-permute-start(bf16[512,128]{1,0:T(8,128)(2,1)S(1)} %get-tuple-element.71), channel_id=1, source_target_pairs={{0,6},{1,7},{2,0},{3,1},{4,2},{5,3},{6,4},{7,5},{8,14},{9,15},{10,... | collective-permute-start | bytes 393224 | tf_op jit(solution)/shard_map/ppermute | solution.py:32
  58.8 9.7 %collective-permute-start.15 = (bf16[512,128]{1,0:T(8,128)(2,1)S(1)}, bf16[512,128]{1,0:T(8,128)(2,1)S(1)}, u32[]{:S(2)}, u32[]{:S(2)}) collective-permute-start(bf16[512,128]{1,0:T(8,128)(2,1)S(1)} %get-tuple-element.73), channel_id=1, source_target_pairs={{0,2},{1,3},{2,4},{3,5},{4,6},{5,7},{6,0},{7,1},{8,10},{9,11},{10,... | collective-permute-start | bytes 393224 | tf_op jit(solution)/shard_map/ppermute | solution.py:32
  71.1 7.7 %collective-permute-start.21 = (bf16[512,128]{1,0:T(8,128)(2,1)S(1)}, bf16[512,128]{1,0:T(8,128)(2,1)S(1)}, u32[]{:S(2)}, u32[]{:S(2)}) collective-permute-start(bf16[512,128]{1,0:T(8,128)(2,1)S(1)} %get-tuple-element.48.refs_4_), channel_id=1, source_target_pairs={{0,6},{1,7},{2,0},{3,1},{4,2},{5,3},{6,4},{7,5},{8,14},{9,15},{10,... | collective-permute-start | bytes 393224 | tf_op jit(solution)/shard_map/ppermute | solution.py:32
  71.1 10.3 %collective-permute-start.20 = (bf16[512,128]{1,0:T(8,128)(2,1)S(1)}, bf16[512,128]{1,0:T(8,128)(2,1)S(1)}, u32[]{:S(2)}, u32[]{:S(2)}) collective-permute-start(bf16[512,128]{1,0:T(8,128)(2,1)S(1)} %get-tuple-element.48.refs_4_), channel_id=1, source_target_pairs={{0,2},{1,3},{2,4},{3,5},{4,6},{5,7},{6,0},{7,1},{8,10},{9,11},{10,... | collective-permute-start | bytes 393224 | tf_op jit(solution)/shard_map/ppermute | solution.py:32
  73.6 10.6 %collective-permute-start.17 = (bf16[512,128]{1,0:T(8,128)(2,1)S(1)}, bf16[512,128]{1,0:T(8,128)(2,1)S(1)}, u32[]{:S(2)}, u32[]{:S(2)}) collective-permute-start(bf16[512,128]{1,0:T(8,128)(2,1)S(1)} %get-tuple-element.48.refs_4_), channel_id=1, source_target_pairs={{0,8},{1,9},{2,10},{3,11},{4,12},{5,13},{6,14},{7,15},{8,0},{9,1},... | collective-permute-start | bytes 393224 | tf_op jit(solution)/shard_map/ppermute | solution.py:32
  83.0 9.0 %collective-permute-start.22 = (bf16[1024,128]{1,0:T(8,128)(2,1)S(1)}, bf16[1024,128]{1,0:T(8,128)(2,1)S(1)}, u32[]{:S(2)}, u32[]{:S(2)}) collective-permute-start(bf16[1024,128]{1,0:T(8,128)(2,1)S(1)} %pad_maximum_fusion.8), channel_id=1, source_target_pairs={{0,8},{1,9},{2,10},{3,11},{4,12},{5,13},{6,14},{7,15},{8,0},{9,1},... | collective-permute-start | bytes 786440 | tf_op jit(solution)/shard_map/ppermute | solution.py:32
  84.2 9.9 %collective-permute-start.27 = (bf16[1536,128]{1,0:T(8,128)(2,1)S(1)}, bf16[1536,128]{1,0:T(8,128)(2,1)S(1)}, u32[]{:S(2)}, u32[]{:S(2)}) collective-permute-start(bf16[1536,128]{1,0:T(8,128)(2,1)S(1)} %get-tuple-element.78), channel_id=1, source_target_pairs={{0,7},{1,0},{2,1},{3,2},{4,3},{5,4},{6,5},{7,6},{8,15},{9,8},{10,9... | collective-permute-start | bytes 1179656 | tf_op jit(solution)/shard_map/ppermute | solution.py:32
  85.2 8.9 %collective-permute-start.26 = (bf16[1536,128]{1,0:T(8,128)(2,1)S(1)}, bf16[1536,128]{1,0:T(8,128)(2,1)S(1)}, u32[]{:S(2)}, u32[]{:S(2)}) collective-permute-start(bf16[1536,128]{1,0:T(8,128)(2,1)S(1)} %get-tuple-element.79), channel_id=1, source_target_pairs={{0,1},{1,2},{2,3},{3,4},{4,5},{5,6},{6,7},{7,0},{8,9},{9,10},{10,1... | collective-permute-start | bytes 1179656 | tf_op jit(solution)/shard_map/ppermute | solution.py:32
  87.6 6.6 %collective-permute-start.30 = (bf16[512,128]{1,0:T(8,128)(2,1)S(1)}, bf16[512,128]{1,0:T(8,128)(2,1)S(1)}, u32[]{:S(2)}, u32[]{:S(2)}) collective-permute-start(bf16[512,128]{1,0:T(8,128)(2,1)S(1)} %collective-permute-done.24.refs_9_), channel_id=1, source_target_pairs={{0,8},{1,9},{2,10},{3,11},{4,12},{5,13},{6,14},{7,15},{8,0},{9,1},... | collective-permute-start | bytes 393224 | tf_op jit(solution)/shard_map/ppermute | solution.py:32
  92.0 6.9 %collective-permute-start.28 = (bf16[512,128]{1,0:T(8,128)(2,1)S(1)}, bf16[512,128]{1,0:T(8,128)(2,1)S(1)}, u32[]{:S(2)}, u32[]{:S(2)}) collective-permute-start(bf16[512,128]{1,0:T(8,128)(2,1)S(1)} %get-tuple-element.77), channel_id=1, source_target_pairs={{0,1},{1,2},{2,3},{3,4},{4,5},{5,6},{6,7},{7,0},{8,9},{9,10},{10,1... | collective-permute-start | bytes 393224 | tf_op jit(solution)/shard_map/ppermute | solution.py:32
  100.9 9.4 %collective-permute-start.33 = (bf16[2048,128]{1,0:T(8,128)(2,1)S(1)}, bf16[2048,128]{1,0:T(8,128)(2,1)S(1)}, u32[]{:S(2)}, u32[]{:S(2)}) collective-permute-start(bf16[2048,128]{1,0:T(8,128)(2,1)S(1)} %get-tuple-element.62), channel_id=1, source_target_pairs={{0,16},{16,0},{32,48},{48,32},{64,80},{80,64},{96,112},{112,96},{1... | collective-permute-start | bytes 1572872 | tf_op jit(solution)/shard_map/ppermute | solution.py:24
  103.4 6.9 %collective-permute-start.32 = (f32[128,128]{1,0:T(8,128)S(1)}, f32[128,128]{1,0:T(8,128)S(1)}, u32[]{:S(2)}, u32[]{:S(2)}) collective-permute-start(f32[128,128]{1,0:T(8,128)S(1)} %add.162), channel_id=1, source_target_pairs={{0,8},{1,9},{2,10},{3,11},{4,12},{5,13},{6,14},{7,15},{8,0},{9,1},... | collective-permute-start | bytes 196616 | tf_op jit(solution)/shard_map/ppermute | solution.py:160
  108.1 5.8 %collective-permute-start.31 = (bf16[2048,128]{1,0:T(8,128)(2,1)S(1)}, bf16[2048,128]{1,0:T(8,128)(2,1)S(1)}, u32[]{:S(2)}, u32[]{:S(2)}) collective-permute-start(bf16[2048,128]{1,0:T(8,128)(2,1)S(1)} %get-tuple-element.59), channel_id=1, source_target_pairs={{0,16},{16,0},{32,48},{48,32},{64,80},{80,64},{96,112},{112,96},{1... | collective-permute-start | bytes 1572872 | tf_op jit(solution)/shard_map/ppermute | solution.py:24
  110.4 7.1 %collective-permute-start.36 = (f32[128,128]{1,0:T(8,128)S(1)}, f32[128,128]{1,0:T(8,128)S(1)}, u32[]{:S(2)}, u32[]{:S(2)}) collective-permute-start(f32[128,128]{1,0:T(8,128)S(1)} %add.164), channel_id=1, source_target_pairs={{0,4},{1,5},{2,6},{3,7},{4,0},{5,1},{6,2},{7,3},{8,12},{9,13},{10,... | collective-permute-start | bytes 196616 | tf_op jit(solution)/shard_map/ppermute | solution.py:160
  111.4 7.7 %collective-permute-start.37 = (bf16[1024,128]{1,0:T(8,128)(2,1)S(1)}, bf16[1024,128]{1,0:T(8,128)(2,1)S(1)}, u32[]{:S(2)}, u32[]{:S(2)}) collective-permute-start(bf16[1024,128]{1,0:T(8,128)(2,1)S(1)} %get-tuple-element.69), channel_id=1, source_target_pairs={{0,32},{16,48},{32,0},{48,16},{64,96},{80,112},{96,64},{112,80},{1... | collective-permute-start | bytes 786440 | tf_op jit(solution)/shard_map/ppermute | solution.py:24
  113.5 8.7 %collective-permute-start.34 = (bf16[1024,128]{1,0:T(8,128)(2,1)S(1)}, bf16[1024,128]{1,0:T(8,128)(2,1)S(1)}, u32[]{:S(2)}, u32[]{:S(2)}) collective-permute-start(bf16[1024,128]{1,0:T(8,128)(2,1)S(1)} %get-tuple-element.70), channel_id=1, source_target_pairs={{0,128},{16,144},{32,160},{48,176},{64,192},{80,208},{96,224},{112... | collective-permute-start | bytes 786440 | tf_op jit(solution)/shard_map/ppermute | solution.py:24
  119.2 12.0 %collective-permute-start.39 = (bf16[512,128]{1,0:T(8,128)(2,1)S(1)}, bf16[512,128]{1,0:T(8,128)(2,1)S(1)}, u32[]{:S(2)}, u32[]{:S(2)}) collective-permute-start(bf16[512,128]{1,0:T(8,128)(2,1)S(1)} %get-tuple-element.74), channel_id=1, source_target_pairs={{0,192},{16,208},{32,224},{48,240},{64,0},{80,16},{96,32},{112,48}... | collective-permute-start | bytes 393224 | tf_op jit(solution)/shard_map/ppermute | solution.py:24
  122.2 9.0 %collective-permute-start.38 = (bf16[512,128]{1,0:T(8,128)(2,1)S(1)}, bf16[512,128]{1,0:T(8,128)(2,1)S(1)}, u32[]{:S(2)}, u32[]{:S(2)}) collective-permute-start(bf16[512,128]{1,0:T(8,128)(2,1)S(1)} %get-tuple-element.75), channel_id=1, source_target_pairs={{0,64},{16,80},{32,96},{48,112},{64,128},{80,144},{96,160},{112,17... | collective-permute-start | bytes 393224 | tf_op jit(solution)/shard_map/ppermute | solution.py:24
  122.2 8.9 %collective-permute-start.35 = (bf16[512,128]{1,0:T(8,128)(2,1)S(1)}, bf16[512,128]{1,0:T(8,128)(2,1)S(1)}, u32[]{:S(2)}, u32[]{:S(2)}) collective-permute-start(bf16[512,128]{1,0:T(8,128)(2,1)S(1)} %get-tuple-element.67), channel_id=1, source_target_pairs={{0,32},{16,48},{32,0},{48,16},{64,96},{80,112},{96,64},{112,80},{1... | collective-permute-start | bytes 393224 | tf_op jit(solution)/shard_map/ppermute | solution.py:24
  (23 other events, 247.3 us)

commit v6 on v4

--- a/solution.py
+++ b/solution.py
@@ -14,6 +14,10 @@
 BLOCK = 128
 ROWS = SHARD + BLOCK
 VMEM_LIMIT = 24 * 1024 * 1024
+
+
+def tied(*arrays):
+    return lax.optimization_barrier(arrays)
 
 
 def send_row(x, dy=0, dx=0, dc=0):
@@ -182,10 +186,11 @@
     a = send_row(features, dx=1)
     u = send_row(features, dy=1)
     d = send_row(features, dy=-1)
-    ud = jnp.concatenate([u, d])
     near = pl.pallas_call(
         copy_kernel, out_shape=jax.ShapeDtypeStruct((S, BLOCK), BF16), compiler_params=params
     )(features)
+    near, u, d = tied(near, u, d)
+    ud = jnp.concatenate([u, d])
     xa = jnp.concatenate([near, a])
     w = send_row(xa, dy=2)
     v = send_row(ud, dx=1)
@@ -200,26 +205,32 @@
 
     O = lambda k: (k % 8 * S, S)
     X = lambda k: ((8 + k % 8) * S, S)
-    outs = [[X(-1), X(-3)], [X(1), X(3)], [X(4)], [O(-1), O(-3)], [O(1), O(3)],
+    outs = [[X(-3)], [X(3)], [X(4)], [O(1)], [O(-1)], [O(-3), X(-1)], [O(3), X(1)],
             [X(-2)], [X(2)], [O(4)], [X(0)], [O(2)], [O(-2)], [O(0)]]
-    m, n, l, e, g, x6, x2, o4, x0, o2, o6, o0 = tile_sums(
+    (x5, x3, x4, o1, o7, e, g, x6, x2, o4, x0, o2, o6, o0) = tile_sums(
         col_at, row_at, count, scan, values, [h1, h2, c1, c2], places, outs,
-        [BF16] * 5 + [F32] * 7, True,
-    )
-    m = send_col(m, dz=-1)
-    n = send_col(n, dz=1)
-    l = send_col(l, dh=1)
-    e = send_col(e, dz=-1)
-    g = send_col(g, dz=1)
-    q = jnp.concatenate([add(x2, n[S:]).astype(BF16), add(x6, m[S:]).astype(BF16)])
-    q = send_col(q, dh=1)
-    h = send_apart(add(o4, l).astype(BF16), -2).astype(F32)
-    rx = send_col(add(x0, m[:S], n[:S]).astype(BF16), dh=1)
-    o2 = add(o2, g[S:], q[:S], jnp.where(core == 0, 0.0, h)).astype(BF16)
-    o6 = add(o6, e[S:], q[S:], jnp.where(core == 0, h, 0.0)).astype(BF16)
+        [BF16] * 7 + [F32] * 7, True,
+    )
+    r5 = send_col(x5, dz=-1)
+    r3 = send_col(x3, dz=1)
+    r4 = send_col(x4, dh=1)
+    s1 = send_col(o1, dz=1)
+    s7 = send_col(o7, dz=-1)
+    re = send_col(e, dz=-1)
+    rg = send_col(g, dz=1)
+    q = jnp.concatenate([add(x2, r3).astype(BF16), add(x6, r5).astype(BF16)])
+    rq = send_col(q, dh=1)
+    o4 = add(o4, r4).astype(BF16)
+    rh = send_col(o4[: S // 2], dz=2)
+    ri = send_col(o4[S // 2:], dz=-2)
+    x0 = add(x0, re[S:], rg[S:]).astype(BF16)
+    rx = send_col(x0, dh=1)
+    zero = jnp.zeros((S // 2, BLOCK), F32)
+    o2 = add(o2, rg[:S], rq[:S], jnp.concatenate([rh.astype(F32), zero])).astype(BF16)
+    o6 = add(o6, re[:S], rq[S:], jnp.concatenate([zero, ri.astype(F32)])).astype(BF16)
     s2 = send_col(o2, dz=2)
     s6 = send_col(o6, dz=-2)
-
+    fin = (o0, s1, s7, rx, s2, s6)
     half = jax.ShapeDtypeStruct((BLOCK, BLOCK), F32)
     activation, gt, keep, give = pl.pallas_call(
         mid_kernel,
@@ -232,7 +243,7 @@
         in_specs=[pl.BlockSpec(memory_space=pltpu.SMEM)] + [pl.BlockSpec(memory_space=pltpu.VMEM)] * 8,
         scratch_shapes=[pltpu.VMEM((BLOCK, 256), F32)],
         compiler_params=params,
-    )(core[None], o0, e, g, rx, s2, s6, weight, grad_out)
+    )(core[None], *fin, weight, grad_out)
     share = keep + send_row(give, dc=1)
     gt = jnp.concatenate([gt, share.astype(BF16)])
 
@@ -241,15 +252,15 @@
     a = send_col(gt, dh=1)
     q = send_col(jnp.concatenate([u2, d2]), dh=1)
     f4 = send_apart(jnp.where(core == 0, u2, d2), 2)
-    e = send_col(jnp.concatenate([gt, u2]), dz=1)
-    g = send_col(jnp.concatenate([gt, d2]), dz=-1)
-    m = send_col(jnp.concatenate([a, q[:ROWS]]), dz=1)
-    n = send_col(jnp.concatenate([a, q[ROWS:]]), dz=-1)
+    e = send_col(jnp.concatenate([gt, u2, a]), dz=1)
+    g = send_col(jnp.concatenate([gt, d2, a]), dz=-1)
+    m = send_col(q[:ROWS], dz=1)
+    n = send_col(q[ROWS:], dz=-1)
     l = send_col(f4, dh=1)
     panels = [gt, a, u2, d2, q, f4, e, g, m, n, l]
     both = lambda *slots: [p for f, r in slots for p in ((f, r), (16 * S + f // 4, BLOCK))]
     places = [both(O(0)), both(X(0)), both(O(-2)), both(O(2)), both(X(-2), X(2)), both(O(4)),
-              both(O(-1), O(-3)), both(O(1), O(3)), both(X(-1), X(-3)), both(X(1), X(3)), both(X(4))]
+              both(O(-1), O(-3), X(-1)), both(O(1), O(3), X(1)), both(X(-3)), both(X(3)), both(X(4))]
 
     k = lambda dy, dx: ((dx * 4 + dy % 4) * S, S)
     last = [k(0, 0), k(0, 1), k(1, 0), k(-1, 0)]
@@ -262,6 +273,7 @@
     own = add(own, send_row(away, dc=1))
     w = send_row(jnp.concatenate([own1[2 * S:], share]), dy=2)
     v = send_row(jnp.concatenate([own1[:2 * S], share]), dx=1)
+
     o = add(own[S:2 * S], w[S:2 * S]).astype(BF16)
     ud = add(own[2 * S:4 * S], v[:2 * S]).astype(BF16)
     here = rounded(add(share, w[2 * S:]))

time: 134 us -> 123 us (0.918)
  waiting for transfers between devices: 55.1 us -> 43.2 us
  starting transfers between devices: 64.8 us -> 69.1 us
  other arithmetic: 3.53 us -> 1.63 us
  Pallas kernels: 7.93 us -> 6.49 us
    ppermute x2 -> x1, waiting for transfers between devices: 7.18 us -> 0.02 us  [send_apart(): return lax.ppermute(x, ('row', 'col'), perm)]
    ppermute x16, starting transfers between devices: 30.2 us -> 34.8 us  [send_row(): return lax.ppermute(x, 'row', perm)]
    ppermute x16, waiting for transfers between devices: 20 us -> 15.8 us  [send_row(): return lax.ppermute(x, 'row', perm)]
    convert_element_type x3 -> x4, other arithmetic: 2.06 us -> 0.25 us  [the longest x1 0.16 us: body(): add(o6, re[:S], rq[S:], jnp.concatenate([zero, ri.astype(F32)]))]
    pallas_call x2, Pallas kernels: 5.75 us -> 4.3 us  [tile_sums(): pl.pallas_call(functools.partial(tile_kernel, places, outs, left), out_sh...]
    ppermute x18 -> x22, waiting for transfers between devices: 28 us -> 27.4 us  [send_col(): return lax.ppermute(x, 'col', perm)]
    ppermute x18 -> x22, starting transfers between devices: 32.3 us -> 32.1 us  [send_col(): return lax.ppermute(x, 'col', perm)]
  transfers between devices with their start and end apart: 36 -> 39, of which waited for: 21 -> 23; matrix products, arithmetic and copies ran while one was open for 2% -> 1% of each run, Pallas kernels for 1% -> 1%
where the time goes in v6:
time: 123 us
  starting transfers between devices  69.1 us (56%)
  waiting for transfers between devices  43.2 us (35%)
  Pallas kernels  6.49 us (5%)
  between operations  1.65 us (1%)
  other arithmetic  1.63 us (1%)
    ppermute x16, starting transfers between devices, send_row(): return lax.ppermute(x, 'row', perm)  34.8 us
    ppermute x22, starting transfers between devices, send_col(): return lax.ppermute(x, 'col', perm)  32.1 us
    ppermute x22, waiting for transfers between devices, send_col(): return lax.ppermute(x, 'col', perm)  27.4 us
    ppermute x16, waiting for transfers between devices, send_row(): return lax.ppermute(x, 'row', perm)  15.8 us
    pallas_call x2, Pallas kernels, tile_sums(): pl.pallas_call(functools.partial(tile_kernel, places, outs, left), out_sh...  4.3 us
  transfers between devices with their start and end apart: 39, of which 23 were waited for; matrix products, arithmetic and copies ran while one was open for 1% of the time, Pallas kernels for 1%

profile of v6, /device:TPU:1, one launch (start us, length us, event | category | flops | bytes accessed | tf_op | source)
XLA Modules:
  0.0 123.2 jit_solution(16914217781762595515)
XLA Ops:
  0.6 2.2 %collective-permute-start = (bf16[512,128]{1,0:T(8,128)(2,1)}, bf16[512,128]{1,0:T(8,128)(2,1)S(1)}, u32[]{:S(2)}, u32[]{:S(2)}) collective-permute-start(bf16[512,128]{1,0:T(8,128)(2,1)} %x_ref.1), channel_id=1, source_target_pairs={{0,64},{16,80},{32,96},{48,112},{64,128},{80,144},{96,160},{112,17... | collective-permute-start | bytes 393224 | tf_op jit(solution)/shard_map/ppermute | solution.py:29
  6.9 1.9 %collective-permute-start.4 = (bf16[1024,128]{1,0:T(8,128)(2,1)S(1)}, bf16[1024,128]{1,0:T(8,128)(2,1)S(1)}, u32[]{:S(2)}, u32[]{:S(2)}) collective-permute-start(bf16[1024,128]{1,0:T(8,128)(2,1)S(1)} %pad_maximum_fusion.7), channel_id=1, source_target_pairs={{0,32},{16,48},{32,0},{48,16},{64,96},{80,112},{96,64},{112,80},{1... | collective-permute-start | bytes 786440 | tf_op jit(solution)/shard_map/ppermute | solution.py:29
  8.8 2.4 %collective-permute-start.3 = (bf16[1024,128]{1,0:T(8,128)(2,1)S(1)}, bf16[1024,128]{1,0:T(8,128)(2,1)S(1)}, u32[]{:S(2)}, u32[]{:S(2)}) collective-permute-start(bf16[1024,128]{1,0:T(8,128)(2,1)S(1)} %pad_maximum_fusion.6), channel_id=1, source_target_pairs={{0,128},{16,144},{32,160},{48,176},{64,192},{80,208},{96,224},{112... | collective-permute-start | bytes 786440 | tf_op jit(solution)/shard_map/ppermute | solution.py:29
  11.3 2.7 %collective-permute-start.5 = (bf16[2048,128]{1,0:T(8,128)(2,1)S(1)}, bf16[2048,128]{1,0:T(8,128)(2,1)S(1)}, u32[]{:S(2)}, u32[]{:S(2)}) collective-permute-start(bf16[2048,128]{1,0:T(8,128)(2,1)S(1)} %constant_dynamic-update-slice_fusion.refs_5_), channel_id=1, source_target_pairs={{0,16},{16,0},{32,48},{48,32},{64,80},{80,64},{96,112},{112,96},{1... | collective-permute-start | bytes 1572872 | tf_op jit(solution)/shard_map/ppermute | solution.py:29
  15.7 6.1 %collective-permute-start.6 = (bf16[2048,128]{1,0:T(8,128)(2,1)S(1)}, bf16[2048,128]{1,0:T(8,128)(2,1)}, u32[]{:S(2)}, u32[]{:S(2)}) collective-permute-start(bf16[2048,128]{1,0:T(8,128)(2,1)S(1)} %constant_dynamic-update-slice_fusion.4.refs_6_), channel_id=1, source_target_pairs={{0,16},{16,0},{32,48},{48,32},{64,80},{80,64},{96,112},{112,96},{1... | collective-permute-start | bytes 1572872 | tf_op jit(solution)/shard_map/ppermute | solution.py:29
  23.5 2.2 %shard_map.95 = (bf16[512,128]{1,0:T(8,128)(2,1)S(1)}, bf16[512,128]{1,0:T(8,128)(2,1)S(1)}, bf16[512,128]{1,0:T(8,128)(2,1)S(1)}, bf16[512,128]{1,0:T(8,128)(2,...) custom-call(s32[48]{0:T(128)S(1)} %get-tuple-element.74.refs_0_.refs, ...), custom_call_target="tpu_custom_call" | custom-call | tf_op jit(solution)/shard_map/pallas_call | solution.py:119
  25.9 3.7 %collective-permute-start.13 = (bf16[512,128]{1,0:T(8,128)(2,1)S(1)}, bf16[512,128]{1,0:T(8,128)(2,1)S(1)}, u32[]{:S(2)}, u32[]{:S(2)}) collective-permute-start(bf16[512,128]{1,0:T(8,128)(2,1)S(1)} %get-tuple-element.42), channel_id=1, source_target_pairs={{0,7},{1,0},{2,1},{3,2},{4,3},{5,4},{6,5},{7,6},{8,15},{9,8},{10,9... | collective-permute-start | bytes 393224 | tf_op jit(solution)/shard_map/ppermute | solution.py:37
  29.5 2.0 %collective-permute-start.15 = (bf16[512,128]{1,0:T(8,128)(2,1)S(1)}, bf16[512,128]{1,0:T(8,128)(2,1)S(1)}, u32[]{:S(2)}, u32[]{:S(2)}) collective-permute-start(bf16[512,128]{1,0:T(8,128)(2,1)S(1)} %get-tuple-element.44), channel_id=1, source_target_pairs={{0,8},{1,9},{2,10},{3,11},{4,12},{5,13},{6,14},{7,15},{8,0},{9,1},... | collective-permute-start | bytes 393224 | tf_op jit(solution)/shard_map/ppermute | solution.py:37
  33.1 1.7 %collective-permute-start.14 = (bf16[1024,128]{1,0:T(8,128)(2,1)S(1)}, bf16[1024,128]{1,0:T(8,128)(2,1)S(1)}, u32[]{:S(2)}, u32[]{:S(2)}) collective-permute-start(bf16[1024,128]{1,0:T(8,128)(2,1)S(1)} %pad_maximum_fusion.8), channel_id=1, source_target_pairs={{0,8},{1,9},{2,10},{3,11},{4,12},{5,13},{6,14},{7,15},{8,0},{9,1},... | collective-permute-start | bytes 786440 | tf_op jit(solution)/shard_map/ppermute | solution.py:37
  35.5 2.1 %collective-permute-start.18 = (bf16[256,128]{1,0:T(8,128)(2,1)S(1)}, bf16[256,128]{1,0:T(8,128)(2,1)S(1)}, u32[]{:S(2)}, u32[]{:S(2)}) collective-permute-start(bf16[256,128]{1,0:T(8,128)(2,1)S(1)} %get-tuple-element.70), channel_id=1, source_target_pairs={{0,6},{1,7},{2,0},{3,1},{4,2},{5,3},{6,4},{7,5},{8,14},{9,15},{10,... | collective-permute-start | bytes 196616 | tf_op jit(solution)/shard_map/ppermute | solution.py:37
  37.9 1.9 %collective-permute-done.18 = bf16[256,128]{1,0:T(8,128)(2,1)S(1)} collective-permute-done((bf16[256,128]{1,0:T(8,128)(2,1)S(1)}, bf16[256,128]{1,0:T(8,128)(2,1)S(1)}, u32[]{:S(2)}, u32[]{:S(2)}) %collective-permute-start.18) | collective-permute-done | bytes 65568 | tf_op jit(solution)/shard_map/ppermute | solution.py:37
  39.9 2.2 %collective-permute-start.7 = (bf16[512,128]{1,0:T(8,128)(2,1)S(1)}, bf16[512,128]{1,0:T(8,128)(2,1)S(1)}, u32[]{:S(2)}, u32[]{:S(2)}) collective-permute-start(bf16[512,128]{1,0:T(8,128)(2,1)S(1)} %get-tuple-element.33), channel_id=1, source_target_pairs={{0,1},{1,2},{2,3},{3,4},{4,5},{5,6},{6,7},{7,0},{8,9},{9,10},{10,1... | collective-permute-start | bytes 393224 | tf_op jit(solution)/shard_map/ppermute | solution.py:37
  43.0 2.0 %collective-permute-start.8 = (bf16[512,128]{1,0:T(8,128)(2,1)S(1)}, bf16[512,128]{1,0:T(8,128)(2,1)S(1)}, u32[]{:S(2)}, u32[]{:S(2)}) collective-permute-start(bf16[512,128]{1,0:T(8,128)(2,1)S(1)} %get-tuple-element.34), channel_id=1, source_target_pairs={{0,7},{1,0},{2,1},{3,2},{4,3},{5,4},{6,5},{7,6},{8,15},{9,8},{10,9... | collective-permute-start | bytes 393224 | tf_op jit(solution)/shard_map/ppermute | solution.py:37
  45.2 3.0 %collective-permute-start.19 = (bf16[512,128]{1,0:T(8,128)(2,1)S(1)}, bf16[512,128]{1,0:T(8,128)(2,1)S(1)}, u32[]{:S(2)}, u32[]{:S(2)}) collective-permute-start(bf16[512,128]{1,0:T(8,128)(2,1)S(1)} %get-tuple-element.65), channel_id=1, source_target_pairs={{0,6},{1,7},{2,0},{3,1},{4,2},{5,3},{6,4},{7,5},{8,14},{9,15},{10,... | collective-permute-start | bytes 393224 | tf_op jit(solution)/shard_map/ppermute | solution.py:37
  49.3 2.1 %collective-permute-done.19.r5 = bf16[512,128]{1,0:T(8,128)(2,1)S(1)} collective-permute-done((bf16[512,128]{1,0:T(8,128)(2,1)S(1)}, bf16[512,128]{1,0:T(8,128)(2,1)S(1)}, u32[]{:S(2)}, u32[]{:S(2)}) %collective-permute-start.19) | collective-permute-done | bytes 131104 | tf_op jit(solution)/shard_map/ppermute | solution.py:37
  51.4 2.0 %collective-permute-done.11.r3 = bf16[512,128]{1,0:T(8,128)(2,1)S(1)} collective-permute-done((bf16[512,128]{1,0:T(8,128)(2,1)S(1)}, bf16[512,128]{1,0:T(8,128)(2,1)S(1)}, u32[]{:S(2)}, u32[]{:S(2)}) %collective-permute-start.11) | collective-permute-done | bytes 131104 | tf_op jit(solution)/shard_map/ppermute | solution.py:37
  56.4 5.5 %collective-permute-start.20 = (f32[128,128]{1,0:T(8,128)S(1)}, f32[128,128]{1,0:T(8,128)S(1)}, u32[]{:S(2)}, u32[]{:S(2)}) collective-permute-start(f32[128,128]{1,0:T(8,128)S(1)} %get-tuple-element.49), channel_id=1, source_target_pairs={{0,16},{16,0},{32,48},{48,32},{64,80},{80,64},{96,112},{112,96},{1... | collective-permute-start | bytes 196616 | tf_op jit(solution)/shard_map/ppermute | solution.py:29
  63.2 2.0 %collective-permute-start.22 = (bf16[640,128]{1,0:T(8,128)(2,1)S(1)}, bf16[640,128]{1,0:T(8,128)(2,1)S(1)}, u32[]{:S(2)}, u32[]{:S(2)}) collective-permute-start(bf16[640,128]{1,0:T(8,128)(2,1)S(1)} %pad_maximum_fusion.10.refs_5_), channel_id=1, source_target_pairs={{0,2},{1,3},{2,4},{3,5},{4,6},{5,7},{6,0},{7,1},{8,10},{9,11},{10,... | collective-permute-start | bytes 491528 | tf_op jit(solution)/shard_map/ppermute | solution.py:37
  65.2 3.4 %collective-permute-start.21 = (bf16[640,128]{1,0:T(8,128)(2,1)S(1)}, bf16[640,128]{1,0:T(8,128)(2,1)S(1)}, u32[]{:S(2)}, u32[]{:S(2)}) collective-permute-start(bf16[640,128]{1,0:T(8,128)(2,1)S(1)} %pad_maximum_fusion.10.refs_5_), channel_id=1, source_target_pairs={{0,8},{1,9},{2,10},{3,11},{4,12},{5,13},{6,14},{7,15},{8,0},{9,1},... | collective-permute-start | bytes 491528 | tf_op jit(solution)/shard_map/ppermute | solution.py:37
  68.6 3.9 %collective-permute-done.23.refs_8_ = bf16[640,128]{1,0:T(8,128)(2,1)S(1)} collective-permute-done((bf16[640,128]{1,0:T(8,128)(2,1)S(1)}, bf16[640,128]{1,0:T(8,128)(2,1)S(1)}, u32[]{:S(2)}, u32[]{:S(2)}) %collective-permute-start.23) | collective-permute-done | bytes 163872 | tf_op jit(solution)/shard_map/ppermute | solution.py:37
  72.5 2.3 %collective-permute-done.22.refs_7_ = bf16[640,128]{1,0:T(8,128)(2,1)S(1)} collective-permute-done((bf16[640,128]{1,0:T(8,128)(2,1)S(1)}, bf16[640,128]{1,0:T(8,128)(2,1)S(1)}, u32[]{:S(2)}, u32[]{:S(2)}) %collective-permute-start.22) | collective-permute-done | bytes 163872 | tf_op jit(solution)/shard_map/ppermute | solution.py:37
  74.8 2.2 %collective-permute-start.25 = (bf16[640,128]{1,0:T(8,128)(2,1)S(1)}, bf16[640,128]{1,0:T(8,128)(2,1)S(1)}, u32[]{:S(2)}, u32[]{:S(2)}) collective-permute-start(bf16[640,128]{1,0:T(8,128)(2,1)S(1)} %broadcast_select_fusion), channel_id=1, source_target_pairs={{0,2},{1,3},{2,4},{3,5},{4,6},{5,7},{6,0},{7,1},{8,10},{9,11},{10,... | collective-permute-start | bytes 491528 | tf_op jit(solution)/shard_map/ppermute | solution.py:47
  80.0 2.2 %collective-permute-start.30 = (bf16[640,128]{1,0:T(8,128)(2,1)S(1)}, bf16[640,128]{1,0:T(8,128)(2,1)S(1)}, u32[]{:S(2)}, u32[]{:S(2)}) collective-permute-start(bf16[640,128]{1,0:T(8,128)(2,1)S(1)} %collective-permute-done.25.refs_10_), channel_id=1, source_target_pairs={{0,8},{1,9},{2,10},{3,11},{4,12},{5,13},{6,14},{7,15},{8,0},{9,1},... | collective-permute-start | bytes 491528 | tf_op jit(solution)/shard_map/ppermute | solution.py:37
  82.2 5.9 %collective-permute-done.24.refs_9_ = bf16[1280,128]{1,0:T(8,128)(2,1)S(1)} collective-permute-done((bf16[1280,128]{1,0:T(8,128)(2,1)S(1)}, bf16[1280,128]{1,0:T(8,128)(2,1)S(1)}, u32[]{:S(2)}, u32[]{:S(2)}) %collective-permute-start.24) | collective-permute-done | bytes 327712 | tf_op jit(solution)/shard_map/ppermute | solution.py:37
  91.2 3.4 %collective-permute-done.29.refs_14_ = bf16[640,128]{1,0:T(8,128)(2,1)S(1)} collective-permute-done((bf16[640,128]{1,0:T(8,128)(2,1)S(1)}, bf16[640,128]{1,0:T(8,128)(2,1)S(1)}, u32[]{:S(2)}, u32[]{:S(2)}) %collective-permute-start.29) | collective-permute-done | bytes 163872 | tf_op jit(solution)/shard_map/ppermute | solution.py:37
  95.8 2.1 %shard_map.97 = (f32[2048,128]{1,0:T(8,128)S(1)}, bf16[2048,128]{1,0:T(8,128)(2,1)S(1)}, f32[2048,128]{1,0:T(8,128)S(1)}, bf16[2048,128]{1,0:T(8,128)(2,1)S(1)}, bf16[128,128]{1,0:T(8,128)(2,1)S(1)}) custom-call(s32[48]{0:T(128)S(1)} %get-tuple-element.75.refs_1_.refs_0_, s32[48]{0:T(128)S(1)} %get-tuple-element.74.refs_0_.refs_1_, s32[1]{0:T(128)} %bitcast.30.refs_2_, ...), custom_call_target="tpu_custom_call" | custom-call | tf_op jit(solution)/shard_map/pallas_call | solution.py:119
  102.4 1.7 %collective-permute-start.33 = (bf16[1152,128]{1,0:T(8,128)(2,1)S(1)}, bf16[1152,128]{1,0:T(8,128)(2,1)S(1)}, u32[]{:S(2)}, u32[]{:S(2)}) collective-permute-start(bf16[1152,128]{1,0:T(8,128)(2,1)S(1)} %get-tuple-element.73), channel_id=1, source_target_pairs={{0,128},{16,144},{32,160},{48,176},{64,192},{80,208},{96,224},{112... | collective-permute-start | bytes 884744 | tf_op jit(solution)/shard_map/ppermute | solution.py:29
  104.2 5.2 %collective-permute-done.35 = bf16[1152,128]{1,0:T(8,128)(2,1)S(1)} collective-permute-done((bf16[1152,128]{1,0:T(8,128)(2,1)S(1)}, bf16[1152,128]{1,0:T(8,128)(2,1)S(1)}, u32[]{:S(2)}, u32[]{:S(2)}) %collective-permute-start.35) | collective-permute-done | bytes 294944 | tf_op jit(solution)/shard_map/ppermute | solution.py:29
  109.5 3.4 %collective-permute-start.37 = (bf16[640,128]{1,0:T(8,128)(2,1)S(1)}, bf16[640,128]{1,0:T(8,128)(2,1)S(1)}, u32[]{:S(2)}, u32[]{:S(2)}) collective-permute-start(bf16[640,128]{1,0:T(8,128)(2,1)S(1)} %pad_maximum_fusion.12), channel_id=1, source_target_pairs={{0,192},{16,208},{32,224},{48,240},{64,0},{80,16},{96,32},{112,48}... | collective-permute-start | bytes 491528 | tf_op jit(solution)/shard_map/ppermute | solution.py:29
  115.1 2.2 %collective-permute-done.34.r1 = bf16[640,128]{1,0:T(8,128)(2,1)S(1)} collective-permute-done((bf16[640,128]{1,0:T(8,128)(2,1)S(1)}, bf16[640,128]{1,0:T(8,128)(2,1)S(1)}, u32[]{:S(2)}, u32[]{:S(2)}) %collective-permute-start.34) | collective-permute-done | bytes 163872 | tf_op jit(solution)/shard_map/ppermute | solution.py:29
  117.3 1.8 %collective-permute-done.36.r2 = bf16[768,128]{1,0:T(8,128)(2,1)S(1)} collective-permute-done((bf16[768,128]{1,0:T(8,128)(2,1)S(1)}, bf16[768,128]{1,0:T(8,128)(2,1)S(1)}, u32[]{:S(2)}, u32[]{:S(2)}) %collective-permute-start.36) | collective-permute-done | bytes 196640 | tf_op jit(solution)/shard_map/ppermute | solution.py:29
  119.2 2.5 %collective-permute-start.38 = (f32[128,128]{1,0:T(8,128)S(1)}, f32[128,128]{1,0:T(8,128)S(1)}, u32[]{:S(2)}, u32[]{:S(2)}) collective-permute-start(f32[128,128]{1,0:T(8,128)S(1)} %add_add_fusion), channel_id=1, source_target_pairs={{0,16},{16,0},{32,48},{48,32},{64,80},{80,64},{96,112},{112,96},{1... | collective-permute-start | bytes 196616 | tf_op jit(solution)/shard_map/ppermute | solution.py:29
  (100 shorter events, 31.9 us)
Async XLA Ops:
  0.6 6.2 %collective-permute-start = (bf16[512,128]{1,0:T(8,128)(2,1)}, bf16[512,128]{1,0:T(8,128)(2,1)S(1)}, u32[]{:S(2)}, u32[]{:S(2)}) collective-permute-start(bf16[512,128]{1,0:T(8,128)(2,1)} %x_ref.1), channel_id=1, source_target_pairs={{0,64},{16,80},{32,96},{48,112},{64,128},{80,144},{96,160},{112,17... | collective-permute-start | bytes 393224 | tf_op jit(solution)/shard_map/ppermute | solution.py:29
  6.9 8.8 %collective-permute-start.4 = (bf16[1024,128]{1,0:T(8,128)(2,1)S(1)}, bf16[1024,128]{1,0:T(8,128)(2,1)S(1)}, u32[]{:S(2)}, u32[]{:S(2)}) collective-permute-start(bf16[1024,128]{1,0:T(8,128)(2,1)S(1)} %pad_maximum_fusion.7), channel_id=1, source_target_pairs={{0,32},{16,48},{32,0},{48,16},{64,96},{80,112},{96,64},{112,80},{1... | collective-permute-start | bytes 786440 | tf_op jit(solution)/shard_map/ppermute | solution.py:29
  8.8 6.8 %collective-permute-start.3 = (bf16[1024,128]{1,0:T(8,128)(2,1)S(1)}, bf16[1024,128]{1,0:T(8,128)(2,1)S(1)}, u32[]{:S(2)}, u32[]{:S(2)}) collective-permute-start(bf16[1024,128]{1,0:T(8,128)(2,1)S(1)} %pad_maximum_fusion.6), channel_id=1, source_target_pairs={{0,128},{16,144},{32,160},{48,176},{64,192},{80,208},{96,224},{112... | collective-permute-start | bytes 786440 | tf_op jit(solution)/shard_map/ppermute | solution.py:29
  11.3 11.3 %collective-permute-start.5 = (bf16[2048,128]{1,0:T(8,128)(2,1)S(1)}, bf16[2048,128]{1,0:T(8,128)(2,1)S(1)}, u32[]{:S(2)}, u32[]{:S(2)}) collective-permute-start(bf16[2048,128]{1,0:T(8,128)(2,1)S(1)} %constant_dynamic-update-slice_fusion.refs_5_), channel_id=1, source_target_pairs={{0,16},{16,0},{32,48},{48,32},{64,80},{80,64},{96,112},{112,96},{1... | collective-permute-start | bytes 1572872 | tf_op jit(solution)/shard_map/ppermute | solution.py:29
  15.7 7.8 %collective-permute-start.6 = (bf16[2048,128]{1,0:T(8,128)(2,1)S(1)}, bf16[2048,128]{1,0:T(8,128)(2,1)}, u32[]{:S(2)}, u32[]{:S(2)}) collective-permute-start(bf16[2048,128]{1,0:T(8,128)(2,1)S(1)} %constant_dynamic-update-slice_fusion.4.refs_6_), channel_id=1, source_target_pairs={{0,16},{16,0},{32,48},{48,32},{64,80},{80,64},{96,112},{112,96},{1... | collective-permute-start | bytes 1572872 | tf_op jit(solution)/shard_map/ppermute | solution.py:29
  25.8 7.2 %collective-permute-start.12 = (bf16[512,128]{1,0:T(8,128)(2,1)S(1)}, bf16[512,128]{1,0:T(8,128)(2,1)S(1)}, u32[]{:S(2)}, u32[]{:S(2)}) collective-permute-start(bf16[512,128]{1,0:T(8,128)(2,1)S(1)} %get-tuple-element.40), channel_id=1, source_target_pairs={{0,1},{1,2},{2,3},{3,4},{4,5},{5,6},{6,7},{7,0},{8,9},{9,10},{10,1... | collective-permute-start | bytes 393224 | tf_op jit(solution)/shard_map/ppermute | solution.py:37
  25.9 7.2 %collective-permute-start.13 = (bf16[512,128]{1,0:T(8,128)(2,1)S(1)}, bf16[512,128]{1,0:T(8,128)(2,1)S(1)}, u32[]{:S(2)}, u32[]{:S(2)}) collective-permute-start(bf16[512,128]{1,0:T(8,128)(2,1)S(1)} %get-tuple-element.42), channel_id=1, source_target_pairs={{0,7},{1,0},{2,1},{3,2},{4,3},{5,4},{6,5},{7,6},{8,15},{9,8},{10,9... | collective-permute-start | bytes 393224 | tf_op jit(solution)/shard_map/ppermute | solution.py:37
  29.5 5.9 %collective-permute-start.15 = (bf16[512,128]{1,0:T(8,128)(2,1)S(1)}, bf16[512,128]{1,0:T(8,128)(2,1)S(1)}, u32[]{:S(2)}, u32[]{:S(2)}) collective-permute-start(bf16[512,128]{1,0:T(8,128)(2,1)S(1)} %get-tuple-element.44), channel_id=1, source_target_pairs={{0,8},{1,9},{2,10},{3,11},{4,12},{5,13},{6,14},{7,15},{8,0},{9,1},... | collective-permute-start | bytes 393224 | tf_op jit(solution)/shard_map/ppermute | solution.py:37
  31.5 13.6 %collective-permute-start.9 = (bf16[1024,128]{1,0:T(8,128)(2,1)S(1)}, bf16[1024,128]{1,0:T(8,128)(2,1)S(1)}, u32[]{:S(2)}, u32[]{:S(2)}) collective-permute-start(bf16[1024,128]{1,0:T(8,128)(2,1)S(1)} %get-tuple-element.36), channel_id=1, source_target_pairs={{0,7},{1,0},{2,1},{3,2},{4,3},{5,4},{6,5},{7,6},{8,15},{9,8},{10,9... | collective-permute-start | bytes 786440 | tf_op jit(solution)/shard_map/ppermute | solution.py:37
  32.8 12.2 %collective-permute-start.10 = (bf16[1024,128]{1,0:T(8,128)(2,1)S(1)}, bf16[1024,128]{1,0:T(8,128)(2,1)S(1)}, u32[]{:S(2)}, u32[]{:S(2)}) collective-permute-start(bf16[1024,128]{1,0:T(8,128)(2,1)S(1)} %get-tuple-element.37), channel_id=1, source_target_pairs={{0,1},{1,2},{2,3},{3,4},{4,5},{5,6},{6,7},{7,0},{8,9},{9,10},{10,1... | collective-permute-start | bytes 786440 | tf_op jit(solution)/shard_map/ppermute | solution.py:37
  33.1 11.9 %collective-permute-start.14 = (bf16[1024,128]{1,0:T(8,128)(2,1)S(1)}, bf16[1024,128]{1,0:T(8,128)(2,1)S(1)}, u32[]{:S(2)}, u32[]{:S(2)}) collective-permute-start(bf16[1024,128]{1,0:T(8,128)(2,1)S(1)} %pad_maximum_fusion.8), channel_id=1, source_target_pairs={{0,8},{1,9},{2,10},{3,11},{4,12},{5,13},{6,14},{7,15},{8,0},{9,1},... | collective-permute-start | bytes 786440 | tf_op jit(solution)/shard_map/ppermute | solution.py:37
  37.5 5.5 %collective-permute-start.16 = (bf16[256,128]{1,0:T(8,128)(2,1)S(1)}, bf16[256,128]{1,0:T(8,128)(2,1)S(1)}, u32[]{:S(2)}, u32[]{:S(2)}) collective-permute-start(bf16[256,128]{1,0:T(8,128)(2,1)S(1)} %get-tuple-element.71), channel_id=1, source_target_pairs={{0,2},{1,3},{2,4},{3,5},{4,6},{5,7},{6,0},{7,1},{8,10},{9,11},{10,... | collective-permute-start | bytes 196616 | tf_op jit(solution)/shard_map/ppermute | solution.py:37
  39.9 9.5 %collective-permute-start.7 = (bf16[512,128]{1,0:T(8,128)(2,1)S(1)}, bf16[512,128]{1,0:T(8,128)(2,1)S(1)}, u32[]{:S(2)}, u32[]{:S(2)}) collective-permute-start(bf16[512,128]{1,0:T(8,128)(2,1)S(1)} %get-tuple-element.33), channel_id=1, source_target_pairs={{0,1},{1,2},{2,3},{3,4},{4,5},{5,6},{6,7},{7,0},{8,9},{9,10},{10,1... | collective-permute-start | bytes 393224 | tf_op jit(solution)/shard_map/ppermute | solution.py:37
  43.0 6.3 %collective-permute-start.8 = (bf16[512,128]{1,0:T(8,128)(2,1)S(1)}, bf16[512,128]{1,0:T(8,128)(2,1)S(1)}, u32[]{:S(2)}, u32[]{:S(2)}) collective-permute-start(bf16[512,128]{1,0:T(8,128)(2,1)S(1)} %get-tuple-element.34), channel_id=1, source_target_pairs={{0,7},{1,0},{2,1},{3,2},{4,3},{5,4},{6,5},{7,6},{8,15},{9,8},{10,9... | collective-permute-start | bytes 393224 | tf_op jit(solution)/shard_map/ppermute | solution.py:37
  45.2 6.2 %collective-permute-start.19 = (bf16[512,128]{1,0:T(8,128)(2,1)S(1)}, bf16[512,128]{1,0:T(8,128)(2,1)S(1)}, u32[]{:S(2)}, u32[]{:S(2)}) collective-permute-start(bf16[512,128]{1,0:T(8,128)(2,1)S(1)} %get-tuple-element.65), channel_id=1, source_target_pairs={{0,6},{1,7},{2,0},{3,1},{4,2},{5,3},{6,4},{7,5},{8,14},{9,15},{10,... | collective-permute-start | bytes 393224 | tf_op jit(solution)/shard_map/ppermute | solution.py:37
  48.1 5.3 %collective-permute-start.11 = (bf16[512,128]{1,0:T(8,128)(2,1)S(1)}, bf16[512,128]{1,0:T(8,128)(2,1)S(1)}, u32[]{:S(2)}, u32[]{:S(2)}) collective-permute-start(bf16[512,128]{1,0:T(8,128)(2,1)S(1)} %get-tuple-element.66), channel_id=1, source_target_pairs={{0,8},{1,9},{2,10},{3,11},{4,12},{5,13},{6,14},{7,15},{8,0},{9,1},... | collective-permute-start | bytes 393224 | tf_op jit(solution)/shard_map/ppermute | solution.py:37
  48.6 6.3 %collective-permute-start.17 = (bf16[512,128]{1,0:T(8,128)(2,1)S(1)}, bf16[512,128]{1,0:T(8,128)(2,1)S(1)}, u32[]{:S(2)}, u32[]{:S(2)}) collective-permute-start(bf16[512,128]{1,0:T(8,128)(2,1)S(1)} %get-tuple-element.67), channel_id=1, source_target_pairs={{0,2},{1,3},{2,4},{3,5},{4,6},{5,7},{6,0},{7,1},{8,10},{9,11},{10,... | collective-permute-start | bytes 393224 | tf_op jit(solution)/shard_map/ppermute | solution.py:37
  56.4 6.4 %collective-permute-start.20 = (f32[128,128]{1,0:T(8,128)S(1)}, f32[128,128]{1,0:T(8,128)S(1)}, u32[]{:S(2)}, u32[]{:S(2)}) collective-permute-start(f32[128,128]{1,0:T(8,128)S(1)} %get-tuple-element.49), channel_id=1, source_target_pairs={{0,16},{16,0},{32,48},{48,32},{64,80},{80,64},{96,112},{112,96},{1... | collective-permute-start | bytes 196616 | tf_op jit(solution)/shard_map/ppermute | solution.py:29
  62.8 9.7 %collective-permute-start.23 = (bf16[640,128]{1,0:T(8,128)(2,1)S(1)}, bf16[640,128]{1,0:T(8,128)(2,1)S(1)}, u32[]{:S(2)}, u32[]{:S(2)}) collective-permute-start(bf16[640,128]{1,0:T(8,128)(2,1)S(1)} %pad_maximum_fusion.10.refs_5_), channel_id=1, source_target_pairs={{0,6},{1,7},{2,0},{3,1},{4,2},{5,3},{6,4},{7,5},{8,14},{9,15},{10,... | collective-permute-start | bytes 491528 | tf_op jit(solution)/shard_map/ppermute | solution.py:37
  63.2 11.6 %collective-permute-start.22 = (bf16[640,128]{1,0:T(8,128)(2,1)S(1)}, bf16[640,128]{1,0:T(8,128)(2,1)S(1)}, u32[]{:S(2)}, u32[]{:S(2)}) collective-permute-start(bf16[640,128]{1,0:T(8,128)(2,1)S(1)} %pad_maximum_fusion.10.refs_5_), channel_id=1, source_target_pairs={{0,2},{1,3},{2,4},{3,5},{4,6},{5,7},{6,0},{7,1},{8,10},{9,11},{10,... | collective-permute-start | bytes 491528 | tf_op jit(solution)/shard_map/ppermute | solution.py:37
  65.2 13.1 %collective-permute-start.21 = (bf16[640,128]{1,0:T(8,128)(2,1)S(1)}, bf16[640,128]{1,0:T(8,128)(2,1)S(1)}, u32[]{:S(2)}, u32[]{:S(2)}) collective-permute-start(bf16[640,128]{1,0:T(8,128)(2,1)S(1)} %pad_maximum_fusion.10.refs_5_), channel_id=1, source_target_pairs={{0,8},{1,9},{2,10},{3,11},{4,12},{5,13},{6,14},{7,15},{8,0},{9,1},... | collective-permute-start | bytes 491528 | tf_op jit(solution)/shard_map/ppermute | solution.py:37
  74.8 5.1 %collective-permute-start.25 = (bf16[640,128]{1,0:T(8,128)(2,1)S(1)}, bf16[640,128]{1,0:T(8,128)(2,1)S(1)}, u32[]{:S(2)}, u32[]{:S(2)}) collective-permute-start(bf16[640,128]{1,0:T(8,128)(2,1)S(1)} %broadcast_select_fusion), channel_id=1, source_target_pairs={{0,2},{1,3},{2,4},{3,5},{4,6},{5,7},{6,0},{7,1},{8,10},{9,11},{10,... | collective-permute-start | bytes 491528 | tf_op jit(solution)/shard_map/ppermute | solution.py:47
  77.0 11.1 %collective-permute-start.24 = (bf16[1280,128]{1,0:T(8,128)(2,1)S(1)}, bf16[1280,128]{1,0:T(8,128)(2,1)S(1)}, u32[]{:S(2)}, u32[]{:S(2)}) collective-permute-start(bf16[1280,128]{1,0:T(8,128)(2,1)S(1)} %pad_maximum_fusion.5), channel_id=1, source_target_pairs={{0,8},{1,9},{2,10},{3,11},{4,12},{5,13},{6,14},{7,15},{8,0},{9,1},... | collective-permute-start | bytes 983048 | tf_op jit(solution)/shard_map/ppermute | solution.py:37
  78.4 17.4 %collective-permute-start.27 = (bf16[1920,128]{1,0:T(8,128)(2,1)S(1)}, bf16[1920,128]{1,0:T(8,128)(2,1)S(1)}, u32[]{:S(2)}, u32[]{:S(2)}) collective-permute-start(bf16[1920,128]{1,0:T(8,128)(2,1)S(1)} %get-tuple-element.61), channel_id=1, source_target_pairs={{0,7},{1,0},{2,1},{3,2},{4,3},{5,4},{6,5},{7,6},{8,15},{9,8},{10,9... | collective-permute-start | bytes 1474568 | tf_op jit(solution)/shard_map/ppermute | solution.py:37
  78.5 17.3 %collective-permute-start.26 = (bf16[1920,128]{1,0:T(8,128)(2,1)S(1)}, bf16[1920,128]{1,0:T(8,128)(2,1)S(1)}, u32[]{:S(2)}, u32[]{:S(2)}) collective-permute-start(bf16[1920,128]{1,0:T(8,128)(2,1)S(1)} %get-tuple-element.62), channel_id=1, source_target_pairs={{0,1},{1,2},{2,3},{3,4},{4,5},{5,6},{6,7},{7,0},{8,9},{9,10},{10,1... | collective-permute-start | bytes 1474568 | tf_op jit(solution)/shard_map/ppermute | solution.py:37
  80.0 11.2 %collective-permute-start.30 = (bf16[640,128]{1,0:T(8,128)(2,1)S(1)}, bf16[640,128]{1,0:T(8,128)(2,1)S(1)}, u32[]{:S(2)}, u32[]{:S(2)}) collective-permute-start(bf16[640,128]{1,0:T(8,128)(2,1)S(1)} %collective-permute-done.25.refs_10_), channel_id=1, source_target_pairs={{0,8},{1,9},{2,10},{3,11},{4,12},{5,13},{6,14},{7,15},{8,0},{9,1},... | collective-permute-start | bytes 491528 | tf_op jit(solution)/shard_map/ppermute | solution.py:37
  88.2 6.4 %collective-permute-start.29 = (bf16[640,128]{1,0:T(8,128)(2,1)S(1)}, bf16[640,128]{1,0:T(8,128)(2,1)S(1)}, u32[]{:S(2)}, u32[]{:S(2)}) collective-permute-start(bf16[640,128]{1,0:T(8,128)(2,1)S(1)} %get-tuple-element.59), channel_id=1, source_target_pairs={{0,7},{1,0},{2,1},{3,2},{4,3},{5,4},{6,5},{7,6},{8,15},{9,8},{10,9... | collective-permute-start | bytes 491528 | tf_op jit(solution)/shard_map/ppermute | solution.py:37
  88.3 7.6 %collective-permute-start.28 = (bf16[640,128]{1,0:T(8,128)(2,1)S(1)}, bf16[640,128]{1,0:T(8,128)(2,1)S(1)}, u32[]{:S(2)}, u32[]{:S(2)}) collective-permute-start(bf16[640,128]{1,0:T(8,128)(2,1)S(1)} %get-tuple-element.60), channel_id=1, source_target_pairs={{0,1},{1,2},{2,3},{3,4},{4,5},{5,6},{6,7},{7,0},{8,9},{9,10},{10,1... | collective-permute-start | bytes 491528 | tf_op jit(solution)/shard_map/ppermute | solution.py:37
  101.1 8.3 %collective-permute-start.35 = (bf16[1152,128]{1,0:T(8,128)(2,1)S(1)}, bf16[1152,128]{1,0:T(8,128)(2,1)S(1)}, u32[]{:S(2)}, u32[]{:S(2)}) collective-permute-start(bf16[1152,128]{1,0:T(8,128)(2,1)S(1)} %get-tuple-element.72), channel_id=1, source_target_pairs={{0,32},{16,48},{32,0},{48,16},{64,96},{80,112},{96,64},{112,80},{1... | collective-permute-start | bytes 884744 | tf_op jit(solution)/shard_map/ppermute | solution.py:29
  102.4 10.4 %collective-permute-start.33 = (bf16[1152,128]{1,0:T(8,128)(2,1)S(1)}, bf16[1152,128]{1,0:T(8,128)(2,1)S(1)}, u32[]{:S(2)}, u32[]{:S(2)}) collective-permute-start(bf16[1152,128]{1,0:T(8,128)(2,1)S(1)} %get-tuple-element.73), channel_id=1, source_target_pairs={{0,128},{16,144},{32,160},{48,176},{64,192},{80,208},{96,224},{112... | collective-permute-start | bytes 884744 | tf_op jit(solution)/shard_map/ppermute | solution.py:29
  109.5 5.6 %collective-permute-start.37 = (bf16[640,128]{1,0:T(8,128)(2,1)S(1)}, bf16[640,128]{1,0:T(8,128)(2,1)S(1)}, u32[]{:S(2)}, u32[]{:S(2)}) collective-permute-start(bf16[640,128]{1,0:T(8,128)(2,1)S(1)} %pad_maximum_fusion.12), channel_id=1, source_target_pairs={{0,192},{16,208},{32,224},{48,240},{64,0},{80,16},{96,32},{112,48}... | collective-permute-start | bytes 491528 | tf_op jit(solution)/shard_map/ppermute | solution.py:29
  112.9 6.2 %collective-permute-start.36 = (bf16[768,128]{1,0:T(8,128)(2,1)S(1)}, bf16[768,128]{1,0:T(8,128)(2,1)S(1)}, u32[]{:S(2)}, u32[]{:S(2)}) collective-permute-start(bf16[768,128]{1,0:T(8,128)(2,1)S(1)} %pad_maximum_fusion.9), channel_id=1, source_target_pairs={{0,64},{16,80},{32,96},{48,112},{64,128},{80,144},{96,160},{112,17... | collective-permute-start | bytes 589832 | tf_op jit(solution)/shard_map/ppermute | solution.py:29
  (13 other events, 122.0 us)

commit v7 on v4

--- a/solution.py
+++ b/solution.py
@@ -14,6 +14,10 @@
 BLOCK = 128
 ROWS = SHARD + BLOCK
 VMEM_LIMIT = 24 * 1024 * 1024
+
+
+def tied(*arrays):
+    return lax.optimization_barrier(arrays)
 
 
 def send_row(x, dy=0, dx=0, dc=0):
@@ -161,6 +165,20 @@
         out_ref[at, :] = total[at, :].T.astype(BF16)
 
 
+def join_kernel(a_ref, b_ref, c_ref, d_ref, out_ref):
+    out_ref[:SHARD, :] = (a_ref[...] + b_ref[...].astype(F32)).astype(BF16)
+    out_ref[SHARD:, :] = (c_ref[...] + d_ref[...].astype(F32)).astype(BF16)
+
+
+def carry_kernel(core_ref, up_ref, down_ref, e_ref, g_ref, q_ref, h_ref, out_up, out_down):
+    first = core_ref[0] == 0
+    extra = h_ref[...].astype(F32)
+    up = up_ref[...] + g_ref[SHARD:2 * SHARD, :].astype(F32) + q_ref[:SHARD, :].astype(F32)
+    down = down_ref[...] + e_ref[SHARD:2 * SHARD, :].astype(F32) + q_ref[SHARD:, :].astype(F32)
+    out_up[...] = (up + jnp.where(first, 0.0, extra)).astype(BF16)
+    out_down[...] = (down + jnp.where(first, extra, 0.0)).astype(BF16)
+
+
 def add(*terms):
     return functools.reduce(lambda a, b: a + b, [t.astype(F32) for t in terms])
 
@@ -182,10 +200,11 @@
     a = send_row(features, dx=1)
     u = send_row(features, dy=1)
     d = send_row(features, dy=-1)
-    ud = jnp.concatenate([u, d])
     near = pl.pallas_call(
         copy_kernel, out_shape=jax.ShapeDtypeStruct((S, BLOCK), BF16), compiler_params=params
     )(features)
+    near, u, d = tied(near, u, d)
+    ud = jnp.concatenate([u, d])
     xa = jnp.concatenate([near, a])
     w = send_row(xa, dy=2)
     v = send_row(ud, dx=1)
@@ -200,7 +219,7 @@
 
     O = lambda k: (k % 8 * S, S)
     X = lambda k: ((8 + k % 8) * S, S)
-    outs = [[X(-1), X(-3)], [X(1), X(3)], [X(4)], [O(-1), O(-3)], [O(1), O(3)],
+    outs = [[X(-3)], [X(3)], [X(4)], [O(-1), O(-3), X(-1)], [O(1), O(3), X(1)],
             [X(-2)], [X(2)], [O(4)], [X(0)], [O(2)], [O(-2)], [O(0)]]
     m, n, l, e, g, x6, x2, o4, x0, o2, o6, o0 = tile_sums(
         col_at, row_at, count, scan, values, [h1, h2, c1, c2], places, outs,
@@ -211,14 +230,21 @@
     l = send_col(l, dh=1)
     e = send_col(e, dz=-1)
     g = send_col(g, dz=1)
-    q = jnp.concatenate([add(x2, n[S:]).astype(BF16), add(x6, m[S:]).astype(BF16)])
+    q = pl.pallas_call(
+        join_kernel, out_shape=jax.ShapeDtypeStruct((2 * S, BLOCK), BF16), compiler_params=params
+    )(x2, n, x6, m)
     q = send_col(q, dh=1)
-    h = send_apart(add(o4, l).astype(BF16), -2).astype(F32)
-    rx = send_col(add(x0, m[:S], n[:S]).astype(BF16), dh=1)
-    o2 = add(o2, g[S:], q[:S], jnp.where(core == 0, 0.0, h)).astype(BF16)
-    o6 = add(o6, e[S:], q[S:], jnp.where(core == 0, h, 0.0)).astype(BF16)
+    h = send_apart(add(o4, l).astype(BF16), -2)
+    rx = send_col(add(x0, e[2 * S:], g[2 * S:]).astype(BF16), dh=1)
+    o2, o6 = pl.pallas_call(
+        carry_kernel,
+        out_shape=[jax.ShapeDtypeStruct((S, BLOCK), BF16)] * 2,
+        in_specs=[pl.BlockSpec(memory_space=pltpu.SMEM)] + [pl.BlockSpec(memory_space=pltpu.VMEM)] * 6,
+        compiler_params=params,
+    )(core[None], o2, o6, e, g, q, h)
     s2 = send_col(o2, dz=2)
     s6 = send_col(o6, dz=-2)
+    fin = (o0, e, g, rx, s2, s6)
 
     half = jax.ShapeDtypeStruct((BLOCK, BLOCK), F32)
     activation, gt, keep, give = pl.pallas_call(
@@ -232,24 +258,27 @@
         in_specs=[pl.BlockSpec(memory_space=pltpu.SMEM)] + [pl.BlockSpec(memory_space=pltpu.VMEM)] * 8,
         scratch_shapes=[pltpu.VMEM((BLOCK, 256), F32)],
         compiler_params=params,
-    )(core[None], o0, e, g, rx, s2, s6, weight, grad_out)
+    )(core[None], *fin, weight, grad_out)
     share = keep + send_row(give, dc=1)
     gt = jnp.concatenate([gt, share.astype(BF16)])
 
     u2 = send_col(gt, dz=2)
     d2 = send_col(gt, dz=-2)
     a = send_col(gt, dh=1)
+    u = send_col(gt, dz=1)
+    d = send_col(gt, dz=-1)
     q = send_col(jnp.concatenate([u2, d2]), dh=1)
     f4 = send_apart(jnp.where(core == 0, u2, d2), 2)
-    e = send_col(jnp.concatenate([gt, u2]), dz=1)
-    g = send_col(jnp.concatenate([gt, d2]), dz=-1)
-    m = send_col(jnp.concatenate([a, q[:ROWS]]), dz=1)
-    n = send_col(jnp.concatenate([a, q[ROWS:]]), dz=-1)
+    e = send_col(jnp.concatenate([u2, a]), dz=1)
+    g = send_col(jnp.concatenate([d2, a]), dz=-1)
+    u, d, q = tied(u, d, q)
+    m = send_col(q[:ROWS], dz=1)
+    n = send_col(q[ROWS:], dz=-1)
     l = send_col(f4, dh=1)
-    panels = [gt, a, u2, d2, q, f4, e, g, m, n, l]
+    panels = [gt, a, u, d, u2, d2, q, f4, e, g, m, n, l]
     both = lambda *slots: [p for f, r in slots for p in ((f, r), (16 * S + f // 4, BLOCK))]
-    places = [both(O(0)), both(X(0)), both(O(-2)), both(O(2)), both(X(-2), X(2)), both(O(4)),
-              both(O(-1), O(-3)), both(O(1), O(3)), both(X(-1), X(-3)), both(X(1), X(3)), both(X(4))]
+    places = [both(O(0)), both(X(0)), both(O(-1)), both(O(1)), both(O(-2)), both(O(2)), both(X(-2), X(2)),
+              both(O(4)), both(O(-3), X(-1)), both(O(3), X(1)), both(X(-3)), both(X(3)), both(X(4))]
 
     k = lambda dy, dx: ((dx * 4 + dy % 4) * S, S)
     last = [k(0, 0), k(0, 1), k(1, 0), k(-1, 0)]
@@ -262,6 +291,7 @@
     own = add(own, send_row(away, dc=1))
     w = send_row(jnp.concatenate([own1[2 * S:], share]), dy=2)
     v = send_row(jnp.concatenate([own1[:2 * S], share]), dx=1)
+
     o = add(own[S:2 * S], w[S:2 * S]).astype(BF16)
     ud = add(own[2 * S:4 * S], v[:2 * S]).astype(BF16)
     here = rounded(add(share, w[2 * S:]))

time: 134 us -> 123 us (0.918)
  waiting for transfers between devices: 55.1 us -> 49.4 us
  starting transfers between devices: 64.8 us -> 62.5 us
  other arithmetic: 3.53 us -> 1.52 us
    ppermute x18 -> x20, starting transfers between devices: 32.3 us -> 24.8 us  [send_col(): return lax.ppermute(x, 'col', perm)]
    ppermute x18 -> x20, waiting for transfers between devices: 28 us -> 22.9 us  [send_col(): return lax.ppermute(x, 'col', perm)]
    ppermute x16, starting transfers between devices: 30.2 us -> 34.7 us  [send_row(): return lax.ppermute(x, 'row', perm)]
    ppermute x16, waiting for transfers between devices: 20 us -> 16.3 us  [send_row(): return lax.ppermute(x, 'row', perm)]
    ppermute x2, waiting for transfers between devices: 7.18 us -> 10.2 us  [send_apart(): return lax.ppermute(x, ('row', 'col'), perm)]
    convert_element_type x3 -> x2, other arithmetic: 2.06 us -> 0.08 us  [the longest x1 0.05 us: body(): rx = send_col(add(x0, e[2 * S:], g[2 * S:]).astype(BF16), dh=1)]
  transfers between devices with their start and end apart: 36 -> 38, of which waited for: 21 -> 24; matrix products, arithmetic and copies ran while one was open for 2% -> 1% of each run, Pallas kernels for 1% -> 1%
where the time goes in v7:
time: 123 us
  starting transfers between devices  62.5 us (51%)
  waiting for transfers between devices  49.4 us (40%)
  Pallas kernels  7.01 us (6%)
  between operations  1.62 us (1%)
  other arithmetic  1.52 us (1%)
    ppermute x16, starting transfers between devices, send_row(): return lax.ppermute(x, 'row', perm)  34.7 us
    ppermute x20, starting transfers between devices, send_col(): return lax.ppermute(x, 'col', perm)  24.8 us
    ppermute x20, waiting for transfers between devices, send_col(): return lax.ppermute(x, 'col', perm)  22.9 us
    ppermute x16, waiting for transfers between devices, send_row(): return lax.ppermute(x, 'row', perm)  16.3 us
    ppermute x2, waiting for transfers between devices, send_apart(): return lax.ppermute(x, ('row', 'col'), perm)  10.2 us
    pallas_call x2, Pallas kernels, tile_sums(): pl.pallas_call(functools.partial(tile_kernel, places, outs, left), out_sh...  4.61 us
    ppermute x2, starting transfers between devices, send_apart(): return lax.ppermute(x, ('row', 'col'), perm)  2.96 us
  transfers between devices with their start and end apart: 38, of which 24 were waited for; matrix products, arithmetic and copies ran while one was open for 1% of the time, Pallas kernels for 1%

profile of v7, /device:TPU:1, one launch (start us, length us, event | category | flops | bytes accessed | tf_op | source)
XLA Modules:
  0.0 123.2 jit_solution(8607790111537331820)
XLA Ops:
  0.6 2.2 %collective-permute-start = (bf16[512,128]{1,0:T(8,128)(2,1)}, bf16[512,128]{1,0:T(8,128)(2,1)S(1)}, u32[]{:S(2)}, u32[]{:S(2)}) collective-permute-start(bf16[512,128]{1,0:T(8,128)(2,1)} %x_ref.1), channel_id=1, source_target_pairs={{0,64},{16,80},{32,96},{48,112},{64,128},{80,144},{96,160},{112,17... | collective-permute-start | bytes 393224 | tf_op jit(solution)/shard_map/ppermute | solution.py:29
  6.9 1.9 %collective-permute-start.4 = (bf16[1024,128]{1,0:T(8,128)(2,1)S(1)}, bf16[1024,128]{1,0:T(8,128)(2,1)S(1)}, u32[]{:S(2)}, u32[]{:S(2)}) collective-permute-start(bf16[1024,128]{1,0:T(8,128)(2,1)S(1)} %pad_maximum_fusion.6), channel_id=1, source_target_pairs={{0,32},{16,48},{32,0},{48,16},{64,96},{80,112},{96,64},{112,80},{1... | collective-permute-start | bytes 786440 | tf_op jit(solution)/shard_map/ppermute | solution.py:29
  8.8 2.4 %collective-permute-start.3 = (bf16[1024,128]{1,0:T(8,128)(2,1)S(1)}, bf16[1024,128]{1,0:T(8,128)(2,1)S(1)}, u32[]{:S(2)}, u32[]{:S(2)}) collective-permute-start(bf16[1024,128]{1,0:T(8,128)(2,1)S(1)} %pad_maximum_fusion.5), channel_id=1, source_target_pairs={{0,128},{16,144},{32,160},{48,176},{64,192},{80,208},{96,224},{112... | collective-permute-start | bytes 786440 | tf_op jit(solution)/shard_map/ppermute | solution.py:29
  11.3 2.7 %collective-permute-start.5 = (bf16[2048,128]{1,0:T(8,128)(2,1)S(1)}, bf16[2048,128]{1,0:T(8,128)(2,1)S(1)}, u32[]{:S(2)}, u32[]{:S(2)}) collective-permute-start(bf16[2048,128]{1,0:T(8,128)(2,1)S(1)} %constant_dynamic-update-slice_fusion.refs_5_), channel_id=1, source_target_pairs={{0,16},{16,0},{32,48},{48,32},{64,80},{80,64},{96,112},{112,96},{1... | collective-permute-start | bytes 1572872 | tf_op jit(solution)/shard_map/ppermute | solution.py:29
  14.0 1.7 %collective-permute-done.3 = bf16[1024,128]{1,0:T(8,128)(2,1)S(1)} collective-permute-done((bf16[1024,128]{1,0:T(8,128)(2,1)S(1)}, bf16[1024,128]{1,0:T(8,128)(2,1)S(1)}, u32[]{:S(2)}, u32[]{:S(2)}) %collective-permute-start.3) | collective-permute-done | bytes 262176 | tf_op jit(solution)/shard_map/ppermute | solution.py:29
  15.7 6.1 %collective-permute-start.6 = (bf16[2048,128]{1,0:T(8,128)(2,1)S(1)}, bf16[2048,128]{1,0:T(8,128)(2,1)}, u32[]{:S(2)}, u32[]{:S(2)}) collective-permute-start(bf16[2048,128]{1,0:T(8,128)(2,1)S(1)} %constant_dynamic-update-slice_fusion.4.refs_6_), channel_id=1, source_target_pairs={{0,16},{16,0},{32,48},{48,32},{64,80},{80,64},{96,112},{112,96},{1... | collective-permute-start | bytes 1572872 | tf_op jit(solution)/shard_map/ppermute | solution.py:29
  23.5 2.5 %shard_map.95 = (bf16[512,128]{1,0:T(8,128)(2,1)S(1)}, bf16[512,128]{1,0:T(8,128)(2,1)S(1)}, bf16[512,128]{1,0:T(8,128)(2,1)S(1)}, bf16[1536,128]{1,0:T(8,128)(2...) custom-call(s32[48]{0:T(128)S(1)} %get-tuple-element.76.refs_0_.refs, ...), custom_call_target="tpu_custom_call" | custom-call | tf_op jit(solution)/shard_map/pallas_call | solution.py:119
  26.1 3.4 %collective-permute-start.11 = (bf16[512,128]{1,0:T(8,128)(2,1)S(1)}, bf16[512,128]{1,0:T(8,128)(2,1)S(1)}, u32[]{:S(2)}, u32[]{:S(2)}) collective-permute-start(bf16[512,128]{1,0:T(8,128)(2,1)S(1)} %get-tuple-element.44), channel_id=1, source_target_pairs={{0,7},{1,0},{2,1},{3,2},{4,3},{5,4},{6,5},{7,6},{8,15},{9,8},{10,9... | collective-permute-start | bytes 393224 | tf_op jit(solution)/shard_map/ppermute | solution.py:37
  29.5 2.2 %collective-permute-start.13 = (bf16[512,128]{1,0:T(8,128)(2,1)S(1)}, bf16[512,128]{1,0:T(8,128)(2,1)S(1)}, u32[]{:S(2)}, u32[]{:S(2)}) collective-permute-start(bf16[512,128]{1,0:T(8,128)(2,1)S(1)} %get-tuple-element.46), channel_id=1, source_target_pairs={{0,8},{1,9},{2,10},{3,11},{4,12},{5,13},{6,14},{7,15},{8,0},{9,1},... | collective-permute-start | bytes 393224 | tf_op jit(solution)/shard_map/ppermute | solution.py:37
  33.3 1.8 %collective-permute-start.12 = (bf16[1024,128]{1,0:T(8,128)(2,1)S(1)}, bf16[1024,128]{1,0:T(8,128)(2,1)S(1)}, u32[]{:S(2)}, u32[]{:S(2)}) collective-permute-start(bf16[1024,128]{1,0:T(8,128)(2,1)S(1)} %shard_map.96), channel_id=1, source_target_pairs={{0,8},{1,9},{2,10},{3,11},{4,12},{5,13},{6,14},{7,15},{8,0},{9,1},... | collective-permute-start | bytes 786440 | tf_op jit(solution)/shard_map/ppermute | solution.py:37
  35.4 2.0 %collective-permute-start.14 = (bf16[512,128]{1,0:T(8,128)(2,1)S(1)}, bf16[512,128]{1,0:T(8,128)(2,1)S(1)}, u32[]{:S(2)}, u32[]{:S(2)}) collective-permute-start(bf16[512,128]{1,0:T(8,128)(2,1)S(1)} %add_convert_fusion.1), channel_id=1, source_target_pairs={{0,6},{1,7},{2,0},{3,1},{4,2},{5,3},{6,4},{7,5},{8,14},{9,15},{10,... | collective-permute-start | bytes 393224 | tf_op jit(solution)/shard_map/ppermute | solution.py:47
  37.4 7.8 %collective-permute-done.14.h_ref = bf16[512,128]{1,0:T(8,128)(2,1)S(1)} collective-permute-done((bf16[512,128]{1,0:T(8,128)(2,1)S(1)}, bf16[512,128]{1,0:T(8,128)(2,1)S(1)}, u32[]{:S(2)}, u32[]{:S(2)}) %collective-permute-start.14) | collective-permute-done | bytes 131104 | tf_op jit(solution)/shard_map/ppermute | solution.py:47
  46.0 3.2 %collective-permute-start.16 = (bf16[512,128]{1,0:T(8,128)(2,1)S(1)}, bf16[512,128]{1,0:T(8,128)(2,1)S(1)}, u32[]{:S(2)}, u32[]{:S(2)}) collective-permute-start(bf16[512,128]{1,0:T(8,128)(2,1)S(1)} %get-tuple-element.48), channel_id=1, source_target_pairs={{0,6},{1,7},{2,0},{3,1},{4,2},{5,3},{6,4},{7,5},{8,14},{9,15},{10,... | collective-permute-start | bytes 393224 | tf_op jit(solution)/shard_map/ppermute | solution.py:37
  49.2 1.7 %collective-permute-start.9 = (bf16[512,128]{1,0:T(8,128)(2,1)S(1)}, bf16[512,128]{1,0:T(8,128)(2,1)S(1)}, u32[]{:S(2)}, u32[]{:S(2)}) collective-permute-start(bf16[512,128]{1,0:T(8,128)(2,1)S(1)} %add_convert_fusion.2), channel_id=1, source_target_pairs={{0,8},{1,9},{2,10},{3,11},{4,12},{5,13},{6,14},{7,15},{8,0},{9,1},... | collective-permute-start | bytes 393224 | tf_op jit(solution)/shard_map/ppermute | solution.py:37
  52.1 2.7 %collective-permute-done.9.r3 = bf16[512,128]{1,0:T(8,128)(2,1)S(1)} collective-permute-done((bf16[512,128]{1,0:T(8,128)(2,1)S(1)}, bf16[512,128]{1,0:T(8,128)(2,1)S(1)}, u32[]{:S(2)}, u32[]{:S(2)}) %collective-permute-start.9) | collective-permute-done | bytes 131104 | tf_op jit(solution)/shard_map/ppermute | solution.py:37
  56.3 4.7 %collective-permute-start.17 = (f32[128,128]{1,0:T(8,128)S(1)}, f32[128,128]{1,0:T(8,128)S(1)}, u32[]{:S(2)}, u32[]{:S(2)}) collective-permute-start(f32[128,128]{1,0:T(8,128)S(1)} %get-tuple-element.52), channel_id=1, source_target_pairs={{0,16},{16,0},{32,48},{48,32},{64,80},{80,64},{96,112},{112,96},{1... | collective-permute-start | bytes 196616 | tf_op jit(solution)/shard_map/ppermute | solution.py:29
  65.7 6.4 %collective-permute-done.22.refs_10_ = bf16[640,128]{1,0:T(8,128)(2,1)S(1)} collective-permute-done((bf16[640,128]{1,0:T(8,128)(2,1)S(1)}, bf16[640,128]{1,0:T(8,128)(2,1)S(1)}, u32[]{:S(2)}, u32[]{:S(2)}) %collective-permute-start.22) | collective-permute-done | bytes 163872 | tf_op jit(solution)/shard_map/ppermute | solution.py:37
  72.2 2.4 %collective-permute-done.21.refs_9_ = bf16[640,128]{1,0:T(8,128)(2,1)S(1)} collective-permute-done((bf16[640,128]{1,0:T(8,128)(2,1)S(1)}, bf16[640,128]{1,0:T(8,128)(2,1)S(1)}, u32[]{:S(2)}, u32[]{:S(2)}) %collective-permute-start.21) | collective-permute-done | bytes 163872 | tf_op jit(solution)/shard_map/ppermute | solution.py:37
  76.0 2.5 %collective-permute-start.26 = (bf16[1280,128]{1,0:T(8,128)(2,1)S(1)}, bf16[1280,128]{1,0:T(8,128)(2,1)S(1)}, u32[]{:S(2)}, u32[]{:S(2)}) collective-permute-start(bf16[1280,128]{1,0:T(8,128)(2,1)S(1)} %get-tuple-element.69), channel_id=1, source_target_pairs={{0,7},{1,0},{2,1},{3,2},{4,3},{5,4},{6,5},{7,6},{8,15},{9,8},{10,9... | collective-permute-start | bytes 983048 | tf_op jit(solution)/shard_map/ppermute | solution.py:37
  78.5 2.4 %collective-permute-done.24.refs_12_ = bf16[640,128]{1,0:T(8,128)(2,1)S(1)} collective-permute-done((bf16[640,128]{1,0:T(8,128)(2,1)S(1)}, bf16[640,128]{1,0:T(8,128)(2,1)S(1)}, u32[]{:S(2)}, u32[]{:S(2)}) %collective-permute-start.24) | collective-permute-done | bytes 163872 | tf_op jit(solution)/shard_map/ppermute | solution.py:47
  80.8 2.3 %collective-permute-start.29 = (bf16[640,128]{1,0:T(8,128)(2,1)S(1)}, bf16[640,128]{1,0:T(8,128)(2,1)S(1)}, u32[]{:S(2)}, u32[]{:S(2)}) collective-permute-start(bf16[640,128]{1,0:T(8,128)(2,1)S(1)} %collective-permute-done.24.refs_12_), channel_id=1, source_target_pairs={{0,8},{1,9},{2,10},{3,11},{4,12},{5,13},{6,14},{7,15},{8,0},{9,1},... | collective-permute-start | bytes 491528 | tf_op jit(solution)/shard_map/ppermute | solution.py:37
  87.0 4.7 %collective-permute-done.25.refs_13_ = bf16[1280,128]{1,0:T(8,128)(2,1)S(1)} collective-permute-done((bf16[1280,128]{1,0:T(8,128)(2,1)S(1)}, bf16[1280,128]{1,0:T(8,128)(2,1)S(1)}, u32[]{:S(2)}, u32[]{:S(2)}) %collective-permute-start.25) | collective-permute-done | bytes 327712 | tf_op jit(solution)/shard_map/ppermute | solution.py:37
  91.7 2.9 %collective-permute-done.27.refs_15_ = bf16[640,128]{1,0:T(8,128)(2,1)S(1)} collective-permute-done((bf16[640,128]{1,0:T(8,128)(2,1)S(1)}, bf16[640,128]{1,0:T(8,128)(2,1)S(1)}, u32[]{:S(2)}, u32[]{:S(2)}) %collective-permute-start.27) | collective-permute-done | bytes 163872 | tf_op jit(solution)/shard_map/ppermute | solution.py:37
  94.6 2.1 %shard_map.99 = (f32[2048,128]{1,0:T(8,128)S(1)}, bf16[2048,128]{1,0:T(8,128)(2,1)S(1)}, f32[2048,128]{1,0:T(8,128)S(1)}, bf16[2048,128]{1,0:T(8,128)(2,1)S(1)}, bf16[128,128]{1,0:T(8,128)(2,1)S(1)}) custom-call(s32[48]{0:T(128)S(1)} %get-tuple-element.77.refs_1_.refs_0_, s32[48]{0:T(128)S(1)} %get-tuple-element.76.refs_0_.refs_1_, s32[1]{0:T(128)} %bitcast.30.refs_2_, ...), custom_call_target="tpu_custom_call" | custom-call | tf_op jit(solution)/shard_map/pallas_call | solution.py:119
  96.7 3.2 %collective-permute-start.31 = (bf16[2048,128]{1,0:T(8,128)(2,1)S(1)}, bf16[2048,128]{1,0:T(8,128)(2,1)S(1)}, u32[]{:S(2)}, u32[]{:S(2)}) collective-permute-start(bf16[2048,128]{1,0:T(8,128)(2,1)S(1)} %get-tuple-element.59), channel_id=1, source_target_pairs={{0,16},{16,0},{32,48},{48,32},{64,80},{80,64},{96,112},{112,96},{1... | collective-permute-start | bytes 1572872 | tf_op jit(solution)/shard_map/ppermute | solution.py:29
  101.6 1.8 %collective-permute-start.34 = (bf16[1152,128]{1,0:T(8,128)(2,1)S(1)}, bf16[1152,128]{1,0:T(8,128)(2,1)S(1)}, u32[]{:S(2)}, u32[]{:S(2)}) collective-permute-start(bf16[1152,128]{1,0:T(8,128)(2,1)S(1)} %get-tuple-element.74), channel_id=1, source_target_pairs={{0,32},{16,48},{32,0},{48,16},{64,96},{80,112},{96,64},{112,80},{1... | collective-permute-start | bytes 884744 | tf_op jit(solution)/shard_map/ppermute | solution.py:29
  105.0 5.5 %collective-permute-done.34 = bf16[1152,128]{1,0:T(8,128)(2,1)S(1)} collective-permute-done((bf16[1152,128]{1,0:T(8,128)(2,1)S(1)}, bf16[1152,128]{1,0:T(8,128)(2,1)S(1)}, u32[]{:S(2)}, u32[]{:S(2)}) %collective-permute-start.34) | collective-permute-done | bytes 294944 | tf_op jit(solution)/shard_map/ppermute | solution.py:29
  110.6 1.6 %collective-permute-start.36 = (bf16[640,128]{1,0:T(8,128)(2,1)S(1)}, bf16[640,128]{1,0:T(8,128)(2,1)S(1)}, u32[]{:S(2)}, u32[]{:S(2)}) collective-permute-start(bf16[640,128]{1,0:T(8,128)(2,1)S(1)} %pad_maximum_fusion.10), channel_id=1, source_target_pairs={{0,192},{16,208},{32,224},{48,240},{64,0},{80,16},{96,32},{112,48}... | collective-permute-start | bytes 491528 | tf_op jit(solution)/shard_map/ppermute | solution.py:29
  114.0 1.6 %collective-permute-done.36.r3 = bf16[640,128]{1,0:T(8,128)(2,1)S(1)} collective-permute-done((bf16[640,128]{1,0:T(8,128)(2,1)S(1)}, bf16[640,128]{1,0:T(8,128)(2,1)S(1)}, u32[]{:S(2)}, u32[]{:S(2)}) %collective-permute-start.36) | collective-permute-done | bytes 163872 | tf_op jit(solution)/shard_map/ppermute | solution.py:29
  115.5 1.8 %collective-permute-done.33.r1 = bf16[640,128]{1,0:T(8,128)(2,1)S(1)} collective-permute-done((bf16[640,128]{1,0:T(8,128)(2,1)S(1)}, bf16[640,128]{1,0:T(8,128)(2,1)S(1)}, u32[]{:S(2)}, u32[]{:S(2)}) %collective-permute-start.33) | collective-permute-done | bytes 163872 | tf_op jit(solution)/shard_map/ppermute | solution.py:29
  117.3 1.7 %collective-permute-done.35.r2 = bf16[768,128]{1,0:T(8,128)(2,1)S(1)} collective-permute-done((bf16[768,128]{1,0:T(8,128)(2,1)S(1)}, bf16[768,128]{1,0:T(8,128)(2,1)S(1)}, u32[]{:S(2)}, u32[]{:S(2)}) %collective-permute-start.35) | collective-permute-done | bytes 196640 | tf_op jit(solution)/shard_map/ppermute | solution.py:29
  119.1 2.5 %collective-permute-start.37 = (f32[128,128]{1,0:T(8,128)S(1)}, f32[128,128]{1,0:T(8,128)S(1)}, u32[]{:S(2)}, u32[]{:S(2)}) collective-permute-start(f32[128,128]{1,0:T(8,128)S(1)} %add_add_fusion), channel_id=1, source_target_pairs={{0,16},{16,0},{32,48},{48,32},{64,80},{80,64},{96,112},{112,96},{1... | collective-permute-start | bytes 196616 | tf_op jit(solution)/shard_map/ppermute | solution.py:29
  (95 shorter events, 27.2 us)
Async XLA Ops:
  0.6 6.2 %collective-permute-start = (bf16[512,128]{1,0:T(8,128)(2,1)}, bf16[512,128]{1,0:T(8,128)(2,1)S(1)}, u32[]{:S(2)}, u32[]{:S(2)}) collective-permute-start(bf16[512,128]{1,0:T(8,128)(2,1)} %x_ref.1), channel_id=1, source_target_pairs={{0,64},{16,80},{32,96},{48,112},{64,128},{80,144},{96,160},{112,17... | collective-permute-start | bytes 393224 | tf_op jit(solution)/shard_map/ppermute | solution.py:29
  6.9 8.8 %collective-permute-start.4 = (bf16[1024,128]{1,0:T(8,128)(2,1)S(1)}, bf16[1024,128]{1,0:T(8,128)(2,1)S(1)}, u32[]{:S(2)}, u32[]{:S(2)}) collective-permute-start(bf16[1024,128]{1,0:T(8,128)(2,1)S(1)} %pad_maximum_fusion.6), channel_id=1, source_target_pairs={{0,32},{16,48},{32,0},{48,16},{64,96},{80,112},{96,64},{112,80},{1... | collective-permute-start | bytes 786440 | tf_op jit(solution)/shard_map/ppermute | solution.py:29
  8.8 6.8 %collective-permute-start.3 = (bf16[1024,128]{1,0:T(8,128)(2,1)S(1)}, bf16[1024,128]{1,0:T(8,128)(2,1)S(1)}, u32[]{:S(2)}, u32[]{:S(2)}) collective-permute-start(bf16[1024,128]{1,0:T(8,128)(2,1)S(1)} %pad_maximum_fusion.5), channel_id=1, source_target_pairs={{0,128},{16,144},{32,160},{48,176},{64,192},{80,208},{96,224},{112... | collective-permute-start | bytes 786440 | tf_op jit(solution)/shard_map/ppermute | solution.py:29
  11.3 11.3 %collective-permute-start.5 = (bf16[2048,128]{1,0:T(8,128)(2,1)S(1)}, bf16[2048,128]{1,0:T(8,128)(2,1)S(1)}, u32[]{:S(2)}, u32[]{:S(2)}) collective-permute-start(bf16[2048,128]{1,0:T(8,128)(2,1)S(1)} %constant_dynamic-update-slice_fusion.refs_5_), channel_id=1, source_target_pairs={{0,16},{16,0},{32,48},{48,32},{64,80},{80,64},{96,112},{112,96},{1... | collective-permute-start | bytes 1572872 | tf_op jit(solution)/shard_map/ppermute | solution.py:29
  15.7 7.8 %collective-permute-start.6 = (bf16[2048,128]{1,0:T(8,128)(2,1)S(1)}, bf16[2048,128]{1,0:T(8,128)(2,1)}, u32[]{:S(2)}, u32[]{:S(2)}) collective-permute-start(bf16[2048,128]{1,0:T(8,128)(2,1)S(1)} %constant_dynamic-update-slice_fusion.4.refs_6_), channel_id=1, source_target_pairs={{0,16},{16,0},{32,48},{48,32},{64,80},{80,64},{96,112},{112,96},{1... | collective-permute-start | bytes 1572872 | tf_op jit(solution)/shard_map/ppermute | solution.py:29
  26.0 7.2 %collective-permute-start.10 = (bf16[512,128]{1,0:T(8,128)(2,1)S(1)}, bf16[512,128]{1,0:T(8,128)(2,1)S(1)}, u32[]{:S(2)}, u32[]{:S(2)}) collective-permute-start(bf16[512,128]{1,0:T(8,128)(2,1)S(1)} %get-tuple-element.42), channel_id=1, source_target_pairs={{0,1},{1,2},{2,3},{3,4},{4,5},{5,6},{6,7},{7,0},{8,9},{9,10},{10,1... | collective-permute-start | bytes 393224 | tf_op jit(solution)/shard_map/ppermute | solution.py:37
  26.1 7.1 %collective-permute-start.11 = (bf16[512,128]{1,0:T(8,128)(2,1)S(1)}, bf16[512,128]{1,0:T(8,128)(2,1)S(1)}, u32[]{:S(2)}, u32[]{:S(2)}) collective-permute-start(bf16[512,128]{1,0:T(8,128)(2,1)S(1)} %get-tuple-element.44), channel_id=1, source_target_pairs={{0,7},{1,0},{2,1},{3,2},{4,3},{5,4},{6,5},{7,6},{8,15},{9,8},{10,9... | collective-permute-start | bytes 393224 | tf_op jit(solution)/shard_map/ppermute | solution.py:37
  29.5 5.9 %collective-permute-start.13 = (bf16[512,128]{1,0:T(8,128)(2,1)S(1)}, bf16[512,128]{1,0:T(8,128)(2,1)S(1)}, u32[]{:S(2)}, u32[]{:S(2)}) collective-permute-start(bf16[512,128]{1,0:T(8,128)(2,1)S(1)} %get-tuple-element.46), channel_id=1, source_target_pairs={{0,8},{1,9},{2,10},{3,11},{4,12},{5,13},{6,14},{7,15},{8,0},{9,1},... | collective-permute-start | bytes 393224 | tf_op jit(solution)/shard_map/ppermute | solution.py:37
  31.7 13.5 %collective-permute-start.7 = (bf16[1536,128]{1,0:T(8,128)(2,1)S(1)}, bf16[1536,128]{1,0:T(8,128)(2,1)S(1)}, u32[]{:S(2)}, u32[]{:S(2)}) collective-permute-start(bf16[1536,128]{1,0:T(8,128)(2,1)S(1)} %get-tuple-element.36), channel_id=1, source_target_pairs={{0,7},{1,0},{2,1},{3,2},{4,3},{5,4},{6,5},{7,6},{8,15},{9,8},{10,9... | collective-permute-start | bytes 1179656 | tf_op jit(solution)/shard_map/ppermute | solution.py:37
  33.1 12.1 %collective-permute-start.8 = (bf16[1536,128]{1,0:T(8,128)(2,1)S(1)}, bf16[1536,128]{1,0:T(8,128)(2,1)S(1)}, u32[]{:S(2)}, u32[]{:S(2)}) collective-permute-start(bf16[1536,128]{1,0:T(8,128)(2,1)S(1)} %get-tuple-element.37), channel_id=1, source_target_pairs={{0,1},{1,2},{2,3},{3,4},{4,5},{5,6},{6,7},{7,0},{8,9},{9,10},{10,1... | collective-permute-start | bytes 1179656 | tf_op jit(solution)/shard_map/ppermute | solution.py:37
  33.3 11.9 %collective-permute-start.12 = (bf16[1024,128]{1,0:T(8,128)(2,1)S(1)}, bf16[1024,128]{1,0:T(8,128)(2,1)S(1)}, u32[]{:S(2)}, u32[]{:S(2)}) collective-permute-start(bf16[1024,128]{1,0:T(8,128)(2,1)S(1)} %shard_map.96), channel_id=1, source_target_pairs={{0,8},{1,9},{2,10},{3,11},{4,12},{5,13},{6,14},{7,15},{8,0},{9,1},... | collective-permute-start | bytes 786440 | tf_op jit(solution)/shard_map/ppermute | solution.py:37
  35.4 9.8 %collective-permute-start.14 = (bf16[512,128]{1,0:T(8,128)(2,1)S(1)}, bf16[512,128]{1,0:T(8,128)(2,1)S(1)}, u32[]{:S(2)}, u32[]{:S(2)}) collective-permute-start(bf16[512,128]{1,0:T(8,128)(2,1)S(1)} %add_convert_fusion.1), channel_id=1, source_target_pairs={{0,6},{1,7},{2,0},{3,1},{4,2},{5,3},{6,4},{7,5},{8,14},{9,15},{10,... | collective-permute-start | bytes 393224 | tf_op jit(solution)/shard_map/ppermute | solution.py:47
  45.4 6.1 %collective-permute-start.15 = (bf16[512,128]{1,0:T(8,128)(2,1)S(1)}, bf16[512,128]{1,0:T(8,128)(2,1)S(1)}, u32[]{:S(2)}, u32[]{:S(2)}) collective-permute-start(bf16[512,128]{1,0:T(8,128)(2,1)S(1)} %get-tuple-element.47), channel_id=1, source_target_pairs={{0,2},{1,3},{2,4},{3,5},{4,6},{5,7},{6,0},{7,1},{8,10},{9,11},{10,... | collective-permute-start | bytes 393224 | tf_op jit(solution)/shard_map/ppermute | solution.py:37
  46.0 6.2 %collective-permute-start.16 = (bf16[512,128]{1,0:T(8,128)(2,1)S(1)}, bf16[512,128]{1,0:T(8,128)(2,1)S(1)}, u32[]{:S(2)}, u32[]{:S(2)}) collective-permute-start(bf16[512,128]{1,0:T(8,128)(2,1)S(1)} %get-tuple-element.48), channel_id=1, source_target_pairs={{0,6},{1,7},{2,0},{3,1},{4,2},{5,3},{6,4},{7,5},{8,14},{9,15},{10,... | collective-permute-start | bytes 393224 | tf_op jit(solution)/shard_map/ppermute | solution.py:37
  49.2 5.7 %collective-permute-start.9 = (bf16[512,128]{1,0:T(8,128)(2,1)S(1)}, bf16[512,128]{1,0:T(8,128)(2,1)S(1)}, u32[]{:S(2)}, u32[]{:S(2)}) collective-permute-start(bf16[512,128]{1,0:T(8,128)(2,1)S(1)} %add_convert_fusion.2), channel_id=1, source_target_pairs={{0,8},{1,9},{2,10},{3,11},{4,12},{5,13},{6,14},{7,15},{8,0},{9,1},... | collective-permute-start | bytes 393224 | tf_op jit(solution)/shard_map/ppermute | solution.py:37
  56.3 5.6 %collective-permute-start.17 = (f32[128,128]{1,0:T(8,128)S(1)}, f32[128,128]{1,0:T(8,128)S(1)}, u32[]{:S(2)}, u32[]{:S(2)}) collective-permute-start(f32[128,128]{1,0:T(8,128)S(1)} %get-tuple-element.52), channel_id=1, source_target_pairs={{0,16},{16,0},{32,48},{48,32},{64,80},{80,64},{96,112},{112,96},{1... | collective-permute-start | bytes 196616 | tf_op jit(solution)/shard_map/ppermute | solution.py:29
  62.0 10.2 %collective-permute-start.22 = (bf16[640,128]{1,0:T(8,128)(2,1)S(1)}, bf16[640,128]{1,0:T(8,128)(2,1)S(1)}, u32[]{:S(2)}, u32[]{:S(2)}) collective-permute-start(bf16[640,128]{1,0:T(8,128)(2,1)S(1)} %pad_maximum_fusion.8.refs_5_), channel_id=1, source_target_pairs={{0,6},{1,7},{2,0},{3,1},{4,2},{5,3},{6,4},{7,5},{8,14},{9,15},{10,... | collective-permute-start | bytes 491528 | tf_op jit(solution)/shard_map/ppermute | solution.py:37
  63.5 11.1 %collective-permute-start.21 = (bf16[640,128]{1,0:T(8,128)(2,1)S(1)}, bf16[640,128]{1,0:T(8,128)(2,1)S(1)}, u32[]{:S(2)}, u32[]{:S(2)}) collective-permute-start(bf16[640,128]{1,0:T(8,128)(2,1)S(1)} %pad_maximum_fusion.8.refs_5_), channel_id=1, source_target_pairs={{0,2},{1,3},{2,4},{3,5},{4,6},{5,7},{6,0},{7,1},{8,10},{9,11},{10,... | collective-permute-start | bytes 491528 | tf_op jit(solution)/shard_map/ppermute | solution.py:37
  64.5 10.1 %collective-permute-start.18 = (bf16[640,128]{1,0:T(8,128)(2,1)S(1)}, bf16[640,128]{1,0:T(8,128)(2,1)S(1)}, u32[]{:S(2)}, u32[]{:S(2)}) collective-permute-start(bf16[640,128]{1,0:T(8,128)(2,1)S(1)} %pad_maximum_fusion.8.refs_5_), channel_id=1, source_target_pairs={{0,8},{1,9},{2,10},{3,11},{4,12},{5,13},{6,14},{7,15},{8,0},{9,1},... | collective-permute-start | bytes 491528 | tf_op jit(solution)/shard_map/ppermute | solution.py:37
  65.1 13.4 %collective-permute-start.20 = (bf16[640,128]{1,0:T(8,128)(2,1)S(1)}, bf16[640,128]{1,0:T(8,128)(2,1)S(1)}, u32[]{:S(2)}, u32[]{:S(2)}) collective-permute-start(bf16[640,128]{1,0:T(8,128)(2,1)S(1)} %pad_maximum_fusion.8.refs_5_), channel_id=1, source_target_pairs={{0,7},{1,0},{2,1},{3,2},{4,3},{5,4},{6,5},{7,6},{8,15},{9,8},{10,9... | collective-permute-start | bytes 491528 | tf_op jit(solution)/shard_map/ppermute | solution.py:37
  74.7 10.1 %collective-permute-start.23 = (bf16[1280,128]{1,0:T(8,128)(2,1)S(1)}, bf16[1280,128]{1,0:T(8,128)(2,1)S(1)}, u32[]{:S(2)}, u32[]{:S(2)}) collective-permute-start(bf16[1280,128]{1,0:T(8,128)(2,1)S(1)} %get-tuple-element.70), channel_id=1, source_target_pairs={{0,8},{1,9},{2,10},{3,11},{4,12},{5,13},{6,14},{7,15},{8,0},{9,1},... | collective-permute-start | bytes 983048 | tf_op jit(solution)/shard_map/ppermute | solution.py:37
  74.8 6.1 %collective-permute-start.24 = (bf16[640,128]{1,0:T(8,128)(2,1)S(1)}, bf16[640,128]{1,0:T(8,128)(2,1)S(1)}, u32[]{:S(2)}, u32[]{:S(2)}) collective-permute-start(bf16[640,128]{1,0:T(8,128)(2,1)S(1)} %broadcast_select_fusion), channel_id=1, source_target_pairs={{0,2},{1,3},{2,4},{3,5},{4,6},{5,7},{6,0},{7,1},{8,10},{9,11},{10,... | collective-permute-start | bytes 491528 | tf_op jit(solution)/shard_map/ppermute | solution.py:47
  75.8 7.6 %collective-permute-start.19 = (bf16[640,128]{1,0:T(8,128)(2,1)S(1)}, bf16[640,128]{1,0:T(8,128)(2,1)S(1)}, u32[]{:S(2)}, u32[]{:S(2)}) collective-permute-start(bf16[640,128]{1,0:T(8,128)(2,1)S(1)} %pad_maximum_fusion.8.refs_5_), channel_id=1, source_target_pairs={{0,1},{1,2},{2,3},{3,4},{4,5},{5,6},{6,7},{7,0},{8,9},{9,10},{10,1... | collective-permute-start | bytes 491528 | tf_op jit(solution)/shard_map/ppermute | solution.py:37
  76.0 11.0 %collective-permute-start.26 = (bf16[1280,128]{1,0:T(8,128)(2,1)S(1)}, bf16[1280,128]{1,0:T(8,128)(2,1)S(1)}, u32[]{:S(2)}, u32[]{:S(2)}) collective-permute-start(bf16[1280,128]{1,0:T(8,128)(2,1)S(1)} %get-tuple-element.69), channel_id=1, source_target_pairs={{0,7},{1,0},{2,1},{3,2},{4,3},{5,4},{6,5},{7,6},{8,15},{9,8},{10,9... | collective-permute-start | bytes 983048 | tf_op jit(solution)/shard_map/ppermute | solution.py:37
  78.5 13.2 %collective-permute-start.25 = (bf16[1280,128]{1,0:T(8,128)(2,1)S(1)}, bf16[1280,128]{1,0:T(8,128)(2,1)S(1)}, u32[]{:S(2)}, u32[]{:S(2)}) collective-permute-start(bf16[1280,128]{1,0:T(8,128)(2,1)S(1)} %get-tuple-element.71), channel_id=1, source_target_pairs={{0,1},{1,2},{2,3},{3,4},{4,5},{5,6},{6,7},{7,0},{8,9},{9,10},{10,1... | collective-permute-start | bytes 983048 | tf_op jit(solution)/shard_map/ppermute | solution.py:37
  80.8 10.8 %collective-permute-start.29 = (bf16[640,128]{1,0:T(8,128)(2,1)S(1)}, bf16[640,128]{1,0:T(8,128)(2,1)S(1)}, u32[]{:S(2)}, u32[]{:S(2)}) collective-permute-start(bf16[640,128]{1,0:T(8,128)(2,1)S(1)} %collective-permute-done.24.refs_12_), channel_id=1, source_target_pairs={{0,8},{1,9},{2,10},{3,11},{4,12},{5,13},{6,14},{7,15},{8,0},{9,1},... | collective-permute-start | bytes 491528 | tf_op jit(solution)/shard_map/ppermute | solution.py:37
  84.8 6.9 %collective-permute-start.28 = (bf16[640,128]{1,0:T(8,128)(2,1)S(1)}, bf16[640,128]{1,0:T(8,128)(2,1)S(1)}, u32[]{:S(2)}, u32[]{:S(2)}) collective-permute-start(bf16[640,128]{1,0:T(8,128)(2,1)S(1)} %get-tuple-element.65), channel_id=1, source_target_pairs={{0,7},{1,0},{2,1},{3,2},{4,3},{5,4},{6,5},{7,6},{8,15},{9,8},{10,9... | collective-permute-start | bytes 491528 | tf_op jit(solution)/shard_map/ppermute | solution.py:37
  84.8 9.7 %collective-permute-start.27 = (bf16[640,128]{1,0:T(8,128)(2,1)S(1)}, bf16[640,128]{1,0:T(8,128)(2,1)S(1)}, u32[]{:S(2)}, u32[]{:S(2)}) collective-permute-start(bf16[640,128]{1,0:T(8,128)(2,1)S(1)} %get-tuple-element.66), channel_id=1, source_target_pairs={{0,1},{1,2},{2,3},{3,4},{4,5},{5,6},{6,7},{7,0},{8,9},{9,10},{10,1... | collective-permute-start | bytes 491528 | tf_op jit(solution)/shard_map/ppermute | solution.py:37
  99.9 5.0 %collective-permute-start.30 = (bf16[2048,128]{1,0:T(8,128)(2,1)S(1)}, bf16[2048,128]{1,0:T(8,128)(2,1)S(1)}, u32[]{:S(2)}, u32[]{:S(2)}) collective-permute-start(bf16[2048,128]{1,0:T(8,128)(2,1)S(1)} %get-tuple-element.57), channel_id=1, source_target_pairs={{0,16},{16,0},{32,48},{48,32},{64,80},{80,64},{96,112},{112,96},{1... | collective-permute-start | bytes 1572872 | tf_op jit(solution)/shard_map/ppermute | solution.py:29
  101.6 8.9 %collective-permute-start.34 = (bf16[1152,128]{1,0:T(8,128)(2,1)S(1)}, bf16[1152,128]{1,0:T(8,128)(2,1)S(1)}, u32[]{:S(2)}, u32[]{:S(2)}) collective-permute-start(bf16[1152,128]{1,0:T(8,128)(2,1)S(1)} %get-tuple-element.74), channel_id=1, source_target_pairs={{0,32},{16,48},{32,0},{48,16},{64,96},{80,112},{96,64},{112,80},{1... | collective-permute-start | bytes 884744 | tf_op jit(solution)/shard_map/ppermute | solution.py:29
  103.4 9.4 %collective-permute-start.32 = (bf16[1152,128]{1,0:T(8,128)(2,1)S(1)}, bf16[1152,128]{1,0:T(8,128)(2,1)S(1)}, u32[]{:S(2)}, u32[]{:S(2)}) collective-permute-start(bf16[1152,128]{1,0:T(8,128)(2,1)S(1)} %get-tuple-element.75), channel_id=1, source_target_pairs={{0,128},{16,144},{32,160},{48,176},{64,192},{80,208},{96,224},{112... | collective-permute-start | bytes 884744 | tf_op jit(solution)/shard_map/ppermute | solution.py:29
  112.9 6.2 %collective-permute-start.35 = (bf16[768,128]{1,0:T(8,128)(2,1)S(1)}, bf16[768,128]{1,0:T(8,128)(2,1)S(1)}, u32[]{:S(2)}, u32[]{:S(2)}) collective-permute-start(bf16[768,128]{1,0:T(8,128)(2,1)S(1)} %pad_maximum_fusion.7), channel_id=1, source_target_pairs={{0,64},{16,80},{32,96},{48,112},{64,128},{80,144},{96,160},{112,17... | collective-permute-start | bytes 589832 | tf_op jit(solution)/shard_map/ppermute | solution.py:29
  (12 other events, 119.0 us)

commit v8 on v6

--- a/solution.py
+++ b/solution.py
@@ -79,7 +79,7 @@
             start += rows
     acc[...] = jnp.zeros_like(acc)
     count = count_ref[0]
-    unroll = 12
+    unroll = 16
 
     def step(i, carry):
         prods = []
@@ -129,7 +129,7 @@
     )(src, dst, count, scan, vals, *panels)
 
 
-def mid_kernel(core_ref, own_ref, r1, r2, r3, r4, r5, weight_ref, gout_ref, act_ref, gt_ref, keep_ref, give_ref, gw_ref):
+def mid_kernel(core_ref, own_ref, r1, r2, r3, r4, r5, weight_ref, gout_ref, act_ref, gp_ref, keep_ref, give_ref, gw_ref):
     ax = own_ref[...]
     for r in (r1, r2, r3, r4, r5):
         ax = ax + r[:SHARD, :].astype(F32)
@@ -142,18 +142,23 @@
     sig = 1.0 / (1.0 + jnp.exp(-pre))
     act_ref[...] = (pre * sig).astype(BF16)
     gp = (gout_ref[...].astype(F32) * sig * (1.0 + pre * (1.0 - sig))).astype(BF16)
+    gp_ref[...] = gp
+    first = (((0,), (0,)), ((), ()))
+    gw_ref[...] = lax.dot_general(high, gp, first, preferred_element_type=F32) + lax.dot_general(
+        low, gp, first, preferred_element_type=F32
+    )
+    core = core_ref[0]
+    for ref, which in ((keep_ref, core), (give_ref, 1 - core)):
+        ref[...] = gw_ref[:, pl.ds(pl.multiple_of(which * BLOCK, BLOCK), BLOCK)]
+
+
+def back_kernel(gp_ref, weight_ref, gt_ref):
+    gp, weight = gp_ref[...], weight_ref[...]
     for q in range(SHARD // BLOCK):
         at = slice(q * BLOCK, (q + 1) * BLOCK)
         gt_ref[at, :] = lax.dot_general(
             weight, gp[at, :], (((1,), (1,)), ((), ())), preferred_element_type=F32
         ).astype(BF16)
-    first = (((0,), (0,)), ((), ()))
-    gw_ref[...] = lax.dot_general(high, gp, first, preferred_element_type=F32) + lax.dot_general(
-        low, gp, first, preferred_element_type=F32
-    )
-    core = core_ref[0]
-    for ref, which in ((keep_ref, core), (give_ref, 1 - core)):
-        ref[...] = gw_ref[:, pl.ds(pl.multiple_of(which * BLOCK, BLOCK), BLOCK)]
 
 
 def last_kernel(own_ref, w_ref, r1, r2, r3, out_ref):
@@ -232,11 +237,11 @@
     s6 = send_col(o6, dz=-2)
     fin = (o0, s1, s7, rx, s2, s6)
     half = jax.ShapeDtypeStruct((BLOCK, BLOCK), F32)
-    activation, gt, keep, give = pl.pallas_call(
+    activation, gp, keep, give = pl.pallas_call(
         mid_kernel,
         out_shape=[
             jax.ShapeDtypeStruct((S, 256), BF16),
-            jax.ShapeDtypeStruct((S, BLOCK), BF16),
+            jax.ShapeDtypeStruct((S, 256), BF16),
             half,
             half,
         ],
@@ -245,6 +250,9 @@
         compiler_params=params,
     )(core[None], *fin, weight, grad_out)
     share = keep + send_row(give, dc=1)
+    gt = pl.pallas_call(
+        back_kernel, out_shape=jax.ShapeDtypeStruct((S, BLOCK), BF16), compiler_params=params
+    )(gp, weight)
     gt = jnp.concatenate([gt, share.astype(BF16)])
 
     u2 = send_col(gt, dz=2)

time: 123 us -> 123 us (level)
  starting transfers between devices: 69.1 us -> 67.8 us
    ppermute x22, starting transfers between devices: 32.1 us -> 30.8 us  [send_col(): return lax.ppermute(x, 'col', perm)]
  transfers between devices with their start and end apart: 39 -> 39, of which waited for: 23 -> 24; matrix products, arithmetic and copies ran while one was open for 1% -> 1% of each run, Pallas kernels for 1% -> 1%
where the time goes in v8:
time: 123 us
  starting transfers between devices  67.8 us (55%)
  waiting for transfers between devices  42.9 us (35%)
  Pallas kernels  7.25 us (6%)
  other arithmetic  1.7 us (1%)
  between operations  1.66 us (1%)
    ppermute x16, starting transfers between devices, send_row(): return lax.ppermute(x, 'row', perm)  34.7 us
    ppermute x22, starting transfers between devices, send_col(): return lax.ppermute(x, 'col', perm)  30.8 us
    ppermute x22, waiting for transfers between devices, send_col(): return lax.ppermute(x, 'col', perm)  26.4 us
    ppermute x16, waiting for transfers between devices, send_row(): return lax.ppermute(x, 'row', perm)  16.6 us
    pallas_call x2, Pallas kernels, tile_sums(): pl.pallas_call(functools.partial(tile_kernel, places, outs, left), out_sh...  5.04 us
  transfers between devices with their start and end apart: 39, of which 24 were waited for; matrix products, arithmetic and copies ran while one was open for 1% of the time, Pallas kernels for 1%

profile of v8, /device:TPU:1, one launch (start us, length us, event | category | flops | bytes accessed | tf_op | source)
XLA Modules:
  0.0 122.5 jit_solution(6849475997022050084)
XLA Ops:
  0.6 2.2 %collective-permute-start = (bf16[512,128]{1,0:T(8,128)(2,1)}, bf16[512,128]{1,0:T(8,128)(2,1)S(1)}, u32[]{:S(2)}, u32[]{:S(2)}) collective-permute-start(bf16[512,128]{1,0:T(8,128)(2,1)} %x_ref.1), channel_id=1, source_target_pairs={{0,64},{16,80},{32,96},{48,112},{64,128},{80,144},{96,160},{112,17... | collective-permute-start | bytes 393224 | tf_op jit(solution)/shard_map/ppermute | solution.py:29
  6.9 1.9 %collective-permute-start.4 = (bf16[1024,128]{1,0:T(8,128)(2,1)S(1)}, bf16[1024,128]{1,0:T(8,128)(2,1)S(1)}, u32[]{:S(2)}, u32[]{:S(2)}) collective-permute-start(bf16[1024,128]{1,0:T(8,128)(2,1)S(1)} %pad_maximum_fusion.7), channel_id=1, source_target_pairs={{0,32},{16,48},{32,0},{48,16},{64,96},{80,112},{96,64},{112,80},{1... | collective-permute-start | bytes 786440 | tf_op jit(solution)/shard_map/ppermute | solution.py:29
  8.8 2.4 %collective-permute-start.3 = (bf16[1024,128]{1,0:T(8,128)(2,1)S(1)}, bf16[1024,128]{1,0:T(8,128)(2,1)S(1)}, u32[]{:S(2)}, u32[]{:S(2)}) collective-permute-start(bf16[1024,128]{1,0:T(8,128)(2,1)S(1)} %pad_maximum_fusion.6), channel_id=1, source_target_pairs={{0,128},{16,144},{32,160},{48,176},{64,192},{80,208},{96,224},{112... | collective-permute-start | bytes 786440 | tf_op jit(solution)/shard_map/ppermute | solution.py:29
  11.3 2.7 %collective-permute-start.5 = (bf16[2048,128]{1,0:T(8,128)(2,1)S(1)}, bf16[2048,128]{1,0:T(8,128)(2,1)S(1)}, u32[]{:S(2)}, u32[]{:S(2)}) collective-permute-start(bf16[2048,128]{1,0:T(8,128)(2,1)S(1)} %constant_dynamic-update-slice_fusion.refs_5_), channel_id=1, source_target_pairs={{0,16},{16,0},{32,48},{48,32},{64,80},{80,64},{96,112},{112,96},{1... | collective-permute-start | bytes 1572872 | tf_op jit(solution)/shard_map/ppermute | solution.py:29
  14.0 1.7 %collective-permute-done.3 = bf16[1024,128]{1,0:T(8,128)(2,1)S(1)} collective-permute-done((bf16[1024,128]{1,0:T(8,128)(2,1)S(1)}, bf16[1024,128]{1,0:T(8,128)(2,1)S(1)}, u32[]{:S(2)}, u32[]{:S(2)}) %collective-permute-start.3) | collective-permute-done | bytes 262176 | tf_op jit(solution)/shard_map/ppermute | solution.py:29
  15.7 6.1 %collective-permute-start.6 = (bf16[2048,128]{1,0:T(8,128)(2,1)S(1)}, bf16[2048,128]{1,0:T(8,128)(2,1)}, u32[]{:S(2)}, u32[]{:S(2)}) collective-permute-start(bf16[2048,128]{1,0:T(8,128)(2,1)S(1)} %constant_dynamic-update-slice_fusion.4.refs_6_), channel_id=1, source_target_pairs={{0,16},{16,0},{32,48},{48,32},{64,80},{80,64},{96,112},{112,96},{1... | collective-permute-start | bytes 1572872 | tf_op jit(solution)/shard_map/ppermute | solution.py:29
  23.5 2.6 %shard_map.95 = (bf16[512,128]{1,0:T(8,128)(2,1)S(1)}, bf16[512,128]{1,0:T(8,128)(2,1)S(1)}, bf16[512,128]{1,0:T(8,128)(2,1)S(1)}, bf16[512,128]{1,0:T(8,128)(2,...) custom-call(s32[48]{0:T(128)S(1)} %get-tuple-element.74.refs_0_.refs, ...), custom_call_target="tpu_custom_call" | custom-call | tf_op jit(solution)/shard_map/pallas_call | solution.py:119
  26.2 3.1 %collective-permute-start.13 = (bf16[512,128]{1,0:T(8,128)(2,1)S(1)}, bf16[512,128]{1,0:T(8,128)(2,1)S(1)}, u32[]{:S(2)}, u32[]{:S(2)}) collective-permute-start(bf16[512,128]{1,0:T(8,128)(2,1)S(1)} %get-tuple-element.42), channel_id=1, source_target_pairs={{0,7},{1,0},{2,1},{3,2},{4,3},{5,4},{6,5},{7,6},{8,15},{9,8},{10,9... | collective-permute-start | bytes 393224 | tf_op jit(solution)/shard_map/ppermute | solution.py:37
  29.3 2.2 %collective-permute-start.15 = (bf16[512,128]{1,0:T(8,128)(2,1)S(1)}, bf16[512,128]{1,0:T(8,128)(2,1)S(1)}, u32[]{:S(2)}, u32[]{:S(2)}) collective-permute-start(bf16[512,128]{1,0:T(8,128)(2,1)S(1)} %get-tuple-element.44), channel_id=1, source_target_pairs={{0,8},{1,9},{2,10},{3,11},{4,12},{5,13},{6,14},{7,15},{8,0},{9,1},... | collective-permute-start | bytes 393224 | tf_op jit(solution)/shard_map/ppermute | solution.py:37
  33.2 1.7 %collective-permute-start.14 = (bf16[1024,128]{1,0:T(8,128)(2,1)S(1)}, bf16[1024,128]{1,0:T(8,128)(2,1)S(1)}, u32[]{:S(2)}, u32[]{:S(2)}) collective-permute-start(bf16[1024,128]{1,0:T(8,128)(2,1)S(1)} %pad_maximum_fusion.8), channel_id=1, source_target_pairs={{0,8},{1,9},{2,10},{3,11},{4,12},{5,13},{6,14},{7,15},{8,0},{9,1},... | collective-permute-start | bytes 786440 | tf_op jit(solution)/shard_map/ppermute | solution.py:37
  38.1 1.9 %collective-permute-done.18 = bf16[256,128]{1,0:T(8,128)(2,1)S(1)} collective-permute-done((bf16[256,128]{1,0:T(8,128)(2,1)S(1)}, bf16[256,128]{1,0:T(8,128)(2,1)S(1)}, u32[]{:S(2)}, u32[]{:S(2)}) %collective-permute-start.18) | collective-permute-done | bytes 65568 | tf_op jit(solution)/shard_map/ppermute | solution.py:37
  42.6 1.8 %collective-permute-start.8 = (bf16[512,128]{1,0:T(8,128)(2,1)S(1)}, bf16[512,128]{1,0:T(8,128)(2,1)S(1)}, u32[]{:S(2)}, u32[]{:S(2)}) collective-permute-start(bf16[512,128]{1,0:T(8,128)(2,1)S(1)} %get-tuple-element.34), channel_id=1, source_target_pairs={{0,7},{1,0},{2,1},{3,2},{4,3},{5,4},{6,5},{7,6},{8,15},{9,8},{10,9... | collective-permute-start | bytes 393224 | tf_op jit(solution)/shard_map/ppermute | solution.py:37
  44.6 2.8 %collective-permute-start.19 = (bf16[512,128]{1,0:T(8,128)(2,1)S(1)}, bf16[512,128]{1,0:T(8,128)(2,1)S(1)}, u32[]{:S(2)}, u32[]{:S(2)}) collective-permute-start(bf16[512,128]{1,0:T(8,128)(2,1)S(1)} %get-tuple-element.65), channel_id=1, source_target_pairs={{0,6},{1,7},{2,0},{3,1},{4,2},{5,3},{6,4},{7,5},{8,14},{9,15},{10,... | collective-permute-start | bytes 393224 | tf_op jit(solution)/shard_map/ppermute | solution.py:37
  48.7 2.5 %collective-permute-done.19.r5 = bf16[512,128]{1,0:T(8,128)(2,1)S(1)} collective-permute-done((bf16[512,128]{1,0:T(8,128)(2,1)S(1)}, bf16[512,128]{1,0:T(8,128)(2,1)S(1)}, u32[]{:S(2)}, u32[]{:S(2)}) %collective-permute-start.19) | collective-permute-done | bytes 131104 | tf_op jit(solution)/shard_map/ppermute | solution.py:37
  55.3 6.2 %collective-permute-start.20 = (f32[128,128]{1,0:T(8,128)S(1)}, f32[128,128]{1,0:T(8,128)S(1)}, u32[]{:S(2)}, u32[]{:S(2)}) collective-permute-start(f32[128,128]{1,0:T(8,128)S(1)} %get-tuple-element.49), channel_id=1, source_target_pairs={{0,16},{16,0},{32,48},{48,32},{64,80},{80,64},{96,112},{112,96},{1... | collective-permute-start | bytes 196616 | tf_op jit(solution)/shard_map/ppermute | solution.py:29
  62.7 2.2 %collective-permute-start.22 = (bf16[640,128]{1,0:T(8,128)(2,1)S(1)}, bf16[640,128]{1,0:T(8,128)(2,1)S(1)}, u32[]{:S(2)}, u32[]{:S(2)}) collective-permute-start(bf16[640,128]{1,0:T(8,128)(2,1)S(1)} %pad_maximum_fusion.10.refs_5_), channel_id=1, source_target_pairs={{0,2},{1,3},{2,4},{3,5},{4,6},{5,7},{6,0},{7,1},{8,10},{9,11},{10,... | collective-permute-start | bytes 491528 | tf_op jit(solution)/shard_map/ppermute | solution.py:37
  64.9 3.8 %collective-permute-start.21 = (bf16[640,128]{1,0:T(8,128)(2,1)S(1)}, bf16[640,128]{1,0:T(8,128)(2,1)S(1)}, u32[]{:S(2)}, u32[]{:S(2)}) collective-permute-start(bf16[640,128]{1,0:T(8,128)(2,1)S(1)} %pad_maximum_fusion.10.refs_5_), channel_id=1, source_target_pairs={{0,8},{1,9},{2,10},{3,11},{4,12},{5,13},{6,14},{7,15},{8,0},{9,1},... | collective-permute-start | bytes 491528 | tf_op jit(solution)/shard_map/ppermute | solution.py:37
  68.7 2.9 %collective-permute-done.23.refs_8_ = bf16[640,128]{1,0:T(8,128)(2,1)S(1)} collective-permute-done((bf16[640,128]{1,0:T(8,128)(2,1)S(1)}, bf16[640,128]{1,0:T(8,128)(2,1)S(1)}, u32[]{:S(2)}, u32[]{:S(2)}) %collective-permute-start.23) | collective-permute-done | bytes 163872 | tf_op jit(solution)/shard_map/ppermute | solution.py:37
  71.6 2.1 %collective-permute-done.22.refs_7_ = bf16[640,128]{1,0:T(8,128)(2,1)S(1)} collective-permute-done((bf16[640,128]{1,0:T(8,128)(2,1)S(1)}, bf16[640,128]{1,0:T(8,128)(2,1)S(1)}, u32[]{:S(2)}, u32[]{:S(2)}) %collective-permute-start.22) | collective-permute-done | bytes 163872 | tf_op jit(solution)/shard_map/ppermute | solution.py:37
  73.8 2.4 %collective-permute-start.25 = (bf16[640,128]{1,0:T(8,128)(2,1)S(1)}, bf16[640,128]{1,0:T(8,128)(2,1)S(1)}, u32[]{:S(2)}, u32[]{:S(2)}) collective-permute-start(bf16[640,128]{1,0:T(8,128)(2,1)S(1)} %broadcast_select_fusion), channel_id=1, source_target_pairs={{0,2},{1,3},{2,4},{3,5},{4,6},{5,7},{6,0},{7,1},{8,10},{9,11},{10,... | collective-permute-start | bytes 491528 | tf_op jit(solution)/shard_map/ppermute | solution.py:47
  76.2 2.2 %collective-permute-start.24 = (bf16[1280,128]{1,0:T(8,128)(2,1)S(1)}, bf16[1280,128]{1,0:T(8,128)(2,1)S(1)}, u32[]{:S(2)}, u32[]{:S(2)}) collective-permute-start(bf16[1280,128]{1,0:T(8,128)(2,1)S(1)} %pad_maximum_fusion.5), channel_id=1, source_target_pairs={{0,8},{1,9},{2,10},{3,11},{4,12},{5,13},{6,14},{7,15},{8,0},{9,1},... | collective-permute-start | bytes 983048 | tf_op jit(solution)/shard_map/ppermute | solution.py:37
  80.0 1.8 %collective-permute-start.30 = (bf16[640,128]{1,0:T(8,128)(2,1)S(1)}, bf16[640,128]{1,0:T(8,128)(2,1)S(1)}, u32[]{:S(2)}, u32[]{:S(2)}) collective-permute-start(bf16[640,128]{1,0:T(8,128)(2,1)S(1)} %collective-permute-done.25.refs_10_), channel_id=1, source_target_pairs={{0,8},{1,9},{2,10},{3,11},{4,12},{5,13},{6,14},{7,15},{8,0},{9,1},... | collective-permute-start | bytes 491528 | tf_op jit(solution)/shard_map/ppermute | solution.py:37
  81.8 5.0 %collective-permute-done.24.refs_9_ = bf16[1280,128]{1,0:T(8,128)(2,1)S(1)} collective-permute-done((bf16[1280,128]{1,0:T(8,128)(2,1)S(1)}, bf16[1280,128]{1,0:T(8,128)(2,1)S(1)}, u32[]{:S(2)}, u32[]{:S(2)}) %collective-permute-start.24) | collective-permute-done | bytes 327712 | tf_op jit(solution)/shard_map/ppermute | solution.py:37
  88.4 1.6 %collective-permute-done.30.refs_15_ = bf16[640,128]{1,0:T(8,128)(2,1)S(1)} collective-permute-done((bf16[640,128]{1,0:T(8,128)(2,1)S(1)}, bf16[640,128]{1,0:T(8,128)(2,1)S(1)}, u32[]{:S(2)}, u32[]{:S(2)}) %collective-permute-start.30) | collective-permute-done | bytes 163872 | tf_op jit(solution)/shard_map/ppermute | solution.py:37
  89.9 3.3 %collective-permute-done.29.refs_14_ = bf16[640,128]{1,0:T(8,128)(2,1)S(1)} collective-permute-done((bf16[640,128]{1,0:T(8,128)(2,1)S(1)}, bf16[640,128]{1,0:T(8,128)(2,1)S(1)}, u32[]{:S(2)}, u32[]{:S(2)}) %collective-permute-start.29) | collective-permute-done | bytes 163872 | tf_op jit(solution)/shard_map/ppermute | solution.py:37
  94.5 2.4 %shard_map.98 = (f32[2048,128]{1,0:T(8,128)S(1)}, bf16[2048,128]{1,0:T(8,128)(2,1)S(1)}, f32[2048,128]{1,0:T(8,128)S(1)}, bf16[2048,128]{1,0:T(8,128)(2,1)S(1)}, bf16[128,128]{1,0:T(8,128)(2,1)S(1)}) custom-call(s32[48]{0:T(128)S(1)} %get-tuple-element.75.refs_1_.refs_0_, s32[48]{0:T(128)S(1)} %get-tuple-element.74.refs_0_.refs_1_, s32[1]{0:T(128)} %bitcast.30.refs_2_, ...), custom_call_target="tpu_custom_call" | custom-call | tf_op jit(solution)/shard_map/pallas_call | solution.py:119
  96.9 2.9 %collective-permute-start.32 = (bf16[2048,128]{1,0:T(8,128)(2,1)S(1)}, bf16[2048,128]{1,0:T(8,128)(2,1)S(1)}, u32[]{:S(2)}, u32[]{:S(2)}) collective-permute-start(bf16[2048,128]{1,0:T(8,128)(2,1)S(1)} %get-tuple-element.53), channel_id=1, source_target_pairs={{0,16},{16,0},{32,48},{48,32},{64,80},{80,64},{96,112},{112,96},{1... | collective-permute-start | bytes 1572872 | tf_op jit(solution)/shard_map/ppermute | solution.py:29
  103.7 6.2 %collective-permute-done.35 = bf16[1152,128]{1,0:T(8,128)(2,1)S(1)} collective-permute-done((bf16[1152,128]{1,0:T(8,128)(2,1)S(1)}, bf16[1152,128]{1,0:T(8,128)(2,1)S(1)}, u32[]{:S(2)}, u32[]{:S(2)}) %collective-permute-start.35) | collective-permute-done | bytes 294944 | tf_op jit(solution)/shard_map/ppermute | solution.py:29
  110.0 1.7 %collective-permute-start.37 = (bf16[640,128]{1,0:T(8,128)(2,1)S(1)}, bf16[640,128]{1,0:T(8,128)(2,1)S(1)}, u32[]{:S(2)}, u32[]{:S(2)}) collective-permute-start(bf16[640,128]{1,0:T(8,128)(2,1)S(1)} %pad_maximum_fusion.12), channel_id=1, source_target_pairs={{0,192},{16,208},{32,224},{48,240},{64,0},{80,16},{96,32},{112,48}... | collective-permute-start | bytes 491528 | tf_op jit(solution)/shard_map/ppermute | solution.py:29
  114.9 1.8 %collective-permute-done.34.r1 = bf16[640,128]{1,0:T(8,128)(2,1)S(1)} collective-permute-done((bf16[640,128]{1,0:T(8,128)(2,1)S(1)}, bf16[640,128]{1,0:T(8,128)(2,1)S(1)}, u32[]{:S(2)}, u32[]{:S(2)}) %collective-permute-start.34) | collective-permute-done | bytes 163872 | tf_op jit(solution)/shard_map/ppermute | solution.py:29
  116.6 1.7 %collective-permute-done.36.r2 = bf16[768,128]{1,0:T(8,128)(2,1)S(1)} collective-permute-done((bf16[768,128]{1,0:T(8,128)(2,1)S(1)}, bf16[768,128]{1,0:T(8,128)(2,1)S(1)}, u32[]{:S(2)}, u32[]{:S(2)}) %collective-permute-start.36) | collective-permute-done | bytes 196640 | tf_op jit(solution)/shard_map/ppermute | solution.py:29
  118.4 2.5 %collective-permute-start.38 = (f32[128,128]{1,0:T(8,128)S(1)}, f32[128,128]{1,0:T(8,128)S(1)}, u32[]{:S(2)}, u32[]{:S(2)}) collective-permute-start(f32[128,128]{1,0:T(8,128)S(1)} %add_add_fusion), channel_id=1, source_target_pairs={{0,16},{16,0},{32,48},{48,32},{64,80},{80,64},{96,112},{112,96},{1... | collective-permute-start | bytes 196616 | tf_op jit(solution)/shard_map/ppermute | solution.py:29
  (101 shorter events, 32.5 us)
Async XLA Ops:
  0.6 6.2 %collective-permute-start = (bf16[512,128]{1,0:T(8,128)(2,1)}, bf16[512,128]{1,0:T(8,128)(2,1)S(1)}, u32[]{:S(2)}, u32[]{:S(2)}) collective-permute-start(bf16[512,128]{1,0:T(8,128)(2,1)} %x_ref.1), channel_id=1, source_target_pairs={{0,64},{16,80},{32,96},{48,112},{64,128},{80,144},{96,160},{112,17... | collective-permute-start | bytes 393224 | tf_op jit(solution)/shard_map/ppermute | solution.py:29
  6.9 8.8 %collective-permute-start.4 = (bf16[1024,128]{1,0:T(8,128)(2,1)S(1)}, bf16[1024,128]{1,0:T(8,128)(2,1)S(1)}, u32[]{:S(2)}, u32[]{:S(2)}) collective-permute-start(bf16[1024,128]{1,0:T(8,128)(2,1)S(1)} %pad_maximum_fusion.7), channel_id=1, source_target_pairs={{0,32},{16,48},{32,0},{48,16},{64,96},{80,112},{96,64},{112,80},{1... | collective-permute-start | bytes 786440 | tf_op jit(solution)/shard_map/ppermute | solution.py:29
  8.8 6.8 %collective-permute-start.3 = (bf16[1024,128]{1,0:T(8,128)(2,1)S(1)}, bf16[1024,128]{1,0:T(8,128)(2,1)S(1)}, u32[]{:S(2)}, u32[]{:S(2)}) collective-permute-start(bf16[1024,128]{1,0:T(8,128)(2,1)S(1)} %pad_maximum_fusion.6), channel_id=1, source_target_pairs={{0,128},{16,144},{32,160},{48,176},{64,192},{80,208},{96,224},{112... | collective-permute-start | bytes 786440 | tf_op jit(solution)/shard_map/ppermute | solution.py:29
  11.3 11.3 %collective-permute-start.5 = (bf16[2048,128]{1,0:T(8,128)(2,1)S(1)}, bf16[2048,128]{1,0:T(8,128)(2,1)S(1)}, u32[]{:S(2)}, u32[]{:S(2)}) collective-permute-start(bf16[2048,128]{1,0:T(8,128)(2,1)S(1)} %constant_dynamic-update-slice_fusion.refs_5_), channel_id=1, source_target_pairs={{0,16},{16,0},{32,48},{48,32},{64,80},{80,64},{96,112},{112,96},{1... | collective-permute-start | bytes 1572872 | tf_op jit(solution)/shard_map/ppermute | solution.py:29
  15.7 7.8 %collective-permute-start.6 = (bf16[2048,128]{1,0:T(8,128)(2,1)S(1)}, bf16[2048,128]{1,0:T(8,128)(2,1)}, u32[]{:S(2)}, u32[]{:S(2)}) collective-permute-start(bf16[2048,128]{1,0:T(8,128)(2,1)S(1)} %constant_dynamic-update-slice_fusion.4.refs_6_), channel_id=1, source_target_pairs={{0,16},{16,0},{32,48},{48,32},{64,80},{80,64},{96,112},{112,96},{1... | collective-permute-start | bytes 1572872 | tf_op jit(solution)/shard_map/ppermute | solution.py:29
  26.1 6.9 %collective-permute-start.12 = (bf16[512,128]{1,0:T(8,128)(2,1)S(1)}, bf16[512,128]{1,0:T(8,128)(2,1)S(1)}, u32[]{:S(2)}, u32[]{:S(2)}) collective-permute-start(bf16[512,128]{1,0:T(8,128)(2,1)S(1)} %get-tuple-element.40), channel_id=1, source_target_pairs={{0,1},{1,2},{2,3},{3,4},{4,5},{5,6},{6,7},{7,0},{8,9},{9,10},{10,1... | collective-permute-start | bytes 393224 | tf_op jit(solution)/shard_map/ppermute | solution.py:37
  26.2 6.9 %collective-permute-start.13 = (bf16[512,128]{1,0:T(8,128)(2,1)S(1)}, bf16[512,128]{1,0:T(8,128)(2,1)S(1)}, u32[]{:S(2)}, u32[]{:S(2)}) collective-permute-start(bf16[512,128]{1,0:T(8,128)(2,1)S(1)} %get-tuple-element.42), channel_id=1, source_target_pairs={{0,7},{1,0},{2,1},{3,2},{4,3},{5,4},{6,5},{7,6},{8,15},{9,8},{10,9... | collective-permute-start | bytes 393224 | tf_op jit(solution)/shard_map/ppermute | solution.py:37
  29.3 6.2 %collective-permute-start.15 = (bf16[512,128]{1,0:T(8,128)(2,1)S(1)}, bf16[512,128]{1,0:T(8,128)(2,1)S(1)}, u32[]{:S(2)}, u32[]{:S(2)}) collective-permute-start(bf16[512,128]{1,0:T(8,128)(2,1)S(1)} %get-tuple-element.44), channel_id=1, source_target_pairs={{0,8},{1,9},{2,10},{3,11},{4,12},{5,13},{6,14},{7,15},{8,0},{9,1},... | collective-permute-start | bytes 393224 | tf_op jit(solution)/shard_map/ppermute | solution.py:37
  31.5 12.8 %collective-permute-start.9 = (bf16[1024,128]{1,0:T(8,128)(2,1)S(1)}, bf16[1024,128]{1,0:T(8,128)(2,1)S(1)}, u32[]{:S(2)}, u32[]{:S(2)}) collective-permute-start(bf16[1024,128]{1,0:T(8,128)(2,1)S(1)} %get-tuple-element.36), channel_id=1, source_target_pairs={{0,7},{1,0},{2,1},{3,2},{4,3},{5,4},{6,5},{7,6},{8,15},{9,8},{10,9... | collective-permute-start | bytes 786440 | tf_op jit(solution)/shard_map/ppermute | solution.py:37
  32.9 11.5 %collective-permute-start.10 = (bf16[1024,128]{1,0:T(8,128)(2,1)S(1)}, bf16[1024,128]{1,0:T(8,128)(2,1)S(1)}, u32[]{:S(2)}, u32[]{:S(2)}) collective-permute-start(bf16[1024,128]{1,0:T(8,128)(2,1)S(1)} %get-tuple-element.37), channel_id=1, source_target_pairs={{0,1},{1,2},{2,3},{3,4},{4,5},{5,6},{6,7},{7,0},{8,9},{9,10},{10,1... | collective-permute-start | bytes 786440 | tf_op jit(solution)/shard_map/ppermute | solution.py:37
  33.2 11.2 %collective-permute-start.14 = (bf16[1024,128]{1,0:T(8,128)(2,1)S(1)}, bf16[1024,128]{1,0:T(8,128)(2,1)S(1)}, u32[]{:S(2)}, u32[]{:S(2)}) collective-permute-start(bf16[1024,128]{1,0:T(8,128)(2,1)S(1)} %pad_maximum_fusion.8), channel_id=1, source_target_pairs={{0,8},{1,9},{2,10},{3,11},{4,12},{5,13},{6,14},{7,15},{8,0},{9,1},... | collective-permute-start | bytes 786440 | tf_op jit(solution)/shard_map/ppermute | solution.py:37
  37.1 5.5 %collective-permute-start.16 = (bf16[256,128]{1,0:T(8,128)(2,1)S(1)}, bf16[256,128]{1,0:T(8,128)(2,1)S(1)}, u32[]{:S(2)}, u32[]{:S(2)}) collective-permute-start(bf16[256,128]{1,0:T(8,128)(2,1)S(1)} %get-tuple-element.71), channel_id=1, source_target_pairs={{0,2},{1,3},{2,4},{3,5},{4,6},{5,7},{6,0},{7,1},{8,10},{9,11},{10,... | collective-permute-start | bytes 196616 | tf_op jit(solution)/shard_map/ppermute | solution.py:37
  40.0 8.7 %collective-permute-start.7 = (bf16[512,128]{1,0:T(8,128)(2,1)S(1)}, bf16[512,128]{1,0:T(8,128)(2,1)S(1)}, u32[]{:S(2)}, u32[]{:S(2)}) collective-permute-start(bf16[512,128]{1,0:T(8,128)(2,1)S(1)} %get-tuple-element.33), channel_id=1, source_target_pairs={{0,1},{1,2},{2,3},{3,4},{4,5},{5,6},{6,7},{7,0},{8,9},{9,10},{10,1... | collective-permute-start | bytes 393224 | tf_op jit(solution)/shard_map/ppermute | solution.py:37
  42.6 6.1 %collective-permute-start.8 = (bf16[512,128]{1,0:T(8,128)(2,1)S(1)}, bf16[512,128]{1,0:T(8,128)(2,1)S(1)}, u32[]{:S(2)}, u32[]{:S(2)}) collective-permute-start(bf16[512,128]{1,0:T(8,128)(2,1)S(1)} %get-tuple-element.34), channel_id=1, source_target_pairs={{0,7},{1,0},{2,1},{3,2},{4,3},{5,4},{6,5},{7,6},{8,15},{9,8},{10,9... | collective-permute-start | bytes 393224 | tf_op jit(solution)/shard_map/ppermute | solution.py:37
  44.6 6.6 %collective-permute-start.19 = (bf16[512,128]{1,0:T(8,128)(2,1)S(1)}, bf16[512,128]{1,0:T(8,128)(2,1)S(1)}, u32[]{:S(2)}, u32[]{:S(2)}) collective-permute-start(bf16[512,128]{1,0:T(8,128)(2,1)S(1)} %get-tuple-element.65), channel_id=1, source_target_pairs={{0,6},{1,7},{2,0},{3,1},{4,2},{5,3},{6,4},{7,5},{8,14},{9,15},{10,... | collective-permute-start | bytes 393224 | tf_op jit(solution)/shard_map/ppermute | solution.py:37
  47.4 5.3 %collective-permute-start.11 = (bf16[512,128]{1,0:T(8,128)(2,1)S(1)}, bf16[512,128]{1,0:T(8,128)(2,1)S(1)}, u32[]{:S(2)}, u32[]{:S(2)}) collective-permute-start(bf16[512,128]{1,0:T(8,128)(2,1)S(1)} %get-tuple-element.66), channel_id=1, source_target_pairs={{0,8},{1,9},{2,10},{3,11},{4,12},{5,13},{6,14},{7,15},{8,0},{9,1},... | collective-permute-start | bytes 393224 | tf_op jit(solution)/shard_map/ppermute | solution.py:37
  47.8 6.4 %collective-permute-start.17 = (bf16[512,128]{1,0:T(8,128)(2,1)S(1)}, bf16[512,128]{1,0:T(8,128)(2,1)S(1)}, u32[]{:S(2)}, u32[]{:S(2)}) collective-permute-start(bf16[512,128]{1,0:T(8,128)(2,1)S(1)} %get-tuple-element.67), channel_id=1, source_target_pairs={{0,2},{1,3},{2,4},{3,5},{4,6},{5,7},{6,0},{7,1},{8,10},{9,11},{10,... | collective-permute-start | bytes 393224 | tf_op jit(solution)/shard_map/ppermute | solution.py:37
  55.3 7.1 %collective-permute-start.20 = (f32[128,128]{1,0:T(8,128)S(1)}, f32[128,128]{1,0:T(8,128)S(1)}, u32[]{:S(2)}, u32[]{:S(2)}) collective-permute-start(f32[128,128]{1,0:T(8,128)S(1)} %get-tuple-element.49), channel_id=1, source_target_pairs={{0,16},{16,0},{32,48},{48,32},{64,80},{80,64},{96,112},{112,96},{1... | collective-permute-start | bytes 196616 | tf_op jit(solution)/shard_map/ppermute | solution.py:29
  62.4 9.2 %collective-permute-start.23 = (bf16[640,128]{1,0:T(8,128)(2,1)S(1)}, bf16[640,128]{1,0:T(8,128)(2,1)S(1)}, u32[]{:S(2)}, u32[]{:S(2)}) collective-permute-start(bf16[640,128]{1,0:T(8,128)(2,1)S(1)} %pad_maximum_fusion.10.refs_5_), channel_id=1, source_target_pairs={{0,6},{1,7},{2,0},{3,1},{4,2},{5,3},{6,4},{7,5},{8,14},{9,15},{10,... | collective-permute-start | bytes 491528 | tf_op jit(solution)/shard_map/ppermute | solution.py:37
  62.7 11.1 %collective-permute-start.22 = (bf16[640,128]{1,0:T(8,128)(2,1)S(1)}, bf16[640,128]{1,0:T(8,128)(2,1)S(1)}, u32[]{:S(2)}, u32[]{:S(2)}) collective-permute-start(bf16[640,128]{1,0:T(8,128)(2,1)S(1)} %pad_maximum_fusion.10.refs_5_), channel_id=1, source_target_pairs={{0,2},{1,3},{2,4},{3,5},{4,6},{5,7},{6,0},{7,1},{8,10},{9,11},{10,... | collective-permute-start | bytes 491528 | tf_op jit(solution)/shard_map/ppermute | solution.py:37
  64.9 13.5 %collective-permute-start.21 = (bf16[640,128]{1,0:T(8,128)(2,1)S(1)}, bf16[640,128]{1,0:T(8,128)(2,1)S(1)}, u32[]{:S(2)}, u32[]{:S(2)}) collective-permute-start(bf16[640,128]{1,0:T(8,128)(2,1)S(1)} %pad_maximum_fusion.10.refs_5_), channel_id=1, source_target_pairs={{0,8},{1,9},{2,10},{3,11},{4,12},{5,13},{6,14},{7,15},{8,0},{9,1},... | collective-permute-start | bytes 491528 | tf_op jit(solution)/shard_map/ppermute | solution.py:37
  73.8 6.2 %collective-permute-start.25 = (bf16[640,128]{1,0:T(8,128)(2,1)S(1)}, bf16[640,128]{1,0:T(8,128)(2,1)S(1)}, u32[]{:S(2)}, u32[]{:S(2)}) collective-permute-start(bf16[640,128]{1,0:T(8,128)(2,1)S(1)} %broadcast_select_fusion), channel_id=1, source_target_pairs={{0,2},{1,3},{2,4},{3,5},{4,6},{5,7},{6,0},{7,1},{8,10},{9,11},{10,... | collective-permute-start | bytes 491528 | tf_op jit(solution)/shard_map/ppermute | solution.py:47
  76.2 10.6 %collective-permute-start.24 = (bf16[1280,128]{1,0:T(8,128)(2,1)S(1)}, bf16[1280,128]{1,0:T(8,128)(2,1)S(1)}, u32[]{:S(2)}, u32[]{:S(2)}) collective-permute-start(bf16[1280,128]{1,0:T(8,128)(2,1)S(1)} %pad_maximum_fusion.5), channel_id=1, source_target_pairs={{0,8},{1,9},{2,10},{3,11},{4,12},{5,13},{6,14},{7,15},{8,0},{9,1},... | collective-permute-start | bytes 983048 | tf_op jit(solution)/shard_map/ppermute | solution.py:37
  78.4 16.0 %collective-permute-start.27 = (bf16[1920,128]{1,0:T(8,128)(2,1)S(1)}, bf16[1920,128]{1,0:T(8,128)(2,1)S(1)}, u32[]{:S(2)}, u32[]{:S(2)}) collective-permute-start(bf16[1920,128]{1,0:T(8,128)(2,1)S(1)} %get-tuple-element.61), channel_id=1, source_target_pairs={{0,7},{1,0},{2,1},{3,2},{4,3},{5,4},{6,5},{7,6},{8,15},{9,8},{10,9... | collective-permute-start | bytes 1474568 | tf_op jit(solution)/shard_map/ppermute | solution.py:37
  78.5 15.9 %collective-permute-start.26 = (bf16[1920,128]{1,0:T(8,128)(2,1)S(1)}, bf16[1920,128]{1,0:T(8,128)(2,1)S(1)}, u32[]{:S(2)}, u32[]{:S(2)}) collective-permute-start(bf16[1920,128]{1,0:T(8,128)(2,1)S(1)} %get-tuple-element.62), channel_id=1, source_target_pairs={{0,1},{1,2},{2,3},{3,4},{4,5},{5,6},{6,7},{7,0},{8,9},{9,10},{10,1... | collective-permute-start | bytes 1474568 | tf_op jit(solution)/shard_map/ppermute | solution.py:37
  80.0 9.9 %collective-permute-start.30 = (bf16[640,128]{1,0:T(8,128)(2,1)S(1)}, bf16[640,128]{1,0:T(8,128)(2,1)S(1)}, u32[]{:S(2)}, u32[]{:S(2)}) collective-permute-start(bf16[640,128]{1,0:T(8,128)(2,1)S(1)} %collective-permute-done.25.refs_10_), channel_id=1, source_target_pairs={{0,8},{1,9},{2,10},{3,11},{4,12},{5,13},{6,14},{7,15},{8,0},{9,1},... | collective-permute-start | bytes 491528 | tf_op jit(solution)/shard_map/ppermute | solution.py:37
  86.8 6.4 %collective-permute-start.29 = (bf16[640,128]{1,0:T(8,128)(2,1)S(1)}, bf16[640,128]{1,0:T(8,128)(2,1)S(1)}, u32[]{:S(2)}, u32[]{:S(2)}) collective-permute-start(bf16[640,128]{1,0:T(8,128)(2,1)S(1)} %get-tuple-element.59), channel_id=1, source_target_pairs={{0,7},{1,0},{2,1},{3,2},{4,3},{5,4},{6,5},{7,6},{8,15},{9,8},{10,9... | collective-permute-start | bytes 491528 | tf_op jit(solution)/shard_map/ppermute | solution.py:37
  86.9 7.6 %collective-permute-start.28 = (bf16[640,128]{1,0:T(8,128)(2,1)S(1)}, bf16[640,128]{1,0:T(8,128)(2,1)S(1)}, u32[]{:S(2)}, u32[]{:S(2)}) collective-permute-start(bf16[640,128]{1,0:T(8,128)(2,1)S(1)} %get-tuple-element.60), channel_id=1, source_target_pairs={{0,1},{1,2},{2,3},{3,4},{4,5},{5,6},{6,7},{7,0},{8,9},{9,10},{10,1... | collective-permute-start | bytes 491528 | tf_op jit(solution)/shard_map/ppermute | solution.py:37
  101.6 8.3 %collective-permute-start.35 = (bf16[1152,128]{1,0:T(8,128)(2,1)S(1)}, bf16[1152,128]{1,0:T(8,128)(2,1)S(1)}, u32[]{:S(2)}, u32[]{:S(2)}) collective-permute-start(bf16[1152,128]{1,0:T(8,128)(2,1)S(1)} %get-tuple-element.72), channel_id=1, source_target_pairs={{0,32},{16,48},{32,0},{48,16},{64,96},{80,112},{96,64},{112,80},{1... | collective-permute-start | bytes 884744 | tf_op jit(solution)/shard_map/ppermute | solution.py:29
  102.8 9.4 %collective-permute-start.33 = (bf16[1152,128]{1,0:T(8,128)(2,1)S(1)}, bf16[1152,128]{1,0:T(8,128)(2,1)S(1)}, u32[]{:S(2)}, u32[]{:S(2)}) collective-permute-start(bf16[1152,128]{1,0:T(8,128)(2,1)S(1)} %get-tuple-element.73), channel_id=1, source_target_pairs={{0,128},{16,144},{32,160},{48,176},{64,192},{80,208},{96,224},{112... | collective-permute-start | bytes 884744 | tf_op jit(solution)/shard_map/ppermute | solution.py:29
  110.0 4.8 %collective-permute-start.37 = (bf16[640,128]{1,0:T(8,128)(2,1)S(1)}, bf16[640,128]{1,0:T(8,128)(2,1)S(1)}, u32[]{:S(2)}, u32[]{:S(2)}) collective-permute-start(bf16[640,128]{1,0:T(8,128)(2,1)S(1)} %pad_maximum_fusion.12), channel_id=1, source_target_pairs={{0,192},{16,208},{32,224},{48,240},{64,0},{80,16},{96,32},{112,48}... | collective-permute-start | bytes 491528 | tf_op jit(solution)/shard_map/ppermute | solution.py:29
  112.2 6.2 %collective-permute-start.36 = (bf16[768,128]{1,0:T(8,128)(2,1)S(1)}, bf16[768,128]{1,0:T(8,128)(2,1)S(1)}, u32[]{:S(2)}, u32[]{:S(2)}) collective-permute-start(bf16[768,128]{1,0:T(8,128)(2,1)S(1)} %pad_maximum_fusion.9), channel_id=1, source_target_pairs={{0,64},{16,80},{32,96},{48,112},{64,128},{80,144},{96,160},{112,17... | collective-permute-start | bytes 589832 | tf_op jit(solution)/shard_map/ppermute | solution.py:29
  (13 other events, 120.6 us)

commit v9 on v8

--- a/solution.py
+++ b/solution.py
@@ -159,6 +159,11 @@
         gt_ref[at, :] = lax.dot_general(
             weight, gp[at, :], (((1,), (1,)), ((), ())), preferred_element_type=F32
         ).astype(BF16)
+
+
+def halves_kernel(core_ref, mine_ref, theirs_ref, out_ref):
+    for ref, which in ((mine_ref, core_ref[0]), (theirs_ref, 1 - core_ref[0])):
+        out_ref[:, pl.ds(pl.multiple_of(which * BLOCK, BLOCK), BLOCK)] = ref[...]
 
 
 def last_kernel(own_ref, w_ref, r1, r2, r3, out_ref):
@@ -297,8 +302,12 @@
         out_shape=jax.ShapeDtypeStruct((S, BLOCK), BF16),
         compiler_params=params,
     )(own[:S], w, ro, ru, rd)
-    first, second = jnp.where(core == 0, mine, theirs), jnp.where(core == 0, theirs, mine)
-    grad_weight = jnp.concatenate([first, second], axis=1)
+    grad_weight = pl.pallas_call(
+        halves_kernel,
+        out_shape=jax.ShapeDtypeStruct((BLOCK, 256), F32),
+        in_specs=[pl.BlockSpec(memory_space=pltpu.SMEM)] + [pl.BlockSpec(memory_space=pltpu.VMEM)] * 2,
+        compiler_params=params,
+    )(core[None], mine, theirs)
     return (activation, grad_features, grad_weight)
 
 

time: 123 us -> 123 us (level)
    ppermute x16, waiting for transfers between devices: 16.6 us -> 15.1 us  [send_row(): return lax.ppermute(x, 'row', perm)]
  transfers between devices with their start and end apart: 39 -> 39, of which waited for: 24 -> 21; matrix products, arithmetic and copies ran while one was open for 1% -> 1% of each run, Pallas kernels for 1% -> 1%
where the time goes in v9:
time: 123 us
  starting transfers between devices  69 us (56%)
  waiting for transfers between devices  42.1 us (34%)
  Pallas kernels  7.9 us (6%)
  between operations  1.65 us (1%)
    ppermute x16, starting transfers between devices, send_row(): return lax.ppermute(x, 'row', perm)  34.6 us
    ppermute x22, starting transfers between devices, send_col(): return lax.ppermute(x, 'col', perm)  31.8 us
    ppermute x22, waiting for transfers between devices, send_col(): return lax.ppermute(x, 'col', perm)  27 us
    ppermute x16, waiting for transfers between devices, send_row(): return lax.ppermute(x, 'row', perm)  15.1 us
    pallas_call x2, Pallas kernels, tile_sums(): pl.pallas_call(functools.partial(tile_kernel, places, outs, left), out_sh...  5.03 us
    ppermute x1, starting transfers between devices, send_apart(): return lax.ppermute(x, ('row', 'col'), perm)  2.53 us
  transfers between devices with their start and end apart: 39, of which 21 were waited for; matrix products, arithmetic and copies ran while one was open for 1% of the time, Pallas kernels for 1%

profile of v9, /device:TPU:1, one launch (start us, length us, event | category | flops | bytes accessed | tf_op | source)
XLA Modules:
  0.0 122.8 jit_solution(13742994920682186745)
XLA Ops:
  0.6 2.2 %collective-permute-start = (bf16[512,128]{1,0:T(8,128)(2,1)}, bf16[512,128]{1,0:T(8,128)(2,1)S(1)}, u32[]{:S(2)}, u32[]{:S(2)}) collective-permute-start(bf16[512,128]{1,0:T(8,128)(2,1)} %x_ref.1), channel_id=1, source_target_pairs={{0,64},{16,80},{32,96},{48,112},{64,128},{80,144},{96,160},{112,17... | collective-permute-start | bytes 393224 | tf_op jit(solution)/shard_map/ppermute | solution.py:29
  6.9 1.9 %collective-permute-start.4 = (bf16[1024,128]{1,0:T(8,128)(2,1)S(1)}, bf16[1024,128]{1,0:T(8,128)(2,1)S(1)}, u32[]{:S(2)}, u32[]{:S(2)}) collective-permute-start(bf16[1024,128]{1,0:T(8,128)(2,1)S(1)} %pad_maximum_fusion.7), channel_id=1, source_target_pairs={{0,32},{16,48},{32,0},{48,16},{64,96},{80,112},{96,64},{112,80},{1... | collective-permute-start | bytes 786440 | tf_op jit(solution)/shard_map/ppermute | solution.py:29
  8.8 2.4 %collective-permute-start.3 = (bf16[1024,128]{1,0:T(8,128)(2,1)S(1)}, bf16[1024,128]{1,0:T(8,128)(2,1)S(1)}, u32[]{:S(2)}, u32[]{:S(2)}) collective-permute-start(bf16[1024,128]{1,0:T(8,128)(2,1)S(1)} %pad_maximum_fusion.6), channel_id=1, source_target_pairs={{0,128},{16,144},{32,160},{48,176},{64,192},{80,208},{96,224},{112... | collective-permute-start | bytes 786440 | tf_op jit(solution)/shard_map/ppermute | solution.py:29
  11.3 2.7 %collective-permute-start.5 = (bf16[2048,128]{1,0:T(8,128)(2,1)S(1)}, bf16[2048,128]{1,0:T(8,128)(2,1)S(1)}, u32[]{:S(2)}, u32[]{:S(2)}) collective-permute-start(bf16[2048,128]{1,0:T(8,128)(2,1)S(1)} %constant_dynamic-update-slice_fusion.refs_5_), channel_id=1, source_target_pairs={{0,16},{16,0},{32,48},{48,32},{64,80},{80,64},{96,112},{112,96},{1... | collective-permute-start | bytes 1572872 | tf_op jit(solution)/shard_map/ppermute | solution.py:29
  14.0 1.7 %collective-permute-done.3 = bf16[1024,128]{1,0:T(8,128)(2,1)S(1)} collective-permute-done((bf16[1024,128]{1,0:T(8,128)(2,1)S(1)}, bf16[1024,128]{1,0:T(8,128)(2,1)S(1)}, u32[]{:S(2)}, u32[]{:S(2)}) %collective-permute-start.3) | collective-permute-done | bytes 262176 | tf_op jit(solution)/shard_map/ppermute | solution.py:29
  15.7 6.1 %collective-permute-start.6 = (bf16[2048,128]{1,0:T(8,128)(2,1)S(1)}, bf16[2048,128]{1,0:T(8,128)(2,1)}, u32[]{:S(2)}, u32[]{:S(2)}) collective-permute-start(bf16[2048,128]{1,0:T(8,128)(2,1)S(1)} %constant_dynamic-update-slice_fusion.4.refs_6_), channel_id=1, source_target_pairs={{0,16},{16,0},{32,48},{48,32},{64,80},{80,64},{96,112},{112,96},{1... | collective-permute-start | bytes 1572872 | tf_op jit(solution)/shard_map/ppermute | solution.py:29
  23.5 2.6 %shard_map.95 = (bf16[512,128]{1,0:T(8,128)(2,1)S(1)}, bf16[512,128]{1,0:T(8,128)(2,1)S(1)}, bf16[512,128]{1,0:T(8,128)(2,1)S(1)}, bf16[512,128]{1,0:T(8,128)(2,...) custom-call(s32[48]{0:T(128)S(1)} %get-tuple-element.72.refs_0_.refs, ...), custom_call_target="tpu_custom_call" | custom-call | tf_op jit(solution)/shard_map/pallas_call | solution.py:119
  26.2 2.8 %collective-permute-start.13 = (bf16[512,128]{1,0:T(8,128)(2,1)S(1)}, bf16[512,128]{1,0:T(8,128)(2,1)S(1)}, u32[]{:S(2)}, u32[]{:S(2)}) collective-permute-start(bf16[512,128]{1,0:T(8,128)(2,1)S(1)} %get-tuple-element.42), channel_id=1, source_target_pairs={{0,7},{1,0},{2,1},{3,2},{4,3},{5,4},{6,5},{7,6},{8,15},{9,8},{10,9... | collective-permute-start | bytes 393224 | tf_op jit(solution)/shard_map/ppermute | solution.py:37
  29.0 2.8 %collective-permute-start.15 = (bf16[512,128]{1,0:T(8,128)(2,1)S(1)}, bf16[512,128]{1,0:T(8,128)(2,1)S(1)}, u32[]{:S(2)}, u32[]{:S(2)}) collective-permute-start(bf16[512,128]{1,0:T(8,128)(2,1)S(1)} %get-tuple-element.44), channel_id=1, source_target_pairs={{0,8},{1,9},{2,10},{3,11},{4,12},{5,13},{6,14},{7,15},{8,0},{9,1},... | collective-permute-start | bytes 393224 | tf_op jit(solution)/shard_map/ppermute | solution.py:37
  33.5 2.1 %collective-permute-start.14 = (bf16[1024,128]{1,0:T(8,128)(2,1)S(1)}, bf16[1024,128]{1,0:T(8,128)(2,1)S(1)}, u32[]{:S(2)}, u32[]{:S(2)}) collective-permute-start(bf16[1024,128]{1,0:T(8,128)(2,1)S(1)} %pad_maximum_fusion.8), channel_id=1, source_target_pairs={{0,8},{1,9},{2,10},{3,11},{4,12},{5,13},{6,14},{7,15},{8,0},{9,1},... | collective-permute-start | bytes 786440 | tf_op jit(solution)/shard_map/ppermute | solution.py:37
  35.6 2.0 %collective-permute-start.18 = (bf16[256,128]{1,0:T(8,128)(2,1)S(1)}, bf16[256,128]{1,0:T(8,128)(2,1)S(1)}, u32[]{:S(2)}, u32[]{:S(2)}) collective-permute-start(bf16[256,128]{1,0:T(8,128)(2,1)S(1)} %get-tuple-element.68), channel_id=1, source_target_pairs={{0,6},{1,7},{2,0},{3,1},{4,2},{5,3},{6,4},{7,5},{8,14},{9,15},{10,... | collective-permute-start | bytes 196616 | tf_op jit(solution)/shard_map/ppermute | solution.py:37
  38.1 1.9 %collective-permute-done.18 = bf16[256,128]{1,0:T(8,128)(2,1)S(1)} collective-permute-done((bf16[256,128]{1,0:T(8,128)(2,1)S(1)}, bf16[256,128]{1,0:T(8,128)(2,1)S(1)}, u32[]{:S(2)}, u32[]{:S(2)}) %collective-permute-start.18) | collective-permute-done | bytes 65568 | tf_op jit(solution)/shard_map/ppermute | solution.py:37
  40.0 1.9 %collective-permute-start.7 = (bf16[512,128]{1,0:T(8,128)(2,1)S(1)}, bf16[512,128]{1,0:T(8,128)(2,1)S(1)}, u32[]{:S(2)}, u32[]{:S(2)}) collective-permute-start(bf16[512,128]{1,0:T(8,128)(2,1)S(1)} %get-tuple-element.33), channel_id=1, source_target_pairs={{0,1},{1,2},{2,3},{3,4},{4,5},{5,6},{6,7},{7,0},{8,9},{9,10},{10,1... | collective-permute-start | bytes 393224 | tf_op jit(solution)/shard_map/ppermute | solution.py:37
  43.2 1.7 %collective-permute-start.8 = (bf16[512,128]{1,0:T(8,128)(2,1)S(1)}, bf16[512,128]{1,0:T(8,128)(2,1)S(1)}, u32[]{:S(2)}, u32[]{:S(2)}) collective-permute-start(bf16[512,128]{1,0:T(8,128)(2,1)S(1)} %get-tuple-element.34), channel_id=1, source_target_pairs={{0,7},{1,0},{2,1},{3,2},{4,3},{5,4},{6,5},{7,6},{8,15},{9,8},{10,9... | collective-permute-start | bytes 393224 | tf_op jit(solution)/shard_map/ppermute | solution.py:37
  45.0 3.0 %collective-permute-start.19 = (bf16[512,128]{1,0:T(8,128)(2,1)S(1)}, bf16[512,128]{1,0:T(8,128)(2,1)S(1)}, u32[]{:S(2)}, u32[]{:S(2)}) collective-permute-start(bf16[512,128]{1,0:T(8,128)(2,1)S(1)} %get-tuple-element.65), channel_id=1, source_target_pairs={{0,6},{1,7},{2,0},{3,1},{4,2},{5,3},{6,4},{7,5},{8,14},{9,15},{10,... | collective-permute-start | bytes 393224 | tf_op jit(solution)/shard_map/ppermute | solution.py:37
  49.3 2.1 %collective-permute-done.19.r5 = bf16[512,128]{1,0:T(8,128)(2,1)S(1)} collective-permute-done((bf16[512,128]{1,0:T(8,128)(2,1)S(1)}, bf16[512,128]{1,0:T(8,128)(2,1)S(1)}, u32[]{:S(2)}, u32[]{:S(2)}) %collective-permute-start.19) | collective-permute-done | bytes 131104 | tf_op jit(solution)/shard_map/ppermute | solution.py:37
  51.4 1.9 %collective-permute-done.11.r3 = bf16[512,128]{1,0:T(8,128)(2,1)S(1)} collective-permute-done((bf16[512,128]{1,0:T(8,128)(2,1)S(1)}, bf16[512,128]{1,0:T(8,128)(2,1)S(1)}, u32[]{:S(2)}, u32[]{:S(2)}) %collective-permute-start.11) | collective-permute-done | bytes 131104 | tf_op jit(solution)/shard_map/ppermute | solution.py:37
  56.1 4.9 %collective-permute-start.20 = (f32[128,128]{1,0:T(8,128)S(1)}, f32[128,128]{1,0:T(8,128)S(1)}, u32[]{:S(2)}, u32[]{:S(2)}) collective-permute-start(f32[128,128]{1,0:T(8,128)S(1)} %get-tuple-element.49), channel_id=1, source_target_pairs={{0,16},{16,0},{32,48},{48,32},{64,80},{80,64},{96,112},{112,96},{1... | collective-permute-start | bytes 196616 | tf_op jit(solution)/shard_map/ppermute | solution.py:29
  62.1 2.4 %collective-permute-start.22 = (bf16[640,128]{1,0:T(8,128)(2,1)S(1)}, bf16[640,128]{1,0:T(8,128)(2,1)S(1)}, u32[]{:S(2)}, u32[]{:S(2)}) collective-permute-start(bf16[640,128]{1,0:T(8,128)(2,1)S(1)} %pad_maximum_fusion.10.refs_5_), channel_id=1, source_target_pairs={{0,2},{1,3},{2,4},{3,5},{4,6},{5,7},{6,0},{7,1},{8,10},{9,11},{10,... | collective-permute-start | bytes 491528 | tf_op jit(solution)/shard_map/ppermute | solution.py:37
  64.4 3.5 %collective-permute-start.21 = (bf16[640,128]{1,0:T(8,128)(2,1)S(1)}, bf16[640,128]{1,0:T(8,128)(2,1)S(1)}, u32[]{:S(2)}, u32[]{:S(2)}) collective-permute-start(bf16[640,128]{1,0:T(8,128)(2,1)S(1)} %pad_maximum_fusion.10.refs_5_), channel_id=1, source_target_pairs={{0,8},{1,9},{2,10},{3,11},{4,12},{5,13},{6,14},{7,15},{8,0},{9,1},... | collective-permute-start | bytes 491528 | tf_op jit(solution)/shard_map/ppermute | solution.py:37
  68.0 4.1 %collective-permute-done.23.refs_8_ = bf16[640,128]{1,0:T(8,128)(2,1)S(1)} collective-permute-done((bf16[640,128]{1,0:T(8,128)(2,1)S(1)}, bf16[640,128]{1,0:T(8,128)(2,1)S(1)}, u32[]{:S(2)}, u32[]{:S(2)}) %collective-permute-start.23) | collective-permute-done | bytes 163872 | tf_op jit(solution)/shard_map/ppermute | solution.py:37
  72.1 2.2 %collective-permute-done.22.refs_7_ = bf16[640,128]{1,0:T(8,128)(2,1)S(1)} collective-permute-done((bf16[640,128]{1,0:T(8,128)(2,1)S(1)}, bf16[640,128]{1,0:T(8,128)(2,1)S(1)}, u32[]{:S(2)}, u32[]{:S(2)}) %collective-permute-start.22) | collective-permute-done | bytes 163872 | tf_op jit(solution)/shard_map/ppermute | solution.py:37
  74.3 2.5 %collective-permute-start.25 = (bf16[640,128]{1,0:T(8,128)(2,1)S(1)}, bf16[640,128]{1,0:T(8,128)(2,1)S(1)}, u32[]{:S(2)}, u32[]{:S(2)}) collective-permute-start(bf16[640,128]{1,0:T(8,128)(2,1)S(1)} %broadcast_select_fusion), channel_id=1, source_target_pairs={{0,2},{1,3},{2,4},{3,5},{4,6},{5,7},{6,0},{7,1},{8,10},{9,11},{10,... | collective-permute-start | bytes 491528 | tf_op jit(solution)/shard_map/ppermute | solution.py:47
  76.8 1.9 %collective-permute-start.24 = (bf16[1280,128]{1,0:T(8,128)(2,1)S(1)}, bf16[1280,128]{1,0:T(8,128)(2,1)S(1)}, u32[]{:S(2)}, u32[]{:S(2)}) collective-permute-start(bf16[1280,128]{1,0:T(8,128)(2,1)S(1)} %pad_maximum_fusion.5), channel_id=1, source_target_pairs={{0,8},{1,9},{2,10},{3,11},{4,12},{5,13},{6,14},{7,15},{8,0},{9,1},... | collective-permute-start | bytes 983048 | tf_op jit(solution)/shard_map/ppermute | solution.py:37
  81.7 5.7 %collective-permute-done.24.refs_9_ = bf16[1280,128]{1,0:T(8,128)(2,1)S(1)} collective-permute-done((bf16[1280,128]{1,0:T(8,128)(2,1)S(1)}, bf16[1280,128]{1,0:T(8,128)(2,1)S(1)}, u32[]{:S(2)}, u32[]{:S(2)}) %collective-permute-start.24) | collective-permute-done | bytes 327712 | tf_op jit(solution)/shard_map/ppermute | solution.py:37
  90.5 3.9 %collective-permute-done.29.refs_14_ = bf16[640,128]{1,0:T(8,128)(2,1)S(1)} collective-permute-done((bf16[640,128]{1,0:T(8,128)(2,1)S(1)}, bf16[640,128]{1,0:T(8,128)(2,1)S(1)}, u32[]{:S(2)}, u32[]{:S(2)}) %collective-permute-start.29) | collective-permute-done | bytes 163872 | tf_op jit(solution)/shard_map/ppermute | solution.py:37
  95.1 2.4 %shard_map.98 = (f32[2048,128]{1,0:T(8,128)S(1)}, bf16[2048,128]{1,0:T(8,128)(2,1)S(1)}, f32[2048,128]{1,0:T(8,128)S(1)}, bf16[2048,128]{1,0:T(8,128)(2,1)S(1)}, bf16[128,128]{1,0:T(8,128)(2,1)S(1)}) custom-call(s32[48]{0:T(128)S(1)} %get-tuple-element.73.refs_1_.refs_0_, s32[48]{0:T(128)S(1)} %get-tuple-element.72.refs_0_.refs_1_, s32[1]{0:T(128)} %bitcast.30.refs_2_, ...), custom_call_target="tpu_custom_call" | custom-call | tf_op jit(solution)/shard_map/pallas_call | solution.py:119
  97.5 1.9 %collective-permute-start.32 = (bf16[2048,128]{1,0:T(8,128)(2,1)S(1)}, bf16[2048,128]{1,0:T(8,128)(2,1)S(1)}, u32[]{:S(2)}, u32[]{:S(2)}) collective-permute-start(bf16[2048,128]{1,0:T(8,128)(2,1)S(1)} %get-tuple-element.53), channel_id=1, source_target_pairs={{0,16},{16,0},{32,48},{48,32},{64,80},{80,64},{96,112},{112,96},{1... | collective-permute-start | bytes 1572872 | tf_op jit(solution)/shard_map/ppermute | solution.py:29
  103.9 5.6 %collective-permute-done.35 = bf16[1152,128]{1,0:T(8,128)(2,1)S(1)} collective-permute-done((bf16[1152,128]{1,0:T(8,128)(2,1)S(1)}, bf16[1152,128]{1,0:T(8,128)(2,1)S(1)}, u32[]{:S(2)}, u32[]{:S(2)}) %collective-permute-start.35) | collective-permute-done | bytes 294944 | tf_op jit(solution)/shard_map/ppermute | solution.py:29
  109.6 2.6 %collective-permute-start.37 = (bf16[640,128]{1,0:T(8,128)(2,1)S(1)}, bf16[640,128]{1,0:T(8,128)(2,1)S(1)}, u32[]{:S(2)}, u32[]{:S(2)}) collective-permute-start(bf16[640,128]{1,0:T(8,128)(2,1)S(1)} %pad_maximum_fusion.12), channel_id=1, source_target_pairs={{0,192},{16,208},{32,224},{48,240},{64,0},{80,16},{96,32},{112,48}... | collective-permute-start | bytes 491528 | tf_op jit(solution)/shard_map/ppermute | solution.py:29
  114.4 3.3 %collective-permute-done.34.r1 = bf16[640,128]{1,0:T(8,128)(2,1)S(1)} collective-permute-done((bf16[640,128]{1,0:T(8,128)(2,1)S(1)}, bf16[640,128]{1,0:T(8,128)(2,1)S(1)}, u32[]{:S(2)}, u32[]{:S(2)}) %collective-permute-start.34) | collective-permute-done | bytes 163872 | tf_op jit(solution)/shard_map/ppermute | solution.py:29
  118.4 2.8 %collective-permute-start.38 = (f32[128,128]{1,0:T(8,128)S(1)}, f32[128,128]{1,0:T(8,128)S(1)}, u32[]{:S(2)}, u32[]{:S(2)}) collective-permute-start(f32[128,128]{1,0:T(8,128)S(1)} %add_add_fusion.mine_ref), channel_id=1, source_target_pairs={{0,16},{16,0},{32,48},{48,32},{64,80},{80,64},{96,112},{112,96},{1... | collective-permute-start | bytes 196616 | tf_op jit(solution)/shard_map/ppermute | solution.py:29
  (100 shorter events, 29.6 us)
Async XLA Ops:
  0.6 6.2 %collective-permute-start = (bf16[512,128]{1,0:T(8,128)(2,1)}, bf16[512,128]{1,0:T(8,128)(2,1)S(1)}, u32[]{:S(2)}, u32[]{:S(2)}) collective-permute-start(bf16[512,128]{1,0:T(8,128)(2,1)} %x_ref.1), channel_id=1, source_target_pairs={{0,64},{16,80},{32,96},{48,112},{64,128},{80,144},{96,160},{112,17... | collective-permute-start | bytes 393224 | tf_op jit(solution)/shard_map/ppermute | solution.py:29
  6.9 8.8 %collective-permute-start.4 = (bf16[1024,128]{1,0:T(8,128)(2,1)S(1)}, bf16[1024,128]{1,0:T(8,128)(2,1)S(1)}, u32[]{:S(2)}, u32[]{:S(2)}) collective-permute-start(bf16[1024,128]{1,0:T(8,128)(2,1)S(1)} %pad_maximum_fusion.7), channel_id=1, source_target_pairs={{0,32},{16,48},{32,0},{48,16},{64,96},{80,112},{96,64},{112,80},{1... | collective-permute-start | bytes 786440 | tf_op jit(solution)/shard_map/ppermute | solution.py:29
  8.8 6.8 %collective-permute-start.3 = (bf16[1024,128]{1,0:T(8,128)(2,1)S(1)}, bf16[1024,128]{1,0:T(8,128)(2,1)S(1)}, u32[]{:S(2)}, u32[]{:S(2)}) collective-permute-start(bf16[1024,128]{1,0:T(8,128)(2,1)S(1)} %pad_maximum_fusion.6), channel_id=1, source_target_pairs={{0,128},{16,144},{32,160},{48,176},{64,192},{80,208},{96,224},{112... | collective-permute-start | bytes 786440 | tf_op jit(solution)/shard_map/ppermute | solution.py:29
  11.3 11.3 %collective-permute-start.5 = (bf16[2048,128]{1,0:T(8,128)(2,1)S(1)}, bf16[2048,128]{1,0:T(8,128)(2,1)S(1)}, u32[]{:S(2)}, u32[]{:S(2)}) collective-permute-start(bf16[2048,128]{1,0:T(8,128)(2,1)S(1)} %constant_dynamic-update-slice_fusion.refs_5_), channel_id=1, source_target_pairs={{0,16},{16,0},{32,48},{48,32},{64,80},{80,64},{96,112},{112,96},{1... | collective-permute-start | bytes 1572872 | tf_op jit(solution)/shard_map/ppermute | solution.py:29
  15.7 7.8 %collective-permute-start.6 = (bf16[2048,128]{1,0:T(8,128)(2,1)S(1)}, bf16[2048,128]{1,0:T(8,128)(2,1)}, u32[]{:S(2)}, u32[]{:S(2)}) collective-permute-start(bf16[2048,128]{1,0:T(8,128)(2,1)S(1)} %constant_dynamic-update-slice_fusion.4.refs_6_), channel_id=1, source_target_pairs={{0,16},{16,0},{32,48},{48,32},{64,80},{80,64},{96,112},{112,96},{1... | collective-permute-start | bytes 1572872 | tf_op jit(solution)/shard_map/ppermute | solution.py:29
  26.1 7.2 %collective-permute-start.12 = (bf16[512,128]{1,0:T(8,128)(2,1)S(1)}, bf16[512,128]{1,0:T(8,128)(2,1)S(1)}, u32[]{:S(2)}, u32[]{:S(2)}) collective-permute-start(bf16[512,128]{1,0:T(8,128)(2,1)S(1)} %get-tuple-element.40), channel_id=1, source_target_pairs={{0,1},{1,2},{2,3},{3,4},{4,5},{5,6},{6,7},{7,0},{8,9},{9,10},{10,1... | collective-permute-start | bytes 393224 | tf_op jit(solution)/shard_map/ppermute | solution.py:37
  26.2 7.1 %collective-permute-start.13 = (bf16[512,128]{1,0:T(8,128)(2,1)S(1)}, bf16[512,128]{1,0:T(8,128)(2,1)S(1)}, u32[]{:S(2)}, u32[]{:S(2)}) collective-permute-start(bf16[512,128]{1,0:T(8,128)(2,1)S(1)} %get-tuple-element.42), channel_id=1, source_target_pairs={{0,7},{1,0},{2,1},{3,2},{4,3},{5,4},{6,5},{7,6},{8,15},{9,8},{10,9... | collective-permute-start | bytes 393224 | tf_op jit(solution)/shard_map/ppermute | solution.py:37
  29.0 6.5 %collective-permute-start.15 = (bf16[512,128]{1,0:T(8,128)(2,1)S(1)}, bf16[512,128]{1,0:T(8,128)(2,1)S(1)}, u32[]{:S(2)}, u32[]{:S(2)}) collective-permute-start(bf16[512,128]{1,0:T(8,128)(2,1)S(1)} %get-tuple-element.44), channel_id=1, source_target_pairs={{0,8},{1,9},{2,10},{3,11},{4,12},{5,13},{6,14},{7,15},{8,0},{9,1},... | collective-permute-start | bytes 393224 | tf_op jit(solution)/shard_map/ppermute | solution.py:37
  31.8 13.0 %collective-permute-start.9 = (bf16[1024,128]{1,0:T(8,128)(2,1)S(1)}, bf16[1024,128]{1,0:T(8,128)(2,1)S(1)}, u32[]{:S(2)}, u32[]{:S(2)}) collective-permute-start(bf16[1024,128]{1,0:T(8,128)(2,1)S(1)} %get-tuple-element.36), channel_id=1, source_target_pairs={{0,7},{1,0},{2,1},{3,2},{4,3},{5,4},{6,5},{7,6},{8,15},{9,8},{10,9... | collective-permute-start | bytes 786440 | tf_op jit(solution)/shard_map/ppermute | solution.py:37
  33.2 11.6 %collective-permute-start.10 = (bf16[1024,128]{1,0:T(8,128)(2,1)S(1)}, bf16[1024,128]{1,0:T(8,128)(2,1)S(1)}, u32[]{:S(2)}, u32[]{:S(2)}) collective-permute-start(bf16[1024,128]{1,0:T(8,128)(2,1)S(1)} %get-tuple-element.37), channel_id=1, source_target_pairs={{0,1},{1,2},{2,3},{3,4},{4,5},{5,6},{6,7},{7,0},{8,9},{9,10},{10,1... | collective-permute-start | bytes 786440 | tf_op jit(solution)/shard_map/ppermute | solution.py:37
  33.5 11.4 %collective-permute-start.14 = (bf16[1024,128]{1,0:T(8,128)(2,1)S(1)}, bf16[1024,128]{1,0:T(8,128)(2,1)S(1)}, u32[]{:S(2)}, u32[]{:S(2)}) collective-permute-start(bf16[1024,128]{1,0:T(8,128)(2,1)S(1)} %pad_maximum_fusion.8), channel_id=1, source_target_pairs={{0,8},{1,9},{2,10},{3,11},{4,12},{5,13},{6,14},{7,15},{8,0},{9,1},... | collective-permute-start | bytes 786440 | tf_op jit(solution)/shard_map/ppermute | solution.py:37
  37.7 5.5 %collective-permute-start.16 = (bf16[256,128]{1,0:T(8,128)(2,1)S(1)}, bf16[256,128]{1,0:T(8,128)(2,1)S(1)}, u32[]{:S(2)}, u32[]{:S(2)}) collective-permute-start(bf16[256,128]{1,0:T(8,128)(2,1)S(1)} %get-tuple-element.69), channel_id=1, source_target_pairs={{0,2},{1,3},{2,4},{3,5},{4,6},{5,7},{6,0},{7,1},{8,10},{9,11},{10,... | collective-permute-start | bytes 196616 | tf_op jit(solution)/shard_map/ppermute | solution.py:37
  40.0 9.3 %collective-permute-start.7 = (bf16[512,128]{1,0:T(8,128)(2,1)S(1)}, bf16[512,128]{1,0:T(8,128)(2,1)S(1)}, u32[]{:S(2)}, u32[]{:S(2)}) collective-permute-start(bf16[512,128]{1,0:T(8,128)(2,1)S(1)} %get-tuple-element.33), channel_id=1, source_target_pairs={{0,1},{1,2},{2,3},{3,4},{4,5},{5,6},{6,7},{7,0},{8,9},{9,10},{10,1... | collective-permute-start | bytes 393224 | tf_op jit(solution)/shard_map/ppermute | solution.py:37
  43.2 6.1 %collective-permute-start.8 = (bf16[512,128]{1,0:T(8,128)(2,1)S(1)}, bf16[512,128]{1,0:T(8,128)(2,1)S(1)}, u32[]{:S(2)}, u32[]{:S(2)}) collective-permute-start(bf16[512,128]{1,0:T(8,128)(2,1)S(1)} %get-tuple-element.34), channel_id=1, source_target_pairs={{0,7},{1,0},{2,1},{3,2},{4,3},{5,4},{6,5},{7,6},{8,15},{9,8},{10,9... | collective-permute-start | bytes 393224 | tf_op jit(solution)/shard_map/ppermute | solution.py:37
  45.0 6.3 %collective-permute-start.19 = (bf16[512,128]{1,0:T(8,128)(2,1)S(1)}, bf16[512,128]{1,0:T(8,128)(2,1)S(1)}, u32[]{:S(2)}, u32[]{:S(2)}) collective-permute-start(bf16[512,128]{1,0:T(8,128)(2,1)S(1)} %get-tuple-element.65), channel_id=1, source_target_pairs={{0,6},{1,7},{2,0},{3,1},{4,2},{5,3},{6,4},{7,5},{8,14},{9,15},{10,... | collective-permute-start | bytes 393224 | tf_op jit(solution)/shard_map/ppermute | solution.py:37
  48.0 5.3 %collective-permute-start.11 = (bf16[512,128]{1,0:T(8,128)(2,1)S(1)}, bf16[512,128]{1,0:T(8,128)(2,1)S(1)}, u32[]{:S(2)}, u32[]{:S(2)}) collective-permute-start(bf16[512,128]{1,0:T(8,128)(2,1)S(1)} %get-tuple-element.66), channel_id=1, source_target_pairs={{0,8},{1,9},{2,10},{3,11},{4,12},{5,13},{6,14},{7,15},{8,0},{9,1},... | collective-permute-start | bytes 393224 | tf_op jit(solution)/shard_map/ppermute | solution.py:37
  48.4 6.5 %collective-permute-start.17 = (bf16[512,128]{1,0:T(8,128)(2,1)S(1)}, bf16[512,128]{1,0:T(8,128)(2,1)S(1)}, u32[]{:S(2)}, u32[]{:S(2)}) collective-permute-start(bf16[512,128]{1,0:T(8,128)(2,1)S(1)} %get-tuple-element.67), channel_id=1, source_target_pairs={{0,2},{1,3},{2,4},{3,5},{4,6},{5,7},{6,0},{7,1},{8,10},{9,11},{10,... | collective-permute-start | bytes 393224 | tf_op jit(solution)/shard_map/ppermute | solution.py:37
  56.1 5.8 %collective-permute-start.20 = (f32[128,128]{1,0:T(8,128)S(1)}, f32[128,128]{1,0:T(8,128)S(1)}, u32[]{:S(2)}, u32[]{:S(2)}) collective-permute-start(f32[128,128]{1,0:T(8,128)S(1)} %get-tuple-element.49), channel_id=1, source_target_pairs={{0,16},{16,0},{32,48},{48,32},{64,80},{80,64},{96,112},{112,96},{1... | collective-permute-start | bytes 196616 | tf_op jit(solution)/shard_map/ppermute | solution.py:29
  62.0 10.1 %collective-permute-start.23 = (bf16[640,128]{1,0:T(8,128)(2,1)S(1)}, bf16[640,128]{1,0:T(8,128)(2,1)S(1)}, u32[]{:S(2)}, u32[]{:S(2)}) collective-permute-start(bf16[640,128]{1,0:T(8,128)(2,1)S(1)} %pad_maximum_fusion.10.refs_5_), channel_id=1, source_target_pairs={{0,6},{1,7},{2,0},{3,1},{4,2},{5,3},{6,4},{7,5},{8,14},{9,15},{10,... | collective-permute-start | bytes 491528 | tf_op jit(solution)/shard_map/ppermute | solution.py:37
  62.1 12.2 %collective-permute-start.22 = (bf16[640,128]{1,0:T(8,128)(2,1)S(1)}, bf16[640,128]{1,0:T(8,128)(2,1)S(1)}, u32[]{:S(2)}, u32[]{:S(2)}) collective-permute-start(bf16[640,128]{1,0:T(8,128)(2,1)S(1)} %pad_maximum_fusion.10.refs_5_), channel_id=1, source_target_pairs={{0,2},{1,3},{2,4},{3,5},{4,6},{5,7},{6,0},{7,1},{8,10},{9,11},{10,... | collective-permute-start | bytes 491528 | tf_op jit(solution)/shard_map/ppermute | solution.py:37
  64.4 14.3 %collective-permute-start.21 = (bf16[640,128]{1,0:T(8,128)(2,1)S(1)}, bf16[640,128]{1,0:T(8,128)(2,1)S(1)}, u32[]{:S(2)}, u32[]{:S(2)}) collective-permute-start(bf16[640,128]{1,0:T(8,128)(2,1)S(1)} %pad_maximum_fusion.10.refs_5_), channel_id=1, source_target_pairs={{0,8},{1,9},{2,10},{3,11},{4,12},{5,13},{6,14},{7,15},{8,0},{9,1},... | collective-permute-start | bytes 491528 | tf_op jit(solution)/shard_map/ppermute | solution.py:37
  74.3 6.1 %collective-permute-start.25 = (bf16[640,128]{1,0:T(8,128)(2,1)S(1)}, bf16[640,128]{1,0:T(8,128)(2,1)S(1)}, u32[]{:S(2)}, u32[]{:S(2)}) collective-permute-start(bf16[640,128]{1,0:T(8,128)(2,1)S(1)} %broadcast_select_fusion), channel_id=1, source_target_pairs={{0,2},{1,3},{2,4},{3,5},{4,6},{5,7},{6,0},{7,1},{8,10},{9,11},{10,... | collective-permute-start | bytes 491528 | tf_op jit(solution)/shard_map/ppermute | solution.py:47
  76.8 10.5 %collective-permute-start.24 = (bf16[1280,128]{1,0:T(8,128)(2,1)S(1)}, bf16[1280,128]{1,0:T(8,128)(2,1)S(1)}, u32[]{:S(2)}, u32[]{:S(2)}) collective-permute-start(bf16[1280,128]{1,0:T(8,128)(2,1)S(1)} %pad_maximum_fusion.5), channel_id=1, source_target_pairs={{0,8},{1,9},{2,10},{3,11},{4,12},{5,13},{6,14},{7,15},{8,0},{9,1},... | collective-permute-start | bytes 983048 | tf_op jit(solution)/shard_map/ppermute | solution.py:37
  78.8 16.2 %collective-permute-start.27 = (bf16[1920,128]{1,0:T(8,128)(2,1)S(1)}, bf16[1920,128]{1,0:T(8,128)(2,1)S(1)}, u32[]{:S(2)}, u32[]{:S(2)}) collective-permute-start(bf16[1920,128]{1,0:T(8,128)(2,1)S(1)} %get-tuple-element.61), channel_id=1, source_target_pairs={{0,7},{1,0},{2,1},{3,2},{4,3},{5,4},{6,5},{7,6},{8,15},{9,8},{10,9... | collective-permute-start | bytes 1474568 | tf_op jit(solution)/shard_map/ppermute | solution.py:37
  78.9 16.2 %collective-permute-start.26 = (bf16[1920,128]{1,0:T(8,128)(2,1)S(1)}, bf16[1920,128]{1,0:T(8,128)(2,1)S(1)}, u32[]{:S(2)}, u32[]{:S(2)}) collective-permute-start(bf16[1920,128]{1,0:T(8,128)(2,1)S(1)} %get-tuple-element.62), channel_id=1, source_target_pairs={{0,1},{1,2},{2,3},{3,4},{4,5},{5,6},{6,7},{7,0},{8,9},{9,10},{10,1... | collective-permute-start | bytes 1474568 | tf_op jit(solution)/shard_map/ppermute | solution.py:37
  80.4 10.2 %collective-permute-start.30 = (bf16[640,128]{1,0:T(8,128)(2,1)S(1)}, bf16[640,128]{1,0:T(8,128)(2,1)S(1)}, u32[]{:S(2)}, u32[]{:S(2)}) collective-permute-start(bf16[640,128]{1,0:T(8,128)(2,1)S(1)} %collective-permute-done.25.refs_10_), channel_id=1, source_target_pairs={{0,8},{1,9},{2,10},{3,11},{4,12},{5,13},{6,14},{7,15},{8,0},{9,1},... | collective-permute-start | bytes 491528 | tf_op jit(solution)/shard_map/ppermute | solution.py:37
  87.4 7.0 %collective-permute-start.29 = (bf16[640,128]{1,0:T(8,128)(2,1)S(1)}, bf16[640,128]{1,0:T(8,128)(2,1)S(1)}, u32[]{:S(2)}, u32[]{:S(2)}) collective-permute-start(bf16[640,128]{1,0:T(8,128)(2,1)S(1)} %get-tuple-element.59), channel_id=1, source_target_pairs={{0,7},{1,0},{2,1},{3,2},{4,3},{5,4},{6,5},{7,6},{8,15},{9,8},{10,9... | collective-permute-start | bytes 491528 | tf_op jit(solution)/shard_map/ppermute | solution.py:37
  87.5 7.6 %collective-permute-start.28 = (bf16[640,128]{1,0:T(8,128)(2,1)S(1)}, bf16[640,128]{1,0:T(8,128)(2,1)S(1)}, u32[]{:S(2)}, u32[]{:S(2)}) collective-permute-start(bf16[640,128]{1,0:T(8,128)(2,1)S(1)} %get-tuple-element.60), channel_id=1, source_target_pairs={{0,1},{1,2},{2,3},{3,4},{4,5},{5,6},{6,7},{7,0},{8,9},{9,10},{10,1... | collective-permute-start | bytes 491528 | tf_op jit(solution)/shard_map/ppermute | solution.py:37
  101.2 8.3 %collective-permute-start.35 = (bf16[1152,128]{1,0:T(8,128)(2,1)S(1)}, bf16[1152,128]{1,0:T(8,128)(2,1)S(1)}, u32[]{:S(2)}, u32[]{:S(2)}) collective-permute-start(bf16[1152,128]{1,0:T(8,128)(2,1)S(1)} %get-tuple-element.70), channel_id=1, source_target_pairs={{0,32},{16,48},{32,0},{48,16},{64,96},{80,112},{96,64},{112,80},{1... | collective-permute-start | bytes 884744 | tf_op jit(solution)/shard_map/ppermute | solution.py:29
  102.6 9.6 %collective-permute-start.33 = (bf16[1152,128]{1,0:T(8,128)(2,1)S(1)}, bf16[1152,128]{1,0:T(8,128)(2,1)S(1)}, u32[]{:S(2)}, u32[]{:S(2)}) collective-permute-start(bf16[1152,128]{1,0:T(8,128)(2,1)S(1)} %get-tuple-element.71), channel_id=1, source_target_pairs={{0,128},{16,144},{32,160},{48,176},{64,192},{80,208},{96,224},{112... | collective-permute-start | bytes 884744 | tf_op jit(solution)/shard_map/ppermute | solution.py:29
  109.6 4.8 %collective-permute-start.37 = (bf16[640,128]{1,0:T(8,128)(2,1)S(1)}, bf16[640,128]{1,0:T(8,128)(2,1)S(1)}, u32[]{:S(2)}, u32[]{:S(2)}) collective-permute-start(bf16[640,128]{1,0:T(8,128)(2,1)S(1)} %pad_maximum_fusion.12), channel_id=1, source_target_pairs={{0,192},{16,208},{32,224},{48,240},{64,0},{80,16},{96,32},{112,48}... | collective-permute-start | bytes 491528 | tf_op jit(solution)/shard_map/ppermute | solution.py:29
  112.2 6.2 %collective-permute-start.36 = (bf16[768,128]{1,0:T(8,128)(2,1)S(1)}, bf16[768,128]{1,0:T(8,128)(2,1)S(1)}, u32[]{:S(2)}, u32[]{:S(2)}) collective-permute-start(bf16[768,128]{1,0:T(8,128)(2,1)S(1)} %pad_maximum_fusion.9), channel_id=1, source_target_pairs={{0,64},{16,80},{32,96},{48,112},{64,128},{80,144},{96,160},{112,17... | collective-permute-start | bytes 589832 | tf_op jit(solution)/shard_map/ppermute | solution.py:29
  (13 other events, 121.5 us)
